TPU v7x, 128 devices: a whole 4x4x4 slice. The times are simulated.
128 devices in a mesh: seq: 4 (over z), fsdp: 32 (over y, x, core).
Axes of the slice: x: 4, y: 4, z: 4, core: 2. Of those that a mesh axis runs over, the one named last changes fastest.
Arguments:
- tokens_in: bfloat16 [32, 512, 1536], P('fsdp', 'seq'), may hold values from -6 to 6
- cotangent: bfloat16 [32, 512, 1536], P('fsdp', 'seq'), may hold values from -6 to 6
- routes: int32 [2, 32, 512, 4], P(None, 'fsdp', 'seq'), may hold values from 0 to 7, all different within a row
- order: int32 [2, 32, 512, 4], P(None, 'fsdp', 'seq'), may hold values from 0 to 511, as said below
- segment_ids: int32 [32, 256], P('fsdp'), may hold values from 0 to 3, never falling along the last dimension, each value on 1 to 128 neighbouring positions
- gain_attn: bfloat16 [2, 1536], P(None, ('seq', 'fsdp')), may hold values from 0.5 to 1.5
- w_query: bfloat16 [2, 1536, 1536], P(None, ('seq', 'fsdp')), may hold values from -0.15625 to 0.15625
- w_key: bfloat16 [2, 1536, 256], P(None, ('seq', 'fsdp')), may hold values from -0.15625 to 0.15625
- w_value: bfloat16 [2, 1536, 256], P(None, ('seq', 'fsdp')), may hold values from -0.15625 to 0.15625
- w_out: bfloat16 [2, 1536, 1536], P(None, ('seq', 'fsdp')), may hold values from -0.625 to 0.625
- gain_ffn: bfloat16 [2, 1536], P(None, ('seq', 'fsdp')), may hold values from 0.5 to 1.5
- w_router: bfloat16 [2, 1536, 8], P(None, ('seq', 'fsdp')), may hold values from -0.078125 to 0.078125
- w_gate: bfloat16 [2, 8, 1536, 768], P(None, 'seq', 'fsdp'), may hold values from -0.15625 to 0.15625
- w_up: bfloat16 [2, 8, 1536, 768], P(None, 'seq', 'fsdp'), may hold values from -0.15625 to 0.15625
- w_down: bfloat16 [2, 8, 768, 1536], P(None, 'seq', 'fsdp'), may hold values from -0.4375 to 0.4375
Outputs:
- result: bfloat16 [32, 512, 1536], P('fsdp', 'seq')
- grad_tokens: float32 [32, 512, 1536], P('fsdp', 'seq')
- grad_gain_attn: float32 [2, 1536], P(None, ('seq', 'fsdp'))
- grad_w_query: float32 [2, 1536, 1536], P(None, ('seq', 'fsdp'))
- grad_w_key: float32 [2, 1536, 256], P(None, ('seq', 'fsdp'))
- grad_w_value: float32 [2, 1536, 256], P(None, ('seq', 'fsdp'))
- grad_w_out: float32 [2, 1536, 1536], P(None, ('seq', 'fsdp'))
- grad_gain_ffn: float32 [2, 1536], P(None, ('seq', 'fsdp'))
- grad_w_router: float32 [2, 1536, 8], P(None, ('seq', 'fsdp'))
- grad_w_gate: float32 [2, 8, 1536, 768], P(None, 'seq', 'fsdp')
- grad_w_up: float32 [2, 8, 1536, 768], P(None, 'seq', 'fsdp')
- grad_w_down: float32 [2, 8, 768, 1536], P(None, 'seq', 'fsdp')
Inputs may be any that keep to these rules, and one draw needn't show every extreme that they name: `routes`: each token names 4 different experts in each layer. `order`: in each layer, the 512 entries of an aligned block of 128 tokens hold each of 0 to 511 once. `segment_ids`: in each row the numbers never fall, each of 0 to 3 stands on 1 to 128 places, one on exactly 128.
All inputs are finite; a program needn't handle non-finite values.
Results may differ from a plain program's by a relative error of at most 0.028.
Values may be sent and summed in bfloat16 or wider, within the bound.
No kernel may reach another device: no remote copies, remote signals or barrier semaphores. Data moves between devices by JAX's collectives and lax.ppermute only.
A program may use at most 320 MiB of HBM per device.

v0:
```python
import jax
import jax.numpy as jnp
import numpy as np
from jax import lax
from jax.sharding import PartitionSpec as P

HEADS = 12
KVHEADS = 2
HD = 128
TOPK = 4
LAYERS = 2
NCONT = 4


norm_eps = 1e-06
rope_base = 10000.0
masked_value = -1e30


def for_sending(array):

    def short(part):
        return part.astype(jnp.bfloat16) if part.dtype == jnp.float32 else part

    return jax.tree.map(short, array)


def rms_scale(values, gain):
    inverse = lax.rsqrt(jnp.mean(values * values, axis=-1, keepdims=True) + norm_eps)
    return values * inverse * gain


def rotary(values, cosines, sines):
    half_width = values.shape[-1] // 2
    first_half = values[..., :half_width]
    second = values[..., half_width:]
    return jnp.concatenate(
        [first_half * cosines - second * sines, second * cosines + first_half * sines], axis=-1
    )


def smooth_gate(values):
    return jax.nn.gelu(values, approximate=True)


def contract_rows(left, right):
    return lax.dot_general(
        left, right, (((0,), (0,)), ((), ())), preferred_element_type=jnp.float32
    )


def contract_cols(left, right):
    return lax.dot_general(
        left, right, (((1,), (1,)), ((), ())), preferred_element_type=jnp.float32
    )


def group_tables(segment_row, prompt_len):
    cont_len = segment_row.shape[0]
    onehot = (segment_row[:, None] == jnp.arange(NCONT, dtype=jnp.int32)[None, :]).astype(jnp.int32)
    counts = jnp.sum(onehot, axis=0)
    starts = jnp.cumsum(counts) - counts
    seg_begin = jnp.sum(onehot * starts[None, :], axis=1)
    within = jnp.arange(cont_len, dtype=jnp.int32) - seg_begin
    positions = jnp.concatenate([jnp.arange(prompt_len, dtype=jnp.int32), prompt_len + within])
    labels = jnp.concatenate([jnp.full((prompt_len,), -1, jnp.int32), segment_row])
    frequency = rope_base ** (-(jnp.arange(HD // 2, dtype=jnp.float32) * 2.0 / HD))
    angles = positions.astype(jnp.float32)[:, None] * frequency[None, :]
    return (jnp.cos(angles), jnp.sin(angles), labels)


def route_tables(expert_rows, order_rows, expert_count, capacity):
    pair_expert = expert_rows.reshape(-1)
    pair_order = order_rows.reshape(-1)
    same_expert = pair_expert[:, None] == pair_expert[None, :]
    earlier = pair_order[None, :] < pair_order[:, None]
    pair_slot = jnp.sum(jnp.logical_and(same_expert, earlier).astype(jnp.int32), axis=1)
    total_slots = expert_count * capacity
    target = jnp.where(pair_slot < capacity, pair_expert * capacity + pair_slot, total_slots)
    pair_index = jnp.arange(pair_expert.shape[0], dtype=jnp.int32)
    slot_pair = jnp.zeros((total_slots + 1,), jnp.int32).at[target].set(pair_index)[:total_slots]
    slot_filled = jnp.zeros((total_slots + 1,), jnp.bool_).at[target].set(True)[:total_slots]
    route_hot = (
        expert_rows[:, :, None] == jnp.arange(expert_count, dtype=jnp.int32)[None, None, :]
    ).astype(jnp.float32)
    return (target, slot_pair, slot_filled, route_hot)


def per_device(
    tokens_in,
    cotangent,
    routes,
    order,
    segment_ids,
    gain_attn,
    w_query,
    w_key,
    w_value,
    w_out,
    gain_ffn,
    w_router,
    w_gate,
    w_up,
    w_down,
):
    tok_count = tokens_in.shape[1]
    width = tokens_in.shape[2]
    seq_count = lax.axis_size("seq")
    seq_index = lax.axis_index("seq")
    group_tok = seq_count * tok_count
    prompt_len = group_tok - segment_ids.shape[1]
    local_experts = w_gate.shape[1]
    expert_count = local_experts * seq_count
    capacity = 9 * tok_count * TOPK // (8 * expert_count)
    total_slots = expert_count * capacity
    head_local = HEADS // seq_count
    local_width = head_local * HD
    scale = HD ** (-0.5)
    block_rows = min(512, group_tok)
    block_total = group_tok // block_rows
    cos_all, sin_all, labels = group_tables(segment_ids[0], prompt_len)
    cos_own = lax.dynamic_slice_in_dim(cos_all, seq_index * tok_count, tok_count, 0)[:, None, :]
    sin_own = lax.dynamic_slice_in_dim(sin_all, seq_index * tok_count, tok_count, 0)[:, None, :]
    kv_pick = np.arange(seq_count) * KVHEADS // seq_count
    key_pos = jnp.arange(group_tok, dtype=jnp.int32)

    def fetch(layer_index):
        dense = (
            lax.all_gather(gain_attn[layer_index], ("seq", "fsdp"), axis=0, tiled=True),
            lax.all_gather(w_query[layer_index], ("seq", "fsdp"), axis=0, tiled=True),
            lax.all_gather(w_key[layer_index], ("seq", "fsdp"), axis=0, tiled=True),
            lax.all_gather(w_value[layer_index], ("seq", "fsdp"), axis=0, tiled=True),
            lax.all_gather(w_out[layer_index], ("seq", "fsdp"), axis=0, tiled=True),
            lax.all_gather(gain_ffn[layer_index], ("seq", "fsdp"), axis=0, tiled=True),
            lax.all_gather(w_router[layer_index], ("seq", "fsdp"), axis=0, tiled=True),
        )
        experts = (
            lax.all_gather(w_gate[layer_index], "fsdp", axis=1, tiled=True),
            lax.all_gather(w_up[layer_index], "fsdp", axis=1, tiled=True),
            lax.all_gather(w_down[layer_index], "fsdp", axis=1, tiled=True),
        )
        return (dense, experts)

    def masked_scores(query_block, key_heads, start):
        raw = (
            jnp.einsum("qhd,kd->hqk", query_block, key_heads, preferred_element_type=jnp.float32)
            * scale
        )
        query_pos = start + jnp.arange(block_rows, dtype=jnp.int32)
        allowed = jnp.logical_and(
            key_pos[None, :] <= query_pos[:, None],
            jnp.logical_or(key_pos[None, :] < prompt_len, labels[None, :] == labels[:, None]),
        )
        return jnp.where(allowed[None], raw, masked_value)

    def attention_backward(query_heads, key_heads, value_heads, lse_rows, grad_heads):

        def one_block(carry, block_index):
            grad_key, grad_value = carry
            start = block_index * block_rows
            scores = masked_scores(query_heads, key_heads, start)
            soft = jnp.exp(scores - lse_rows[block_index][..., None])
            grad_soft = jnp.einsum(
                "qhd,kd->hqk", grad_heads, value_heads, preferred_element_type=jnp.float32
            )
            center = jnp.sum(soft * grad_soft, axis=-1, keepdims=True)
            grad_scores = (soft * (grad_soft - center)).astype(jnp.bfloat16)
            grad_query = (
                jnp.einsum(
                    "hqk,kd->qhd", grad_scores, key_heads, preferred_element_type=jnp.float32
                )
                * scale
            )
            grad_key = (
                grad_key
                + jnp.einsum(
                    "hqk,qhd->kd", grad_scores, query_heads, preferred_element_type=jnp.float32
                )
                * scale
            )
            grad_value = grad_value + jnp.einsum(
                "hqk,qhd->kd",
                soft.astype(jnp.bfloat16),
                grad_heads,
                preferred_element_type=jnp.float32,
            )
            return ((grad_key, grad_value), grad_query)

        zero_rows = jnp.zeros((group_tok, HD), jnp.float32)
        (grad_key, grad_value), grad_query = lax.scan(
            one_block, (zero_rows, zero_rows), jnp.arange(block_total)
        )
        return (grad_query.reshape(group_tok, local_width), grad_key, grad_value)

    hidden = tokens_in[0].astype(jnp.float32)
    records = []
    for layer_index in range(LAYERS):
        dense, experts = fetch(layer_index)
        routing = route_tables(
            routes[layer_index, 0], order[layer_index, 0], expert_count, capacity
        )
        (
            forward_gain_norm,
            forward_query_w,
            forward_key_w,
            forward_value_w,
            forward_out_w,
            forward_gain_mix,
            forward_router_w,
        ) = dense
        forward_gate_w, forward_up_w, forward_down_w = experts
        forward_target, forward_slot_pair, forward_slot_filled, forward_route_hot = routing
        forward_normed = rms_scale(hidden, forward_gain_norm.astype(jnp.float32)).astype(
            jnp.bfloat16
        )
        query_raw = jnp.dot(forward_normed, forward_query_w, preferred_element_type=jnp.float32)
        key_raw = jnp.dot(forward_normed, forward_key_w, preferred_element_type=jnp.float32)
        value_raw = jnp.dot(forward_normed, forward_value_w, preferred_element_type=jnp.float32)
        queries = rotary(query_raw.reshape(tok_count, HEADS, HD), cos_own, sin_own).astype(
            jnp.bfloat16
        )
        key_rows = rotary(key_raw.reshape(tok_count, KVHEADS, HD), cos_own, sin_own).astype(
            jnp.bfloat16
        )
        value_rows = value_raw.astype(jnp.bfloat16).reshape(tok_count, KVHEADS, HD)
        pair_send = jnp.concatenate([key_rows[:, kv_pick], value_rows[:, kv_pick]], axis=-1)
        query_send = queries.reshape(tok_count, seq_count, local_width)
        forward_query_heads = lax.all_to_all(
            query_send, "seq", split_axis=1, concat_axis=0, tiled=True
        )
        pair_heads = lax.all_to_all(pair_send, "seq", split_axis=1, concat_axis=0, tiled=True)
        forward_query_heads = forward_query_heads.reshape(group_tok, head_local, HD)
        forward_key_heads = pair_heads[:, 0, :HD]
        forward_value_heads = pair_heads[:, 0, HD:]
        attention_query_heads = forward_query_heads
        attention_key_heads = forward_key_heads
        attention_value_heads = forward_value_heads

        def attention_one_block(block_index):
            start = block_index * block_rows
            scores = masked_scores(attention_query_heads, attention_key_heads, start)
            row_peak = jnp.max(scores, axis=-1, keepdims=True)
            exponent = jnp.exp(scores - row_peak)
            row_total = jnp.sum(exponent, axis=-1, keepdims=True)
            weights_low = (exponent / row_total).astype(jnp.bfloat16)
            attended = jnp.einsum(
                "hqk,kd->qhd",
                weights_low,
                attention_value_heads,
                preferred_element_type=jnp.float32,
            )
            return (attended.astype(jnp.bfloat16), (row_peak + jnp.log(row_total))[..., 0])

        outputs, attention_lse_rows = lax.map(attention_one_block, jnp.arange(block_total))
        forward_attended = outputs.reshape(group_tok, local_width)
        returned_heads = lax.all_to_all(
            for_sending(forward_attended.reshape(seq_count, tok_count, 1, local_width)),
            "seq",
            split_axis=0,
            concat_axis=2,
            tiled=True,
        )
        forward_attn_tok = returned_heads.reshape(tok_count, HEADS * HD)
        forward_middle = hidden + jnp.dot(
            forward_attn_tok, forward_out_w, preferred_element_type=jnp.float32
        )
        forward_normed_ffn = rms_scale(forward_middle, forward_gain_mix.astype(jnp.float32)).astype(
            jnp.bfloat16
        )
        logits = jnp.dot(forward_normed_ffn, forward_router_w, preferred_element_type=jnp.float32)
        chosen = jnp.sum(forward_route_hot * logits[:, None, :], axis=-1)
        forward_gate_weights = jax.nn.softmax(chosen, axis=-1)
        forward_slot_token = forward_slot_pair // TOPK
        send_rows = jnp.where(
            forward_slot_filled[:, None],
            forward_normed_ffn[forward_slot_token],
            jnp.zeros((), jnp.bfloat16),
        )
        forward_received = lax.all_to_all(
            send_rows.reshape(seq_count, local_experts, capacity, width),
            "seq",
            split_axis=0,
            concat_axis=0,
            tiled=True,
        )
        forward_gate_val = jnp.einsum(
            "secd,edf->secf", forward_received, forward_gate_w, preferred_element_type=jnp.float32
        )
        forward_up_val = jnp.einsum(
            "secd,edf->secf", forward_received, forward_up_w, preferred_element_type=jnp.float32
        )
        forward_inner_act = (smooth_gate(forward_gate_val) * forward_up_val).astype(jnp.bfloat16)
        expert_out = jnp.einsum(
            "secf,efd->secd", forward_inner_act, forward_down_w, preferred_element_type=jnp.float32
        ).astype(jnp.bfloat16)
        combined = lax.all_to_all(expert_out, "seq", split_axis=0, concat_axis=0, tiled=True)
        flat_out = jnp.concatenate(
            [combined.reshape(total_slots, width), jnp.zeros((1, width), jnp.bfloat16)], axis=0
        )
        forward_pair_out = flat_out[forward_target].reshape(tok_count, TOPK, width)
        mixture = jnp.sum(
            forward_gate_weights[:, :, None] * forward_pair_out.astype(jnp.float32), axis=1
        )
        forward_saved = (
            hidden,
            forward_normed,
            forward_query_heads,
            forward_key_heads,
            forward_value_heads,
            attention_lse_rows,
            forward_attn_tok,
            forward_middle,
            forward_normed_ffn,
            forward_gate_weights,
            forward_pair_out,
            forward_received,
            forward_gate_val,
            forward_up_val,
            forward_inner_act,
        )
        hidden = forward_middle + mixture
        saved = forward_saved
        records.append((dense, experts, routing, saved))
    result = hidden.astype(jnp.bfloat16)[None]
    grad_hidden = cotangent[0].astype(jnp.float32)
    layer_grads = [None] * LAYERS
    for layer_index in range(LAYERS - 1, -1, -1):
        dense, experts, routing, saved = records[layer_index]
        dense, experts = fetch(layer_index)
        gain_norm, query_w, key_w, value_w, out_w, gain_mix, router_w = dense
        gate_w, up_w, down_w = experts
        target, slot_pair, slot_filled, route_hot = routing
        (
            backward_hidden,
            normed,
            backward_query_heads,
            backward_key_heads,
            backward_value_heads,
            backward_lse_rows,
            attn_tok,
            middle,
            normed_ffn,
            gate_weights,
            pair_out,
            received,
            gate_val,
            up_val,
            inner_act,
        ) = saved
        grad_gates = jnp.sum(pair_out.astype(jnp.float32) * grad_hidden[:, None, :], axis=-1)
        gate_flat = gate_weights.reshape(-1)
        slot_token = slot_pair // TOPK
        grad_slots = jnp.where(
            slot_filled[:, None], gate_flat[slot_pair][:, None] * grad_hidden[slot_token], 0.0
        ).astype(jnp.bfloat16)
        grad_expert = lax.all_to_all(
            grad_slots.reshape(seq_count, local_experts, capacity, width),
            "seq",
            split_axis=0,
            concat_axis=0,
            tiled=True,
        )
        grad_inner = jnp.einsum(
            "secd,efd->secf", grad_expert, down_w, preferred_element_type=jnp.float32
        )
        grad_down = jnp.einsum(
            "secf,secd->efd", inner_act, grad_expert, preferred_element_type=jnp.float32
        )
        activated, gate_back = jax.vjp(smooth_gate, gate_val)
        grad_gate_val = gate_back(grad_inner * up_val)[0].astype(jnp.bfloat16)
        grad_up_val = (grad_inner * activated).astype(jnp.bfloat16)
        grad_gate = jnp.einsum(
            "secd,secf->edf", received, grad_gate_val, preferred_element_type=jnp.float32
        )
        grad_up = jnp.einsum(
            "secd,secf->edf", received, grad_up_val, preferred_element_type=jnp.float32
        )
        grad_rows = jnp.einsum(
            "secf,edf->secd", grad_gate_val, gate_w, preferred_element_type=jnp.float32
        )
        grad_rows = (
            grad_rows
            + jnp.einsum("secf,edf->secd", grad_up_val, up_w, preferred_element_type=jnp.float32)
        ).astype(jnp.bfloat16)
        grad_sent = lax.all_to_all(grad_rows, "seq", split_axis=0, concat_axis=0, tiled=True)
        flat_grad = jnp.concatenate(
            [grad_sent.reshape(total_slots, width), jnp.zeros((1, width), jnp.bfloat16)], axis=0
        )
        grad_normed_ffn = jnp.sum(
            flat_grad[target].reshape(tok_count, TOPK, width).astype(jnp.float32), axis=1
        )
        grad_chosen = gate_weights * (
            grad_gates - jnp.sum(gate_weights * grad_gates, axis=-1, keepdims=True)
        )
        grad_logits = jnp.sum(route_hot * grad_chosen[:, :, None], axis=1).astype(jnp.bfloat16)
        grad_router = contract_rows(normed_ffn, grad_logits)
        grad_normed_ffn = grad_normed_ffn + contract_cols(grad_logits, router_w)
        normed_again, norm_back = jax.vjp(rms_scale, middle, gain_mix.astype(jnp.float32))
        grad_middle_part, grad_gain_mix = norm_back(grad_normed_ffn)
        grad_middle = grad_hidden + grad_middle_part
        grad_branch = grad_middle.astype(jnp.bfloat16)
        grad_out_w = contract_rows(attn_tok, grad_branch)
        grad_attn = contract_cols(grad_branch, out_w).astype(jnp.bfloat16)
        backward_grad_heads = lax.all_to_all(
            grad_attn.reshape(tok_count, seq_count, local_width),
            "seq",
            split_axis=1,
            concat_axis=0,
            tiled=True,
        )
        backward_grad_query, backward_grad_key, backward_grad_value = attention_backward(
            backward_query_heads,
            backward_key_heads,
            backward_value_heads,
            backward_lse_rows,
            backward_grad_heads.reshape(group_tok, head_local, HD),
        )
        grad_pair_heads = jnp.concatenate([backward_grad_key, backward_grad_value], axis=-1)
        grad_query_tok = lax.all_to_all(
            backward_grad_query.reshape(seq_count, tok_count, 1, local_width).astype(jnp.bfloat16),
            "seq",
            split_axis=0,
            concat_axis=2,
            tiled=True,
        ).astype(jnp.float32)
        grad_pair_tok = lax.all_to_all(
            grad_pair_heads.reshape(seq_count, tok_count, 1, 2 * HD).astype(jnp.bfloat16),
            "seq",
            split_axis=0,
            concat_axis=2,
            tiled=True,
        ).astype(jnp.float32)
        grad_pair = jnp.sum(
            grad_pair_tok.reshape(tok_count, KVHEADS, seq_count // KVHEADS, 2 * HD), axis=2
        )
        grad_query_raw = (
            rotary(grad_query_tok.reshape(tok_count, HEADS, HD), cos_own, -sin_own)
            .reshape(tok_count, HEADS * HD)
            .astype(jnp.bfloat16)
        )
        grad_key_raw = (
            rotary(grad_pair[:, :, :HD], cos_own, -sin_own)
            .reshape(tok_count, KVHEADS * HD)
            .astype(jnp.bfloat16)
        )
        grad_value_raw = grad_pair[:, :, HD:].reshape(tok_count, KVHEADS * HD).astype(jnp.bfloat16)
        grad_key_w = contract_rows(normed, grad_key_raw)
        grad_value_w = contract_rows(normed, grad_value_raw)
        grad_normed = (
            contract_cols(grad_query_raw, query_w)
            + contract_cols(grad_key_raw, key_w)
            + contract_cols(grad_value_raw, value_w)
        )
        normed_first, norm_back_attn = jax.vjp(
            rms_scale, backward_hidden, gain_norm.astype(jnp.float32)
        )
        grad_hidden_part, grad_gain_norm = norm_back_attn(grad_normed)
        grad_query_w = contract_rows(normed, grad_query_raw)
        dense_grads = (
            lax.psum_scatter(grad_gain_norm, ("seq", "fsdp"), scatter_dimension=0, tiled=True),
            lax.psum_scatter(grad_query_w, ("seq", "fsdp"), scatter_dimension=0, tiled=True),
            lax.psum_scatter(grad_key_w, ("seq", "fsdp"), scatter_dimension=0, tiled=True),
            lax.psum_scatter(grad_value_w, ("seq", "fsdp"), scatter_dimension=0, tiled=True),
            lax.psum_scatter(grad_out_w, ("seq", "fsdp"), scatter_dimension=0, tiled=True),
            lax.psum_scatter(grad_gain_mix, ("seq", "fsdp"), scatter_dimension=0, tiled=True),
            lax.psum_scatter(grad_router, ("seq", "fsdp"), scatter_dimension=0, tiled=True),
        )
        expert_grads = (
            lax.psum_scatter(
                grad_gate.astype(jnp.bfloat16), "fsdp", scatter_dimension=1, tiled=True
            ).astype(jnp.float32),
            lax.psum_scatter(
                grad_up.astype(jnp.bfloat16), "fsdp", scatter_dimension=1, tiled=True
            ).astype(jnp.float32),
            lax.psum_scatter(
                grad_down.astype(jnp.bfloat16), "fsdp", scatter_dimension=1, tiled=True
            ).astype(jnp.float32),
        )
        grad_hidden, layer_grads[layer_index] = (
            grad_middle + grad_hidden_part,
            tuple(dense_grads) + tuple(expert_grads),
        )
    grad_columns = [
        jnp.stack([layer_grads[layer_index][member] for layer_index in range(LAYERS)])
        for member in range(10)
    ]
    return (
        result,
        grad_hidden[None],
        grad_columns[0],
        grad_columns[1],
        grad_columns[2],
        grad_columns[3],
        grad_columns[4],
        grad_columns[5],
        grad_columns[6],
        grad_columns[7],
        grad_columns[8],
        grad_columns[9],
    )


def solution(mesh):
    in_specs = (
        P("fsdp", "seq", None),
        P("fsdp", "seq", None),
        P(None, "fsdp", "seq", None),
        P(None, "fsdp", "seq", None),
        P("fsdp", None),
        P(None, ("seq", "fsdp")),
        P(None, ("seq", "fsdp"), None),
        P(None, ("seq", "fsdp"), None),
        P(None, ("seq", "fsdp"), None),
        P(None, ("seq", "fsdp"), None),
        P(None, ("seq", "fsdp")),
        P(None, ("seq", "fsdp"), None),
        P(None, "seq", "fsdp", None),
        P(None, "seq", "fsdp", None),
        P(None, "seq", "fsdp", None),
    )
    out_specs = (
        P("fsdp", "seq", None),
        P("fsdp", "seq", None),
        P(None, ("seq", "fsdp")),
        P(None, ("seq", "fsdp"), None),
        P(None, ("seq", "fsdp"), None),
        P(None, ("seq", "fsdp"), None),
        P(None, ("seq", "fsdp"), None),
        P(None, ("seq", "fsdp")),
        P(None, ("seq", "fsdp"), None),
        P(None, "seq", "fsdp", None),
        P(None, "seq", "fsdp", None),
        P(None, "seq", "fsdp", None),
    )
    return jax.shard_map(
        per_device, mesh=mesh, in_specs=in_specs, out_specs=out_specs, check_vma=False
    )
```

profile of v0, /device:TPU:0, one launch (start us, length us, event | category | flops | bytes accessed | tf_op | source)
XLA Modules:
  0.0 2701.3 jit_solution(14396794947783748735)
XLA Ops:
  20.1 79.5 %all-reduce.32 = (bf16[1536]{0:T(1024)(128)(2,1)S(1)}, bf16[1536]{0:T(1024)(128)(2,1)S(1)}, bf16[1536]{0:T(1024)(128)(2,1)S(1)}, bf16[1536]{0:T(1024)(128)(2,1)S(1)}) all-reduce(bf16[1536]{0:T(1024)(128)(2,1)S(1)} %dynamic-update-slice, bf16[1536]{0:T(1024)(128)(2,1)S(1)} %dynamic-update-slice.1, ...), channel_id=2, replica_groups=mesh['seq'=4,'fsdp'=32] {'seq','fsdp'}, use_global_device_ids=true, to_apply=%add.5 | all-reduce | flops 6144 | bytes 24576
  99.6 34.8 %all-gather.2 = bf16[1,1536,256]{2,0,1:T(2,128)(2,1)S(1)} all-gather(bf16[1,12,256]{2,0,1:T(2,128)(2,1)S(1)} %get-tuple-element.275), channel_id=4, replica_groups=mesh['seq'=4,'fsdp'=32] {'seq','fsdp'}, dimensions={1}, use_global_device_ids=true | all-gather | bytes 792576 | tf_op jit(solution)/shard_map/all_gather | solution.py:132
  136.7 34.5 %all-gather.1 = bf16[1,1536,256]{2,0,1:T(2,128)(2,1)S(1)} all-gather(bf16[1,12,256]{2,0,1:T(2,128)(2,1)S(1)} %get-tuple-element.273), channel_id=3, replica_groups=mesh['seq'=4,'fsdp'=32] {'seq','fsdp'}, dimensions={1}, use_global_device_ids=true | all-gather | bytes 792576 | tf_op jit(solution)/shard_map/all_gather | solution.py:131
  186.3 22.6 copy.519
  260.4 42.8 %all-gather.6 = bf16[1,1536,8]{2,0,1:T(2,128)(2,1)S(1)} all-gather(bf16[1,12,8]{2,0,1:T(2,128)(2,1)S(1)} %copy.511), channel_id=8, replica_groups=mesh['seq'=4,'fsdp'=32] {'seq','fsdp'}, dimensions={1}, use_global_device_ids=true | all-gather | bytes 24768 | tf_op jit(solution)/shard_map/all_gather | solution.py:135
  324.6 56.4 %all-gather.12 = bf16[1,1536,256]{2,0,1:T(2,128)(2,1)} all-gather(bf16[1,12,256]{2,0,1:T(2,128)(2,1)S(1)} %get-tuple-element.274), channel_id=14, replica_groups=mesh['seq'=4,'fsdp'=32] {'seq','fsdp'}, dimensions={1}, use_global_device_ids=true | all-gather | bytes 792576 | tf_op jit(solution)/shard_map/all_gather | solution.py:132
  381.0 38.1 %all-gather.11 = bf16[1,1536,256]{2,0,1:T(2,128)(2,1)} all-gather(bf16[1,12,256]{2,0,1:T(2,128)(2,1)S(1)} %get-tuple-element.272), channel_id=13, replica_groups=mesh['seq'=4,'fsdp'=32] {'seq','fsdp'}, dimensions={1}, use_global_device_ids=true | all-gather | bytes 792576 | tf_op jit(solution)/shard_map/all_gather | solution.py:131
  493.0 47.2 %all-gather.16 = bf16[1,1536,8]{2,0,1:T(2,128)(2,1)S(1)} all-gather(bf16[1,12,8]{2,0,1:T(2,128)(2,1)S(1)} %copy.513), channel_id=18, replica_groups=mesh['seq'=4,'fsdp'=32] {'seq','fsdp'}, dimensions={1}, use_global_device_ids=true | all-gather | bytes 24768 | tf_op jit(solution)/shard_map/all_gather | solution.py:135
  562.1 17.9 all-to-all-done.10
  585.8 14.0 all-gather.45.cloned.1.call-done
  625.3 17.7 all-to-all-done.11
  652.0 17.8 all-to-all-done.9
  756.6 20.9 all_to_all.202
  795.6 14.1 all-to-all-done.16
  958.1 369.0 %fusion.6 = f32[16,1536]{1,0:T(8,128)} fusion(f32[1536,1536]{1,0:T(8,128)} %fusion.212), kind=kCustom, calls=%all-reduce-scatter.6 | all-reduce-scatter fusion | flops 3145729 | bytes 9535488
  1441.1 424.5 %fusion.261 = (f32[16,1536]{1,0:T(8,128)S(1)}, f32[16,1536]{1,0:T(8,128)S(1)}, f32[16,256]{1,0:T(8,128)S(1)}, f32[16,256]{1,0:T(8,128)S(1)}, f32[16,256]{1,0:T(8...) fusion(f32[1536,1536]{1,0:T(8,128)} %fusion.275, f32[1536,1536]{1,0:T(8,128)} %fusion.198, ...), kind=kCustom, calls=%all-reduce-scatter.8 | all-reduce-scatter fusion | flops 11534337 | bytes 34963456
  2156.0 52.4 %concatenate.90 = f32[524,1536]{1,0:T(8,128)} concatenate(f32[12,1536]{1,0:T(8,128)S(1)} %copy-done.99, f32[16,1536]{1,0:T(8,128)S(1)} %copy-done.97, f32[16,1536]{1,0:T(8,128)S(1)} %copy-done.101, f32[16,1536]{1,0:T(8,128)S(1)} %copy-done.103, f32[16,1536]{1,0:T(8,128)} %copy-done.104, f32[16,1536]{1,0:T(8,128)} %copy-done.105, f32[16,1536]{1,0:T(8,128)} %copy-done.106, ...), dimensions={0} | concatenate | bytes 6438912
  2250.9 20.4 concatenate.87
  2271.4 24.5 concatenate.86
  2333.5 24.5 concatenate.89
  2358.2 16.4 concatenate.88
  2549.9 31.7 %concatenate.85 = f32[524,1536]{1,0:T(8,128)S(1)} concatenate(f32[12,1536]{1,0:T(8,128)} %copy-done.131, f32[16,1536]{1,0:T(8,128)} %copy-done.128, f32[16,1536]{1,0:T(8,128)} %copy-done.129, f32[16,1536]{1,0:T(8,128)} %copy-done.130, f32[16,1536]{1,0:T(8,128)} %copy-done.132, f32[16,1536]{1,0:T(8,128)} %copy-done.133, f32[16,1536]{1,0:T(8,128)} %copy-done.134, ...), dimensions={0} | concatenate | bytes 6438912
  2596.5 31.7 %concatenate.84 = f32[524,1536]{1,0:T(8,128)S(1)} concatenate(f32[12,1536]{1,0:T(8,128)} %copy-done.127, f32[16,1536]{1,0:T(8,128)} %copy-done.154, f32[16,1536]{1,0:T(8,128)} %copy-done.156, f32[16,1536]{1,0:T(8,128)} %copy-done.159, f32[16,1536]{1,0:T(8,128)} %copy-done.160, f32[16,1536]{1,0:T(8,128)} %copy-done.161, f32[16,1536]{1,0:T(8,128)} %copy-done.163, ...), dimensions={0} | concatenate | bytes 6438912
  2655.3 31.7 %concatenate.91 = f32[524,1536]{1,0:T(8,128)S(1)} concatenate(f32[12,1536]{1,0:T(8,128)} %copy-done.121, f32[16,1536]{1,0:T(8,128)} %collective-permute-done.254, f32[16,1536]{1,0:T(8,128)} %collective-permute-done.253, f32[16,1536]{1,0:T(8,128)} %collective-permute-done.252, f32[16,1536]{1,0:T(8,128)} %collective-permute-done.251, f32[16,1536]{1,0:T(8,128)} %collective-permute-done.250, ...), dimensions={0} | concatenate | bytes 6438912
  (1534 shorter events, 1194.5 us)
Async XLA Ops:
  7.2 179.1 %all-gather.31.cloned.1.call-start = ((), (), s32[]{:S(2)}) async-start(), calls=%async_computation.30 | async-start | bytes 9510912 | tf_op jit(solution)/shard_map/all_gather | solution.py:130
  9.1 226.5 %all-gather.33.cloned.1.call-start = ((), (), s32[]{:S(2)}) async-start(), calls=%async_computation.31 | async-start | bytes 9510912 | tf_op jit(solution)/shard_map/all_gather | solution.py:133
  10.9 292.7 %all-gather.35.cloned.1.call-start = ((), (), s32[]{:S(2)}) async-start(), calls=%async_computation.32 | async-start | bytes 4866048 | tf_op jit(solution)/shard_map/all_gather | solution.py:138
  12.7 296.8 %all-gather.37.cloned.1.call-start = ((), (), s32[]{:S(2)}) async-start(), calls=%async_computation.33 | async-start | bytes 4866048 | tf_op jit(solution)/shard_map/all_gather | solution.py:139
  14.5 301.0 %all-gather.39.cloned.1.call-start = ((), (), s32[]{:S(2)}) async-start(), calls=%async_computation.34 | async-start | bytes 4866048 | tf_op jit(solution)/shard_map/all_gather | solution.py:140
  15.3 425.6 %all-gather.41.cloned.1.call-start = ((), (), s32[]{:S(2)}) async-start(), calls=%async_computation.35 | async-start | bytes 9510912 | tf_op jit(solution)/shard_map/all_gather | solution.py:130
  15.9 454.7 %all-gather.43.cloned.1.call-start = ((), (), s32[]{:S(2)}) async-start(), calls=%async_computation.36 | async-start | bytes 9510912 | tf_op jit(solution)/shard_map/all_gather | solution.py:133
  16.6 539.9 %all-gather.47.cloned.1.call-start = ((), (), s32[]{:S(2)}) async-start(), calls=%async_computation.38 | async-start | bytes 4866048 | tf_op jit(solution)/shard_map/all_gather | solution.py:139
  17.4 544.8 %all-gather.49.cloned.1.call-start = ((), (), s32[]{:S(2)}) async-start(), calls=%async_computation.39 | async-start | bytes 4866048 | tf_op jit(solution)/shard_map/all_gather | solution.py:140
  256.7 343.1 %all-gather.45.cloned.1.call-start = ((), (), s32[]{:S(2)}) async-start(), calls=%async_computation.37 | async-start | bytes 4866048 | tf_op jit(solution)/shard_map/all_gather | solution.py:138
  321.0 99.1 %all-to-all-start.4 = ((bf16[4,2,72,1536]{3,2,1,0:T(8,128)(2,1)}), bf16[4,2,72,1536]{3,2,1,0:T(8,128)(2,1)S(1)}, u32[]{:S(2)}, u32[]{:S(2)}) async-start(bf16[4,2,72,1536]{3,2,1,0:T(8,128)(2,1)} %copy.392), calls=%async_computation.4 | async-start | bytes 3538944 | tf_op jit(solution)/shard_map/all_to_all | solution.py:296
  867.3 1561.2 %all-reduce.36.cloned.1.call-start = ((), (), s32[]{:S(2)}) async-start(), calls=%async_computation.42 | async-start | bytes 262144
  883.9 1803.9 %reduce-scatter.39.cloned.1.call-start = ((), (), s32[]{:S(2)}) async-start(), calls=%async_computation.41 | async-start | bytes 4866048
  903.4 1785.5 %reduce-scatter.37.cloned.1.call-start = ((), (), s32[]{:S(2)}) async-start(), calls=%async_computation.40 | async-start | bytes 4866048
  924.4 1765.5 %reduce-scatter.31.cloned.1.call-start = ((), (), s32[]{:S(2)}) async-start(), calls=%async_computation.27 | async-start | bytes 4866048 | tf_op jit(solution)/shard_map/reduce_scatter | solution.py:469
  931.9 1758.1 %reduce-scatter.29.cloned.1.call-start = ((), (), s32[]{:S(2)}) async-start(), calls=%async_computation.26 | async-start | bytes 4866048 | tf_op jit(solution)/shard_map/reduce_scatter | solution.py:469
  937.8 1754.9 %reduce-scatter.35.cloned.1.call-start = ((), (), s32[]{:S(2)}) async-start(), calls=%async_computation.29 | async-start | bytes 4866048 | tf_op jit(solution)/shard_map/reduce_scatter | solution.py:472
  945.3 1747.4 %reduce-scatter.33.cloned.1.call-start = ((), (), s32[]{:S(2)}) async-start(), calls=%async_computation.28 | async-start | bytes 4866048 | tf_op jit(solution)/shard_map/reduce_scatter | solution.py:472
  1424.5 441.1 %collective-permute-start.196 = (f32[16,1536]{1,0:T(8,128)}, f32[16,1536]{1,0:T(8,128)}, u32[]{:S(2)}, u32[]{:S(2)}) collective-permute-start(f32[16,1536]{1,0:T(8,128)} %fusion.6), channel_id=1, source_target_pairs={{0,5},{1,6},{2,7},{3,8},{4,9},{5,10},{6,11},{7,12},{8,13},{9,14},{... | collective-permute-start | bytes 294920
  1428.3 439.7 %collective-permute-start.195 = (f32[16,1536]{1,0:T(8,128)}, f32[16,1536]{1,0:T(8,128)}, u32[]{:S(2)}, u32[]{:S(2)}) collective-permute-start(f32[16,1536]{1,0:T(8,128)} %fusion.6), channel_id=1, source_target_pairs={{0,4},{1,5},{2,6},{3,7},{4,8},{5,9},{6,10},{7,11},{8,12},{9,13},{1... | collective-permute-start | bytes 294920
  1433.3 444.9 %collective-permute-start.194 = (f32[16,1536]{1,0:T(8,128)}, f32[16,1536]{1,0:T(8,128)}, u32[]{:S(2)}, u32[]{:S(2)}) collective-permute-start(f32[16,1536]{1,0:T(8,128)} %fusion.6), channel_id=1, source_target_pairs={{0,3},{1,4},{2,5},{3,6},{4,7},{5,8},{6,9},{7,10},{8,11},{9,12},{10... | collective-permute-start | bytes 294920
  1435.2 446.1 %collective-permute-start.193 = (f32[16,1536]{1,0:T(8,128)}, f32[16,1536]{1,0:T(8,128)}, u32[]{:S(2)}, u32[]{:S(2)}) collective-permute-start(f32[16,1536]{1,0:T(8,128)} %fusion.6), channel_id=1, source_target_pairs={{0,2},{1,3},{2,4},{3,5},{4,6},{5,7},{6,8},{7,9},{8,10},{9,11},{10,... | collective-permute-start | bytes 294920
  1438.4 446.6 %collective-permute-start.192 = (f32[16,1536]{1,0:T(8,128)}, f32[16,1536]{1,0:T(8,128)}, u32[]{:S(2)}, u32[]{:S(2)}) collective-permute-start(f32[16,1536]{1,0:T(8,128)} %fusion.6), channel_id=1, source_target_pairs={{0,1},{1,2},{2,3},{3,4},{4,5},{5,6},{6,7},{7,8},{8,9},{9,10},{10,1... | collective-permute-start | bytes 294920
  2153.6 66.1 %collective-permute-start.137 = (f32[16,256]{1,0:T(8,128)S(1)}, f32[16,256]{1,0:T(8,128)S(1)}, u32[]{:S(2)}, u32[]{:S(2)}) collective-permute-start(f32[16,256]{1,0:T(8,128)S(1)} %get-tuple-element.230), channel_id=1, source_target_pairs={{0,10},{1,11},{2,12},{3,13},{4,14},{5,15},{6,16},{7,17},{8,18},{9,... | collective-permute-start | bytes 49160
  (577 other events, 26549.4 us)
Sparse Core Ops, SparseCore 0:
  11.7 73.5 all-gather.30
  88.8 69.0 all-gather.32
  160.8 44.2 all-gather.34
  207.8 46.1 all-gather.36
  256.2 46.8 all-gather.38
  306.0 75.5 all-gather.40
  384.6 69.3 all-gather.42
  456.3 46.1 all-gather.46
  504.8 46.0 all-gather.48
  553.6 46.1 all-gather.44
  884.1 140.4 all-reduce.35
  1028.6 82.3 reduce-scatter.38
  1114.7 84.9 reduce-scatter.36
  1203.8 84.3 reduce-scatter.30
  1291.8 104.0 reduce-scatter.28
  1399.9 99.6 reduce-scatter.34
  1503.2 88.0 reduce-scatter.32
where the time goes:
time: 2730 us; the launch traced here: 2700 us
  blocking collectives  1150 us (42%)
  starting transfers between devices  737 us (27%)
  local copies, waits for them, and re-layouts  426 us (16%)
  matrix products  175 us (6%)
  waiting for transfers between devices  144 us (5%)
  other arithmetic  49.8 us (2%)
    unnamed x3, blocking collectives  873 us
    unnamed x259, starting transfers between devices  663 us
    unnamed x660, local copies, waits for them, and re-layouts  296 us
    all_gather x2, blocking collectives, fetch(): lax.all_gather(w_value[layer_index], ('seq', 'fsdp'), axis=0, tiled=True)  91.2 us
    all_gather x2, blocking collectives, fetch(): lax.all_gather(w_router[layer_index], ('seq', 'fsdp'), axis=0, tiled=True)  90 us
    all_gather x2, blocking collectives, fetch(): lax.all_gather(w_key[layer_index], ('seq', 'fsdp'), axis=0, tiled=True)  72.6 us
  transfers between devices with their start and end apart: 292, of which 16 were waited for; matrix products, arithmetic and copies ran while one was open for 48% of the time, Pallas kernels for 0%

commit v1 on v0

v1 whole, which is shorter than its diff:
```python
import functools

import jax
import jax.numpy as jnp
import numpy as np
from jax import lax
from jax.experimental import pallas as pl
from jax.experimental.pallas import tpu as pltpu
from jax.sharding import PartitionSpec as P

HEADS = 12
KVHEADS = 2
HD = 128
TOPK = 4
LAYERS = 2
NCONT = 4

norm_eps = 1e-06
rope_base = 10000.0
masked_value = -1e30

bf16 = jnp.bfloat16
f32 = jnp.float32
MIB = 1024 * 1024


def group_tables(segment_row, prompt_len):
    cont_len = segment_row.shape[0]
    onehot = (segment_row[:, None] == jnp.arange(NCONT, dtype=jnp.int32)[None, :]).astype(jnp.int32)
    counts = jnp.sum(onehot, axis=0)
    starts = jnp.cumsum(counts) - counts
    seg_begin = jnp.sum(onehot * starts[None, :], axis=1)
    within = jnp.arange(cont_len, dtype=jnp.int32) - seg_begin
    positions = jnp.concatenate([jnp.arange(prompt_len, dtype=jnp.int32), prompt_len + within])
    labels = jnp.concatenate([jnp.full((prompt_len,), -1, jnp.int32), segment_row])
    frequency = rope_base ** (-(jnp.arange(HD // 2, dtype=jnp.float32) * 2.0 / HD))
    angles = positions.astype(jnp.float32)[:, None] * frequency[None, :]
    return (jnp.cos(angles), jnp.sin(angles), labels)


def slot_table(expert_rows, order_rows, expert_count, capacity):
    pair_expert = expert_rows.reshape(-1)
    pair_order = order_rows.reshape(-1)
    same_expert = pair_expert[:, None] == pair_expert[None, :]
    earlier = pair_order[None, :] < pair_order[:, None]
    pair_slot = jnp.sum(jnp.logical_and(same_expert, earlier).astype(jnp.int32), axis=1)
    target = jnp.where(
        pair_slot < capacity, pair_expert * capacity + pair_slot, expert_count * capacity
    )
    return target.reshape(expert_rows.shape).T


def nn(left, right):
    return lax.dot_general(left, right, (((1,), (0,)), ((), ())), preferred_element_type=f32)


def nt(left, right):
    return lax.dot_general(left, right, (((1,), (1,)), ((), ())), preferred_element_type=f32)


def tn(left, right):
    return lax.dot_general(left, right, (((0,), (0,)), ((), ())), preferred_element_type=f32)


def split(value):
    high = value.astype(bf16)
    return high, (value - high.astype(f32)).astype(bf16)


def run(kernel, outs, *args, limit=48, flops=0, grid=None, in_specs=None, out_specs=None):
    moved = sum(int(np.prod(a.shape)) * a.dtype.itemsize for a in args)
    moved += sum(int(np.prod(o.shape)) * o.dtype.itemsize for o in outs)
    extra = {}
    if grid is not None:
        extra["grid"] = grid
    if in_specs is not None:
        extra["in_specs"] = in_specs
    if out_specs is not None:
        extra["out_specs"] = out_specs
    return pl.pallas_call(
        kernel,
        out_shape=list(outs),
        compiler_params=pltpu.CompilerParams(vmem_limit_bytes=limit * MIB),
        cost_estimate=pl.CostEstimate(flops=flops, bytes_accessed=moved, transcendentals=0),
        **extra,
    )(*args)


def shape(dims, dtype):
    return jax.ShapeDtypeStruct(dims, dtype)


def normalize(value, gain):
    inverse = lax.rsqrt(jnp.mean(value * value, axis=-1, keepdims=True) + norm_eps)
    return value * inverse * gain


def normalize_back(value, gain, grad):
    inverse = lax.rsqrt(jnp.mean(value * value, axis=-1, keepdims=True) + norm_eps)
    unit = value * inverse
    grad_gain = jnp.sum(grad * unit, axis=0, keepdims=True)
    scaled = grad * gain
    grad_value = inverse * (scaled - unit * jnp.mean(scaled * unit, axis=-1, keepdims=True))
    return grad_value, grad_gain


def turn(block, cosines, sines):
    return block * cosines + pltpu.roll(block, HD // 2, 1) * sines


def smooth_parts(value):
    root = np.float32(np.sqrt(2.0 / np.pi))
    square = value * value
    high = jnp.tanh(root * (value + 0.044715 * value * square))
    half = 0.5 * (1.0 + high)
    slope = half + 0.5 * value * (1.0 - high * high) * root * (1.0 + 3 * 0.044715 * square)
    return value * half, slope


def choose(target_t, slots):
    place = lax.broadcasted_iota(jnp.int32, (slots, target_t.shape[1]), 0)
    total = jnp.zeros(place.shape, f32)
    for k in range(TOPK):
        total = total + jnp.where(place == target_t[k : k + 1], 1.0, 0.0)
    return total


def choose_weighted(target_t, gates_t, slots):
    place = lax.broadcasted_iota(jnp.int32, (slots, target_t.shape[1]), 0)
    total = jnp.zeros(place.shape, f32)
    for k in range(TOPK):
        total = total + jnp.where(place == target_t[k : k + 1], gates_t[k : k + 1], 0.0)
    return total


def attention_input(hidden, small, spread, weight, cosines, sines, send_ref, normed_ref):
    expert_count = 8
    gain = small[expert_count : expert_count + 1].astype(f32)
    normed = normalize(hidden, gain).astype(bf16)
    normed = nn(normed, spread).astype(bf16)
    normed_ref[...] = normed
    raw = nn(normed, weight)
    seq_count = send_ref.shape[0]
    local = HEADS // seq_count
    for s in range(seq_count):
        pick = s * KVHEADS // seq_count
        for j in range(local):
            at = (s * local + j) * HD
            send_ref[s, :, j * HD : (j + 1) * HD] = turn(
                raw[:, at : at + HD], cosines, sines
            ).astype(bf16)
        at = (HEADS + pick) * HD
        send_ref[s, :, local * HD : (local + 1) * HD] = turn(
            raw[:, at : at + HD], cosines, sines
        ).astype(bf16)
        at = (HEADS + KVHEADS + pick) * HD
        send_ref[s, :, (local + 1) * HD :] = raw[:, at : at + HD].astype(bf16)


def first_input_kernel(tokens, small, spread, weight, cosines, sines, send_ref, normed_ref):
    hidden = tokens[...].astype(f32)
    qkv = weight[:, : (HEADS + 2 * KVHEADS) * HD]
    attention_input(
        hidden, small[...], spread[...], qkv, cosines[...], sines[...], send_ref, normed_ref
    )


def next_input_kernel(
    middle, combined, gates_t, target_t, small, spread, weight, cosines, sines,
    send_ref, normed_ref, hidden_ref,
):
    hidden = middle[...] + mix(combined[...], gates_t[...], target_t[...])
    hidden_ref[...] = hidden
    qkv = weight[:, : (HEADS + 2 * KVHEADS) * HD]
    attention_input(
        hidden, small[...], spread[...], qkv, cosines[...], sines[...], send_ref, normed_ref
    )


def mix(combined, gates_t, target_t):
    high, low = split(choose_weighted(target_t, gates_t, combined.shape[0]))
    return tn(high, combined) + tn(low, combined)


def result_kernel(middle, combined, gates_t, target_t, result_ref):
    mixture = mix(combined[...], gates_t[...], target_t[...])
    result_ref[...] = (middle[...] + mixture).astype(bf16)


def attention_kernel(heads_ref, bias_ref, out_ref):
    seq_count, tokens, columns = heads_ref.shape
    group = seq_count * tokens
    heads = heads_ref[...].reshape(group, columns)
    local = columns // HD - 2
    prompt = group // 2
    key = heads[:, local * HD : (local + 1) * HD]
    value = heads[:, (local + 1) * HD :]
    scale = HD ** (-0.5)
    for j in range(local):
        query = heads[:, j * HD : (j + 1) * HD]
        for rows, seen in ((slice(0, prompt), prompt), (slice(prompt, group), group)):
            scores = nt(query[rows], key[:seen]) * scale + bias_ref[rows, :seen]
            peak = jnp.max(scores, axis=-1, keepdims=True)
            weights = jnp.exp(scores - peak)
            weights = weights / jnp.sum(weights, axis=-1, keepdims=True)
            part = nn(weights.astype(bf16), value[:seen]).astype(bf16)
            first = rows.start // tokens
            out_ref[first : first + prompt // tokens, :, j * HD : (j + 1) * HD] = part.reshape(
                prompt // tokens, tokens, HD
            )


def after_attention_kernel(
    back, hidden, small, spread, out_w, routes_t, target_t,
    middle_ref, normed_ref, gates_ref, send_ref,
):
    expert_count = 8
    seq_count, tokens, part = back.shape
    width = seq_count * part
    attended = jnp.zeros((tokens, width), f32)
    for s in range(seq_count):
        attended = attended + nn(back[s], spread[s * part : (s + 1) * part])
    attended = attended.astype(bf16)
    rows = out_w.shape[1] // 2
    half = out_w.shape[2]
    for side in range(2):
        weight = out_w[:, side * rows : (side + 1) * rows].reshape(width, half)
        cols = slice(side * half, (side + 1) * half)
        middle_ref[:, cols] = hidden[:, cols].astype(f32) + nn(attended, weight)
    middle = middle_ref[...]
    gain = small[expert_count + 1 : expert_count + 2].astype(f32)
    normed = normalize(middle, gain).astype(bf16)
    normed_ref[...] = normed
    logits = nt(small[...], normed)
    chosen = []
    for k in range(TOPK):
        route = routes_t[k : k + 1]
        value = jnp.zeros((1, tokens), f32)
        for e in range(expert_count):
            value = value + jnp.where(route == e, logits[e : e + 1], 0.0)
        chosen.append(value)
    peak = functools.reduce(jnp.maximum, chosen)
    powers = [jnp.exp(value - peak) for value in chosen]
    total = functools.reduce(jnp.add, powers)
    for k in range(TOPK):
        gates_ref[k : k + 1] = powers[k] / total
    gates_ref[TOPK:] = jnp.zeros((gates_ref.shape[0] - TOPK, tokens), f32)
    send_ref[...] = nn(choose(target_t[...], send_ref.shape[0]).astype(bf16), normed).astype(bf16)


def flat_rows(block):
    sources, capacity, width = block.shape
    return block.astype(f32).reshape(sources * capacity, width).astype(bf16)


def down_parts(block):
    shards, rows, half = block.shape
    wide = block.astype(f32)
    left = wide[:, : rows // 2].reshape(shards * rows // 2, half).astype(bf16)
    right = wide[:, rows // 2 :].reshape(shards * rows // 2, half).astype(bf16)
    return left, right


def expert_kernel(rows_ref, weights_ref, out_ref, gate_ref, up_ref):
    shards, rows, half = weights_ref.shape
    rows = rows // 3
    width = shards * rows
    tokens = flat_rows(rows_ref[:, 0])
    gate_val = nn(tokens, weights_ref[:, :rows].reshape(width, half))
    up_val = nn(tokens, weights_ref[:, rows : 2 * rows].reshape(width, half))
    gate_ref[0] = gate_val
    up_ref[0] = up_val
    activated, slope = smooth_parts(gate_val)
    inner = (activated * up_val).astype(bf16)
    left, right = down_parts(weights_ref[:, 2 * rows :])
    sources, capacity = rows_ref.shape[0], rows_ref.shape[2]
    out_ref[:, 0, :, :half] = nn(inner, left).reshape(sources, capacity, half).astype(bf16)
    out_ref[:, 0, :, half:] = nn(inner, right).reshape(sources, capacity, half).astype(bf16)


def slot_grad_kernel(grad, combined, gates_t, routes_t, target_t, send_ref, logits_ref):
    tokens = grad.shape[0]
    slots = combined.shape[0]
    high, low = split(grad[...])
    weights_high, weights_low = split(choose_weighted(target_t[...], gates_t[...], slots))
    send = nn(weights_high, high) + (nn(weights_high, low) + nn(weights_low, high))
    send_ref[...] = send.astype(bf16)
    products = nt(combined[...], high) + nt(combined[...], low)
    place = lax.broadcasted_iota(jnp.int32, (slots, tokens), 0)
    grad_gates = [
        jnp.sum(jnp.where(place == target_t[k : k + 1], products, 0.0), axis=0, keepdims=True)
        for k in range(TOPK)
    ]
    gates = [gates_t[k : k + 1] for k in range(TOPK)]
    center = functools.reduce(jnp.add, [a * b for a, b in zip(gates, grad_gates)])
    label = lax.broadcasted_iota(jnp.int32, logits_ref.shape, 0)
    total = jnp.zeros(logits_ref.shape, f32)
    for k in range(TOPK):
        choice = gates[k] * (grad_gates[k] - center)
        total = total + jnp.where(label == routes_t[k : k + 1], choice, 0.0)
    logits_ref[...] = total.astype(bf16)


def expert_back_kernel(
    grad_ref, weights_ref, gate_ref, up_ref, out_ref, gate_grad_ref, up_grad_ref, inner_ref
):
    shards, rows, half = weights_ref.shape
    rows = rows // 3
    width = shards * rows
    sources, capacity = grad_ref.shape[0], grad_ref.shape[2]
    grad = flat_rows(grad_ref[:, 0])
    left, right = down_parts(weights_ref[:, 2 * rows :])
    grad_inner = nt(grad[:, :half], left) + nt(grad[:, half:], right)
    up_val = up_ref[0]
    activated, slope = smooth_parts(gate_ref[0])
    inner_ref[0] = (activated * up_val).astype(bf16)
    grad_gate = (grad_inner * up_val * slope).astype(bf16)
    grad_up = (grad_inner * activated).astype(bf16)
    gate_grad_ref[0] = grad_gate
    up_grad_ref[0] = grad_up
    total = nt(grad_gate, weights_ref[:, :rows].reshape(width, half))
    total = total + nt(grad_up, weights_ref[:, rows : 2 * rows].reshape(width, half))
    out_ref[:, 0] = total.reshape(sources, capacity, width).astype(bf16)


def expert_weight_kernel(
    rows_ref, grad_ref, gate_grad_ref, up_grad_ref, inner_ref, *rest, experts
):
    pack_ref = rest[-1]
    shards, rows, half = pack_ref.shape
    rows = rows // 3

    @pl.when(pl.program_id(0) < experts)
    def _():
        tokens = flat_rows(rows_ref[:, 0])
        grad = flat_rows(grad_ref[:, 0])
        pack_ref[:, :rows] = tn(tokens, gate_grad_ref[0]).astype(bf16).reshape(shards, rows, half)
        pack_ref[:, rows : 2 * rows] = (
            tn(tokens, up_grad_ref[0]).astype(bf16).reshape(shards, rows, half)
        )
        left = tn(inner_ref[0], grad[:, :half]).reshape(shards, rows // 2, half)
        right = tn(inner_ref[0], grad[:, half:]).reshape(shards, rows // 2, half)
        pack_ref[:, 2 * rows :] = jnp.concatenate([left, right], axis=1).astype(bf16)

    if len(rest) > 1:
        qkv_ref, out_ref = rest[:2]
        cut = qkv_ref.shape[1]

        @pl.when(pl.program_id(0) == experts)
        def _():
            pack_ref[:, :cut] = qkv_ref[...]
            pack_ref[:, cut : cut + out_ref.shape[1]] = out_ref[...]


def after_experts_kernel(
    grad, sent, middle, normed, logits_grad, target_t, small, spread, out_w,
    grad_ref, branch_ref, send_ref, small_ref,
):
    expert_count = 8
    seq_count, tokens, part = send_ref.shape
    width = seq_count * part
    chosen = choose(target_t[...], sent.shape[0]).astype(bf16)
    grad_normed = tn(chosen, sent[...]) + tn(logits_grad[...], small[...])
    router = nn(logits_grad[...], normed[...])
    gain = small[expert_count + 1 : expert_count + 2].astype(f32)
    grad_value, grad_gain = normalize_back(middle[...], gain, grad_normed)
    label = lax.broadcasted_iota(jnp.int32, small_ref.shape, 0)
    small_ref[...] = jnp.where(label == expert_count + 1, grad_gain, router)
    grad_middle = grad[...] + grad_value
    grad_ref[...] = grad_middle
    branch = grad_middle.astype(bf16)
    branch_ref[...] = branch
    rows = out_w.shape[1] // 2
    half = out_w.shape[2]
    parts = [
        nt(branch[:, :half], out_w[:, :rows].reshape(width, half)),
        nt(branch[:, half:], out_w[:, rows:].reshape(width, half)),
    ]
    attended = (parts[0] + parts[1]).astype(bf16)
    for s in range(seq_count):
        send_ref[s] = nt(attended, spread[s * part : (s + 1) * part]).astype(bf16)


def attention_back_kernel(heads_ref, grad_ref, bias_ref, cosines, sines, out_ref):
    seq_count, tokens, columns = heads_ref.shape
    group = seq_count * tokens
    heads = heads_ref[...].reshape(group, columns)
    grads = grad_ref[...].reshape(group, grad_ref.shape[2])
    local = columns // HD - 2
    prompt = group // 2
    key = heads[:, local * HD : (local + 1) * HD]
    value = heads[:, (local + 1) * HD :]
    scale = HD ** (-0.5)

    def keep(at, block):
        out_ref[:, :, at * HD : (at + 1) * HD] = block.astype(bf16).reshape(seq_count, tokens, HD)

    def unturn(block):
        return block * cosines[...] - pltpu.roll(block, HD // 2, 1) * sines[...]

    grad_key = [jnp.zeros((prompt, HD), f32), jnp.zeros((prompt, HD), f32)]
    grad_value = [jnp.zeros((prompt, HD), f32), jnp.zeros((prompt, HD), f32)]
    for j in range(local):
        query = heads[:, j * HD : (j + 1) * HD]
        grad = grads[:, j * HD : (j + 1) * HD]
        grad_query = []
        for rows, seen in ((slice(0, prompt), prompt), (slice(prompt, group), group)):
            scores = nt(query[rows], key[:seen]) * scale + bias_ref[rows, :seen]
            peak = jnp.max(scores, axis=-1, keepdims=True)
            weights = jnp.exp(scores - peak)
            weights = weights / jnp.sum(weights, axis=-1, keepdims=True)
            grad_weights = nt(grad[rows], value[:seen])
            center = jnp.sum(weights * grad_weights, axis=-1, keepdims=True)
            grad_scores = (weights * (grad_weights - center)).astype(bf16)
            low = weights.astype(bf16)
            grad_query.append(nn(grad_scores, key[:seen]) * scale)
            for side in range(seen // prompt):
                cols = slice(side * prompt, (side + 1) * prompt)
                grad_key[side] = grad_key[side] + tn(grad_scores[:, cols], query[rows])
                grad_value[side] = grad_value[side] + tn(low[:, cols], grad[rows])
        keep(j, unturn(jnp.concatenate(grad_query, axis=0)))
    keep(local, unturn(jnp.concatenate(grad_key, axis=0) * scale))
    keep(local + 1, jnp.concatenate(grad_value, axis=0))


def before_attention_kernel(
    grad_middle, sent, hidden, small, spread, weight, small_grad, out_ref, small_ref
):
    expert_count = 8
    seq_count, tokens, columns = sent.shape
    local = columns // HD - 2
    share = seq_count // KVHEADS
    blocks = [sent[s, :, : local * HD] for s in range(seq_count)]
    for at in (local, local + 1):
        for c in range(KVHEADS):
            total = jnp.zeros((tokens, HD), f32)
            for s in range(c * share, (c + 1) * share):
                total = total + sent[s, :, at * HD : (at + 1) * HD].astype(f32)
            blocks.append(total.astype(bf16))
    raw = jnp.concatenate(blocks, axis=1)
    high, low = split(nt(raw, weight[:, : raw.shape[1]]))
    grad_normed = nt(high, spread[...]) + nt(low, spread[...])
    gain = small[expert_count : expert_count + 1].astype(f32)
    grad_value, grad_gain = normalize_back(hidden[...].astype(f32), gain, grad_normed)
    out_ref[...] = grad_middle[...] + grad_value
    label = lax.broadcasted_iota(jnp.int32, small_ref.shape, 0)
    small_ref[...] = jnp.where(label == expert_count, grad_gain, small_grad[...])


def qkv_weight_kernel(place, own, one, two, three, grads, small, spread, out_ref):
    me = place[0]
    seq_count, tokens, columns = grads.shape
    shards, rows, wide = out_ref.shape
    inputs = jnp.concatenate([own[...], one[...], two[...], three[...]], axis=0)
    grad = jnp.concatenate([grads[lax.rem(me + k, seq_count)] for k in range(seq_count)], axis=0)
    total = tn(inputs, grad)
    out_ref[:, :, :columns] = total.astype(bf16).reshape(shards, rows, columns)
    extra = small[...].astype(bf16)
    extra = jnp.concatenate([extra, jnp.zeros((HD - extra.shape[0], extra.shape[1]), bf16)], axis=0)
    extra = nn(extra, spread[...]).T
    out_ref[:, :, columns:] = extra.astype(bf16).reshape(shards, rows, wide - columns)


def out_weight_kernel(place, own, one, two, three, attended, out_ref):
    me = place[0]
    seq_count, tokens, part = attended.shape
    shards, rows, half = out_ref.shape
    rows = rows // 2
    valid = part // shards
    branch = jnp.concatenate([own[...], one[...], two[...], three[...]], axis=0)
    heads = jnp.concatenate([attended[lax.rem(me + k, seq_count)] for k in range(seq_count)], axis=0)
    place_in = lax.broadcasted_iota(jnp.int32, (part, shards * rows), 0)
    place_out = lax.broadcasted_iota(jnp.int32, (part, shards * rows), 1)
    source = place_out // rows * valid + place_out % rows
    same = jnp.logical_and(place_in == source, place_out % rows < valid)
    heads = nn(heads, jnp.where(same, 1.0, 0.0).astype(bf16)).astype(bf16)
    for side in range(2):
        total = tn(heads, branch[:, side * half : (side + 1) * half])
        out_ref[:, side * rows : (side + 1) * rows] = total.astype(bf16).reshape(shards, rows, half)


def gather_seq(block):
    return lax.all_gather(block, "seq", axis=0, tiled=False)


def swap_seq(block):
    return lax.all_to_all(block, "seq", split_axis=0, concat_axis=0, tiled=True)


def around_seq(block):
    count = lax.axis_size("seq")
    others = [
        lax.ppermute(block, "seq", [((i + k) % count, i) for i in range(count)])
        for k in range(1, count)
    ]
    return [block] + others


def halves(block):
    cut = block.shape[-1] // 2
    return jnp.concatenate([block[..., :cut], block[..., cut:]], axis=-2)


def per_device(
    tokens_in,
    cotangent,
    routes,
    order,
    segment_ids,
    gain_attn,
    w_query,
    w_key,
    w_value,
    w_out,
    gain_ffn,
    w_router,
    w_gate,
    w_up,
    w_down,
):
    tok_count = tokens_in.shape[1]
    width = tokens_in.shape[2]
    seq_count = lax.axis_size("seq")
    shard_count = lax.axis_size("fsdp")
    seq_index = lax.axis_index("seq")
    place = jnp.full((1,), seq_index, jnp.int32)
    group_tok = seq_count * tok_count
    prompt_len = group_tok - segment_ids.shape[1]
    local_experts = w_gate.shape[1]
    expert_count = local_experts * seq_count
    capacity = 9 * tok_count * TOPK // (8 * expert_count)
    total_slots = expert_count * capacity
    head_local = HEADS // seq_count
    local_width = head_local * HD
    dense_rows = w_query.shape[1]
    shard_rows = dense_rows * seq_count
    gate_rows = w_gate.shape[2]
    down_rows = w_down.shape[2]
    expert_rows = 2 * gate_rows + 2 * down_rows
    qkv_width = (HEADS + 2 * KVHEADS) * HD
    half_width = width // 2
    inner_width = w_gate.shape[3]
    slot_rows = seq_count * capacity

    cos_half, sin_half, labels = group_tables(segment_ids[0], prompt_len)
    cos_all = jnp.concatenate([cos_half, cos_half], axis=1)
    sin_all = jnp.concatenate([-sin_half, sin_half], axis=1)
    cos_own = lax.dynamic_slice_in_dim(cos_all, seq_index * tok_count, tok_count, 0)
    sin_own = lax.dynamic_slice_in_dim(sin_all, seq_index * tok_count, tok_count, 0)
    key_pos = jnp.arange(group_tok, dtype=jnp.int32)
    allowed = jnp.logical_and(
        key_pos[None, :] <= key_pos[:, None],
        jnp.logical_or(key_pos[None, :] < prompt_len, labels[None, :] == labels[:, None]),
    )
    bias = jnp.where(allowed, 0.0, masked_value)

    column = jnp.arange(width, dtype=jnp.int32)
    natural = (
        column % shard_rows // dense_rows * (width // seq_count)
        + column // shard_rows * dense_rows
        + column % dense_rows
    )
    spread = (column[:, None] == natural[None, :]).astype(bf16)

    def fetch(layer):
        extras = jnp.concatenate(
            [
                w_router[layer],
                gain_attn[layer][:, None],
                gain_ffn[layer][:, None],
                jnp.zeros((dense_rows, HD - 2 - expert_count), bf16),
            ],
            axis=1,
        )
        dense = jnp.concatenate(
            [w_query[layer], w_key[layer], w_value[layer], extras, w_out[layer]], axis=1
        )
        dense = gather_seq(dense).reshape(shard_rows, dense.shape[1])
        qkv = lax.all_gather(dense[:, : qkv_width + HD], "fsdp", axis=0, tiled=True)
        pack = [
            part
            for e in range(local_experts)
            for part in (w_gate[layer, e], w_up[layer, e], halves(w_down[layer, e]))
        ]
        pack = jnp.concatenate(pack + [halves(dense[:, qkv_width + HD :])], axis=0)
        pack = lax.all_gather(pack, "fsdp", axis=0, tiled=False)
        small = lax.dot_general(
            qkv[:, qkv_width : qkv_width + 16],
            spread,
            (((0,), (1,)), ((), ())),
            preferred_element_type=f32,
        ).astype(bf16)
        return qkv, pack, small

    whole = pl.BlockSpec(memory_space=pltpu.VMEM)
    slots_spec = pl.BlockSpec(
        (seq_count, 1, capacity, width), lambda e: (0, jnp.minimum(e, local_experts - 1), 0, 0)
    )
    weights_spec = pl.BlockSpec(
        (shard_count, expert_rows, half_width), lambda e: (0, jnp.minimum(e, local_experts - 1), 0)
    )
    inner_spec = pl.BlockSpec(
        (1, slot_rows, inner_width), lambda e: (jnp.minimum(e, local_experts - 1), 0, 0)
    )
    out_block = 2 * shard_rows
    out_at = local_experts * expert_rows // out_block
    out_w_spec = pl.BlockSpec((shard_count, out_block, half_width), lambda i: (0, out_at, 0))

    def fixed(array):
        return pl.BlockSpec(array.shape, lambda i: (0,) * array.ndim)

    def once(kernel, outs, *args, weight=None, **kw):
        specs = [out_w_spec if n == weight else fixed(a) for n, a in enumerate(args)]
        return run(
            kernel, outs, *args, grid=(1,), in_specs=specs, out_specs=[fixed(o) for o in outs], **kw
        )

    slots_shape = shape((seq_count, local_experts, capacity, width), bf16)
    inner_shape = (local_experts, slot_rows, inner_width)
    expert_flops = 6 * total_slots * width * inner_width
    dense_flops = 2 * tok_count * width * width
    records = []
    hidden = tokens_in[0]
    for layer in range(LAYERS):
        qkv_w, pack, small = fetch(layer)
        routes_t = routes[layer, 0].T
        target_t = slot_table(routes[layer, 0], order[layer, 0], expert_count, capacity)
        send_shape = shape((seq_count, tok_count, local_width + 2 * HD), bf16)
        normed_shape = shape((tok_count, width), bf16)
        if layer == 0:
            send, normed_p = once(
                first_input_kernel, [send_shape, normed_shape],
                hidden, small, spread, qkv_w, cos_own, sin_own, flops=3 * dense_flops,
            )
        else:
            send, normed_p, hidden = once(
                next_input_kernel, [send_shape, normed_shape, shape((tok_count, width), f32)],
                middle, combined, gates_t, above_target, small, spread, qkv_w, cos_own, sin_own,
                flops=4 * dense_flops,
            )
        heads = swap_seq(send)
        normed_all = around_seq(normed_p)
        (attended,) = once(
            attention_kernel, [shape((seq_count, tok_count, local_width), bf16)], heads, bias,
            flops=4 * head_local * group_tok * group_tok * HD,
        )
        back = swap_seq(attended)
        middle, normed_ffn, gates_t, send_rows = once(
            after_attention_kernel,
            [
                shape((tok_count, width), f32),
                shape((tok_count, width), bf16),
                shape((2 * TOPK, tok_count), f32),
                shape((total_slots, width), bf16),
            ],
            back, hidden, small, spread, pack, routes_t, target_t, weight=4, flops=3 * dense_flops,
        )
        received = swap_seq(send_rows.reshape(slots_shape.shape))
        expert_out, gate_val, up_val = run(
            expert_kernel,
            [slots_shape, shape(inner_shape, f32), shape(inner_shape, f32)],
            received, pack,
            grid=(local_experts,),
            in_specs=[slots_spec, weights_spec],
            out_specs=[slots_spec, inner_spec, inner_spec],
            flops=expert_flops,
        )
        combined = swap_seq(expert_out).reshape(total_slots, width)
        above_target = target_t
        records.append(
            (
                (qkv_w, pack, small, routes_t, target_t),
                (hidden, normed_all, heads, attended),
                (middle, normed_ffn, gates_t, combined),
                (received, gate_val, up_val),
            )
        )
    (result,) = once(
        result_kernel, [shape((tok_count, width), bf16)], middle, combined, gates_t, target_t,
        flops=dense_flops,
    )

    def scatter(block):
        return lax.psum_scatter(block, "fsdp", scatter_dimension=0, tiled=False)

    def expert_unpack(block):
        block = block[: local_experts * expert_rows].astype(f32)
        block = block.reshape(local_experts, expert_rows, half_width)
        down = block[:, 2 * gate_rows :].reshape(local_experts, 2, down_rows, half_width)
        return (
            block[:, :gate_rows],
            block[:, gate_rows : 2 * gate_rows],
            down.transpose(0, 2, 1, 3).reshape(local_experts, down_rows, width),
        )

    def qkv_unpack(block):
        part = swap_seq(block.reshape(seq_count, dense_rows, local_width + 3 * HD)).astype(f32)
        query = part[:, :, :local_width].transpose(1, 0, 2).reshape(dense_rows, HEADS * HD)

        def pairs(block):
            block = block.reshape(KVHEADS, seq_count // KVHEADS, dense_rows, HD)
            return jnp.sum(block, axis=1).transpose(1, 0, 2).reshape(dense_rows, KVHEADS * HD)

        key = pairs(part[:, :, local_width : local_width + HD])
        value = pairs(part[:, :, local_width + HD : local_width + 2 * HD])
        extra = jnp.sum(part[:, :, local_width + 2 * HD :], axis=0)
        router = extra[:, :expert_count]
        return query, key, value, extra[:, expert_count], extra[:, expert_count + 1], router

    out_rows = 16

    def out_unpack(block):
        block = block.astype(f32)
        return jnp.concatenate(
            [block[:dense_rows], block[out_rows : out_rows + dense_rows]], axis=1
        )

    grad_hidden = cotangent[0].astype(f32)
    grads = [None] * LAYERS
    waiting = None
    for layer in range(LAYERS - 1, -1, -1):
        weights, attn_saved, mid_saved, expert_saved = records[layer]
        qkv_w, pack, small, routes_t, target_t = weights
        below, normed_all, heads, attended = attn_saved
        middle, normed_ffn, gates_t, combined = mid_saved
        received, gate_val, up_val = expert_saved
        grad_slots, logits_grad = once(
            slot_grad_kernel,
            [shape((total_slots, width), bf16), shape((2 * expert_count, tok_count), bf16)],
            grad_hidden, combined, gates_t, routes_t, target_t, flops=3 * dense_flops,
        )
        grad_expert = swap_seq(grad_slots.reshape(slots_shape.shape))
        grad_rows, gate_grad, up_grad, inner = run(
            expert_back_kernel,
            [slots_shape] + [shape(inner_shape, bf16)] * 3,
            grad_expert, pack, gate_val, up_val,
            grid=(local_experts,),
            in_specs=[slots_spec, weights_spec, inner_spec, inner_spec],
            out_specs=[slots_spec] + [inner_spec] * 3,
            flops=expert_flops,
        )
        sent = swap_seq(grad_rows)
        extra = () if layer == LAYERS - 1 else waiting
        extra_rows = sum(a.shape[1] for a in extra)
        (packed,) = run(
            functools.partial(expert_weight_kernel, experts=local_experts),
            [shape((shard_count, local_experts * expert_rows + extra_rows, half_width), bf16)],
            received, grad_expert, gate_grad, up_grad, inner, *extra,
            grid=(local_experts + (1 if extra else 0),),
            in_specs=[slots_spec, slots_spec] + [inner_spec] * 3 + [fixed(a) for a in extra],
            out_specs=[
                pl.BlockSpec((shard_count, expert_rows, half_width), lambda e: (0, e, 0))
            ],
            flops=expert_flops,
        )
        sent, packed = lax.optimization_barrier((sent, packed))
        summed = scatter(packed)
        if extra:
            above_block = summed[local_experts * expert_rows :]
        grad_middle, branch, send, small_grad = once(
            after_experts_kernel,
            [
                shape((tok_count, width), f32),
                shape((tok_count, width), bf16),
                shape((seq_count, tok_count, local_width), bf16),
                shape((2 * expert_count, width), f32),
            ],
            grad_hidden, sent.reshape(total_slots, width), middle, normed_ffn, logits_grad,
            target_t, small, spread, pack, weight=8, flops=4 * dense_flops,
        )
        grad_heads = swap_seq(send)
        branch_all = around_seq(branch)
        (grad_own,) = once(
            attention_back_kernel,
            [shape((seq_count, tok_count, local_width + 2 * HD), bf16)],
            heads, grad_heads, bias, cos_all, sin_all,
            flops=10 * head_local * group_tok * group_tok * HD,
        )
        sent = swap_seq(grad_own)
        (out_block_grad,) = run(
            out_weight_kernel,
            [shape((shard_count, 2 * out_rows, half_width), bf16)],
            place, *branch_all, attended,
            in_specs=[pl.BlockSpec(memory_space=pltpu.SMEM)] + [whole] * 5,
            out_specs=[whole],
            flops=dense_flops,
        )
        grad_hidden, small_grad = once(
            before_attention_kernel,
            [shape((tok_count, width), f32), shape((2 * expert_count, width), f32)],
            grad_middle, sent, below, small, spread, qkv_w, small_grad, flops=4 * dense_flops,
        )
        (qkv_block_grad,) = run(
            qkv_weight_kernel,
            [shape((shard_count, shard_rows, half_width), bf16)],
            place, *normed_all, grad_own, small_grad, spread,
            in_specs=[pl.BlockSpec(memory_space=pltpu.SMEM)] + [whole] * 7,
            out_specs=[whole],
            flops=2 * dense_flops,
        )
        expert_grads = expert_unpack(summed)
        if layer > 0:
            waiting = (qkv_block_grad, out_block_grad)
        else:

            def shard_sum(block):
                block = lax.all_to_all(block, "fsdp", split_axis=0, concat_axis=0, tiled=True)
                return jnp.sum(block.astype(f32), axis=0)

            own_out = out_unpack(shard_sum(out_block_grad))
            own_qkv = qkv_unpack(shard_sum(qkv_block_grad))
            above_qkv = qkv_unpack(above_block[:shard_rows])
            above_out = out_unpack(above_block[shard_rows:])
        grads[layer] = expert_grads

    def both(first, second):
        return jnp.stack([first, second])

    return (
        result[None],
        grad_hidden[None],
        both(own_qkv[3], above_qkv[3]),
        both(own_qkv[0], above_qkv[0]),
        both(own_qkv[1], above_qkv[1]),
        both(own_qkv[2], above_qkv[2]),
        both(own_out, above_out),
        both(own_qkv[4], above_qkv[4]),
        both(own_qkv[5], above_qkv[5]),
        both(grads[0][0], grads[1][0]),
        both(grads[0][1], grads[1][1]),
        both(grads[0][2], grads[1][2]),
    )


def solution(mesh):
    in_specs = (
        P("fsdp", "seq", None),
        P("fsdp", "seq", None),
        P(None, "fsdp", "seq", None),
        P(None, "fsdp", "seq", None),
        P("fsdp", None),
        P(None, ("seq", "fsdp")),
        P(None, ("seq", "fsdp"), None),
        P(None, ("seq", "fsdp"), None),
        P(None, ("seq", "fsdp"), None),
        P(None, ("seq", "fsdp"), None),
        P(None, ("seq", "fsdp")),
        P(None, ("seq", "fsdp"), None),
        P(None, "seq", "fsdp", None),
        P(None, "seq", "fsdp", None),
        P(None, "seq", "fsdp", None),
    )
    out_specs = (
        P("fsdp", "seq", None),
        P("fsdp", "seq", None),
        P(None, ("seq", "fsdp")),
        P(None, ("seq", "fsdp"), None),
        P(None, ("seq", "fsdp"), None),
        P(None, ("seq", "fsdp"), None),
        P(None, ("seq", "fsdp"), None),
        P(None, ("seq", "fsdp")),
        P(None, ("seq", "fsdp"), None),
        P(None, "seq", "fsdp", None),
        P(None, "seq", "fsdp", None),
        P(None, "seq", "fsdp", None),
    )
    return jax.shard_map(
        per_device, mesh=mesh, in_specs=in_specs, out_specs=out_specs, check_vma=False
    )
```

time: 2730 us -> 783 us (0.29)
  blocking collectives: 1150 us -> 159 us
  starting transfers between devices: 737 us -> 74 us
  local copies, waits for them, and re-layouts: 426 us -> 60.4 us
  matrix products: 175 us -> 5.25 us
  Pallas kernels: 0 us -> 165 us
  waiting for transfers between devices: 144 us -> 275 us
  other arithmetic: 49.8 us -> 18.2 us
    unnamed x3 -> x0, blocking collectives: 873 us -> none
    unnamed x259 -> x0, starting transfers between devices: 663 us -> none
    unnamed x660 -> x207, local copies, waits for them, and re-layouts: 296 us -> 45.8 us
    all_gather x6 -> x2, blocking collectives: 254 us -> 26.9 us  [gather_seq(): return lax.all_gather(block, 'seq', axis=0, tiled=False)]
    dot_general x60 -> x2, matrix products: 175 us -> 5.25 us  [fetch(): lax.dot_general(qkv[:, qkv_width:qkv_width + 16], spread, (((0,), (1,)),...]
    pallas_call x0 -> x25, Pallas kernels: none -> 165 us  [run(): pl.pallas_call(kernel, out_shape=list(outs), compiler_params=pltpu.Compil...]
    all_to_all x1 -> x7, blocking collectives: 20.9 us -> 132 us  [swap_seq(): return lax.all_to_all(block, 'seq', split_axis=0, concat_axis=0, tiled=True)]
    all_gather x10 -> x4, waiting for transfers between devices: 14.1 us -> 95 us  [the longest x2 66.3 us: fetch(): pack = lax.all_gather(pack, 'fsdp', axis=0, tiled=False)]
  transfers between devices with their start and end apart: 292 -> 31, of which waited for: 16 -> 24; matrix products, arithmetic and copies ran while one was open for 48% -> 4% of each run, Pallas kernels for 0% -> 18%
where the time goes in v1:
time: 783 us; the launch traced here: 773 us
  waiting for transfers between devices  275 us (35%)
  Pallas kernels  165 us (21%)
  blocking collectives  159 us (20%)
  starting transfers between devices  74 us (9%)
  local copies, waits for them, and re-layouts  60.4 us (8%)
  other arithmetic  18.2 us (2%)
  between operations  15.6 us (2%)
    pallas_call x25, Pallas kernels, run(): pl.pallas_call(kernel, out_shape=list(outs), compiler_params=pltpu.Compil...  165 us
    all_to_all x7, blocking collectives, swap_seq(): return lax.all_to_all(block, 'seq', split_axis=0, concat_axis=0, tiled=True)  132 us
    all_to_all x11, waiting for transfers between devices, swap_seq(): return lax.all_to_all(block, 'seq', split_axis=0, concat_axis=0, tiled=True)  77 us
    all_gather x2, waiting for transfers between devices, fetch(): pack = lax.all_gather(pack, 'fsdp', axis=0, tiled=False)  66.3 us
    ppermute x12, waiting for transfers between devices, around_seq(): lax.ppermute(block, 'seq', [((i + k) % count, i) for i in range(count)])  57.6 us
    unnamed x207, local copies, waits for them, and re-layouts  45.8 us
    all_to_all x11, starting transfers between devices, swap_seq(): return lax.all_to_all(block, 'seq', split_axis=0, concat_axis=0, tiled=True)  43 us
    all_to_all x2, waiting for transfers between devices, shard_sum(): lax.all_to_all(block, 'fsdp', split_axis=0, concat_axis=0, tiled=True)  41.3 us
  transfers between devices with their start and end apart: 31, of which 24 were waited for; matrix products, arithmetic and copies ran while one was open for 4% of the time, Pallas kernels for 18%

profile of v1, /device:TPU:0, one launch (start us, length us, event | category | flops | bytes accessed | tf_op | source)
XLA Modules:
  0.0 772.9 jit_solution(7199581979328542249)
XLA Ops:
  13.8 14.0 %all-gather.4 = bf16[4,12,3712]{2,1,0:T(8,128)(2,1)S(1)} all-gather(bf16[1,12,3712]{2,1,0:T(8,128)(2,1)S(1)} %bitcast.190), channel_id=2, replica_groups=mesh['seq'=4,'fsdp'=32] {'seq'}, dimensions={0}, use_global_device_ids=true | all-gather | bytes 445440 | tf_op jit(solution)/shard_map/all_gather | solution.py:483
  30.2 13.0 %all-gather.5 = bf16[4,12,3712]{2,1,0:T(8,128)(2,1)S(1)} all-gather(bf16[1,12,3712]{2,1,0:T(8,128)(2,1)S(1)} %bitcast.189), channel_id=4, replica_groups=mesh['seq'=4,'fsdp'=32] {'seq'}, dimensions={0}, use_global_device_ids=true | all-gather | bytes 445440 | tf_op jit(solution)/shard_map/all_gather | solution.py:483
  51.9 28.1 %all-gather.11.cloned.1.call-done.weight = bf16[1536,2176]{1,0:T(8,128)(2,1)} async-done(((bf16[48,2176]{1,0:T(8,128)(2,1)}), bf16[1536,2176]{1,0:T(8,128)(2,1)}) %all-gather.11.cloned.1.call-update) | async-done | bytes 6684688 | tf_op jit(solution)/shard_map/all_gather | solution.py:579
  95.3 10.1 %all-to-all-done.heads_ref = bf16[4,128,640]{2,1,0:T(8,128)(2,1)S(1)} async-done(((bf16[4,128,640]{2,1,0:T(8,128)(2,1)}), bf16[4,128,640]{2,1,0:T(8,128)(2,1)S(1)}, u32[]{:S(2)}, u32[]{:S(2)}) %all-to-all-start) | async-done | bytes 655392 | tf_op jit(solution)/shard_map/all_to_all | solution.py:487
  120.0 39.2 %all-gather.15.cloned.1.call-done = bf16[12288,768]{1,0:T(8,128)(2,1)} async-done(((bf16[384,768]{1,0:T(8,128)(2,1)}), bf16[12288,768]{1,0:T(8,128)(2,1)}) %all-gather.15.cloned.1.call-update) | async-done | bytes 18874384 | tf_op jit(solution)/shard_map/all_gather | solution.py:586
  167.0 27.6 %all_to_all.100.rows_ref = bf16[4,2,72,1536]{3,2,1,0:T(8,128)(2,1)} all-to-all(bf16[4,2,72,1536]{3,2,1,0:T(8,128)(2,1)S(1)} %bitcast.169), channel_id=1, replica_groups=mesh['seq'=4,'fsdp'=32] {'seq'}, dimensions={0} | all-to-all | bytes 3538944 | tf_op jit(solution)/shard_map/all_to_all | solution.py:487
  213.4 18.9 %all-to-all-done.3 = bf16[4,2,72,1536]{3,2,1,0:T(8,128)(2,1)S(1)} async-done(((bf16[4,2,72,1536]{3,2,1,0:T(8,128)(2,1)}), bf16[4,2,72,1536]{3,2,1,0:T(8,128)(2,1)S(1)}, u32[]{:S(2)}, u32[]{:S(2)}) %all-to-all-start.3) | async-done | bytes 1769504 | tf_op jit(solution)/shard_map/all_to_all | solution.py:487
  242.7 11.8 %all_to_all.101.heads_ref = bf16[4,128,640]{2,1,0:T(8,128)(2,1)S(1)} all-to-all(bf16[4,128,640]{2,1,0:T(8,128)(2,1)S(1)} %get-tuple-element.64), channel_id=1, replica_groups=mesh['seq'=4,'fsdp'=32] {'seq'}, dimensions={0} | all-to-all | bytes 1310720 | tf_op jit(solution)/shard_map/all_to_all | solution.py:487
  262.6 27.1 %all-gather.17.cloned.1.call-done = bf16[12288,768]{1,0:T(8,128)(2,1)} async-done(((bf16[384,768]{1,0:T(8,128)(2,1)}), bf16[12288,768]{1,0:T(8,128)(2,1)}) %all-gather.17.cloned.1.call-update) | async-done | bytes 18874384 | tf_op jit(solution)/shard_map/all_gather | solution.py:586
  297.6 27.6 %all_to_all.102.rows_ref = bf16[4,2,72,1536]{3,2,1,0:T(8,128)(2,1)} all-to-all(bf16[4,2,72,1536]{3,2,1,0:T(8,128)(2,1)S(1)} %bitcast.170), channel_id=1, replica_groups=mesh['seq'=4,'fsdp'=32] {'seq'}, dimensions={0} | all-to-all | bytes 3538944 | tf_op jit(solution)/shard_map/all_to_all | solution.py:487
  340.1 22.1 %all-to-all-done.7 = bf16[4,2,72,1536]{3,2,1,0:T(8,128)(2,1)S(1)} async-done(((bf16[4,2,72,1536]{3,2,1,0:T(8,128)(2,1)}), bf16[4,2,72,1536]{3,2,1,0:T(8,128)(2,1)S(1)}, u32[]{:S(2)}, u32[]{:S(2)}) %all-to-all-start.7) | async-done | bytes 1769504 | tf_op jit(solution)/shard_map/all_to_all | solution.py:487
  364.8 23.8 %all_to_all.103.grad_ref = bf16[4,2,72,1536]{3,2,1,0:T(8,128)(2,1)S(1)} all-to-all(bf16[4,2,72,1536]{3,2,1,0:T(8,128)(2,1)S(1)} %bitcast.172), channel_id=1, replica_groups=mesh['seq'=4,'fsdp'=32] {'seq'}, dimensions={0} | all-to-all | bytes 3538944 | tf_op jit(solution)/shard_map/all_to_all | solution.py:487
  388.6 10.0 %shard_map.248 = (bf16[4,2,72,1536]{3,2,1,0:T(8,128)(2,1)S(1)}, bf16[2,288,768]{2,1,0:T(8,128)(2,1)S(1)}, bf16[2,288,768]{2,1,0:T(8,128)(2,1)S(1)}, bf16[2,288,768]{2,1,0:T(8,128)(2,1)S(1)}) custom-call(bf16[4,2,72,1536]{3,2,1,0:T(8,128)(2,1)S(1)} %all_to_all.103.grad_ref, bf16[32,384,768]{2,1,0:T(8,128)(2,1)} %bitcast.179, f32[2,288,768]{2,1,0:T(8,128)} %copy-done.29, ...), custom_call_target="tpu_custom_call" | custom-call | flops 4076863488 | bytes 28606464 | tf_op jit(solution)/shard_map/pallas_call | solution.py:80
  410.8 10.9 %shard_map.249 = bf16[32,288,768]{2,1,0:T(8,128)(2,1)} custom-call(bf16[4,2,72,1536]{3,2,1,0:T(8,128)(2,1)S(1)} %copy-done, bf16[4,2,72,1536]{3,2,1,0:T(8,128)(2,1)S(1)} %all_to_all.103.grad_ref, bf16[2,288,768]{2,1,0:T(8,128)(2,1)S(1)} %copy-done.41, bf16[2,288,768]{2,1,0:T(8,128)(2,1)S(1)} %copy-done.43, bf16[2,288,768]{2,1,0:T(8,128)(2,1)S(1)} %copy-done.45), custom_call_target="tpu_custom_call" | custom-call | flops 4076863488 | bytes 20348928 | tf_op jit(solution)/shard_map/pallas_call | solution.py:80
  458.3 11.4 %all_to_all.104.sent = bf16[4,128,640]{2,1,0:T(8,128)(2,1)S(1)} all-to-all(bf16[4,128,640]{2,1,0:T(8,128)(2,1)S(1)} %shard_map.251.grads), channel_id=1, replica_groups=mesh['seq'=4,'fsdp'=32] {'seq'}, dimensions={0} | all-to-all | bytes 1310720 | tf_op jit(solution)/shard_map/all_to_all | solution.py:487
  469.7 9.8 %shard_map.252 = (f32[128,1536]{1,0:T(8,128)S(1)}, f32[16,1536]{1,0:T(8,128)S(1)}) custom-call(f32[128,1536]{1,0:T(8,128)S(1)} %copy-done.51, bf16[4,128,640]{2,1,0:T(8,128)(2,1)S(1)} %all_to_all.104.sent, f32[128,1536]{1,0:T(8,128)S(1)} %copy-done.17, bf16[16,1536]{1,0:T(8,128)(2,1)S(1)} %copy-done.55, bf16[1536,1536]{1,0:T(8,128)(2,1)} %fusion.1.spread, ...), custom_call_target="tpu_custom_call" | custom-call | flops 2415919104 | bytes 14663680 | tf_op jit(solution)/shard_map/pallas_call | solution.py:80
  482.7 19.8 %all_to_all.105.grad_ref = bf16[4,2,72,1536]{3,2,1,0:T(8,128)(2,1)S(1)} all-to-all(bf16[4,2,72,1536]{3,2,1,0:T(8,128)(2,1)S(1)} %bitcast.171), channel_id=1, replica_groups=mesh['seq'=4,'fsdp'=32] {'seq'}, dimensions={0} | all-to-all | bytes 3538944 | tf_op jit(solution)/shard_map/all_to_all | solution.py:487
  502.5 10.7 %shard_map.254 = (bf16[4,2,72,1536]{3,2,1,0:T(8,128)(2,1)S(1)}, bf16[2,288,768]{2,1,0:T(8,128)(2,1)S(1)}, bf16[2,288,768]{2,1,0:T(8,128)(2,1)S(1)}, bf16[2,288,768]{2,1,0:T(8,128)(2,1)S(1)}) custom-call(bf16[4,2,72,1536]{3,2,1,0:T(8,128)(2,1)S(1)} %all_to_all.105.grad_ref, bf16[32,384,768]{2,1,0:T(8,128)(2,1)} %bitcast.175, f32[2,288,768]{2,1,0:T(8,128)} %copy-done.27, ...), custom_call_target="tpu_custom_call" | custom-call | flops 4076863488 | bytes 28606464 | tf_op jit(solution)/shard_map/pallas_call | solution.py:80
  529.6 22.5 %collective-permute-done.3.one = bf16[128,1536]{1,0:T(8,128)(2,1)S(1)} collective-permute-done((bf16[128,1536]{1,0:T(8,128)(2,1)}, bf16[128,1536]{1,0:T(8,128)(2,1)S(1)}, u32[]{:S(2)}, u32[]{:S(2)}) %collective-permute-start.3) | collective-permute-done | bytes 393248 | tf_op jit(solution)/shard_map/ppermute | solution.py:493
  576.6 14.0 %shard_map.257 = bf16[32,368,768]{2,1,0:T(8,128)(2,1)} custom-call(bf16[4,2,72,1536]{3,2,1,0:T(8,128)(2,1)S(1)} %copy-done.1, bf16[4,2,72,1536]{3,2,1,0:T(8,128)(2,1)} %copy-done.2, bf16[2,288,768]{2,1,0:T(8,128)(2,1)S(1)} %copy-done.35, bf16[2,288,768]{2,1,0:T(8,128)(2,1)S(1)} %copy-done.37, bf16[2,288,768]{2,1,0:T(8,128)(2,1)S(1)} %copy-done.39, ...), custom_call_target="tpu_custom_call" | custom-call | flops 4076863488 | bytes 28213248 | tf_op jit(solution)/shard_map/pallas_call | solution.py:80
  603.6 9.9 %all_to_all.106.grad_ref = bf16[4,128,384]{2,1,0:T(8,128)(2,1)S(1)} all-to-all(bf16[4,128,384]{2,1,0:T(8,128)(2,1)S(1)} %get-tuple-element.98), channel_id=1, replica_groups=mesh['seq'=4,'fsdp'=32] {'seq'}, dimensions={0} | all-to-all | bytes 786432 | tf_op jit(solution)/shard_map/all_to_all | solution.py:487
  653.4 10.7 %shard_map.260 = (f32[128,1536]{1,0:T(8,128)}, f32[16,1536]{1,0:T(8,128)S(1)}) custom-call(f32[128,1536]{1,0:T(8,128)S(1)} %copy-done.47, bf16[4,128,640]{2,1,0:T(8,128)(2,1)S(1)} %all-to-all-done.15.sent, bf16[128,1536]{1,0:T(8,128)(2,1)S(1)} %bitcast.168, bf16[16,1536]{1,0:T(8,128)(2,1)S(1)} %copy-done.53, bf16[1536,1536]{1,0:T(8,128)(2,1)} %fusion.1.spread, ...), custom_call_target="tpu_custom_call" | custom-call | flops 2415919104 | bytes 14270464 | tf_op jit(solution)/shard_map/pallas_call | solution.py:80
  678.9 10.0 %all-to-all-done.19 = bf16[32,32,768]{2,1,0:T(8,128)(2,1)} async-done(((bf16[32,32,768]{2,1,0:T(8,128)(2,1)}), bf16[32,32,768]{2,1,0:T(8,128)(2,1)}, u32[]{:S(2)}, u32[]{:S(2)}) %all-to-all-start.19) | async-done | bytes 1572896 | tf_op jit(solution)/shard_map/all_to_all | solution.py:807
  697.5 31.3 %all-to-all-done.16 = bf16[32,48,768]{2,1,0:T(8,128)(2,1)} async-done(((bf16[32,48,768]{2,1,0:T(8,128)(2,1)}), bf16[32,48,768]{2,1,0:T(8,128)(2,1)}, u32[]{:S(2)}, u32[]{:S(2)}) %all-to-all-start.16) | async-done | bytes 2359328 | tf_op jit(solution)/shard_map/all_to_all | solution.py:807
  (401 shorter events, 323.1 us)
Async XLA Ops:
  7.2 72.9 %all-gather.11.cloned.1.call-start = ((), (), s32[]{:S(2)}) async-start(), calls=%async_computation.22 | async-start | bytes 6893568 | tf_op jit(solution)/shard_map/all_gather | solution.py:579
  28.5 130.7 %all-gather.15.cloned.1.call-start = ((), (), s32[]{:S(2)}) async-start(), calls=%async_computation.26 | async-start | bytes 19464192 | tf_op jit(solution)/shard_map/all_gather | solution.py:586
  29.7 181.1 %all-gather.13.cloned.1.call-start = ((), (), s32[]{:S(2)}) async-start(), calls=%async_computation.23 | async-start | bytes 6893568 | tf_op jit(solution)/shard_map/all_gather | solution.py:579
  43.9 245.8 %all-gather.17.cloned.1.call-start = ((), (), s32[]{:S(2)}) async-start(), calls=%async_computation.27 | async-start | bytes 19464192 | tf_op jit(solution)/shard_map/all_gather | solution.py:586
  89.7 15.7 %all-to-all-start = ((bf16[4,128,640]{2,1,0:T(8,128)(2,1)}), bf16[4,128,640]{2,1,0:T(8,128)(2,1)S(1)}, u32[]{:S(2)}, u32[]{:S(2)}) async-start(bf16[4,128,640]{2,1,0:T(8,128)(2,1)} %get-tuple-element.59), calls=%async_computation | async-start | bytes 1310720 | tf_op jit(solution)/shard_map/all_to_all | solution.py:487
  206.6 25.7 %all-to-all-start.3 = ((bf16[4,2,72,1536]{3,2,1,0:T(8,128)(2,1)}), bf16[4,2,72,1536]{3,2,1,0:T(8,128)(2,1)S(1)}, u32[]{:S(2)}, u32[]{:S(2)}) async-start(bf16[4,2,72,1536]{3,2,1,0:T(8,128)(2,1)} %copy-done.33), calls=%async_computation.3 | async-start | bytes 3538944 | tf_op jit(solution)/shard_map/all_to_all | solution.py:487
  258.8 31.0 %all-to-all-start.5 = ((bf16[4,128,384]{2,1,0:T(8,128)(2,1)}), bf16[4,128,384]{2,1,0:T(8,128)(2,1)S(1)}, u32[]{:S(2)}, u32[]{:S(2)}) async-start(bf16[4,128,384]{2,1,0:T(8,128)(2,1)} %shard_map.243.attended), calls=%async_computation.5 | async-start | bytes 786432 | tf_op jit(solution)/shard_map/all_to_all | solution.py:487
  336.3 25.9 %all-to-all-start.7 = ((bf16[4,2,72,1536]{3,2,1,0:T(8,128)(2,1)}), bf16[4,2,72,1536]{3,2,1,0:T(8,128)(2,1)S(1)}, u32[]{:S(2)}, u32[]{:S(2)}) async-start(bf16[4,2,72,1536]{3,2,1,0:T(8,128)(2,1)} %get-tuple-element.68), calls=%async_computation.7 | async-start | bytes 3538944 | tf_op jit(solution)/shard_map/all_to_all | solution.py:487
  402.6 24.7 %all-to-all-start.9 = ((bf16[4,2,72,1536]{3,2,1,0:T(8,128)(2,1)}), bf16[4,2,72,1536]{3,2,1,0:T(8,128)(2,1)}, u32[]{:S(2)}, u32[]{:S(2)}) async-start(bf16[4,2,72,1536]{3,2,1,0:T(8,128)(2,1)} %copy-done.32), calls=%async_computation.9 | async-start | bytes 3538944 | tf_op jit(solution)/shard_map/all_to_all | solution.py:487
  407.1 335.6 %reduce-scatter.5.cloned.1.call-start = ((), (), s32[]{:S(2)}) async-start(), calls=%async_computation.25 | async-start | bytes 14598144 | tf_op jit(solution)/shard_map/reduce_scatter | solution.py:684
  517.2 73.5 %all-to-all-start.13 = ((bf16[4,2,72,1536]{3,2,1,0:T(8,128)(2,1)}), bf16[4,2,72,1536]{3,2,1,0:T(8,128)(2,1)S(1)}, u32[]{:S(2)}, u32[]{:S(2)}) async-start(bf16[4,2,72,1536]{3,2,1,0:T(8,128)(2,1)} %copy-done.31), calls=%async_computation.13 | async-start | bytes 3538944 | tf_op jit(solution)/shard_map/all_to_all | solution.py:487
  520.8 228.7 %reduce-scatter.3.cloned.1.call-start = ((), (), s32[]{:S(2)}) async-start(), calls=%async_computation.24 | async-start | bytes 18653184 | tf_op jit(solution)/shard_map/reduce_scatter | solution.py:684
  520.9 31.2 %collective-permute-start.3 = (bf16[128,1536]{1,0:T(8,128)(2,1)}, bf16[128,1536]{1,0:T(8,128)(2,1)S(1)}, u32[]{:S(2)}, u32[]{:S(2)}) collective-permute-start(bf16[128,1536]{1,0:T(8,128)(2,1)} %copy-done.62), channel_id=1, source_target_pairs={{32,0},{64,32},{96,64},{0,96},{33,1},{65,33},{97,65},{1,97},{34,2}... | collective-permute-start | bytes 1179656 | tf_op jit(solution)/shard_map/ppermute | solution.py:493
  524.0 30.4 %collective-permute-start.4 = (bf16[128,1536]{1,0:T(8,128)(2,1)}, bf16[128,1536]{1,0:T(8,128)(2,1)S(1)}, u32[]{:S(2)}, u32[]{:S(2)}) collective-permute-start(bf16[128,1536]{1,0:T(8,128)(2,1)} %copy-done.62), channel_id=1, source_target_pairs={{64,0},{96,32},{0,64},{32,96},{65,1},{97,33},{1,65},{33,97},{66,2}... | collective-permute-start | bytes 1179656 | tf_op jit(solution)/shard_map/ppermute | solution.py:493
  524.9 37.5 %collective-permute-start.5 = (bf16[128,1536]{1,0:T(8,128)(2,1)}, bf16[128,1536]{1,0:T(8,128)(2,1)S(1)}, u32[]{:S(2)}, u32[]{:S(2)}) collective-permute-start(bf16[128,1536]{1,0:T(8,128)(2,1)} %copy-done.62), channel_id=1, source_target_pairs={{96,0},{0,32},{32,64},{64,96},{97,1},{1,33},{33,65},{65,97},{98,2}... | collective-permute-start | bytes 1179656 | tf_op jit(solution)/shard_map/ppermute | solution.py:493
  525.7 40.1 %collective-permute-start = (bf16[128,1536]{1,0:T(8,128)(2,1)}, bf16[128,1536]{1,0:T(8,128)(2,1)S(1)}, u32[]{:S(2)}, u32[]{:S(2)}) collective-permute-start(bf16[128,1536]{1,0:T(8,128)(2,1)} %copy-done.58), channel_id=1, source_target_pairs={{32,0},{64,32},{96,64},{0,96},{33,1},{65,33},{97,65},{1,97},{34,2}... | collective-permute-start | bytes 1179656 | tf_op jit(solution)/shard_map/ppermute | solution.py:493
  528.1 38.7 %collective-permute-start.1 = (bf16[128,1536]{1,0:T(8,128)(2,1)}, bf16[128,1536]{1,0:T(8,128)(2,1)S(1)}, u32[]{:S(2)}, u32[]{:S(2)}) collective-permute-start(bf16[128,1536]{1,0:T(8,128)(2,1)} %copy-done.58), channel_id=1, source_target_pairs={{64,0},{96,32},{0,64},{32,96},{65,1},{97,33},{1,65},{33,97},{66,2}... | collective-permute-start | bytes 1179656 | tf_op jit(solution)/shard_map/ppermute | solution.py:493
  552.0 18.6 %collective-permute-start.2 = (bf16[128,1536]{1,0:T(8,128)(2,1)}, bf16[128,1536]{1,0:T(8,128)(2,1)S(1)}, u32[]{:S(2)}, u32[]{:S(2)}) collective-permute-start(bf16[128,1536]{1,0:T(8,128)(2,1)} %copy-done.58), channel_id=1, source_target_pairs={{96,0},{0,32},{32,64},{64,96},{97,1},{1,33},{33,65},{65,97},{98,2}... | collective-permute-start | bytes 1179656 | tf_op jit(solution)/shard_map/ppermute | solution.py:493
  618.4 25.7 %all-to-all-start.15 = ((bf16[4,128,640]{2,1,0:T(8,128)(2,1)}), bf16[4,128,640]{2,1,0:T(8,128)(2,1)S(1)}, u32[]{:S(2)}, u32[]{:S(2)}) async-start(bf16[4,128,640]{2,1,0:T(8,128)(2,1)} %shard_map.259.grads), calls=%async_computation.15 | async-start | bytes 1310720 | tf_op jit(solution)/shard_map/all_to_all | solution.py:487
  626.0 14.5 %collective-permute-start.11 = (bf16[128,1536]{1,0:T(8,128)(2,1)S(1)}, bf16[128,1536]{1,0:T(8,128)(2,1)S(1)}, u32[]{:S(2)}, u32[]{:S(2)}) collective-permute-start(bf16[128,1536]{1,0:T(8,128)(2,1)S(1)} %get-tuple-element.104.own), channel_id=1, source_target_pairs={{96,0},{0,32},{32,64},{64,96},{97,1},{1,33},{33,65},{65,97},{98,2}... | collective-permute-start | bytes 1179656 | tf_op jit(solution)/shard_map/ppermute | solution.py:493
  644.1 44.8 %all-to-all-start.19 = ((bf16[32,32,768]{2,1,0:T(8,128)(2,1)}), bf16[32,32,768]{2,1,0:T(8,128)(2,1)}, u32[]{:S(2)}, u32[]{:S(2)}) async-start(bf16[32,32,768]{2,1,0:T(8,128)(2,1)} %shard_map.262), calls=%async_computation.20 | async-start | bytes 3145728 | tf_op jit(solution)/shard_map/all_to_all | solution.py:807
  651.9 13.5 %collective-permute-start.7 = (bf16[128,1536]{1,0:T(8,128)(2,1)S(1)}, bf16[128,1536]{1,0:T(8,128)(2,1)S(1)}, u32[]{:S(2)}, u32[]{:S(2)}) collective-permute-start(bf16[128,1536]{1,0:T(8,128)(2,1)S(1)} %copy-done.57), channel_id=1, source_target_pairs={{64,0},{96,32},{0,64},{32,96},{65,1},{97,33},{1,65},{33,97},{66,2}... | collective-permute-start | bytes 1179656 | tf_op jit(solution)/shard_map/ppermute | solution.py:493
  653.4 19.4 %collective-permute-start.8 = (bf16[128,1536]{1,0:T(8,128)(2,1)S(1)}, bf16[128,1536]{1,0:T(8,128)(2,1)S(1)}, u32[]{:S(2)}, u32[]{:S(2)}) collective-permute-start(bf16[128,1536]{1,0:T(8,128)(2,1)S(1)} %copy-done.57), channel_id=1, source_target_pairs={{96,0},{0,32},{32,64},{64,96},{97,1},{1,33},{33,65},{65,97},{98,2}... | collective-permute-start | bytes 1179656 | tf_op jit(solution)/shard_map/ppermute | solution.py:493
  688.9 39.9 %all-to-all-start.16 = ((bf16[32,48,768]{2,1,0:T(8,128)(2,1)}), bf16[32,48,768]{2,1,0:T(8,128)(2,1)}, u32[]{:S(2)}, u32[]{:S(2)}) async-start(bf16[32,48,768]{2,1,0:T(8,128)(2,1)} %shard_map.261), calls=%async_computation.16 | async-start | bytes 4718592 | tf_op jit(solution)/shard_map/all_to_all | solution.py:807
  (102 other events, 1191.4 us)
Sparse Core Ops, SparseCore 0:
  28.7 51.3 all-gather.10
  82.9 76.3 all-gather.14
  161.6 49.1 all-gather.12
  213.5 76.2 all-gather.16
  427.4 105.9 reduce-scatter.4
  590.8 158.6 reduce-scatter.2

commit v2 on v1

v2 whole, which is shorter than its diff:
```python
import functools

import jax
import jax.numpy as jnp
import numpy as np
from jax import lax
from jax.experimental import pallas as pl
from jax.experimental.pallas import tpu as pltpu
from jax.sharding import PartitionSpec as P

HEADS = 12
KVHEADS = 2
HD = 128
TOPK = 4
LAYERS = 2
NCONT = 4

norm_eps = 1e-06
rope_base = 10000.0
masked_value = -1e30

bf16 = jnp.bfloat16
f32 = jnp.float32
VMEM_BYTES = 64 * 1024 * 1024 - 256 * 1024


def group_tables(segment_row, prompt_len):
    cont_len = segment_row.shape[0]
    onehot = (segment_row[:, None] == jnp.arange(NCONT, dtype=jnp.int32)[None, :]).astype(jnp.int32)
    counts = jnp.sum(onehot, axis=0)
    starts = jnp.cumsum(counts) - counts
    seg_begin = jnp.sum(onehot * starts[None, :], axis=1)
    within = jnp.arange(cont_len, dtype=jnp.int32) - seg_begin
    positions = jnp.concatenate([jnp.arange(prompt_len, dtype=jnp.int32), prompt_len + within])
    labels = jnp.concatenate([jnp.full((prompt_len,), -1, jnp.int32), segment_row])
    frequency = rope_base ** (-(jnp.arange(HD // 2, dtype=jnp.float32) * 2.0 / HD))
    angles = positions.astype(jnp.float32)[:, None] * frequency[None, :]
    return (jnp.cos(angles), jnp.sin(angles), labels)


def slot_table(expert_rows, order_rows, expert_count, capacity):
    pair_expert = expert_rows.reshape(-1)
    pair_order = order_rows.reshape(-1)
    same_expert = pair_expert[:, None] == pair_expert[None, :]
    earlier = pair_order[None, :] < pair_order[:, None]
    pair_slot = jnp.sum(jnp.logical_and(same_expert, earlier).astype(jnp.int32), axis=1)
    target = jnp.where(
        pair_slot < capacity, pair_expert * capacity + pair_slot, expert_count * capacity
    )
    return target.reshape(expert_rows.shape).T


def nn(left, right):
    return lax.dot_general(left, right, (((1,), (0,)), ((), ())), preferred_element_type=f32)


def nt(left, right):
    return lax.dot_general(left, right, (((1,), (1,)), ((), ())), preferred_element_type=f32)


def tn(left, right):
    return lax.dot_general(left, right, (((0,), (0,)), ((), ())), preferred_element_type=f32)


def split(value):
    high = value.astype(bf16)
    return high, (value - high.astype(f32)).astype(bf16)


class Late:
    def __init__(self, ref, copy):
        self.ref, self.copy, self.shape = ref, copy, ref.shape
        copy.start()

    def wait(self):
        if self.copy is not None:
            self.copy.wait()
            self.copy = None

    def __getitem__(self, index):
        self.wait()
        return self.ref[index]


class Out:
    def __init__(self, ref, copies):
        self.ref, self.copies, self.shape = ref, copies, ref.shape
        self.sent = [False] * len(copies)

    def send(self, piece=None):
        for n in range(len(self.copies)) if piece is None else (piece,):
            if not self.sent[n]:
                self.copies[n].start()
                self.sent[n] = True

    def __getitem__(self, index):
        return self.ref[index]

    def __setitem__(self, index, value):
        self.ref[index] = value


def cost(args, outs, flops):
    moved = sum(int(np.prod(a.shape)) * a.dtype.itemsize for a in (*args, *outs))
    return pl.CostEstimate(flops=flops, bytes_accessed=moved, transcendentals=0)


def once(kernel, outs, *args, scalar=False, cut=None, pieces=None, flops=0):
    cut, pieces = cut or {}, pieces or {}
    hbm = pl.BlockSpec(memory_space=pltpu.HBM)
    late = [n for n in range(len(args)) if not (scalar and n == 0)]
    specs = [hbm] * len(args)
    if scalar:
        specs[0] = pl.BlockSpec(memory_space=pltpu.SMEM)
    scratch = []
    for n in late:
        dims = list(args[n].shape)
        for dim, start, size in cut.get(n, ()):
            dims[dim] = size
        scratch.append(pltpu.VMEM(tuple(dims), args[n].dtype))
    scratch += [pltpu.VMEM(o.shape, o.dtype) for o in outs]
    parts = [pieces.get(n, (0, 1)) for n in range(len(outs))]
    scratch.append(pltpu.SemaphoreType.DMA((len(late) + sum(count for _, count in parts),)))

    def body(*refs):
        ins = list(refs[: len(args)])
        out_refs = refs[len(args) : len(args) + len(outs)]
        rooms = refs[len(args) + len(outs) : -1]
        sems = refs[-1]
        for i, n in enumerate(late):
            source = ins[n]
            for dim, start, size in cut.get(n, ()):
                if callable(start):
                    start = pl.multiple_of(start(ins[0][0]), 16 if dim == 1 else HD)
                source = source.at[(slice(None),) * dim + (pl.ds(start, size),)]
            ins[n] = Late(rooms[i], pltpu.make_async_copy(source, rooms[i], sems.at[i]))
        results = []
        used = len(late)
        for i, out in enumerate(out_refs):
            room = rooms[len(late) + i]
            dim, count = parts[i]
            size = room.shape[dim] // count
            copies = []
            for n in range(count):
                at = (slice(None),) * dim + (pl.ds(n * size, size),)
                copies.append(pltpu.make_async_copy(room.at[at], out.at[at], sems.at[used]))
                used += 1
            results.append(Out(room, copies))
        kernel(*ins, *results)
        for result in results:
            result.send()
        for n in late:
            ins[n].wait()
        for result in results:
            for copy in result.copies:
                copy.wait()

    return pl.pallas_call(
        body,
        out_shape=list(outs),
        in_specs=specs,
        out_specs=[hbm] * len(outs),
        scratch_shapes=scratch,
        compiler_params=pltpu.CompilerParams(vmem_limit_bytes=VMEM_BYTES),
        cost_estimate=cost(args, outs, flops),
    )(*args)


def shape(dims, dtype):
    return jax.ShapeDtypeStruct(dims, dtype)


def normalize(value, gain):
    inverse = lax.rsqrt(jnp.mean(value * value, axis=-1, keepdims=True) + norm_eps)
    return value * inverse * gain


def normalize_back(value, gain, grad):
    inverse = lax.rsqrt(jnp.mean(value * value, axis=-1, keepdims=True) + norm_eps)
    unit = value * inverse
    grad_gain = jnp.sum(grad * unit, axis=0, keepdims=True)
    scaled = grad * gain
    grad_value = inverse * (scaled - unit * jnp.mean(scaled * unit, axis=-1, keepdims=True))
    return grad_value, grad_gain


def to_gathered(parts, order):
    count = len(parts)
    share = parts[0].shape[1] // count
    done = []
    for j in range(count):
        piece = jnp.concatenate([part[:, j * share : (j + 1) * share] for part in parts], axis=1)
        done.append(nn(piece, order))
    return jnp.concatenate(done, axis=1)


def to_natural(value, order):
    count = value.shape[1] // order.shape[0]
    size = order.shape[0]
    share = size // count
    done = [nt(value[:, j * size : (j + 1) * size], order) for j in range(count)]
    return [
        jnp.concatenate([part[:, s * share : (s + 1) * share] for part in done], axis=1)
        for s in range(count)
    ]


def column_blocks(value, count):
    size = value.shape[1] // count
    return [value[:, s * size : (s + 1) * size] for s in range(count)]


def turn(block, cosines, sines):
    return block * cosines + pltpu.roll(block, HD // 2, 1) * sines


def smooth_parts(value):
    root = np.float32(np.sqrt(2.0 / np.pi))
    square = value * value
    high = jnp.tanh(root * (value + 0.044715 * value * square))
    half = 0.5 * (1.0 + high)
    slope = half + 0.5 * value * (1.0 - high * high) * root * (1.0 + 3 * 0.044715 * square)
    return value * half, slope


def choose(target_t, slots):
    place = lax.broadcasted_iota(jnp.int32, (slots, target_t.shape[1]), 0)
    total = jnp.zeros(place.shape, f32)
    for k in range(TOPK):
        total = total + jnp.where(place == target_t[k : k + 1], 1.0, 0.0)
    return total


def choose_weighted(target_t, gates_t, slots):
    place = lax.broadcasted_iota(jnp.int32, (slots, target_t.shape[1]), 0)
    total = jnp.zeros(place.shape, f32)
    for k in range(TOPK):
        total = total + jnp.where(place == target_t[k : k + 1], gates_t[k : k + 1], 0.0)
    return total


def input_kernel(
    middle, combined, gates_t, target_t, small, spread, normed_ref, hidden_ref
):
    expert_count = 8
    hidden = middle[...] + mix(combined[...], gates_t[...], target_t[...])
    hidden_ref[...] = hidden
    hidden_ref.send()
    gain = small[expert_count : expert_count + 1].astype(f32)
    normed = normalize(hidden, gain).astype(bf16)
    count = normed.shape[1] // spread.shape[0]
    normed_ref[...] = to_gathered(column_blocks(normed, count), spread[...]).astype(bf16)


def mix(combined, gates_t, target_t):
    high, low = split(choose_weighted(target_t, gates_t, combined.shape[0]))
    tokens = high.shape[1]
    both = tn(jnp.concatenate([high, low], axis=1), combined)
    return both[:tokens] + both[tokens:]


def result_kernel(middle, combined, gates_t, target_t, result_ref):
    mixture = mix(combined[...], gates_t[...], target_t[...])
    result_ref[...] = (middle[...] + mixture).astype(bf16)


def attend(rows, weight, cosines, sines, bias_ref, heads_ref, out_ref):
    seq_count, tokens, columns = heads_ref.shape
    group = seq_count * tokens
    local = columns // HD - 2
    prompt = group // 2
    raw = nn(rows, weight)
    heads = []
    for j in range(local + 2):
        block = raw[:, j * HD : (j + 1) * HD]
        if j <= local:
            block = turn(block, cosines, sines)
        heads.append(block.astype(bf16))
        heads_ref[:, :, j * HD : (j + 1) * HD] = heads[j].reshape(seq_count, tokens, HD)
    heads_ref.send()
    key, value = heads[local], heads[local + 1]
    scale = HD ** (-0.5)
    for j in range(local):
        query = heads[j]
        for rows, seen in ((slice(0, prompt), prompt), (slice(prompt, group), group)):
            scores = nt(query[rows], key[:seen]) * scale + bias_ref[rows, :seen]
            peak = jnp.max(scores, axis=-1, keepdims=True)
            weights = jnp.exp(scores - peak)
            weights = weights / jnp.sum(weights, axis=-1, keepdims=True)
            part = nn(weights.astype(bf16), value[:seen]).astype(bf16)
            first = rows.start // tokens
            out_ref[first : first + prompt // tokens, :, j * HD : (j + 1) * HD] = part.reshape(
                prompt // tokens, tokens, HD
            )


def first_attention_kernel(
    place, own, one, two, three, weight, spread, cosines, sines, bias_ref,
    heads_ref, out_ref, normed_ref, small_ref,
):
    expert_count = 8
    me = place[0]
    seq_count, tokens, width = normed_ref.shape
    columns = heads_ref.shape[2]
    count = small_ref.shape[1]
    extras = weight[:, columns:].astype(f32).T.astype(bf16)
    extras = jnp.concatenate([extras[:count], extras[HD : HD + count]], axis=0)
    small = jnp.concatenate(to_natural(extras, spread[...]), axis=1)
    small_ref[0] = small[:count].astype(bf16)
    small_ref[1] = small[count:].astype(bf16)
    small_ref.send()
    gain = small[expert_count : expert_count + 1]
    for k, block in enumerate((own, one, two, three)):
        normed = normalize(block[...].astype(f32), gain).astype(bf16)
        normed = to_gathered(column_blocks(normed, seq_count), spread[...]).astype(bf16)
        normed_ref[lax.rem(me + k, seq_count)] = normed
    normed_ref.send()
    rows = normed_ref[...].reshape(seq_count * tokens, width)
    attend(rows, weight[:, :columns], cosines[...], sines[...], bias_ref, heads_ref, out_ref)


def next_attention_kernel(
    place, own, one, two, three, query_w, key_w, value_w, cosines, sines, bias_ref,
    heads_ref, out_ref, normed_ref,
):
    me = place[0]
    seq_count, tokens, width = normed_ref.shape
    weight = [w[...].reshape(width, w.shape[2]) for w in (query_w, key_w, value_w)]
    weight = jnp.concatenate(weight, axis=1)
    for k, block in enumerate((own, one, two, three)):
        normed_ref[lax.rem(me + k, seq_count)] = block[...]
    normed_ref.send()
    rows = normed_ref[...].reshape(seq_count * tokens, width)
    attend(rows, weight, cosines[...], sines[...], bias_ref, heads_ref, out_ref)


def after_attention_kernel(
    back, spread, hidden, small, out_w, routes_t, target_t,
    middle_ref, normed_ref, gates_ref, send_ref,
):
    expert_count = 8
    seq_count, tokens, part = back.shape
    width = seq_count * part
    attended = to_gathered([back[s] for s in range(seq_count)], spread[...]).astype(bf16)
    rows = out_w.shape[1] // 2
    half = out_w.shape[2]
    for side in range(2):
        weight = out_w[:, side * rows : (side + 1) * rows].reshape(width, half)
        cols = slice(side * half, (side + 1) * half)
        middle_ref[:, cols] = hidden[:, cols].astype(f32) + nn(attended, weight)
    middle_ref.send()
    middle = middle_ref[...]
    gain = small[expert_count + 1 : expert_count + 2].astype(f32)
    normed = normalize(middle, gain).astype(bf16)
    normed_ref[...] = normed
    normed_ref.send()
    send_ref[...] = nn(choose(target_t[...], send_ref.shape[0]).astype(bf16), normed).astype(bf16)
    send_ref.send()
    logits = nt(small[...], normed)
    chosen = []
    for k in range(TOPK):
        route = routes_t[k : k + 1]
        value = jnp.zeros((1, tokens), f32)
        for e in range(expert_count):
            value = value + jnp.where(route == e, logits[e : e + 1], 0.0)
        chosen.append(value)
    peak = functools.reduce(jnp.maximum, chosen)
    powers = [jnp.exp(value - peak) for value in chosen]
    total = functools.reduce(jnp.add, powers)
    for k in range(TOPK):
        gates_ref[k : k + 1] = powers[k] / total
    gates_ref[TOPK:] = jnp.zeros((gates_ref.shape[0] - TOPK, tokens), f32)


def flat_rows(block):
    sources, capacity, width = block.shape
    return block.astype(f32).reshape(sources * capacity, width).astype(bf16)


def down_parts(block):
    shards, rows, half = block.shape
    wide = block.astype(f32)
    left = wide[:, : rows // 2].reshape(shards * rows // 2, half).astype(bf16)
    right = wide[:, rows // 2 :].reshape(shards * rows // 2, half).astype(bf16)
    return left, right


def expert_kernel(rows_ref, *rest):
    experts = rows_ref.shape[1]
    weights = rest[: 3 * experts]
    out_ref, gate_ref, up_ref = rest[3 * experts :]
    sources, capacity = rows_ref.shape[0], rows_ref.shape[2]
    for e in range(experts):
        gate_w, up_w, down_w = weights[3 * e : 3 * e + 3]
        shards, rows, half = gate_w.shape
        tokens = flat_rows(rows_ref[:, e])
        gate_val = nn(tokens, gate_w[...].reshape(shards * rows, half))
        gate_ref[e] = gate_val.astype(bf16)
        gate_ref.send(e)
        up_val = nn(tokens, up_w[...].reshape(shards * rows, half))
        up_ref[e] = up_val.astype(bf16)
        up_ref.send(e)
        activated, slope = smooth_parts(gate_val)
        inner = (activated * up_val).astype(bf16)
        for side, part in enumerate(down_parts(down_w[...])):
            block = nn(inner, part).reshape(sources, capacity, half).astype(bf16)
            out_ref[:, e, :, side * half : (side + 1) * half] = block
        out_ref.send(e)


def slot_grad_kernel(grad, combined, gates_t, routes_t, target_t, send_ref, logits_ref):
    tokens = grad.shape[0]
    slots = combined.shape[0]
    high, low = split(grad[...])
    weights_high, weights_low = split(choose_weighted(target_t[...], gates_t[...], slots))
    weights = jnp.concatenate([weights_high, weights_low, weights_high], axis=1)
    send = nn(weights, jnp.concatenate([high, high, low], axis=0))
    send_ref[...] = send.astype(bf16)
    send_ref.send()
    products = nt(combined[...], jnp.concatenate([high, low], axis=0))
    products = products[:, :tokens] + products[:, tokens:]
    place = lax.broadcasted_iota(jnp.int32, (slots, tokens), 0)
    grad_gates = [
        jnp.sum(jnp.where(place == target_t[k : k + 1], products, 0.0), axis=0, keepdims=True)
        for k in range(TOPK)
    ]
    gates = [gates_t[k : k + 1] for k in range(TOPK)]
    center = functools.reduce(jnp.add, [a * b for a, b in zip(gates, grad_gates)])
    label = lax.broadcasted_iota(jnp.int32, logits_ref.shape, 0)
    total = jnp.zeros(logits_ref.shape, f32)
    for k in range(TOPK):
        choice = gates[k] * (grad_gates[k] - center)
        total = total + jnp.where(label == routes_t[k : k + 1], choice, 0.0)
    logits_ref[...] = total.astype(bf16)


def expert_back_kernel(grad_ref, down_first, gate_ref, up_ref, *rest):
    experts = grad_ref.shape[1]
    weights = (down_first,) + rest[: 3 * experts - 1]
    out_ref, gate_grad_ref, up_grad_ref, inner_ref = rest[3 * experts - 1 :]
    sources, capacity = grad_ref.shape[0], grad_ref.shape[2]
    for e in range(experts):
        down_w, gate_w, up_w = weights[3 * e : 3 * e + 3]
        shards, rows, half = gate_w.shape
        grad = flat_rows(grad_ref[:, e])
        left, right = down_parts(down_w[...])
        grad_inner = nt(grad[:, :half], left) + nt(grad[:, half:], right)
        up_val = up_ref[e].astype(f32)
        activated, slope = smooth_parts(gate_ref[e].astype(f32))
        inner_ref[e] = (activated * up_val).astype(bf16)
        inner_ref.send(e)
        gate_grad_ref[e] = (grad_inner * up_val * slope).astype(bf16)
        gate_grad_ref.send(e)
        up_grad_ref[e] = (grad_inner * activated).astype(bf16)
        up_grad_ref.send(e)
        parts = 4
        some, size = shards // parts, shards * rows // parts
        for c in range(parts):
            at = slice(c * some, (c + 1) * some)
            total = nt(gate_grad_ref[e], gate_w[at].reshape(size, half))
            total = total + nt(up_grad_ref[e], up_w[at].reshape(size, half))
            total = total.reshape(sources, capacity, size).astype(bf16)
            out_ref[:, e, :, c * size : (c + 1) * size] = total
        out_ref.send(e)


def expert_weight_kernel(rows_ref, grad_ref, gate_grad_ref, up_grad_ref, inner_ref, *rest):
    pack_ref = rest[-1]
    experts = rows_ref.shape[1]
    shards, rows, half = pack_ref.shape
    width = rows_ref.shape[3]
    rows = width // shards
    at = 0

    def send(start, count):
        for piece in range(start // 16, (start + count) // 16):
            pack_ref.send(piece)

    for e in range(experts):
        tokens = flat_rows(rows_ref[:, e])
        grad = flat_rows(grad_ref[:, e])
        grads = jnp.concatenate([gate_grad_ref[e], up_grad_ref[e]], axis=1)
        both = tn(tokens, grads).astype(bf16)
        pack_ref[:, at : at + rows] = both[:, :half].reshape(shards, rows, half)
        pack_ref[:, at + rows : at + 2 * rows] = both[:, half:].reshape(shards, rows, half)
        send(at, 2 * rows)
        down = tn(inner_ref[e], grad)
        left = down[:, :half].reshape(shards, rows // 2, half)
        right = down[:, half:].reshape(shards, rows // 2, half)
        down = jnp.concatenate([left, right], axis=1).astype(bf16)
        pack_ref[:, at + 2 * rows : at + 3 * rows] = down
        send(at + 2 * rows, rows)
        at += 3 * rows
    for extra in rest[:-1]:
        pack_ref[:, at : at + extra.shape[1]] = extra[...]
        at += extra.shape[1]


def after_experts_kernel(
    grad, sent, middle, normed, logits_grad, target_t, small, out_w, spread,
    grad_ref, branch_ref, send_ref, small_ref,
):
    expert_count = 8
    seq_count, tokens, part = send_ref.shape
    width = seq_count * part
    chosen = choose(target_t[...], sent.shape[0]).astype(bf16)
    grad_normed = tn(chosen, sent[...]) + tn(logits_grad[...], small[...])
    router = nn(logits_grad[...], normed[...])
    gain = small[expert_count + 1 : expert_count + 2].astype(f32)
    grad_value, grad_gain = normalize_back(middle[...], gain, grad_normed)
    label = lax.broadcasted_iota(jnp.int32, small_ref.shape, 0)
    small_ref[...] = jnp.where(label == expert_count + 1, grad_gain, router)
    grad_middle = grad[...] + grad_value
    grad_ref[...] = grad_middle
    grad_ref.send()
    branch = grad_middle.astype(bf16)
    branch_ref[...] = branch
    branch_ref.send()
    rows = out_w.shape[1] // 2
    half = out_w.shape[2]
    parts = [
        nt(branch[:, :half], out_w[:, :rows].reshape(width, half)),
        nt(branch[:, half:], out_w[:, rows:].reshape(width, half)),
    ]
    attended = (parts[0] + parts[1]).astype(bf16)
    for s, block in enumerate(to_natural(attended, spread[...])):
        send_ref[s] = block.astype(bf16)


def attention_back_kernel(heads_ref, grad_ref, bias_ref, cosines, sines, out_ref):
    seq_count, tokens, columns = heads_ref.shape
    group = seq_count * tokens
    heads = heads_ref[...].reshape(group, columns)
    grads = grad_ref[...].reshape(group, grad_ref.shape[2])
    local = columns // HD - 2
    prompt = group // 2
    key = heads[:, local * HD : (local + 1) * HD]
    value = heads[:, (local + 1) * HD :]
    scale = HD ** (-0.5)

    def keep(at, block):
        out_ref[:, :, at * HD : (at + 1) * HD] = block.astype(bf16).reshape(seq_count, tokens, HD)

    cosines, sines = cosines[...], sines[...]

    def unturn(block):
        return block * cosines - pltpu.roll(block, HD // 2, 1) * sines

    grad_key = [jnp.zeros((prompt, HD), f32), jnp.zeros((prompt, HD), f32)]
    grad_value = [jnp.zeros((prompt, HD), f32), jnp.zeros((prompt, HD), f32)]
    for j in range(local):
        query = heads[:, j * HD : (j + 1) * HD]
        grad = grads[:, j * HD : (j + 1) * HD]
        grad_query = []
        for rows, seen in ((slice(0, prompt), prompt), (slice(prompt, group), group)):
            scores = nt(query[rows], key[:seen]) * scale + bias_ref[rows, :seen]
            peak = jnp.max(scores, axis=-1, keepdims=True)
            weights = jnp.exp(scores - peak)
            weights = weights / jnp.sum(weights, axis=-1, keepdims=True)
            grad_weights = nt(grad[rows], value[:seen])
            center = jnp.sum(weights * grad_weights, axis=-1, keepdims=True)
            grad_scores = (weights * (grad_weights - center)).astype(bf16)
            low = weights.astype(bf16)
            grad_query.append(nn(grad_scores, key[:seen]) * scale)
            for side in range(seen // prompt):
                cols = slice(side * prompt, (side + 1) * prompt)
                grad_key[side] = grad_key[side] + tn(grad_scores[:, cols], query[rows])
                grad_value[side] = grad_value[side] + tn(low[:, cols], grad[rows])
        keep(j, unturn(jnp.concatenate(grad_query, axis=0)))
    keep(local, unturn(jnp.concatenate(grad_key, axis=0) * scale))
    keep(local + 1, jnp.concatenate(grad_value, axis=0))


def before_attention_kernel(
    sent, left_w, right_w, kv_w, spread, small, hidden, grad_middle, out_ref, gain_ref
):
    expert_count = 8
    seq_count, tokens, columns = sent.shape
    local = columns // HD - 2
    share = seq_count // KVHEADS
    blocks = [sent[s, :, : local * HD] for s in range(seq_count)]
    for at in (local, local + 1):
        for c in range(KVHEADS):
            total = jnp.zeros((tokens, HD), f32)
            for s in range(c * share, (c + 1) * share):
                total = total + sent[s, :, at * HD : (at + 1) * HD].astype(f32)
            blocks.append(total.astype(bf16))
    raw = jnp.concatenate(blocks, axis=1)
    at, total = 0, 0.0
    for part in (left_w, right_w, kv_w):
        shards, rows, columns = part.shape
        weight = part[...].reshape(shards * rows, columns)
        total = total + nt(raw[:, at : at + columns], weight)
        at += columns
    high, low = split(total)
    both = to_natural(jnp.concatenate([high, low], axis=0), spread[...])
    both = jnp.concatenate(both, axis=1)
    grad_normed = both[:tokens] + both[tokens:]
    gain = small[expert_count : expert_count + 1].astype(f32)
    grad_value, grad_gain = normalize_back(hidden[...].astype(f32), gain, grad_normed)
    out_ref[...] = grad_middle[...] + grad_value
    out_ref.send()
    shards = gain_ref.shape[0]
    width = grad_gain.shape[1]
    share = width // seq_count
    part = share // shards
    shard = lax.broadcasted_iota(jnp.int32, (shards, width), 0)
    at = lax.broadcasted_iota(jnp.int32, (shards, width), 1)
    kept = jnp.where(at % share // part == shard, grad_gain, 0.0).astype(bf16)
    source = lax.broadcasted_iota(jnp.int32, (width, HD), 0)
    wanted = lax.broadcasted_iota(jnp.int32, (width, HD), 1)
    place = source // share * part + source % part
    gain_ref[...] = nn(kept, jnp.where(place == wanted, 1.0, 0.0).astype(bf16))


def qkv_weight_kernel(normed, grads, small, spread, out_ref):
    seq_count, tokens, columns = grads.shape
    shards, rows, wide = out_ref.shape
    inputs = normed[...].reshape(seq_count * tokens, normed.shape[2])
    total = tn(inputs, grads[...].reshape(seq_count * tokens, columns))
    out_ref[:, :, :columns] = total.astype(bf16).reshape(shards, rows, columns)
    extra = column_blocks(small[...].astype(bf16), seq_count)
    extra = to_gathered(extra, spread[...])
    extra = jnp.concatenate([extra, jnp.zeros((HD - extra.shape[0], extra.shape[1]), f32)], axis=0).T
    out_ref[:, :, columns:] = extra.astype(bf16).reshape(shards, rows, wide - columns)


def out_weight_kernel(place, own, one, two, three, attended, gain, out_ref):
    me = place[0]
    seq_count, tokens, part = attended.shape
    shards, rows, half = out_ref.shape
    rows = rows // 2
    valid = part // shards
    branch = jnp.concatenate([own[...], one[...], two[...], three[...]], axis=0)
    heads = jnp.concatenate([attended[lax.rem(me + k, seq_count)] for k in range(seq_count)], axis=0)
    place_in = lax.broadcasted_iota(jnp.int32, (part, shards * rows), 0)
    place_out = lax.broadcasted_iota(jnp.int32, (part, shards * rows), 1)
    source = place_out // rows * valid + place_out % rows
    same = jnp.logical_and(place_in == source, place_out % rows < valid)
    heads = nn(heads, jnp.where(same, 1.0, 0.0).astype(bf16)).astype(bf16)
    wide = jnp.concatenate([gain[...], jnp.zeros((shards, half - HD), f32)], axis=1)
    row = lax.broadcasted_iota(jnp.int32, (shards, rows, half), 1)
    for side in range(2):
        total = tn(heads, branch[:, side * half : (side + 1) * half]).reshape(shards, rows, half)
        if side == 0:
            total = jnp.where(row == valid, wide[:, None, :], total)
        out_ref[:, side * rows : (side + 1) * rows] = total.astype(bf16)


def expert_grads_kernel(*refs):
    sums, (gate_ref, up_ref, down_ref) = refs[:LAYERS], refs[LAYERS:]
    rows = gate_ref.shape[2]
    half = gate_ref.shape[3]
    for layer in range(LAYERS):
        block = sums[layer][...].astype(f32)
        for e in range(gate_ref.shape[1]):
            at = 3 * rows * e
            gate_ref[layer, e] = block[at : at + rows]
            up_ref[layer, e] = block[at + rows : at + 2 * rows]
            at += 2 * rows
            down_ref[layer, e, :, :half] = block[at : at + rows // 2]
            down_ref[layer, e, :, half:] = block[at + rows // 2 : at + rows]


def dense_grads_kernel(*refs):
    blocks, outs = refs[:LAYERS], refs[LAYERS : 2 * LAYERS]
    query_ref, key_ref, value_ref, out_ref, small_ref = refs[2 * LAYERS :]
    seq_count, rows, columns = blocks[0].shape
    local = columns - 3 * HD
    share = seq_count // KVHEADS
    for layer in range(LAYERS):
        parts = [blocks[layer][s].astype(f32) for s in range(seq_count)]
        for s in range(seq_count):
            query_ref[:, layer, s * local : (s + 1) * local] = parts[s][:, :local]
        for c in range(KVHEADS):
            total = functools.reduce(jnp.add, parts[c * share : (c + 1) * share])
            key_ref[:, layer, c * HD : (c + 1) * HD] = total[:, local : local + HD]
            value_ref[:, layer, c * HD : (c + 1) * HD] = total[:, local + HD : local + 2 * HD]
        total = functools.reduce(jnp.add, parts)
        small_ref[layer] = total[:, local + 2 * HD :]
        block = outs[layer][...].astype(f32)
        half = block.shape[1]
        out_ref[:, layer, :half] = block[:rows]
        out_ref[:, layer, half:] = block[block.shape[0] // 2 :][:rows]


def swap_seq(block):
    return lax.all_to_all(block, "seq", split_axis=0, concat_axis=0, tiled=True)


def around_seq(block):
    count = lax.axis_size("seq")
    others = [
        lax.ppermute(block, "seq", [((i + k) % count, i) for i in range(count)])
        for k in range(1, count)
    ]
    return [block] + others


def halves(block):
    cut = block.shape[-1] // 2
    return jnp.concatenate([block[..., :cut], block[..., cut:]], axis=-2)


def per_device(
    tokens_in,
    cotangent,
    routes,
    order,
    segment_ids,
    gain_attn,
    w_query,
    w_key,
    w_value,
    w_out,
    gain_ffn,
    w_router,
    w_gate,
    w_up,
    w_down,
):
    tok_count = tokens_in.shape[1]
    width = tokens_in.shape[2]
    seq_count = lax.axis_size("seq")
    shard_count = lax.axis_size("fsdp")
    seq_index = lax.axis_index("seq")
    place = jnp.full((1,), seq_index, jnp.int32)
    group_tok = seq_count * tok_count
    prompt_len = group_tok - segment_ids.shape[1]
    local_experts = w_gate.shape[1]
    expert_count = local_experts * seq_count
    capacity = 9 * tok_count * TOPK // (8 * expert_count)
    total_slots = expert_count * capacity
    head_local = HEADS // seq_count
    local_width = head_local * HD
    dense_rows = w_query.shape[1]
    shard_rows = dense_rows * seq_count
    gate_rows = w_gate.shape[2]
    down_rows = w_down.shape[2]
    expert_rows = 2 * gate_rows + 2 * down_rows
    qkv_width = (HEADS + 2 * KVHEADS) * HD
    half_width = width // 2
    inner_width = w_gate.shape[3]
    slot_rows = seq_count * capacity

    cos_half, sin_half, labels = group_tables(segment_ids[0], prompt_len)
    cos_all = jnp.concatenate([cos_half, cos_half], axis=1)
    sin_all = jnp.concatenate([-sin_half, sin_half], axis=1)
    cos_own = lax.dynamic_slice_in_dim(cos_all, seq_index * tok_count, tok_count, 0)
    sin_own = lax.dynamic_slice_in_dim(sin_all, seq_index * tok_count, tok_count, 0)
    key_pos = jnp.arange(group_tok, dtype=jnp.int32)
    allowed = jnp.logical_and(
        key_pos[None, :] <= key_pos[:, None],
        jnp.logical_or(key_pos[None, :] < prompt_len, labels[None, :] == labels[:, None]),
    )
    bias = jnp.where(allowed, 0.0, masked_value)

    column = jnp.arange(width // seq_count, dtype=jnp.int32)
    natural = (
        column % shard_rows // dense_rows * (width // seq_count // seq_count)
        + column // shard_rows * dense_rows
        + column % dense_rows
    )
    spread = (column[:, None] == natural[None, :]).astype(bf16)

    def small_rows_of(layer):
        return jnp.concatenate(
            [
                w_router[layer],
                gain_attn[layer][:, None],
                gain_ffn[layer][:, None],
                jnp.zeros((dense_rows, HD - 2 - expert_count), bf16),
            ],
            axis=1,
        )

    def dense_rows_of(layer):
        return jnp.concatenate(
            [w_query[layer], w_key[layer], w_value[layer], small_rows_of(layer), w_out[layer]],
            axis=1,
        )

    def spread_seq(dense):
        dense = swap_seq(jnp.broadcast_to(dense[None], (seq_count,) + dense.shape))
        return dense.reshape(shard_rows, dense.shape[2])

    def own_columns(weight):
        pick = seq_index * KVHEADS // seq_count
        starts = (seq_index * local_width, (HEADS + pick) * HD, (HEADS + KVHEADS + pick) * HD)
        parts = [
            lax.dynamic_slice_in_dim(weight, start, size, 1)
            for start, size in zip(starts, (local_width, HD, HD))
        ]
        return jnp.concatenate(parts + [weight[:, qkv_width : qkv_width + HD]], axis=1)

    def expert_part(layer):
        return [
            part
            for e in range(local_experts)
            for part in (w_gate[layer, e], w_up[layer, e], halves(w_down[layer, e]))
        ]

    def out_part(dense):
        return [halves(dense[:, qkv_width + HD :])]

    def qkv_part(dense):
        wide = jnp.concatenate(
            [dense[:, : qkv_width + HD], jnp.zeros((shard_rows, HD), bf16)], axis=1
        )
        return [wide[:, at : at + half_width] for at in range(0, wide.shape[1], half_width)]

    def fetch(parts):
        return lax.all_gather(jnp.concatenate(parts, axis=0), "fsdp", axis=0, tiled=False)

    core = lax.rem(lax.axis_index("fsdp"), 2)
    chips = [[i + c for i in range(0, shard_count, 2)] for c in range(2)]

    def swap_chips(block):
        return lax.all_to_all(
            block, "fsdp", split_axis=0, concat_axis=0, tiled=True, axis_index_groups=chips
        )

    def swap_cores(block):
        return lax.ppermute(block, "fsdp", [(i, i ^ 1) for i in range(shard_count)])

    def both_cores(block):
        other = swap_cores(block)
        first = jnp.where(core == 0, block, other)
        second = jnp.where(core == 0, other, block)
        return jnp.stack([first, second], axis=1).reshape((shard_count,) + block.shape[1:])

    def to_chips(block):
        return swap_chips(jnp.broadcast_to(block[None], (shard_count // 2,) + block.shape))

    weight_parts = [
        (e * expert_rows + k * gate_rows, gate_rows) for e in range(local_experts) for k in range(3)
    ]
    back_parts = [weight_parts[3 * e + k] for e in range(local_experts) for k in (2, 0, 1)]
    out_cut = ((1, local_experts * expert_rows, 2 * shard_rows),)

    slots_shape = shape((seq_count, local_experts, capacity, width), bf16)
    inner_shape = (local_experts, slot_rows, inner_width)
    expert_flops = 6 * total_slots * width * inner_width
    dense_flops = 2 * tok_count * width * width
    records = []
    hidden = tokens_in[0]
    dense = spread_seq(jnp.concatenate([dense_rows_of(0), small_rows_of(1)], axis=1))
    columns = jnp.concatenate([own_columns(dense), dense[:, -HD:]], axis=1)
    dense = dense[:, :-HD]
    columns, hidden = lax.optimization_barrier((columns, hidden))
    token_blocks = around_seq(hidden)
    packs = [fetch(expert_part(0) + out_part(dense)), None]
    columns = to_chips(columns)
    targets = [
        slot_table(routes[layer, 0], order[layer, 0], expert_count, capacity)
        for layer in range(LAYERS)
    ]
    routes_ts = [routes[layer, 0].T for layer in range(LAYERS)]
    early = (token_blocks, targets, routes_ts, cos_all, sin_all, bias, spread)
    columns, early, next_rows = lax.optimization_barrier((columns, early, dense_rows_of(1)))
    token_blocks, targets, routes_ts, cos_all, sin_all, bias, spread = early
    first_columns = both_cores(columns).reshape(width, columns.shape[2])
    next_dense = spread_seq(next_rows)
    qkv_at = local_experts * expert_rows + 2 * shard_rows
    qkv_ws = [None, None]
    blocks = half_width // local_width

    def query_row(me):
        return qkv_at + me // blocks * shard_rows

    def query_column(me):
        return me % blocks * local_width

    def key_column(me):
        return me * KVHEADS // seq_count * HD

    def value_column(me):
        return KVHEADS * HD + me * KVHEADS // seq_count * HD

    kv_rows = (1, qkv_at + 2 * shard_rows, shard_rows)
    own_cuts = {
        5: ((1, query_row, shard_rows), (2, query_column, local_width)),
        6: (kv_rows, (2, key_column, HD)),
        7: (kv_rows, (2, value_column, HD)),
    }
    heads_shape = shape((seq_count, tok_count, local_width + 2 * HD), bf16)
    attended_shape = shape((seq_count, tok_count, local_width), bf16)
    normed_shape = shape((seq_count, tok_count, width), bf16)
    small_shape = shape((LAYERS, 2 * expert_count, width), bf16)
    attention_flops = 4 * head_local * group_tok * group_tok * HD + 2 * dense_flops
    for layer in range(LAYERS):
        pack, routes_t, target_t = packs[layer], routes_ts[layer], targets[layer]
        if layer == 0:
            heads, attended, normed_all, smalls = once(
                first_attention_kernel,
                [heads_shape, attended_shape, normed_shape, small_shape],
                place, *token_blocks, first_columns, spread, cos_all, sin_all, bias,
                scalar=True, flops=attention_flops + 4 * dense_flops,
            )
            small = smalls[layer]
        else:
            small = smalls[layer]
            normed_p, hidden = once(
                input_kernel,
                [shape((tok_count, width), bf16), shape((tok_count, width), f32)],
                middle, combined, gates_t, above_target, small, spread, flops=2 * dense_flops,
            )
            heads, attended, normed_all = once(
                next_attention_kernel,
                [heads_shape, attended_shape, normed_shape],
                place, *around_seq(normed_p), pack, pack, pack, cos_all, sin_all, bias,
                scalar=True, cut=own_cuts, flops=attention_flops,
            )
        back = swap_seq(attended)
        if layer == 0:
            next_parts = expert_part(1) + out_part(next_dense) + qkv_part(next_dense)
            next_parts = jnp.concatenate(next_parts, axis=0)
            pack, next_parts, back = lax.optimization_barrier((pack, next_parts, back))
            packs = [pack, fetch([next_parts])]
            qkv_ws[1] = (packs[1], qkv_at)
        else:
            first_parts = jnp.concatenate(qkv_part(dense), axis=0)
            first_parts, back = lax.optimization_barrier((first_parts, back))
            qkv_ws[0] = (fetch([first_parts]), 0)
        middle, normed_ffn, gates_t, send_rows = once(
            after_attention_kernel,
            [
                shape((tok_count, width), f32),
                shape((tok_count, width), bf16),
                shape((2 * TOPK, tok_count), f32),
                shape((total_slots, width), bf16),
            ],
            back, spread, hidden, small, pack, routes_t, target_t,
            cut={4: out_cut}, flops=3 * dense_flops,
        )
        received = swap_seq(send_rows.reshape(slots_shape.shape))
        expert_out, gate_val, up_val = once(
            expert_kernel,
            [slots_shape, shape(inner_shape, bf16), shape(inner_shape, bf16)],
            received, *[pack] * len(weight_parts),
            cut={n + 1: ((1, *part),) for n, part in enumerate(weight_parts)},
            pieces={0: (1, local_experts), 1: (0, local_experts), 2: (0, local_experts)},
            flops=expert_flops,
        )
        combined = swap_seq(expert_out).reshape(total_slots, width)
        above_target = target_t
        records.append(
            (
                (pack, small, routes_t, target_t),
                (hidden, normed_all, heads, attended),
                (middle, normed_ffn, gates_t, combined),
                (received, gate_val, up_val),
            )
        )
    (result,) = once(
        result_kernel, [shape((tok_count, width), bf16)], middle, combined, gates_t, target_t,
        flops=dense_flops,
    )

    def scatter(block):
        return lax.psum_scatter(block, "fsdp", scatter_dimension=0, tiled=False)

    def spread_qkv(block, out_block):
        gain = out_block[dense_rows, :shard_rows]
        label = jnp.arange(local_width + 3 * HD)[None, :]
        block = jnp.where(label == local_width + 2 * HD + expert_count, gain[:, None], block)
        return swap_seq(block.reshape(seq_count, dense_rows, local_width + 3 * HD))

    out_rows = 16

    grad_hidden = cotangent[0].astype(f32)
    sums = [None] * LAYERS
    waiting = None
    for layer in range(LAYERS - 1, -1, -1):
        weights, attn_saved, mid_saved, expert_saved = records[layer]
        pack, small, routes_t, target_t = weights
        qkv_w, row = qkv_ws[layer]
        below, normed_all, heads, attended = attn_saved
        middle, normed_ffn, gates_t, combined = mid_saved
        received, gate_val, up_val = expert_saved
        grad_slots, logits_grad = once(
            slot_grad_kernel,
            [shape((total_slots, width), bf16), shape((2 * expert_count, tok_count), bf16)],
            grad_hidden, combined, gates_t, routes_t, target_t, flops=3 * dense_flops,
        )
        grad_expert = swap_seq(grad_slots.reshape(slots_shape.shape))
        if waiting is None:
            tied = lax.optimization_barrier((grad_expert, qkv_ws[0][0], result))
            grad_expert, result = tied[0], tied[2]
            qkv_ws[0] = (tied[1], 0)
        else:
            grad_expert, waiting = lax.optimization_barrier((grad_expert, waiting))
        grad_rows, gate_grad, up_grad, inner = once(
            expert_back_kernel,
            [slots_shape] + [shape(inner_shape, bf16)] * 3,
            grad_expert, pack, gate_val, up_val, *[pack] * (len(back_parts) - 1),
            cut={n + 3 if n else 1: ((1, *part),) for n, part in enumerate(back_parts)},
            pieces={0: (1, local_experts), 1: (0, local_experts), 2: (0, local_experts), 3: (0, local_experts)},
            flops=expert_flops,
        )
        sent = swap_seq(grad_rows)
        extra = () if layer == LAYERS - 1 else waiting
        extra_rows = sum(a.shape[1] for a in extra)
        (packed,) = once(
            expert_weight_kernel,
            [shape((shard_count, local_experts * expert_rows + extra_rows, half_width), bf16)],
            received, grad_expert, gate_grad, up_grad, inner, *extra,
            pieces={0: (1, (local_experts * expert_rows + extra_rows) // 16)}, flops=expert_flops,
        )
        sent, packed = lax.optimization_barrier((sent, packed))
        if layer < LAYERS - 1:
            packed, sums[layer + 1] = lax.optimization_barrier((packed, sums[layer + 1]))
        summed = scatter(packed)
        grad_middle, branch, send, small_grad = once(
            after_experts_kernel,
            [
                shape((tok_count, width), f32),
                shape((tok_count, width), bf16),
                shape((seq_count, tok_count, local_width), bf16),
                shape((2 * expert_count, width), f32),
            ],
            grad_hidden, sent.reshape(total_slots, width), middle, normed_ffn, logits_grad,
            target_t, small, pack, spread,
            cut={7: out_cut}, flops=4 * dense_flops,
        )
        grad_heads = swap_seq(send)
        grad_heads, branch = lax.optimization_barrier((grad_heads, branch))
        branch_all = around_seq(branch)
        (grad_own,) = once(
            attention_back_kernel,
            [shape((seq_count, tok_count, local_width + 2 * HD), bf16)],
            heads, grad_heads, bias, cos_all, sin_all,
            flops=10 * head_local * group_tok * group_tok * HD,
        )
        (qkv_block_grad,) = once(
            qkv_weight_kernel,
            [shape((shard_count, shard_rows, half_width), bf16)],
            normed_all, grad_own, small_grad, spread, flops=2 * dense_flops,
        )
        sent, qkv_block_grad = lax.optimization_barrier((swap_seq(grad_own), qkv_block_grad))
        grad_hidden, gain_grad = once(
            before_attention_kernel,
            [shape((tok_count, width), f32), shape((shard_count, HD), f32)],
            sent, qkv_w, qkv_w, qkv_w, spread, small, below, grad_middle,
            cut={
                1: ((1, row, shard_rows),),
                2: ((1, row + shard_rows, shard_rows),),
                3: ((1, row + 2 * shard_rows, shard_rows), (2, 0, 2 * KVHEADS * HD)),
            },
            flops=4 * dense_flops,
        )
        grad_hidden, branch_all = lax.optimization_barrier((grad_hidden, branch_all))
        (out_block_grad,) = once(
            out_weight_kernel,
            [shape((shard_count, 2 * out_rows, half_width), bf16)],
            place, *branch_all, attended, gain_grad, scalar=True, flops=dense_flops,
        )
        sums[layer] = summed
        if layer > 0:
            waiting = (qkv_block_grad, out_block_grad)

    def shard_sum(block):
        block = block.reshape((shard_count // 2, 2) + block.shape[1:])
        own = lax.dynamic_index_in_dim(block, core, 1, False)
        other = swap_cores(lax.dynamic_index_in_dim(block, 1 - core, 1, False))
        block = (own.astype(f32) + other.astype(f32)).astype(bf16)
        return jnp.sum(swap_chips(block).astype(f32), axis=0)

    qkv_sum = shard_sum(qkv_block_grad)
    out_sum = shard_sum(out_block_grad)
    above = sums[0][local_experts * expert_rows :]
    above_out = above[shard_rows:]
    own_rows = spread_qkv(qkv_sum, out_sum)
    above_rows = spread_qkv(above[:shard_rows], above_out)
    gate_grads, up_grads, down_grads = once(
        expert_grads_kernel,
        [
            shape((LAYERS,) + w_gate.shape[1:], f32),
            shape((LAYERS,) + w_up.shape[1:], f32),
            shape((LAYERS,) + w_down.shape[1:], f32),
        ],
        *sums,
        cut={0: ((0, 0, local_experts * expert_rows),)},
    )
    query_grads, key_grads, value_grads, out_grads, small_grads = once(
        dense_grads_kernel,
        [
            shape((dense_rows, LAYERS, HEADS * HD), f32),
            shape((dense_rows, LAYERS, KVHEADS * HD), f32),
            shape((dense_rows, LAYERS, KVHEADS * HD), f32),
            shape((dense_rows, LAYERS, width), f32),
            shape((LAYERS, dense_rows, HD), f32),
        ],
        own_rows, above_rows, out_sum, above_out,
    )
    return (
        result[None],
        grad_hidden[None],
        small_grads[:, :, expert_count],
        query_grads.transpose(1, 0, 2),
        key_grads.transpose(1, 0, 2),
        value_grads.transpose(1, 0, 2),
        out_grads.transpose(1, 0, 2),
        small_grads[:, :, expert_count + 1],
        small_grads[:, :, :expert_count],
        gate_grads,
        up_grads,
        down_grads,
    )


def solution(mesh):
    in_specs = (
        P("fsdp", "seq", None),
        P("fsdp", "seq", None),
        P(None, "fsdp", "seq", None),
        P(None, "fsdp", "seq", None),
        P("fsdp", None),
        P(None, ("seq", "fsdp")),
        P(None, ("seq", "fsdp"), None),
        P(None, ("seq", "fsdp"), None),
        P(None, ("seq", "fsdp"), None),
        P(None, ("seq", "fsdp"), None),
        P(None, ("seq", "fsdp")),
        P(None, ("seq", "fsdp"), None),
        P(None, "seq", "fsdp", None),
        P(None, "seq", "fsdp", None),
        P(None, "seq", "fsdp", None),
    )
    out_specs = (
        P("fsdp", "seq", None),
        P("fsdp", "seq", None),
        P(None, ("seq", "fsdp")),
        P(None, ("seq", "fsdp"), None),
        P(None, ("seq", "fsdp"), None),
        P(None, ("seq", "fsdp"), None),
        P(None, ("seq", "fsdp"), None),
        P(None, ("seq", "fsdp")),
        P(None, ("seq", "fsdp"), None),
        P(None, "seq", "fsdp", None),
        P(None, "seq", "fsdp", None),
        P(None, "seq", "fsdp", None),
    )
    return jax.shard_map(
        per_device, mesh=mesh, in_specs=in_specs, out_specs=out_specs, check_vma=False
    )
```

time: 783 us -> 652 us (0.83)
  waiting for transfers between devices: 275 us -> 202 us
  blocking collectives: 159 us -> 105 us
  local copies, waits for them, and re-layouts: 60.4 us -> 31.5 us
  starting transfers between devices: 74 us -> 90.1 us
  Pallas kernels: 165 us -> 181 us
    all_gather x4 -> x3, waiting for transfers between devices: 95 us -> 6.67 us  [fetch(): lax.all_gather(jnp.concatenate(parts, axis=0), 'fsdp', axis=0, tiled=False)]
    unnamed x207 -> x53, local copies, waits for them, and re-layouts: 45.8 us -> 8.67 us
    all_to_all x11 -> x13, waiting for transfers between devices: 77 us -> 106 us  [swap_seq(): return lax.all_to_all(block, 'seq', split_axis=0, concat_axis=0, tiled=True)]
    all_to_all x7 -> x5, blocking collectives: 132 us -> 105 us  [swap_seq(): return lax.all_to_all(block, 'seq', split_axis=0, concat_axis=0, tiled=True)]
    all_gather x2 -> x0, blocking collectives: 26.9 us -> none  [gather_seq(): return lax.all_gather(block, 'seq', axis=0, tiled=False)]
    ppermute x12, waiting for transfers between devices: 57.6 us -> 36.1 us  [around_seq(): lax.ppermute(block, 'seq', [((i + k) % count, i) for i in range(count)])]
    pallas_call x25 -> x26, Pallas kernels: 165 us -> 181 us  [once(): pl.pallas_call(body, out_shape=list(outs), in_specs=specs, out_specs=[hbm...]
    all_to_all x11 -> x13, starting transfers between devices: 43 us -> 58.5 us  [swap_seq(): return lax.all_to_all(block, 'seq', split_axis=0, concat_axis=0, tiled=True)]
  transfers between devices with their start and end apart: 31 -> 36, of which waited for: 24 -> 26; matrix products, arithmetic and copies ran while one was open for 4% -> 6% of each run, Pallas kernels for 18% -> 25%
where the time goes in v2:
time: 652 us; the launch traced here: 645 us
  waiting for transfers between devices  202 us (31%)
  Pallas kernels  181 us (28%)
  blocking collectives  105 us (16%)
  starting transfers between devices  90.1 us (14%)
  local copies, waits for them, and re-layouts  31.5 us (5%)
  other arithmetic  20.3 us (3%)
  between operations  14.8 us (2%)
    pallas_call x26, Pallas kernels, once(): pl.pallas_call(body, out_shape=list(outs), in_specs=specs, out_specs=[hbm...  181 us
    all_to_all x13, waiting for transfers between devices, swap_seq(): return lax.all_to_all(block, 'seq', split_axis=0, concat_axis=0, tiled=True)  106 us
    all_to_all x5, blocking collectives, swap_seq(): return lax.all_to_all(block, 'seq', split_axis=0, concat_axis=0, tiled=True)  105 us
    all_to_all x13, starting transfers between devices, swap_seq(): return lax.all_to_all(block, 'seq', split_axis=0, concat_axis=0, tiled=True)  58.5 us
    all_to_all x3, waiting for transfers between devices, swap_chips(): lax.all_to_all(block, 'fsdp', split_axis=0, concat_axis=0, tiled=True, ax...  44.9 us
    ppermute x12, waiting for transfers between devices, around_seq(): lax.ppermute(block, 'seq', [((i + k) % count, i) for i in range(count)])  36.1 us
    ppermute x12, starting transfers between devices, around_seq(): lax.ppermute(block, 'seq', [((i + k) % count, i) for i in range(count)])  15.2 us
    all_to_all x3, starting transfers between devices, swap_chips(): lax.all_to_all(block, 'fsdp', split_axis=0, concat_axis=0, tiled=True, ax...  15.2 us
  transfers between devices with their start and end apart: 36, of which 26 were waited for; matrix products, arithmetic and copies ran while one was open for 6% of the time, Pallas kernels for 25%

profile of v2, /device:TPU:0, one launch (start us, length us, event | category | flops | bytes accessed | tf_op | source)
XLA Modules:
  0.0 644.9 jit_solution(12563663614137117902)
XLA Ops:
  21.4 7.9 %all-to-all-done = bf16[4,12,3840]{2,1,0:T(8,128)(2,1)S(1)} async-done(((bf16[4,12,3840]{2,1,0:T(8,128)(2,1)}), bf16[4,12,3840]{2,1,0:T(8,128)(2,1)S(1)}, u32[]{:S(2)}, u32[]{:S(2)}) %all-to-all-start) | async-done | bytes 368672 | tf_op jit(solution)/shard_map/all_to_all | solution.py:688
  90.7 11.0 %shard_map.238 = (bf16[4,128,640]{2,1,0:T(8,128)(2,1)}, bf16[4,128,384]{2,1,0:T(8,128)(2,1)}, bf16[4,128,1536]{2,1,0:T(8,128)(2,1)}, bf16[2,16,1536]{2,1,0:T(8,128)(2,1)}) custom-call(s32[1]{0:T(128)} %bitcast.11.refs_0_, bf16[128,1536]{1,0:T(8,128)(2,1)} %bitcast.188, bf16[128,1536]{1,0:T(8,128)(2,1)} %collective-permute-done.refs_2_, ...), custom_call_target="tpu_custom_call" | custom-call | flops 4026531840 | bytes 8912900 | tf_op jit(solution)/shard_map/pallas_call | solution.py:158
  126.5 28.2 %all_to_all.105.refs_0_ = bf16[4,2,72,1536]{3,2,1,0:T(8,128)(2,1)} all-to-all(bf16[4,2,72,1536]{3,2,1,0:T(8,128)(2,1)} %bitcast.186), channel_id=1, replica_groups=mesh['seq'=4,'fsdp'=32] {'seq'}, dimensions={0} | all-to-all | bytes 3538944 | tf_op jit(solution)/shard_map/all_to_all | solution.py:688
  154.6 10.0 %shard_map.240 = (bf16[4,2,72,1536]{3,2,1,0:T(8,128)(2,1)}, bf16[2,288,768]{2,1,0:T(8,128)(2,1)}, bf16[2,288,768]{2,1,0:T(8,128)(2,1)}) custom-call(bf16[4,2,72,1536]{3,2,1,0:T(8,128)(2,1)} %all_to_all.105.refs_0_, bf16[32,384,768]{2,1,0:T(8,128)(2,1)} %bitcast.161, bf16[32,384,768]{2,1,0:T(8,128)(2,1)} %bitcast.162, bf16[32,384,768]{2,1,0:T(8,128)(2,1)} %bitcast.163, ...), custom_call_target="tpu_custom_call" | custom-call | flops 4076863488 | bytes 118554624 | tf_op jit(solution)/shard_map/pallas_call | solution.py:158
  164.7 26.1 %all_to_all.106 = bf16[4,2,72,1536]{3,2,1,0:T(8,128)(2,1)} all-to-all(bf16[4,2,72,1536]{3,2,1,0:T(8,128)(2,1)} %get-tuple-element.138), channel_id=1, replica_groups=mesh['seq'=4,'fsdp'=32] {'seq'}, dimensions={0} | all-to-all | bytes 3538944 | tf_op jit(solution)/shard_map/all_to_all | solution.py:688
  197.6 9.7 %collective-permute-done.4.refs_2_ = bf16[128,1536]{1,0:T(8,128)(2,1)} collective-permute-done((bf16[128,1536]{1,0:T(8,128)(2,1)}, bf16[128,1536]{1,0:T(8,128)(2,1)}, u32[]{:S(2)}, u32[]{:S(2)}) %collective-permute-start.4) | collective-permute-done | bytes 393248 | tf_op jit(solution)/shard_map/ppermute | solution.py:694
  215.6 7.3 %shard_map.242 = (bf16[4,128,640]{2,1,0:T(8,128)(2,1)}, bf16[4,128,384]{2,1,0:T(8,128)(2,1)}, bf16[4,128,1536]{2,1,0:T(8,128)(2,1)}) custom-call(s32[1]{0:T(128)} %bitcast.11.refs_0_, bf16[128,1536]{1,0:T(8,128)(2,1)} %get-tuple-element.140.refs_1_, bf16[128,1536]{1,0:T(8,128)(2,1)} %collective-permute-done.4.refs_2_, ...), custom_call_target="tpu_custom_call" | custom-call | flops 1610612736 | bytes 83623936 | tf_op jit(solution)/shard_map/pallas_call | solution.py:158
  242.0 26.8 %all_to_all.107.refs_0_ = bf16[4,2,72,1536]{3,2,1,0:T(8,128)(2,1)} all-to-all(bf16[4,2,72,1536]{3,2,1,0:T(8,128)(2,1)} %bitcast.187), channel_id=1, replica_groups=mesh['seq'=4,'fsdp'=32] {'seq'}, dimensions={0} | all-to-all | bytes 3538944 | tf_op jit(solution)/shard_map/all_to_all | solution.py:688
  268.9 9.5 %shard_map.244 = (bf16[4,2,72,1536]{3,2,1,0:T(8,128)(2,1)}, bf16[2,288,768]{2,1,0:T(8,128)(2,1)}, bf16[2,288,768]{2,1,0:T(8,128)(2,1)}) custom-call(bf16[4,2,72,1536]{3,2,1,0:T(8,128)(2,1)} %all_to_all.107.refs_0_, bf16[32,528,768]{2,1,0:T(8,128)(2,1)} %bitcast.144, bf16[32,528,768]{2,1,0:T(8,128)(2,1)} %bitcast.145, bf16[32,528,768]{2,1,0:T(8,128)(2,1)} %bitcast.146, ...), custom_call_target="tpu_custom_call" | custom-call | flops 4076863488 | bytes 161021952 | tf_op jit(solution)/shard_map/pallas_call | solution.py:158
  283.9 20.4 %all-to-all-done.8 = bf16[4,2,72,1536]{3,2,1,0:T(8,128)(2,1)} async-done(((bf16[4,2,72,1536]{3,2,1,0:T(8,128)(2,1)}), bf16[4,2,72,1536]{3,2,1,0:T(8,128)(2,1)}, u32[]{:S(2)}, u32[]{:S(2)}) %all-to-all-start.8) | async-done | bytes 1769504 | tf_op jit(solution)/shard_map/all_to_all | solution.py:688
  317.4 16.9 %all-to-all-done.9.refs_0_.refs_1_ = bf16[4,2,72,1536]{3,2,1,0:T(8,128)(2,1)} async-done(((bf16[4,2,72,1536]{3,2,1,0:T(8,128)(2,1)}), bf16[4,2,72,1536]{3,2,1,0:T(8,128)(2,1)}, u32[]{:S(2)}, u32[]{:S(2)}) %all-to-all-start.9) | async-done | bytes 1769504 | tf_op jit(solution)/shard_map/all_to_all | solution.py:688
  334.3 11.5 %shard_map.247 = (bf16[4,2,72,1536]{3,2,1,0:T(8,128)(2,1)}, bf16[2,288,768]{2,1,0:T(8,128)(2,1)}, bf16[2,288,768]{2,1,0:T(8,128)(2,1)}, bf16[2,288,768]{2,1,0:T(8,128)(2,1)}) custom-call(bf16[4,2,72,1536]{3,2,1,0:T(8,128)(2,1)} %all-to-all-done.9.refs_0_.refs_1_, bf16[32,528,768]{2,1,0:T(8,128)(2,1)} %bitcast.150, ...), custom_call_target="tpu_custom_call" | custom-call | flops 4076863488 | bytes 163676160 | tf_op jit(solution)/shard_map/pallas_call | solution.py:158
  350.5 12.1 %shard_map.248 = bf16[32,288,768]{2,1,0:T(8,128)(2,1)} custom-call(bf16[4,2,72,1536]{3,2,1,0:T(8,128)(2,1)} %all_to_all.107.refs_0_, bf16[4,2,72,1536]{3,2,1,0:T(8,128)(2,1)} %all-to-all-done.9.refs_0_.refs_1_, bf16[2,288,768]{2,1,0:T(8,128)(2,1)} %get-tuple-element.160.refs_2_, bf16[2,288,768]{2,1,0:T(8,128)(2,1)} %get-tuple-element.161.refs_3_, ...), custom_call_target="tpu_custom_call" | custom-call | flops 4076863488 | bytes 20348928 | tf_op jit(solution)/shard_map/pallas_call | solution.py:158
  376.4 11.8 %all_to_all.108.refs_1_ = bf16[4,128,384]{2,1,0:T(8,128)(2,1)} all-to-all(bf16[4,128,384]{2,1,0:T(8,128)(2,1)} %get-tuple-element.166), channel_id=1, replica_groups=mesh['seq'=4,'fsdp'=32] {'seq'}, dimensions={0} | all-to-all | bytes 786432 | tf_op jit(solution)/shard_map/all_to_all | solution.py:688
  411.7 7.6 %shard_map.252 = (f32[128,1536]{1,0:T(8,128)}, f32[32,128]{1,0:T(8,128)}) custom-call(bf16[4,128,640]{2,1,0:T(8,128)(2,1)} %all-to-all-done.12.refs_0_, bf16[32,528,768]{2,1,0:T(8,128)(2,1)} %bitcast.157, bf16[32,528,768]{2,1,0:T(8,128)(2,1)} %bitcast.158, bf16[32,528,768]{2,1,0:T(8,128)(2,1)} %bitcast.159, ...), custom_call_target="tpu_custom_call" | custom-call | flops 2415919104 | bytes 81231872 | tf_op jit(solution)/shard_map/pallas_call | solution.py:158
  435.2 18.0 %all-to-all-done.13.refs_0_.refs_1_ = bf16[4,2,72,1536]{3,2,1,0:T(8,128)(2,1)} async-done(((bf16[4,2,72,1536]{3,2,1,0:T(8,128)(2,1)}), bf16[4,2,72,1536]{3,2,1,0:T(8,128)(2,1)}, u32[]{:S(2)}, u32[]{:S(2)}) %all-to-all-start.13) | async-done | bytes 1769504 | tf_op jit(solution)/shard_map/all_to_all | solution.py:688
  453.2 11.5 %shard_map.255 = (bf16[4,2,72,1536]{3,2,1,0:T(8,128)(2,1)}, bf16[2,288,768]{2,1,0:T(8,128)(2,1)}, bf16[2,288,768]{2,1,0:T(8,128)(2,1)}, bf16[2,288,768]{2,1,0:T(8,128)(2,1)}) custom-call(bf16[4,2,72,1536]{3,2,1,0:T(8,128)(2,1)} %all-to-all-done.13.refs_0_.refs_1_, bf16[32,384,768]{2,1,0:T(8,128)(2,1)} %bitcast.167, ...), custom_call_target="tpu_custom_call" | custom-call | flops 4076863488 | bytes 121208832 | tf_op jit(solution)/shard_map/pallas_call | solution.py:158
  469.4 13.5 %shard_map.256 = bf16[32,368,768]{2,1,0:T(8,128)(2,1)} custom-call(bf16[4,2,72,1536]{3,2,1,0:T(8,128)(2,1)} %all_to_all.105.refs_0_, bf16[4,2,72,1536]{3,2,1,0:T(8,128)(2,1)} %all-to-all-done.13.refs_0_.refs_1_, bf16[2,288,768]{2,1,0:T(8,128)(2,1)} %get-tuple-element.187.refs_2_, bf16[2,288,768]{2,1,0:T(8,128)(2,1)} %get-tuple-element.188.refs_3_, ...), custom_call_target="tpu_custom_call" | custom-call | flops 4076863488 | bytes 28213248 | tf_op jit(solution)/shard_map/pallas_call | solution.py:158
  482.9 7.8 %all-to-all-done.14 = bf16[4,2,72,1536]{3,2,1,0:T(8,128)(2,1)} async-done(((bf16[4,2,72,1536]{3,2,1,0:T(8,128)(2,1)}), bf16[4,2,72,1536]{3,2,1,0:T(8,128)(2,1)}, u32[]{:S(2)}, u32[]{:S(2)}) %all-to-all-start.14) | async-done | bytes 1769504 | tf_op jit(solution)/shard_map/all_to_all | solution.py:688
  497.3 11.8 %all_to_all.109.refs_1_ = bf16[4,128,384]{2,1,0:T(8,128)(2,1)} all-to-all(bf16[4,128,384]{2,1,0:T(8,128)(2,1)} %get-tuple-element.195), channel_id=1, replica_groups=mesh['seq'=4,'fsdp'=32] {'seq'}, dimensions={0} | all-to-all | bytes 786432 | tf_op jit(solution)/shard_map/all_to_all | solution.py:688
  534.9 7.6 %shard_map.260 = (f32[128,1536]{1,0:T(8,128)}, f32[32,128]{1,0:T(8,128)}) custom-call(bf16[4,128,640]{2,1,0:T(8,128)(2,1)} %all-to-all-done.16.refs_0_, bf16[32,144,768]{2,1,0:T(8,128)(2,1)} %bitcast.174, bf16[32,144,768]{2,1,0:T(8,128)(2,1)} %bitcast.175, bf16[32,144,768]{2,1,0:T(8,128)(2,1)} %bitcast.176, ...), custom_call_target="tpu_custom_call" | custom-call | flops 2415919104 | bytes 24215552 | tf_op jit(solution)/shard_map/pallas_call | solution.py:158
  563.5 20.9 %all-to-all-done.17 = bf16[16,32,768]{2,1,0:T(8,128)(2,1)S(1)} async-done(((bf16[16,32,768]{2,1,0:T(8,128)(2,1)}), bf16[16,32,768]{2,1,0:T(8,128)(2,1)S(1)}, u32[]{:S(2)}, u32[]{:S(2)}) %all-to-all-start.17) | async-done | bytes 786464 | tf_op jit(solution)/shard_map/all_to_all | solution.py:819
  589.0 17.5 %all-to-all-done.18 = bf16[16,48,768]{2,1,0:T(8,128)(2,1)S(1)} async-done(((bf16[16,48,768]{2,1,0:T(8,128)(2,1)}), bf16[16,48,768]{2,1,0:T(8,128)(2,1)S(1)}, u32[]{:S(2)}, u32[]{:S(2)}) %all-to-all-start.18) | async-done | bytes 1179680 | tf_op jit(solution)/shard_map/all_to_all | solution.py:819
  612.3 8.2 %reduce-scatter.5.cloned.1.call-done = bf16[1,368,768]{2,1,0:T(8,128)(2,1)} async-done(((bf16[32,368,768]{2,1,0:T(8,128)(2,1)}), bf16[1,368,768]{2,1,0:T(8,128)(2,1)}) %reduce-scatter.5.cloned.1.call-update) | async-done | bytes 565264 | tf_op jit(solution)/shard_map/reduce_scatter | solution.py:961
  (224 shorter events, 296.5 us)
Async XLA Ops:
  20.2 99.7 %all-gather.7.cloned.1.call-start = ((), (), s32[]{:S(2)}) async-start(), calls=%async_computation.25 | async-start | bytes 19464192 | tf_op jit(solution)/shard_map/all_gather | solution.py:813
  36.1 34.9 %all-to-all-start.1 = ((bf16[16,48,896]{2,1,0:T(8,128)(2,1)}), bf16[16,48,896]{2,1,0:T(8,128)(2,1)S(1)}, u32[]{:S(2)}, u32[]{:S(2)}) async-start(bf16[16,48,896]{2,1,0:T(8,128)(2,1)} %broadcast_in_dim.92), calls=%async_computation.1 | async-start | bytes 2752512 | tf_op jit(solution)/shard_map/all_to_all | solution.py:819
  47.0 17.4 %collective-permute-start.2 = (bf16[128,1536]{1,0:T(8,128)(2,1)S(1)}, bf16[128,1536]{1,0:T(8,128)(2,1)}, u32[]{:S(2)}, u32[]{:S(2)}) collective-permute-start(bf16[128,1536]{1,0:T(8,128)(2,1)S(1)} %bitcast.193), channel_id=1, source_target_pairs={{96,0},{0,32},{32,64},{64,96},{97,1},{1,33},{33,65},{65,97},{98,2}... | collective-permute-start | bytes 1179656 | tf_op jit(solution)/shard_map/ppermute | solution.py:694
  70.9 16.4 %collective-permute-start.3 = (bf16[16,48,896]{2,1,0:T(8,128)(2,1)S(1)}, bf16[16,48,896]{2,1,0:T(8,128)(2,1)}, u32[]{:S(2)}, u32[]{:S(2)}) collective-permute-start(bf16[16,48,896]{2,1,0:T(8,128)(2,1)S(1)} %all-to-all-done.1), channel_id=1, source_target_pairs={{0,1},{1,0},{2,3},{3,2},{4,5},{5,4},{6,7},{7,6},{8,9},{9,8},{10,11... | collective-permute-start | bytes 4128776 | tf_op jit(solution)/shard_map/ppermute | solution.py:824
  106.1 109.6 %all-gather.9.cloned.1.call-start = ((), (), s32[]{:S(2)}) async-start(), calls=%async_computation.26 | async-start | bytes 26763264 | tf_op jit(solution)/shard_map/all_gather | solution.py:813
  197.6 16.9 %collective-permute-start.6 = (bf16[128,1536]{1,0:T(8,128)(2,1)}, bf16[128,1536]{1,0:T(8,128)(2,1)}, u32[]{:S(2)}, u32[]{:S(2)}) collective-permute-start(bf16[128,1536]{1,0:T(8,128)(2,1)} %get-tuple-element.140.refs_1_), channel_id=1, source_target_pairs={{96,0},{0,32},{32,64},{64,96},{97,1},{1,33},{33,65},{65,97},{98,2}... | collective-permute-start | bytes 1179656 | tf_op jit(solution)/shard_map/ppermute | solution.py:694
  227.4 106.9 %all-gather.11.cloned.1.call-start = ((), (), s32[]{:S(2)}) async-start(), calls=%async_computation.27 | async-start | bytes 7299072 | tf_op jit(solution)/shard_map/all_gather | solution.py:813
  278.4 25.9 %all-to-all-start.8 = ((bf16[4,2,72,1536]{3,2,1,0:T(8,128)(2,1)}), bf16[4,2,72,1536]{3,2,1,0:T(8,128)(2,1)}, u32[]{:S(2)}, u32[]{:S(2)}) async-start(bf16[4,2,72,1536]{3,2,1,0:T(8,128)(2,1)} %get-tuple-element.148), calls=%async_computation.8 | async-start | bytes 3538944 | tf_op jit(solution)/shard_map/all_to_all | solution.py:688
  309.0 25.3 %all-to-all-start.9 = ((bf16[4,2,72,1536]{3,2,1,0:T(8,128)(2,1)}), bf16[4,2,72,1536]{3,2,1,0:T(8,128)(2,1)}, u32[]{:S(2)}, u32[]{:S(2)}) async-start(bf16[4,2,72,1536]{3,2,1,0:T(8,128)(2,1)} %bitcast.185), calls=%async_computation.9 | async-start | bytes 3538944 | tf_op jit(solution)/shard_map/all_to_all | solution.py:688
  345.8 24.0 %all-to-all-start.10 = ((bf16[4,2,72,1536]{3,2,1,0:T(8,128)(2,1)}), bf16[4,2,72,1536]{3,2,1,0:T(8,128)(2,1)}, u32[]{:S(2)}, u32[]{:S(2)}) async-start(bf16[4,2,72,1536]{3,2,1,0:T(8,128)(2,1)} %get-tuple-element.159), calls=%async_computation.10 | async-start | bytes 3538944 | tf_op jit(solution)/shard_map/all_to_all | solution.py:688
  350.3 140.4 %reduce-scatter.3.cloned.1.call-start = ((), (), s32[]{:S(2)}) async-start(), calls=%async_computation.23 | async-start | bytes 14598144 | tf_op jit(solution)/shard_map/reduce_scatter | solution.py:961
  395.1 16.6 %all-to-all-start.12 = ((bf16[4,128,640]{2,1,0:T(8,128)(2,1)}), bf16[4,128,640]{2,1,0:T(8,128)(2,1)}, u32[]{:S(2)}, u32[]{:S(2)}) async-start(bf16[4,128,640]{2,1,0:T(8,128)(2,1)} %shard_map.250.refs_1_), calls=%async_computation.12 | async-start | bytes 1310720 | tf_op jit(solution)/shard_map/all_to_all | solution.py:688
  399.3 20.1 %collective-permute-start.7 = (bf16[128,1536]{1,0:T(8,128)(2,1)}, bf16[128,1536]{1,0:T(8,128)(2,1)}, u32[]{:S(2)}, u32[]{:S(2)}) collective-permute-start(bf16[128,1536]{1,0:T(8,128)(2,1)} %get-tuple-element.178.refs_1_), channel_id=1, source_target_pairs={{32,0},{64,32},{96,64},{0,96},{33,1},{65,33},{97,65},{1,97},{34,2}... | collective-permute-start | bytes 1179656 | tf_op jit(solution)/shard_map/ppermute | solution.py:694
  402.5 16.9 %collective-permute-start.8 = (bf16[128,1536]{1,0:T(8,128)(2,1)}, bf16[128,1536]{1,0:T(8,128)(2,1)}, u32[]{:S(2)}, u32[]{:S(2)}) collective-permute-start(bf16[128,1536]{1,0:T(8,128)(2,1)} %get-tuple-element.178.refs_1_), channel_id=1, source_target_pairs={{64,0},{96,32},{0,64},{32,96},{65,1},{97,33},{1,65},{33,97},{66,2}... | collective-permute-start | bytes 1179656 | tf_op jit(solution)/shard_map/ppermute | solution.py:694
  403.3 18.0 %collective-permute-start.9 = (bf16[128,1536]{1,0:T(8,128)(2,1)}, bf16[128,1536]{1,0:T(8,128)(2,1)}, u32[]{:S(2)}, u32[]{:S(2)}) collective-permute-start(bf16[128,1536]{1,0:T(8,128)(2,1)} %get-tuple-element.178.refs_1_), channel_id=1, source_target_pairs={{96,0},{0,32},{32,64},{64,96},{97,1},{1,33},{33,65},{65,97},{98,2}... | collective-permute-start | bytes 1179656 | tf_op jit(solution)/shard_map/ppermute | solution.py:694
  426.1 27.1 %all-to-all-start.13 = ((bf16[4,2,72,1536]{3,2,1,0:T(8,128)(2,1)}), bf16[4,2,72,1536]{3,2,1,0:T(8,128)(2,1)}, u32[]{:S(2)}, u32[]{:S(2)}) async-start(bf16[4,2,72,1536]{3,2,1,0:T(8,128)(2,1)} %bitcast.184), calls=%async_computation.13 | async-start | bytes 3538944 | tf_op jit(solution)/shard_map/all_to_all | solution.py:688
  464.7 25.9 %all-to-all-start.14 = ((bf16[4,2,72,1536]{3,2,1,0:T(8,128)(2,1)}), bf16[4,2,72,1536]{3,2,1,0:T(8,128)(2,1)}, u32[]{:S(2)}, u32[]{:S(2)}) async-start(bf16[4,2,72,1536]{3,2,1,0:T(8,128)(2,1)} %get-tuple-element.186), calls=%async_computation.14 | async-start | bytes 3538944 | tf_op jit(solution)/shard_map/all_to_all | solution.py:688
  469.2 151.3 %reduce-scatter.5.cloned.1.call-start = ((), (), s32[]{:S(2)}) async-start(), calls=%async_computation.24 | async-start | bytes 18653184 | tf_op jit(solution)/shard_map/reduce_scatter | solution.py:961
  516.0 18.9 %all-to-all-start.16 = ((bf16[4,128,640]{2,1,0:T(8,128)(2,1)}), bf16[4,128,640]{2,1,0:T(8,128)(2,1)}, u32[]{:S(2)}, u32[]{:S(2)}) async-start(bf16[4,128,640]{2,1,0:T(8,128)(2,1)} %shard_map.258.refs_1_), calls=%async_computation.16 | async-start | bytes 1310720 | tf_op jit(solution)/shard_map/all_to_all | solution.py:688
  520.2 22.3 %collective-permute-start.10 = (bf16[128,1536]{1,0:T(8,128)(2,1)}, bf16[128,1536]{1,0:T(8,128)(2,1)}, u32[]{:S(2)}, u32[]{:S(2)}) collective-permute-start(bf16[128,1536]{1,0:T(8,128)(2,1)} %get-tuple-element.206.refs_1_), channel_id=1, source_target_pairs={{32,0},{64,32},{96,64},{0,96},{33,1},{65,33},{97,65},{1,97},{34,2}... | collective-permute-start | bytes 1179656 | tf_op jit(solution)/shard_map/ppermute | solution.py:694
  523.4 19.1 %collective-permute-start.11 = (bf16[128,1536]{1,0:T(8,128)(2,1)}, bf16[128,1536]{1,0:T(8,128)(2,1)}, u32[]{:S(2)}, u32[]{:S(2)}) collective-permute-start(bf16[128,1536]{1,0:T(8,128)(2,1)} %get-tuple-element.206.refs_1_), channel_id=1, source_target_pairs={{64,0},{96,32},{0,64},{32,96},{65,1},{97,33},{1,65},{33,97},{66,2}... | collective-permute-start | bytes 1179656 | tf_op jit(solution)/shard_map/ppermute | solution.py:694
  524.3 20.3 %collective-permute-start.12 = (bf16[128,1536]{1,0:T(8,128)(2,1)}, bf16[128,1536]{1,0:T(8,128)(2,1)}, u32[]{:S(2)}, u32[]{:S(2)}) collective-permute-start(bf16[128,1536]{1,0:T(8,128)(2,1)} %get-tuple-element.206.refs_1_), channel_id=1, source_target_pairs={{96,0},{0,32},{32,64},{64,96},{97,1},{1,33},{33,65},{65,97},{98,2}... | collective-permute-start | bytes 1179656 | tf_op jit(solution)/shard_map/ppermute | solution.py:694
  556.4 28.0 %all-to-all-start.17 = ((bf16[16,32,768]{2,1,0:T(8,128)(2,1)}), bf16[16,32,768]{2,1,0:T(8,128)(2,1)S(1)}, u32[]{:S(2)}, u32[]{:S(2)}) async-start(bf16[16,32,768]{2,1,0:T(8,128)(2,1)} %fusion.1), calls=%async_computation.17 | async-start | bytes 1572864 | tf_op jit(solution)/shard_map/all_to_all | solution.py:819
  584.4 22.0 %all-to-all-start.18 = ((bf16[16,48,768]{2,1,0:T(8,128)(2,1)}), bf16[16,48,768]{2,1,0:T(8,128)(2,1)S(1)}, u32[]{:S(2)}, u32[]{:S(2)}) async-start(bf16[16,48,768]{2,1,0:T(8,128)(2,1)} %fusion), calls=%async_computation.18 | async-start | bytes 2359296 | tf_op jit(solution)/shard_map/all_to_all | solution.py:819
  (28 other events, 267.8 us)
Sparse Core Ops, SparseCore 0:
  30.4 89.4 all-gather.6
  122.2 93.4 all-gather.8
  236.1 47.7 all-gather.10
  369.9 105.7 reduce-scatter.2
  490.8 129.6 reduce-scatter.4

commit v3 on v2

--- a/solution.py
+++ b/solution.py
@@ -38,16 +38,16 @@
     return (jnp.cos(angles), jnp.sin(angles), labels)
 
 
-def slot_table(expert_rows, order_rows, expert_count, capacity):
-    pair_expert = expert_rows.reshape(-1)
-    pair_order = order_rows.reshape(-1)
+def slot_table(routes_t, order_t, expert_count, capacity):
+    pair_expert = routes_t.reshape(-1)
+    pair_order = order_t.reshape(-1)
     same_expert = pair_expert[:, None] == pair_expert[None, :]
     earlier = pair_order[None, :] < pair_order[:, None]
     pair_slot = jnp.sum(jnp.logical_and(same_expert, earlier).astype(jnp.int32), axis=1)
     target = jnp.where(
         pair_slot < capacity, pair_expert * capacity + pair_slot, expert_count * capacity
     )
-    return target.reshape(expert_rows.shape).T
+    return target.reshape(routes_t.shape)
 
 
 def nn(left, right):
@@ -320,13 +320,11 @@
 
 
 def next_attention_kernel(
-    place, own, one, two, three, query_w, key_w, value_w, cosines, sines, bias_ref,
-    heads_ref, out_ref, normed_ref,
+    place, own, one, two, three, weight, cosines, sines, bias_ref, heads_ref, out_ref, normed_ref
 ):
     me = place[0]
     seq_count, tokens, width = normed_ref.shape
-    weight = [w[...].reshape(width, w.shape[2]) for w in (query_w, key_w, value_w)]
-    weight = jnp.concatenate(weight, axis=1)
+    weight = weight[...].reshape(width, weight.shape[2])[:, : heads_ref.shape[2]]
     for k, block in enumerate((own, one, two, three)):
         normed_ref[lax.rem(me + k, seq_count)] = block[...]
     normed_ref.send()
@@ -334,9 +332,25 @@
     attend(rows, weight, cosines[...], sines[...], bias_ref, heads_ref, out_ref)
 
 
+def gates_of(logits, routes_t, rows):
+    expert_count = 8
+    tokens = logits.shape[1]
+    chosen = []
+    for k in range(TOPK):
+        route = routes_t[k : k + 1]
+        value = jnp.zeros((1, tokens), f32)
+        for e in range(expert_count):
+            value = value + jnp.where(route == e, logits[e : e + 1], 0.0)
+        chosen.append(value)
+    peak = functools.reduce(jnp.maximum, chosen)
+    powers = [jnp.exp(value - peak) for value in chosen]
+    total = functools.reduce(jnp.add, powers)
+    gates = [power / total for power in powers]
+    return jnp.concatenate(gates + [jnp.zeros((rows - TOPK, tokens), f32)], axis=0)
+
+
 def after_attention_kernel(
-    back, spread, hidden, small, out_w, routes_t, target_t,
-    middle_ref, normed_ref, gates_ref, send_ref,
+    back, spread, hidden, small, out_w, routes_t, middle_ref, normed_ref, gates_ref
 ):
     expert_count = 8
     seq_count, tokens, part = back.shape
@@ -354,27 +368,7 @@
     normed = normalize(middle, gain).astype(bf16)
     normed_ref[...] = normed
     normed_ref.send()
-    send_ref[...] = nn(choose(target_t[...], send_ref.shape[0]).astype(bf16), normed).astype(bf16)
-    send_ref.send()
-    logits = nt(small[...], normed)
-    chosen = []
-    for k in range(TOPK):
-        route = routes_t[k : k + 1]
-        value = jnp.zeros((1, tokens), f32)
-        for e in range(expert_count):
-            value = value + jnp.where(route == e, logits[e : e + 1], 0.0)
-        chosen.append(value)
-    peak = functools.reduce(jnp.maximum, chosen)
-    powers = [jnp.exp(value - peak) for value in chosen]
-    total = functools.reduce(jnp.add, powers)
-    for k in range(TOPK):
-        gates_ref[k : k + 1] = powers[k] / total
-    gates_ref[TOPK:] = jnp.zeros((gates_ref.shape[0] - TOPK, tokens), f32)
-
-
-def flat_rows(block):
-    sources, capacity, width = block.shape
-    return block.astype(f32).reshape(sources * capacity, width).astype(bf16)
+    gates_ref[...] = gates_of(nt(small[...], normed), routes_t[...], gates_ref.shape[0])
 
 
 def down_parts(block):
@@ -385,38 +379,47 @@
     return left, right
 
 
-def expert_kernel(rows_ref, *rest):
-    experts = rows_ref.shape[1]
-    weights = rest[: 3 * experts]
-    out_ref, gate_ref, up_ref = rest[3 * experts :]
-    sources, capacity = rows_ref.shape[0], rows_ref.shape[2]
+def expert_kernel(place, own, one, two, three, targets, routes, small, *rest):
+    me = place[0]
+    blocks = (own, one, two, three)
+    out_ref, rows_ref, gate_ref, up_ref, gates_ref = rest[-5:]
+    weights = rest[:-5]
+    sources, experts, capacity, width = out_ref.shape
+    half = width // 2
     for e in range(experts):
         gate_w, up_w, down_w = weights[3 * e : 3 * e + 3]
-        shards, rows, half = gate_w.shape
-        tokens = flat_rows(rows_ref[:, e])
-        gate_val = nn(tokens, gate_w[...].reshape(shards * rows, half))
+        first = (me * experts + e) * capacity
+        parts = []
+        for k, block in enumerate(blocks):
+            hot = choose(targets[lax.rem(me + k, sources)] - first, capacity)
+            parts.append(nn(hot.astype(bf16), block[...]))
+        tokens = jnp.concatenate(parts, axis=0).astype(bf16)
+        rows_ref[e] = tokens
+        rows_ref.send(e)
+        gate_val = nn(tokens, gate_w[...].reshape(width, half))
         gate_ref[e] = gate_val.astype(bf16)
         gate_ref.send(e)
-        up_val = nn(tokens, up_w[...].reshape(shards * rows, half))
+        up_val = nn(tokens, up_w[...].reshape(width, half))
         up_ref[e] = up_val.astype(bf16)
         up_ref.send(e)
         activated, slope = smooth_parts(gate_val)
         inner = (activated * up_val).astype(bf16)
         for side, part in enumerate(down_parts(down_w[...])):
-            block = nn(inner, part).reshape(sources, capacity, half).astype(bf16)
-            out_ref[:, e, :, side * half : (side + 1) * half] = block
+            done = nn(inner, part).astype(bf16)
+            for k in range(sources):
+                out_ref[lax.rem(me + k, sources), e, :, side * half : (side + 1) * half] = done[
+                    k * capacity : (k + 1) * capacity
+                ]
         out_ref.send(e)
-
-
-def slot_grad_kernel(grad, combined, gates_t, routes_t, target_t, send_ref, logits_ref):
+    for k, block in enumerate(blocks):
+        logits = nt(small[...], block[...])
+        gates_ref[k] = gates_of(logits, routes[lax.rem(me + k, sources)], gates_ref.shape[1])
+
+
+def logits_grad_kernel(grad, combined, gates_t, routes_t, target_t, logits_ref):
     tokens = grad.shape[0]
     slots = combined.shape[0]
     high, low = split(grad[...])
-    weights_high, weights_low = split(choose_weighted(target_t[...], gates_t[...], slots))
-    weights = jnp.concatenate([weights_high, weights_low, weights_high], axis=1)
-    send = nn(weights, jnp.concatenate([high, high, low], axis=0))
-    send_ref[...] = send.astype(bf16)
-    send_ref.send()
     products = nt(combined[...], jnp.concatenate([high, low], axis=0))
     products = products[:, :tokens] + products[:, tokens:]
     place = lax.broadcasted_iota(jnp.int32, (slots, tokens), 0)
@@ -434,15 +437,28 @@
     logits_ref[...] = total.astype(bf16)
 
 
-def expert_back_kernel(grad_ref, down_first, gate_ref, up_ref, *rest):
-    experts = grad_ref.shape[1]
-    weights = (down_first,) + rest[: 3 * experts - 1]
-    out_ref, gate_grad_ref, up_grad_ref, inner_ref = rest[3 * experts - 1 :]
-    sources, capacity = grad_ref.shape[0], grad_ref.shape[2]
+def expert_back_kernel(
+    place, own, one, two, three, targets, gates, down_first, gate_ref, up_ref, *rest
+):
+    me = place[0]
+    blocks = (own, one, two, three)
+    out_ref, rows_ref, gate_grad_ref, up_grad_ref, inner_ref = rest[-5:]
+    weights = (down_first,) + rest[:-5]
+    sources, experts, capacity, width = out_ref.shape
+    half = width // 2
     for e in range(experts):
         down_w, gate_w, up_w = weights[3 * e : 3 * e + 3]
-        shards, rows, half = gate_w.shape
-        grad = flat_rows(grad_ref[:, e])
+        shards, rows, _ = gate_w.shape
+        first = (me * experts + e) * capacity
+        parts = []
+        for k, block in enumerate(blocks):
+            target = targets[lax.rem(me + k, sources)] - first
+            hot = jnp.concatenate(split(choose_weighted(target, gates[k], capacity)), axis=1)
+            twice = jnp.concatenate([block[...], block[...]], axis=0)
+            parts.append(nn(hot, twice))
+        grad = jnp.concatenate(parts, axis=0).astype(bf16)
+        rows_ref[e] = grad
+        rows_ref.send(e)
         left, right = down_parts(down_w[...])
         grad_inner = nt(grad[:, :half], left) + nt(grad[:, half:], right)
         up_val = up_ref[e].astype(f32)
@@ -459,16 +475,18 @@
             at = slice(c * some, (c + 1) * some)
             total = nt(gate_grad_ref[e], gate_w[at].reshape(size, half))
             total = total + nt(up_grad_ref[e], up_w[at].reshape(size, half))
-            total = total.reshape(sources, capacity, size).astype(bf16)
-            out_ref[:, e, :, c * size : (c + 1) * size] = total
+            total = total.astype(bf16)
+            for k in range(sources):
+                out_ref[lax.rem(me + k, sources), e, :, c * size : (c + 1) * size] = total[
+                    k * capacity : (k + 1) * capacity
+                ]
         out_ref.send(e)
 
 
 def expert_weight_kernel(rows_ref, grad_ref, gate_grad_ref, up_grad_ref, inner_ref, *rest):
     pack_ref = rest[-1]
-    experts = rows_ref.shape[1]
-    shards, rows, half = pack_ref.shape
-    width = rows_ref.shape[3]
+    experts, _, width = rows_ref.shape
+    shards, _, half = pack_ref.shape
     rows = width // shards
     at = 0
 
@@ -477,14 +495,12 @@
             pack_ref.send(piece)
 
     for e in range(experts):
-        tokens = flat_rows(rows_ref[:, e])
-        grad = flat_rows(grad_ref[:, e])
         grads = jnp.concatenate([gate_grad_ref[e], up_grad_ref[e]], axis=1)
-        both = tn(tokens, grads).astype(bf16)
+        both = tn(rows_ref[e], grads).astype(bf16)
         pack_ref[:, at : at + rows] = both[:, :half].reshape(shards, rows, half)
         pack_ref[:, at + rows : at + 2 * rows] = both[:, half:].reshape(shards, rows, half)
         send(at, 2 * rows)
-        down = tn(inner_ref[e], grad)
+        down = tn(inner_ref[e], grad_ref[e])
         left = down[:, :half].reshape(shards, rows // 2, half)
         right = down[:, half:].reshape(shards, rows // 2, half)
         down = jnp.concatenate([left, right], axis=1).astype(bf16)
@@ -572,7 +588,7 @@
 
 
 def before_attention_kernel(
-    sent, left_w, right_w, kv_w, spread, small, hidden, grad_middle, out_ref, gain_ref
+    sent, left_w, right_w, kv_w, spread, small, hidden, grad_middle, out_ref, low_ref, gain_ref
 ):
     expert_count = 8
     seq_count, tokens, columns = sent.shape
@@ -598,7 +614,10 @@
     grad_normed = both[:tokens] + both[tokens:]
     gain = small[expert_count : expert_count + 1].astype(f32)
     grad_value, grad_gain = normalize_back(hidden[...].astype(f32), gain, grad_normed)
-    out_ref[...] = grad_middle[...] + grad_value
+    total = grad_middle[...] + grad_value
+    low_ref[...] = total.astype(bf16)
+    low_ref.send()
+    out_ref[...] = total
     out_ref.send()
     shards = gain_ref.shape[0]
     width = grad_gain.shape[1]
@@ -625,26 +644,33 @@
     out_ref[:, :, columns:] = extra.astype(bf16).reshape(shards, rows, wide - columns)
 
 
-def out_weight_kernel(place, own, one, two, three, attended, gain, out_ref):
+def out_weight_kernel(place, own, one, two, three, *rest):
+    out_ref = rest[-1]
     me = place[0]
-    seq_count, tokens, part = attended.shape
     shards, rows, half = out_ref.shape
-    rows = rows // 2
-    valid = part // shards
-    branch = jnp.concatenate([own[...], one[...], two[...], three[...]], axis=0)
-    heads = jnp.concatenate([attended[lax.rem(me + k, seq_count)] for k in range(seq_count)], axis=0)
-    place_in = lax.broadcasted_iota(jnp.int32, (part, shards * rows), 0)
-    place_out = lax.broadcasted_iota(jnp.int32, (part, shards * rows), 1)
-    source = place_out // rows * valid + place_out % rows
-    same = jnp.logical_and(place_in == source, place_out % rows < valid)
-    heads = nn(heads, jnp.where(same, 1.0, 0.0).astype(bf16)).astype(bf16)
-    wide = jnp.concatenate([gain[...], jnp.zeros((shards, half - HD), f32)], axis=1)
-    row = lax.broadcasted_iota(jnp.int32, (shards, rows, half), 1)
-    for side in range(2):
-        total = tn(heads, branch[:, side * half : (side + 1) * half]).reshape(shards, rows, half)
-        if side == 0:
-            total = jnp.where(row == valid, wide[:, None, :], total)
-        out_ref[:, side * rows : (side + 1) * rows] = total.astype(bf16)
+    rows = rows // (2 * LAYERS)
+    for layer in range(LAYERS):
+        attended, gain = rest[layer], rest[LAYERS + layer]
+        seq_count, tokens, part = attended.shape
+        valid = part // shards
+        branch = jnp.concatenate([block[layer] for block in (own, one, two, three)], axis=0)
+        heads = jnp.concatenate(
+            [attended[lax.rem(me + k, seq_count)] for k in range(seq_count)], axis=0
+        )
+        place_in = lax.broadcasted_iota(jnp.int32, (part, shards * rows), 0)
+        place_out = lax.broadcasted_iota(jnp.int32, (part, shards * rows), 1)
+        source = place_out // rows * valid + place_out % rows
+        same = jnp.logical_and(place_in == source, place_out % rows < valid)
+        heads = nn(heads, jnp.where(same, 1.0, 0.0).astype(bf16)).astype(bf16)
+        wide = jnp.concatenate([gain[...], jnp.zeros((shards, half - HD), f32)], axis=1)
+        row = lax.broadcasted_iota(jnp.int32, (shards, rows, half), 1)
+        for side in range(2):
+            total = tn(heads, branch[:, side * half : (side + 1) * half])
+            total = total.reshape(shards, rows, half)
+            if side == 0:
+                total = jnp.where(row == valid, wide[:, None, :], total)
+            at = (2 * layer + side) * rows
+            out_ref[:, at : at + rows] = total.astype(bf16)
 
 
 def expert_grads_kernel(*refs):
@@ -851,38 +877,26 @@
     token_blocks = around_seq(hidden)
     packs = [fetch(expert_part(0) + out_part(dense)), None]
     columns = to_chips(columns)
-    targets = [
-        slot_table(routes[layer, 0], order[layer, 0], expert_count, capacity)
-        for layer in range(LAYERS)
+    pairs = jnp.concatenate(
+        [array[layer, 0].T for array in (routes, order) for layer in range(LAYERS)], axis=0
+    )
+    pairs = swap_seq(jnp.broadcast_to(pairs[None], (seq_count,) + pairs.shape))
+    pairs = pairs.reshape(seq_count, 2, LAYERS, TOPK, tok_count)
+    slots_of = functools.partial(slot_table, expert_count=expert_count, capacity=capacity)
+    all_routes = [pairs[:, 0, layer] for layer in range(LAYERS)]
+    all_targets = [
+        jax.vmap(slots_of)(pairs[:, 0, layer], pairs[:, 1, layer]) for layer in range(LAYERS)
     ]
-    routes_ts = [routes[layer, 0].T for layer in range(LAYERS)]
-    early = (token_blocks, targets, routes_ts, cos_all, sin_all, bias, spread)
+    early = (token_blocks, all_targets, all_routes, cos_all, sin_all, bias, spread)
     columns, early, next_rows = lax.optimization_barrier((columns, early, dense_rows_of(1)))
-    token_blocks, targets, routes_ts, cos_all, sin_all, bias, spread = early
+    token_blocks, all_targets, all_routes, cos_all, sin_all, bias, spread = early
+    targets = [lax.dynamic_index_in_dim(t, seq_index, 0, False) for t in all_targets]
+    routes_ts = [lax.dynamic_index_in_dim(t, seq_index, 0, False) for t in all_routes]
     first_columns = both_cores(columns).reshape(width, columns.shape[2])
     next_dense = spread_seq(next_rows)
-    qkv_at = local_experts * expert_rows + 2 * shard_rows
-    qkv_ws = [None, None]
-    blocks = half_width // local_width
-
-    def query_row(me):
-        return qkv_at + me // blocks * shard_rows
-
-    def query_column(me):
-        return me % blocks * local_width
-
-    def key_column(me):
-        return me * KVHEADS // seq_count * HD
-
-    def value_column(me):
-        return KVHEADS * HD + me * KVHEADS // seq_count * HD
-
-    kv_rows = (1, qkv_at + 2 * shard_rows, shard_rows)
-    own_cuts = {
-        5: ((1, query_row, shard_rows), (2, query_column, local_width)),
-        6: (kv_rows, (2, key_column, HD)),
-        7: (kv_rows, (2, value_column, HD)),
-    }
+    own_at = local_experts * expert_rows + 2 * shard_rows
+    grad_blocks = around_seq(cotangent[0])
+
     heads_shape = shape((seq_count, tok_count, local_width + 2 * HD), bf16)
     attended_shape = shape((seq_count, tok_count, local_width), bf16)
     normed_shape = shape((seq_count, tok_count, width), bf16)
@@ -908,38 +922,44 @@
             heads, attended, normed_all = once(
                 next_attention_kernel,
                 [heads_shape, attended_shape, normed_shape],
-                place, *around_seq(normed_p), pack, pack, pack, cos_all, sin_all, bias,
-                scalar=True, cut=own_cuts, flops=attention_flops,
+                place, *around_seq(normed_p), pack, cos_all, sin_all, bias,
+                scalar=True, cut={5: ((1, own_at, shard_rows),)}, flops=attention_flops,
             )
         back = swap_seq(attended)
         if layer == 0:
-            next_parts = expert_part(1) + out_part(next_dense) + qkv_part(next_dense)
+            next_parts = expert_part(1) + out_part(next_dense) + [own_columns(next_dense)]
             next_parts = jnp.concatenate(next_parts, axis=0)
-            pack, next_parts, back = lax.optimization_barrier((pack, next_parts, back))
+            tied = lax.optimization_barrier((pack, next_parts, back, grad_blocks))
+            pack, next_parts, back, grad_blocks = tied
             packs = [pack, fetch([next_parts])]
-            qkv_ws[1] = (packs[1], qkv_at)
         else:
-            first_parts = jnp.concatenate(qkv_part(dense), axis=0)
-            first_parts, back = lax.optimization_barrier((first_parts, back))
-            qkv_ws[0] = (fetch([first_parts]), 0)
-        middle, normed_ffn, gates_t, send_rows = once(
+            qkv_parts = jnp.concatenate(qkv_part(dense) + qkv_part(next_dense), axis=0)
+            qkv_parts, back = lax.optimization_barrier((qkv_parts, back))
+            qkv_w = fetch([qkv_parts])
+        middle, normed_ffn, gates_t = once(
             after_attention_kernel,
             [
                 shape((tok_count, width), f32),
                 shape((tok_count, width), bf16),
                 shape((2 * TOPK, tok_count), f32),
-                shape((total_slots, width), bf16),
             ],
-            back, spread, hidden, small, pack, routes_t, target_t,
+            back, spread, hidden, small, pack, routes_t,
             cut={4: out_cut}, flops=3 * dense_flops,
         )
-        received = swap_seq(send_rows.reshape(slots_shape.shape))
-        expert_out, gate_val, up_val = once(
+        expert_out, received, gate_val, up_val, all_gates = once(
             expert_kernel,
-            [slots_shape, shape(inner_shape, bf16), shape(inner_shape, bf16)],
-            received, *[pack] * len(weight_parts),
-            cut={n + 1: ((1, *part),) for n, part in enumerate(weight_parts)},
-            pieces={0: (1, local_experts), 1: (0, local_experts), 2: (0, local_experts)},
+            [
+                slots_shape,
+                shape((local_experts, slot_rows, width), bf16),
+                shape(inner_shape, bf16),
+                shape(inner_shape, bf16),
+                shape((seq_count, 2 * TOPK, tok_count), f32),
+            ],
+            place, *around_seq(normed_ffn), all_targets[layer], all_routes[layer], small,
+            *[pack] * len(weight_parts),
+            scalar=True,
+            cut={n + 8: ((1, *part),) for n, part in enumerate(weight_parts)},
+            pieces={n: (1 if n == 0 else 0, local_experts) for n in range(4)},
             flops=expert_flops,
         )
         combined = swap_seq(expert_out).reshape(total_slots, width)
@@ -949,7 +969,7 @@
                 (pack, small, routes_t, target_t),
                 (hidden, normed_all, heads, attended),
                 (middle, normed_ffn, gates_t, combined),
-                (received, gate_val, up_val),
+                (received, gate_val, up_val, all_gates),
             )
         )
     (result,) = once(
@@ -969,34 +989,36 @@
     out_rows = 16
 
     grad_hidden = cotangent[0].astype(f32)
-    sums = [None] * LAYERS
+    sums, gains = [None] * LAYERS, [None] * LAYERS
+    branches, attendeds = [None] * LAYERS, [None] * LAYERS
     waiting = None
     for layer in range(LAYERS - 1, -1, -1):
         weights, attn_saved, mid_saved, expert_saved = records[layer]
         pack, small, routes_t, target_t = weights
-        qkv_w, row = qkv_ws[layer]
+        row = layer * 3 * shard_rows
         below, normed_all, heads, attended = attn_saved
         middle, normed_ffn, gates_t, combined = mid_saved
-        received, gate_val, up_val = expert_saved
-        grad_slots, logits_grad = once(
-            slot_grad_kernel,
-            [shape((total_slots, width), bf16), shape((2 * expert_count, tok_count), bf16)],
+        received, gate_val, up_val, all_gates = expert_saved
+        if waiting is None:
+            tied = lax.optimization_barrier((grad_blocks, qkv_w, result, combined))
+            grad_blocks, qkv_w, result, combined = tied
+        else:
+            grad_blocks, waiting = lax.optimization_barrier((grad_blocks, waiting))
+        grad_rows, grad_expert, gate_grad, up_grad, inner = once(
+            expert_back_kernel,
+            [slots_shape, shape((local_experts, slot_rows, width), bf16)]
+            + [shape(inner_shape, bf16)] * 3,
+            place, *grad_blocks, all_targets[layer], all_gates, pack, gate_val, up_val,
+            *[pack] * (len(back_parts) - 1),
+            scalar=True,
+            cut={n + 9 if n else 7: ((1, *part),) for n, part in enumerate(back_parts)},
+            pieces={n: (1 if n == 0 else 0, local_experts) for n in range(5)},
+            flops=expert_flops,
+        )
+        (logits_grad,) = once(
+            logits_grad_kernel,
+            [shape((2 * expert_count, tok_count), bf16)],
             grad_hidden, combined, gates_t, routes_t, target_t, flops=3 * dense_flops,
-        )
-        grad_expert = swap_seq(grad_slots.reshape(slots_shape.shape))
-        if waiting is None:
-            tied = lax.optimization_barrier((grad_expert, qkv_ws[0][0], result))
-            grad_expert, result = tied[0], tied[2]
-            qkv_ws[0] = (tied[1], 0)
-        else:
-            grad_expert, waiting = lax.optimization_barrier((grad_expert, waiting))
-        grad_rows, gate_grad, up_grad, inner = once(
-            expert_back_kernel,
-            [slots_shape] + [shape(inner_shape, bf16)] * 3,
-            grad_expert, pack, gate_val, up_val, *[pack] * (len(back_parts) - 1),
-            cut={n + 3 if n else 1: ((1, *part),) for n, part in enumerate(back_parts)},
-            pieces={0: (1, local_experts), 1: (0, local_experts), 2: (0, local_experts), 3: (0, local_experts)},
-            flops=expert_flops,
         )
         sent = swap_seq(grad_rows)
         extra = () if layer == LAYERS - 1 else waiting
@@ -1007,7 +1029,7 @@
             received, grad_expert, gate_grad, up_grad, inner, *extra,
             pieces={0: (1, (local_experts * expert_rows + extra_rows) // 16)}, flops=expert_flops,
         )
-        sent, packed = lax.optimization_barrier((sent, packed))
+        sent, packed, logits_grad = lax.optimization_barrier((sent, packed, logits_grad))
         if layer < LAYERS - 1:
             packed, sums[layer + 1] = lax.optimization_barrier((packed, sums[layer + 1]))
         summed = scatter(packed)
@@ -1024,8 +1046,6 @@
             cut={7: out_cut}, flops=4 * dense_flops,
         )
         grad_heads = swap_seq(send)
-        grad_heads, branch = lax.optimization_barrier((grad_heads, branch))
-        branch_all = around_seq(branch)
         (grad_own,) = once(
             attention_back_kernel,
             [shape((seq_count, tok_count, local_width + 2 * HD), bf16)],
@@ -1038,9 +1058,13 @@
             normed_all, grad_own, small_grad, spread, flops=2 * dense_flops,
         )
         sent, qkv_block_grad = lax.optimization_barrier((swap_seq(grad_own), qkv_block_grad))
-        grad_hidden, gain_grad = once(
+        grad_hidden, grad_low, gains[layer] = once(
             before_attention_kernel,
-            [shape((tok_count, width), f32), shape((shard_count, HD), f32)],
+            [
+                shape((tok_count, width), f32),
+                shape((tok_count, width), bf16),
+                shape((shard_count, HD), f32),
+            ],
             sent, qkv_w, qkv_w, qkv_w, spread, small, below, grad_middle,
             cut={
                 1: ((1, row, shard_rows),),
@@ -1049,15 +1073,16 @@
             },
             flops=4 * dense_flops,
         )
-        grad_hidden, branch_all = lax.optimization_barrier((grad_hidden, branch_all))
-        (out_block_grad,) = once(
-            out_weight_kernel,
-            [shape((shard_count, 2 * out_rows, half_width), bf16)],
-            place, *branch_all, attended, gain_grad, scalar=True, flops=dense_flops,
-        )
-        sums[layer] = summed
+        branches[layer], attendeds[layer], sums[layer] = branch, attended, summed
         if layer > 0:
-            waiting = (qkv_block_grad, out_block_grad)
+            grad_blocks = around_seq(grad_low)
+            waiting = (qkv_block_grad,)
+    (out_block_grad,) = once(
+        out_weight_kernel,
+        [shape((shard_count, 2 * LAYERS * out_rows, half_width), bf16)],
+        place, *around_seq(jnp.stack(branches)), *attendeds, *gains,
+        scalar=True, flops=2 * dense_flops,
+    )
 
     def shard_sum(block):
         block = block.reshape((shard_count // 2, 2) + block.shape[1:])
@@ -1068,10 +1093,9 @@
 
     qkv_sum = shard_sum(qkv_block_grad)
     out_sum = shard_sum(out_block_grad)
-    above = sums[0][local_experts * expert_rows :]
-    above_out = above[shard_rows:]
-    own_rows = spread_qkv(qkv_sum, out_sum)
-    above_rows = spread_qkv(above[:shard_rows], above_out)
+    out_sums = [out_sum[2 * out_rows * n : 2 * out_rows * (n + 1)] for n in range(LAYERS)]
+    own_rows = spread_qkv(qkv_sum, out_sums[0])
+    above_rows = spread_qkv(sums[0][local_experts * expert_rows :].astype(f32), out_sums[1])
     gate_grads, up_grads, down_grads = once(
         expert_grads_kernel,
         [
@@ -1091,7 +1115,7 @@
             shape((dense_rows, LAYERS, width), f32),
             shape((LAYERS, dense_rows, HD), f32),
         ],
-        own_rows, above_rows, out_sum, above_out,
+        own_rows, above_rows, *out_sums,
     )
     return (
         result[None],

time: 652 us -> 647 us (level)
  blocking collectives: 105 us -> 35.2 us
  waiting for transfers between devices: 202 us -> 259 us
    all_to_all x5 -> x3, blocking collectives: 105 us -> 35.2 us  [swap_seq(): return lax.all_to_all(block, 'seq', split_axis=0, concat_axis=0, tiled=True)]
    ppermute x12 -> x21, waiting for transfers between devices: 36.1 us -> 93.4 us  [around_seq(): lax.ppermute(block, 'seq', [((i + k) % count, i) for i in range(count)])]
    all_to_all x13 -> x12, starting transfers between devices: 58.5 us -> 51.6 us  [swap_seq(): return lax.all_to_all(block, 'seq', split_axis=0, concat_axis=0, tiled=True)]
    all_gather x3, waiting for transfers between devices: 6.67 us -> 0.02 us  [fetch(): lax.all_gather(jnp.concatenate(parts, axis=0), 'fsdp', axis=0, tiled=False)]
    ppermute x12 -> x21, starting transfers between devices: 15.2 us -> 21.8 us  [around_seq(): lax.ppermute(block, 'seq', [((i + k) % count, i) for i in range(count)])]
    all_to_all x13 -> x12, waiting for transfers between devices: 106 us -> 111 us  [swap_seq(): return lax.all_to_all(block, 'seq', split_axis=0, concat_axis=0, tiled=True)]
    pallas_call x26 -> x25, Pallas kernels: 181 us -> 178 us  [once(): pl.pallas_call(body, out_shape=list(outs), in_specs=specs, out_specs=[hbm...]
  transfers between devices with their start and end apart: 36 -> 44, of which waited for: 26 -> 31; matrix products, arithmetic and copies ran while one was open for 6% -> 7% of each run, Pallas kernels for 25% -> 24%
where the time goes in v3:
time: 647 us; the launch traced here: 639 us
  waiting for transfers between devices  259 us (40%)
  Pallas kernels  178 us (28%)
  starting transfers between devices  90.2 us (14%)
  blocking collectives  35.2 us (5%)
  local copies, waits for them, and re-layouts  35.1 us (5%)
  other arithmetic  26.8 us (4%)
  between operations  15.2 us (2%)
    pallas_call x25, Pallas kernels, once(): pl.pallas_call(body, out_shape=list(outs), in_specs=specs, out_specs=[hbm...  178 us
    all_to_all x12, waiting for transfers between devices, swap_seq(): return lax.all_to_all(block, 'seq', split_axis=0, concat_axis=0, tiled=True)  111 us
    ppermute x21, waiting for transfers between devices, around_seq(): lax.ppermute(block, 'seq', [((i + k) % count, i) for i in range(count)])  93.4 us
    all_to_all x12, starting transfers between devices, swap_seq(): return lax.all_to_all(block, 'seq', split_axis=0, concat_axis=0, tiled=True)  51.6 us
    all_to_all x3, waiting for transfers between devices, swap_chips(): lax.all_to_all(block, 'fsdp', split_axis=0, concat_axis=0, tiled=True, ax...  50.2 us
    all_to_all x3, blocking collectives, swap_seq(): return lax.all_to_all(block, 'seq', split_axis=0, concat_axis=0, tiled=True)  35.2 us
    ppermute x21, starting transfers between devices, around_seq(): lax.ppermute(block, 'seq', [((i + k) % count, i) for i in range(count)])  21.8 us
    all_to_all x3, starting transfers between devices, swap_chips(): lax.all_to_all(block, 'fsdp', split_axis=0, concat_axis=0, tiled=True, ax...  15.8 us
  transfers between devices with their start and end apart: 44, of which 31 were waited for; matrix products, arithmetic and copies ran while one was open for 7% of the time, Pallas kernels for 24%

profile of v3, /device:TPU:0, one launch (start us, length us, event | category | flops | bytes accessed | tf_op | source)
XLA Modules:
  0.0 639.2 jit_solution(13664804523112445328)
XLA Ops:
  57.8 7.7 %collective-permute-done.refs_2_ = bf16[128,1536]{1,0:T(8,128)(2,1)S(1)} collective-permute-done((bf16[128,1536]{1,0:T(8,128)(2,1)S(1)}, bf16[128,1536]{1,0:T(8,128)(2,1)S(1)}, u32[]{:S(2)}, u32[]{:S(2)}) %collective-permute-start) | collective-permute-done | bytes 393248 | tf_op jit(solution)/shard_map/ppermute | solution.py:720
  84.0 16.2 %all-to-all-done.3 = bf16[4,12,3712]{2,1,0:T(8,128)(2,1)S(1)} async-done(((bf16[4,12,3712]{2,1,0:T(8,128)(2,1)}), bf16[4,12,3712]{2,1,0:T(8,128)(2,1)S(1)}, u32[]{:S(2)}, u32[]{:S(2)}) %all-to-all-start.3) | async-done | bytes 356384 | tf_op jit(solution)/shard_map/all_to_all | solution.py:714
  105.2 11.2 %shard_map.238 = (bf16[4,128,640]{2,1,0:T(8,128)(2,1)}, bf16[4,128,384]{2,1,0:T(8,128)(2,1)}, bf16[4,128,1536]{2,1,0:T(8,128)(2,1)}, bf16[2,16,1536]{2,1,0:T(8,128)(2,1)}) custom-call(s32[1]{0:T(128)} %bitcast.42.refs_0_, bf16[128,1536]{1,0:T(8,128)(2,1)} %bitcast.204, bf16[128,1536]{1,0:T(8,128)(2,1)} %copy-done.16, ...), custom_call_target="tpu_custom_call" | custom-call | flops 4026531840 | bytes 8912900 | tf_op jit(solution)/shard_map/pallas_call | solution.py:158
  138.5 9.3 %collective-permute-done.7.refs_2_ = bf16[128,1536]{1,0:T(8,128)(2,1)} collective-permute-done((bf16[128,1536]{1,0:T(8,128)(2,1)}, bf16[128,1536]{1,0:T(8,128)(2,1)}, u32[]{:S(2)}, u32[]{:S(2)}) %collective-permute-start.7) | collective-permute-done | bytes 393248 | tf_op jit(solution)/shard_map/ppermute | solution.py:720
  155.8 10.1 %shard_map.240 = (bf16[4,2,72,1536]{3,2,1,0:T(8,128)(2,1)}, bf16[2,288,1536]{2,1,0:T(8,128)(2,1)}, bf16[2,288,768]{2,1,0:T(8,128)(2,1)}, bf16[2,288,768]{2,1,0:T(8,128)(2,1)}, f32[4,8,128]{2,1,0:T(8,128)}) custom-call(s32[1]{0:T(128)} %bitcast.42.refs_0_, bf16[128,1536]{1,0:T(8,128)(2,1)} %get-tuple-element.139.refs_1_.refs_3_, ...), custom_call_target="tpu_custom_call" | custom-call | flops 4076863488 | bytes 120209408 | tf_op jit(solution)/shard_map/pallas_call | solution.py:158
  171.6 22.1 %all-to-all-done.5 = bf16[4,2,72,1536]{3,2,1,0:T(8,128)(2,1)} async-done(((bf16[4,2,72,1536]{3,2,1,0:T(8,128)(2,1)}), bf16[4,2,72,1536]{3,2,1,0:T(8,128)(2,1)}, u32[]{:S(2)}, u32[]{:S(2)}) %all-to-all-start.5) | async-done | bytes 1769504 | tf_op jit(solution)/shard_map/all_to_all | solution.py:714
  200.6 9.7 %collective-permute-done.10.refs_2_ = bf16[128,1536]{1,0:T(8,128)(2,1)} collective-permute-done((bf16[128,1536]{1,0:T(8,128)(2,1)}, bf16[128,1536]{1,0:T(8,128)(2,1)}, u32[]{:S(2)}, u32[]{:S(2)}) %collective-permute-start.10) | collective-permute-done | bytes 393248 | tf_op jit(solution)/shard_map/ppermute | solution.py:720
  247.9 9.7 %collective-permute-done.13.refs_2_ = bf16[128,1536]{1,0:T(8,128)(2,1)} collective-permute-done((bf16[128,1536]{1,0:T(8,128)(2,1)}, bf16[128,1536]{1,0:T(8,128)(2,1)}, u32[]{:S(2)}, u32[]{:S(2)}) %collective-permute-start.13) | collective-permute-done | bytes 393248 | tf_op jit(solution)/shard_map/ppermute | solution.py:720
  266.6 10.1 %shard_map.244 = (bf16[4,2,72,1536]{3,2,1,0:T(8,128)(2,1)}, bf16[2,288,1536]{2,1,0:T(8,128)(2,1)}, bf16[2,288,768]{2,1,0:T(8,128)(2,1)}, bf16[2,288,768]{2,1,0:T(8,128)(2,1)}, f32[4,8,128]{2,1,0:T(8,128)}) custom-call(s32[1]{0:T(128)} %bitcast.42.refs_0_, bf16[128,1536]{1,0:T(8,128)(2,1)} %get-tuple-element.151.refs_1_.refs_3_, ...), custom_call_target="tpu_custom_call" | custom-call | flops 4076863488 | bytes 134365184 | tf_op jit(solution)/shard_map/pallas_call | solution.py:158
  282.6 22.1 %all-to-all-done.7 = bf16[4,2,72,1536]{3,2,1,0:T(8,128)(2,1)} async-done(((bf16[4,2,72,1536]{3,2,1,0:T(8,128)(2,1)}), bf16[4,2,72,1536]{3,2,1,0:T(8,128)(2,1)}, u32[]{:S(2)}, u32[]{:S(2)}) %all-to-all-start.7) | async-done | bytes 1769504 | tf_op jit(solution)/shard_map/all_to_all | solution.py:714
  308.3 12.4 %shard_map.246 = (bf16[4,2,72,1536]{3,2,1,0:T(8,128)(2,1)}, bf16[2,288,1536]{2,1,0:T(8,128)(2,1)}, bf16[2,288,768]{2,1,0:T(8,128)(2,1)}, bf16[2,288,768]{2,1,0:T(8,128)(2,1)}, bf16[2,288,768]{2,1,0:T(8,128)(2,1)}) custom-call(s32[1]{0:T(128)} %bitcast.42.refs_0_, bf16[128,1536]{1,0:T(8,128)(2,1)} %bitcast.47.refs_1_, ...), custom_call_target="tpu_custom_call" | custom-call | flops 4076863488 | bytes 136962048 | tf_op jit(solution)/shard_map/pallas_call | solution.py:158
  330.7 12.2 %shard_map.247 = bf16[32,288,768]{2,1,0:T(8,128)(2,1)} custom-call(bf16[2,288,1536]{2,1,0:T(8,128)(2,1)} %get-tuple-element.166.refs_0_, bf16[2,288,1536]{2,1,0:T(8,128)(2,1)} %get-tuple-element.167.refs_1_, bf16[2,288,768]{2,1,0:T(8,128)(2,1)} %get-tuple-element.168.refs_2_, bf16[2,288,768]{2,1,0:T(8,128)(2,1)} %get-tuple-element.169.refs_3_, ...), custom_call_target="tpu_custom_call" | custom-call | flops 4076863488 | bytes 20348928 | tf_op jit(solution)/shard_map/pallas_call | solution.py:158
  354.3 12.0 %all_to_all.90.refs_1_ = bf16[4,128,384]{2,1,0:T(8,128)(2,1)} all-to-all(bf16[4,128,384]{2,1,0:T(8,128)(2,1)} %get-tuple-element.174), channel_id=1, replica_groups=mesh['seq'=4,'fsdp'=32] {'seq'}, dimensions={0} | all-to-all | bytes 786432 | tf_op jit(solution)/shard_map/all_to_all | solution.py:714
  386.3 8.0 %shard_map.252 = (f32[128,1536]{1,0:T(8,128)}, bf16[128,1536]{1,0:T(8,128)(2,1)}, f32[32,128]{1,0:T(8,128)}) custom-call(bf16[4,128,640]{2,1,0:T(8,128)(2,1)} %all-to-all-done.10.refs_0_, bf16[32,288,768]{2,1,0:T(8,128)(2,1)} %bitcast.193, bf16[32,288,768]{2,1,0:T(8,128)(2,1)} %bitcast.194, bf16[32,288,768]{2,1,0:T(8,128)(2,1)} %bitcast.195, ...), custom_call_target="tpu_custom_call" | custom-call | flops 2415919104 | bytes 46235648 | tf_op jit(solution)/shard_map/pallas_call | solution.py:158
  397.3 8.8 %collective-permute-done.16.refs_2_ = bf16[128,1536]{1,0:T(8,128)(2,1)} collective-permute-done((bf16[128,1536]{1,0:T(8,128)(2,1)}, bf16[128,1536]{1,0:T(8,128)(2,1)}, u32[]{:S(2)}, u32[]{:S(2)}) %collective-permute-start.16) | collective-permute-done | bytes 393248 | tf_op jit(solution)/shard_map/ppermute | solution.py:720
  412.8 12.4 %shard_map.253 = (bf16[4,2,72,1536]{3,2,1,0:T(8,128)(2,1)}, bf16[2,288,1536]{2,1,0:T(8,128)(2,1)}, bf16[2,288,768]{2,1,0:T(8,128)(2,1)}, bf16[2,288,768]{2,1,0:T(8,128)(2,1)}, bf16[2,288,768]{2,1,0:T(8,128)(2,1)}) custom-call(s32[1]{0:T(128)} %bitcast.42.refs_0_, bf16[128,1536]{1,0:T(8,128)(2,1)} %get-tuple-element.183.refs_1_, ...), custom_call_target="tpu_custom_call" | custom-call | flops 4076863488 | bytes 122806272 | tf_op jit(solution)/shard_map/pallas_call | solution.py:158
  433.2 12.9 %shard_map.254 = bf16[32,336,768]{2,1,0:T(8,128)(2,1)} custom-call(bf16[2,288,1536]{2,1,0:T(8,128)(2,1)} %get-tuple-element.191.refs_0_, bf16[2,288,1536]{2,1,0:T(8,128)(2,1)} %get-tuple-element.192.refs_1_, bf16[2,288,768]{2,1,0:T(8,128)(2,1)} %get-tuple-element.193.refs_2_, bf16[2,288,768]{2,1,0:T(8,128)(2,1)} %get-tuple-element.194.refs_3_, ...), custom_call_target="tpu_custom_call" | custom-call | flops 4076863488 | bytes 25067520 | tf_op jit(solution)/shard_map/pallas_call | solution.py:158
  461.9 12.2 %all_to_all.91.refs_1_ = bf16[4,128,384]{2,1,0:T(8,128)(2,1)} all-to-all(bf16[4,128,384]{2,1,0:T(8,128)(2,1)} %get-tuple-element.199), channel_id=1, replica_groups=mesh['seq'=4,'fsdp'=32] {'seq'}, dimensions={0} | all-to-all | bytes 786432 | tf_op jit(solution)/shard_map/all_to_all | solution.py:714
  497.7 11.1 %all-to-all-done.13.refs_0_ = bf16[4,128,640]{2,1,0:T(8,128)(2,1)} async-done(((bf16[4,128,640]{2,1,0:T(8,128)(2,1)}), bf16[4,128,640]{2,1,0:T(8,128)(2,1)}, u32[]{:S(2)}, u32[]{:S(2)}) %all-to-all-start.13) | async-done | bytes 655392 | tf_op jit(solution)/shard_map/all_to_all | solution.py:714
  511.5 8.0 %shard_map.259 = (f32[128,1536]{1,0:T(8,128)}, bf16[128,1536]{1,0:T(8,128)(2,1)}, f32[32,128]{1,0:T(8,128)}) custom-call(bf16[4,128,640]{2,1,0:T(8,128)(2,1)} %all-to-all-done.13.refs_0_, bf16[32,288,768]{2,1,0:T(8,128)(2,1)} %bitcast.196, bf16[32,288,768]{2,1,0:T(8,128)(2,1)} %bitcast.197, bf16[32,288,768]{2,1,0:T(8,128)(2,1)} %bitcast.198, ...), custom_call_target="tpu_custom_call" | custom-call | flops 2415919104 | bytes 45842432 | tf_op jit(solution)/shard_map/pallas_call | solution.py:158
  519.5 8.2 %collective-permute-done.21.refs_4_ = bf16[2,128,1536]{2,1,0:T(8,128)(2,1)} collective-permute-done((bf16[2,128,1536]{2,1,0:T(8,128)(2,1)}, bf16[2,128,1536]{2,1,0:T(8,128)(2,1)}, u32[]{:S(2)}, u32[]{:S(2)}) %collective-permute-start.21) | collective-permute-done | bytes 786464 | tf_op jit(solution)/shard_map/ppermute | solution.py:720
  548.6 19.1 %all-to-all-done.15 = bf16[16,48,768]{2,1,0:T(8,128)(2,1)} async-done(((bf16[16,48,768]{2,1,0:T(8,128)(2,1)}), bf16[16,48,768]{2,1,0:T(8,128)(2,1)}, u32[]{:S(2)}, u32[]{:S(2)}) %all-to-all-start.15) | async-done | bytes 1179680 | tf_op jit(solution)/shard_map/all_to_all | solution.py:845
  572.9 31.0 %all-to-all-done.14 = bf16[16,64,768]{2,1,0:T(8,128)(2,1)S(1)} async-done(((bf16[16,64,768]{2,1,0:T(8,128)(2,1)}), bf16[16,64,768]{2,1,0:T(8,128)(2,1)S(1)}, u32[]{:S(2)}, u32[]{:S(2)}) %all-to-all-start.14) | async-done | bytes 1572896 | tf_op jit(solution)/shard_map/all_to_all | solution.py:845
  606.0 11.0 %all_to_all.92.refs_0_ = f32[4,12,768]{2,1,0:T(8,128)} all-to-all(f32[4,12,768]{2,1,0:T(8,128)S(1)} %get-tuple-element.317), channel_id=1, replica_groups=mesh['seq'=4,'fsdp'=32] {'seq'}, dimensions={0} | all-to-all | bytes 294912 | tf_op jit(solution)/shard_map/all_to_all | solution.py:714
  (239 shorter events, 316.4 us)
Async XLA Ops:
  20.2 108.4 %all-gather.7.cloned.1.call-start = ((), (), s32[]{:S(2)}) async-start(), calls=%async_computation.22 | async-start | bytes 19464192 | tf_op jit(solution)/shard_map/all_gather | solution.py:839
  40.8 31.9 %all-to-all-start.1 = ((bf16[16,48,896]{2,1,0:T(8,128)(2,1)}), bf16[16,48,896]{2,1,0:T(8,128)(2,1)S(1)}, u32[]{:S(2)}, u32[]{:S(2)}) async-start(bf16[16,48,896]{2,1,0:T(8,128)(2,1)} %broadcast_in_dim.91), calls=%async_computation.1 | async-start | bytes 2752512 | tf_op jit(solution)/shard_map/all_to_all | solution.py:845
  72.8 28.9 %collective-permute-start.3 = (bf16[16,48,896]{2,1,0:T(8,128)(2,1)S(1)}, bf16[16,48,896]{2,1,0:T(8,128)(2,1)}, u32[]{:S(2)}, u32[]{:S(2)}) collective-permute-start(bf16[16,48,896]{2,1,0:T(8,128)(2,1)S(1)} %all-to-all-done.1), channel_id=1, source_target_pairs={{0,1},{1,0},{2,3},{3,2},{4,5},{5,4},{6,7},{7,6},{8,9},{9,8},{10,11... | collective-permute-start | bytes 4128776 | tf_op jit(solution)/shard_map/ppermute | solution.py:850
  72.8 49.3 %collective-permute-start.4 = (bf16[128,1536]{1,0:T(8,128)(2,1)}, bf16[128,1536]{1,0:T(8,128)(2,1)}, u32[]{:S(2)}, u32[]{:S(2)}) collective-permute-start(bf16[128,1536]{1,0:T(8,128)(2,1)} %bitcast.47.refs_1_), channel_id=1, source_target_pairs={{32,0},{64,32},{96,64},{0,96},{33,1},{65,33},{97,65},{1,97},{34,2}... | collective-permute-start | bytes 1179656 | tf_op jit(solution)/shard_map/ppermute | solution.py:720
  73.7 48.4 %collective-permute-start.5 = (bf16[128,1536]{1,0:T(8,128)(2,1)}, bf16[128,1536]{1,0:T(8,128)(2,1)}, u32[]{:S(2)}, u32[]{:S(2)}) collective-permute-start(bf16[128,1536]{1,0:T(8,128)(2,1)} %bitcast.47.refs_1_), channel_id=1, source_target_pairs={{64,0},{96,32},{0,64},{32,96},{65,1},{97,33},{1,65},{33,97},{66,2}... | collective-permute-start | bytes 1179656 | tf_op jit(solution)/shard_map/ppermute | solution.py:720
  74.4 47.7 %collective-permute-start.6 = (bf16[128,1536]{1,0:T(8,128)(2,1)}, bf16[128,1536]{1,0:T(8,128)(2,1)}, u32[]{:S(2)}, u32[]{:S(2)}) collective-permute-start(bf16[128,1536]{1,0:T(8,128)(2,1)} %bitcast.47.refs_1_), channel_id=1, source_target_pairs={{96,0},{0,32},{32,64},{64,96},{97,1},{1,33},{33,65},{65,97},{98,2}... | collective-permute-start | bytes 1179656 | tf_op jit(solution)/shard_map/ppermute | solution.py:720
  77.7 22.5 %all-to-all-start.3 = ((bf16[4,12,3712]{2,1,0:T(8,128)(2,1)}), bf16[4,12,3712]{2,1,0:T(8,128)(2,1)S(1)}, u32[]{:S(2)}, u32[]{:S(2)}) async-start(bf16[4,12,3712]{2,1,0:T(8,128)(2,1)} %broadcast_in_dim.96), calls=%async_computation.3 | async-start | bytes 950272 | tf_op jit(solution)/shard_map/all_to_all | solution.py:714
  120.7 98.7 %all-gather.9.cloned.1.call-start = ((), (), s32[]{:S(2)}) async-start(), calls=%async_computation.23 | async-start | bytes 21897216 | tf_op jit(solution)/shard_map/all_gather | solution.py:839
  165.9 27.8 %all-to-all-start.5 = ((bf16[4,2,72,1536]{3,2,1,0:T(8,128)(2,1)}), bf16[4,2,72,1536]{3,2,1,0:T(8,128)(2,1)}, u32[]{:S(2)}, u32[]{:S(2)}) async-start(bf16[4,2,72,1536]{3,2,1,0:T(8,128)(2,1)} %get-tuple-element.141), calls=%async_computation.5 | async-start | bytes 3538944 | tf_op jit(solution)/shard_map/all_to_all | solution.py:714
  200.6 18.8 %collective-permute-start.12 = (bf16[128,1536]{1,0:T(8,128)(2,1)}, bf16[128,1536]{1,0:T(8,128)(2,1)}, u32[]{:S(2)}, u32[]{:S(2)}) collective-permute-start(bf16[128,1536]{1,0:T(8,128)(2,1)} %get-tuple-element.143.refs_1_), channel_id=1, source_target_pairs={{96,0},{0,32},{32,64},{64,96},{97,1},{1,33},{33,65},{65,97},{98,2}... | collective-permute-start | bytes 1179656 | tf_op jit(solution)/shard_map/ppermute | solution.py:720
  231.1 77.2 %all-gather.11.cloned.1.call-start = ((), (), s32[]{:S(2)}) async-start(), calls=%async_computation.24 | async-start | bytes 14598144 | tf_op jit(solution)/shard_map/all_gather | solution.py:839
  247.9 18.7 %collective-permute-start.15 = (bf16[128,1536]{1,0:T(8,128)(2,1)}, bf16[128,1536]{1,0:T(8,128)(2,1)}, u32[]{:S(2)}, u32[]{:S(2)}) collective-permute-start(bf16[128,1536]{1,0:T(8,128)(2,1)} %get-tuple-element.151.refs_1_.refs_3_), channel_id=1, source_target_pairs={{96,0},{0,32},{32,64},{64,96},{97,1},{1,33},{33,65},{65,97},{98,2}... | collective-permute-start | bytes 1179656 | tf_op jit(solution)/shard_map/ppermute | solution.py:720
  276.8 27.9 %all-to-all-start.7 = ((bf16[4,2,72,1536]{3,2,1,0:T(8,128)(2,1)}), bf16[4,2,72,1536]{3,2,1,0:T(8,128)(2,1)}, u32[]{:S(2)}, u32[]{:S(2)}) async-start(bf16[4,2,72,1536]{3,2,1,0:T(8,128)(2,1)} %get-tuple-element.153), calls=%async_computation.7 | async-start | bytes 3538944 | tf_op jit(solution)/shard_map/all_to_all | solution.py:714
  320.7 26.9 %all-to-all-start.8 = ((bf16[4,2,72,1536]{3,2,1,0:T(8,128)(2,1)}), bf16[4,2,72,1536]{3,2,1,0:T(8,128)(2,1)}, u32[]{:S(2)}, u32[]{:S(2)}) async-start(bf16[4,2,72,1536]{3,2,1,0:T(8,128)(2,1)} %get-tuple-element.165), calls=%async_computation.8 | async-start | bytes 3538944 | tf_op jit(solution)/shard_map/all_to_all | solution.py:714
  325.2 130.1 %reduce-scatter.3.cloned.1.call-start = ((), (), s32[]{:S(2)}) async-start(), calls=%async_computation.20 | async-start | bytes 14598144 | tf_op jit(solution)/shard_map/reduce_scatter | solution.py:981
  425.2 26.2 %all-to-all-start.11 = ((bf16[4,2,72,1536]{3,2,1,0:T(8,128)(2,1)}), bf16[4,2,72,1536]{3,2,1,0:T(8,128)(2,1)}, u32[]{:S(2)}, u32[]{:S(2)}) async-start(bf16[4,2,72,1536]{3,2,1,0:T(8,128)(2,1)} %get-tuple-element.190), calls=%async_computation.11 | async-start | bytes 3538944 | tf_op jit(solution)/shard_map/all_to_all | solution.py:714
  429.6 174.8 %reduce-scatter.5.cloned.1.call-start = ((), (), s32[]{:S(2)}) async-start(), calls=%async_computation.21 | async-start | bytes 17031168 | tf_op jit(solution)/shard_map/reduce_scatter | solution.py:981
  481.0 27.8 %all-to-all-start.13 = ((bf16[4,128,640]{2,1,0:T(8,128)(2,1)}), bf16[4,128,640]{2,1,0:T(8,128)(2,1)}, u32[]{:S(2)}, u32[]{:S(2)}) async-start(bf16[4,128,640]{2,1,0:T(8,128)(2,1)} %shard_map.257.refs_1_), calls=%async_computation.13 | async-start | bytes 1310720 | tf_op jit(solution)/shard_map/all_to_all | solution.py:714
  487.4 32.1 %collective-permute-start.19 = (bf16[2,128,1536]{2,1,0:T(8,128)(2,1)}, bf16[2,128,1536]{2,1,0:T(8,128)(2,1)}, u32[]{:S(2)}, u32[]{:S(2)}) collective-permute-start(bf16[2,128,1536]{2,1,0:T(8,128)(2,1)} %pad_maximum_fusion.1.refs_1_), channel_id=1, source_target_pairs={{32,0},{64,32},{96,64},{0,96},{33,1},{65,33},{97,65},{1,97},{34,2}... | collective-permute-start | bytes 2359304 | tf_op jit(solution)/shard_map/ppermute | solution.py:720
  490.6 28.9 %collective-permute-start.20 = (bf16[2,128,1536]{2,1,0:T(8,128)(2,1)}, bf16[2,128,1536]{2,1,0:T(8,128)(2,1)}, u32[]{:S(2)}, u32[]{:S(2)}) collective-permute-start(bf16[2,128,1536]{2,1,0:T(8,128)(2,1)} %pad_maximum_fusion.1.refs_1_), channel_id=1, source_target_pairs={{64,0},{96,32},{0,64},{32,96},{65,1},{97,33},{1,65},{33,97},{66,2}... | collective-permute-start | bytes 2359304 | tf_op jit(solution)/shard_map/ppermute | solution.py:720
  491.4 36.3 %collective-permute-start.21 = (bf16[2,128,1536]{2,1,0:T(8,128)(2,1)}, bf16[2,128,1536]{2,1,0:T(8,128)(2,1)}, u32[]{:S(2)}, u32[]{:S(2)}) collective-permute-start(bf16[2,128,1536]{2,1,0:T(8,128)(2,1)} %pad_maximum_fusion.1.refs_1_), channel_id=1, source_target_pairs={{96,0},{0,32},{32,64},{64,96},{97,1},{1,33},{33,65},{65,97},{98,2}... | collective-permute-start | bytes 2359304 | tf_op jit(solution)/shard_map/ppermute | solution.py:720
  511.2 26.1 %collective-permute-start.23 = (bf16[16,48,768]{2,1,0:T(8,128)(2,1)}, bf16[16,48,768]{2,1,0:T(8,128)(2,1)}, u32[]{:S(2)}, u32[]{:S(2)}) collective-permute-start(bf16[16,48,768]{2,1,0:T(8,128)(2,1)} %dynamic-slice_bitcast_fusion.1), channel_id=1, source_target_pairs={{0,1},{1,0},{2,3},{3,2},{4,5},{5,4},{6,7},{7,6},{8,9},{9,8},{10,11... | collective-permute-start | bytes 3538952 | tf_op jit(solution)/shard_map/ppermute | solution.py:850
  540.4 27.3 %all-to-all-start.15 = ((bf16[16,48,768]{2,1,0:T(8,128)(2,1)}), bf16[16,48,768]{2,1,0:T(8,128)(2,1)}, u32[]{:S(2)}, u32[]{:S(2)}) async-start(bf16[16,48,768]{2,1,0:T(8,128)(2,1)} %fusion.1), calls=%async_computation.15 | async-start | bytes 2359296 | tf_op jit(solution)/shard_map/all_to_all | solution.py:845
  567.7 36.3 %all-to-all-start.14 = ((bf16[16,64,768]{2,1,0:T(8,128)(2,1)}), bf16[16,64,768]{2,1,0:T(8,128)(2,1)S(1)}, u32[]{:S(2)}, u32[]{:S(2)}) async-start(bf16[16,64,768]{2,1,0:T(8,128)(2,1)} %fusion), calls=%async_computation.14 | async-start | bytes 3145728 | tf_op jit(solution)/shard_map/all_to_all | solution.py:845
  (37 other events, 665.5 us)
Sparse Core Ops, SparseCore 0:
  30.4 89.7 all-gather.6
  128.7 81.7 all-gather.8
  239.8 65.4 all-gather.10
  347.8 107.4 reduce-scatter.2
  459.6 143.2 reduce-scatter.4

commit v4 on v3

--- a/solution.py
+++ b/solution.py
@@ -483,33 +483,49 @@
         out_ref.send(e)
 
 
-def expert_weight_kernel(rows_ref, grad_ref, gate_grad_ref, up_grad_ref, inner_ref, *rest):
-    pack_ref = rest[-1]
+def expert_weight_kernel(rows_ref, grad_ref, gate_grad_ref, up_grad_ref, inner_ref, pack_ref):
+    weight_grads(rows_ref, grad_ref, gate_grad_ref, up_grad_ref, inner_ref, (pack_ref,), None)
+
+
+def expert_weight_apart_kernel(
+    core, rows_ref, grad_ref, gate_grad_ref, up_grad_ref, inner_ref, extra, own_ref, other_ref
+):
+    outs = (own_ref, other_ref)
+    at = weight_grads(rows_ref, grad_ref, gate_grad_ref, up_grad_ref, inner_ref, outs, core[0])
+    keep_shards(outs, core[0], at, extra[...])
+
+
+def keep_shards(outs, core, at, value):
+    shards, rows, half = value.shape
+    if core is None:
+        outs[0][:, at : at + rows] = value
+    else:
+        value = value.reshape(shards // 2, 2, rows, half)
+        outs[0][:, at : at + rows] = jnp.where(core == 0, value[:, 0], value[:, 1])
+        outs[1][:, at : at + rows] = jnp.where(core == 0, value[:, 1], value[:, 0])
+    for out in outs:
+        for piece in range(at // 16, (at + rows) // 16):
+            out.send(piece)
+
+
+def weight_grads(rows_ref, grad_ref, gate_grad_ref, up_grad_ref, inner_ref, outs, core):
     experts, _, width = rows_ref.shape
-    shards, _, half = pack_ref.shape
+    half = outs[0].shape[2]
+    shards = outs[0].shape[0] * len(outs)
     rows = width // shards
     at = 0
-
-    def send(start, count):
-        for piece in range(start // 16, (start + count) // 16):
-            pack_ref.send(piece)
-
     for e in range(experts):
         grads = jnp.concatenate([gate_grad_ref[e], up_grad_ref[e]], axis=1)
         both = tn(rows_ref[e], grads).astype(bf16)
-        pack_ref[:, at : at + rows] = both[:, :half].reshape(shards, rows, half)
-        pack_ref[:, at + rows : at + 2 * rows] = both[:, half:].reshape(shards, rows, half)
-        send(at, 2 * rows)
+        keep_shards(outs, core, at, both[:, :half].reshape(shards, rows, half))
+        keep_shards(outs, core, at + rows, both[:, half:].reshape(shards, rows, half))
         down = tn(inner_ref[e], grad_ref[e])
         left = down[:, :half].reshape(shards, rows // 2, half)
         right = down[:, half:].reshape(shards, rows // 2, half)
         down = jnp.concatenate([left, right], axis=1).astype(bf16)
-        pack_ref[:, at + 2 * rows : at + 3 * rows] = down
-        send(at + 2 * rows, rows)
+        keep_shards(outs, core, at + 2 * rows, down)
         at += 3 * rows
-    for extra in rest[:-1]:
-        pack_ref[:, at : at + extra.shape[1]] = extra[...]
-        at += extra.shape[1]
+    return at
 
 
 def after_experts_kernel(
@@ -644,16 +660,19 @@
     out_ref[:, :, columns:] = extra.astype(bf16).reshape(shards, rows, wide - columns)
 
 
-def out_weight_kernel(place, own, one, two, three, *rest):
+def out_weight_kernel(place, *rest):
     out_ref = rest[-1]
     me = place[0]
+    around = len(rest) // LAYERS - 2
+    blocks, rest = rest[: LAYERS * around], rest[LAYERS * around :]
     shards, rows, half = out_ref.shape
     rows = rows // (2 * LAYERS)
     for layer in range(LAYERS):
         attended, gain = rest[layer], rest[LAYERS + layer]
         seq_count, tokens, part = attended.shape
         valid = part // shards
-        branch = jnp.concatenate([block[layer] for block in (own, one, two, three)], axis=0)
+        branch = [block[...] for block in blocks[layer * around : (layer + 1) * around]]
+        branch = jnp.concatenate(branch, axis=0)
         heads = jnp.concatenate(
             [attended[lax.rem(me + k, seq_count)] for k in range(seq_count)], axis=0
         )
@@ -751,6 +770,7 @@
     shard_count = lax.axis_size("fsdp")
     seq_index = lax.axis_index("seq")
     place = jnp.full((1,), seq_index, jnp.int32)
+    core_place = jnp.full((1,), lax.rem(lax.axis_index("fsdp"), 2), jnp.int32)
     group_tok = seq_count * tok_count
     prompt_len = group_tok - segment_ids.shape[1]
     local_experts = w_gate.shape[1]
@@ -887,16 +907,15 @@
     all_targets = [
         jax.vmap(slots_of)(pairs[:, 0, layer], pairs[:, 1, layer]) for layer in range(LAYERS)
     ]
-    early = (token_blocks, all_targets, all_routes, cos_all, sin_all, bias, spread)
-    columns, early, next_rows = lax.optimization_barrier((columns, early, dense_rows_of(1)))
-    token_blocks, all_targets, all_routes, cos_all, sin_all, bias, spread = early
     targets = [lax.dynamic_index_in_dim(t, seq_index, 0, False) for t in all_targets]
     routes_ts = [lax.dynamic_index_in_dim(t, seq_index, 0, False) for t in all_routes]
+    early = (token_blocks, all_targets, all_routes, targets, routes_ts)
+    columns, early = lax.optimization_barrier((columns, early + (cos_all, sin_all, bias, spread)))
+    token_blocks, all_targets, all_routes, targets, routes_ts, cos_all, sin_all, bias, spread = early
     first_columns = both_cores(columns).reshape(width, columns.shape[2])
-    next_dense = spread_seq(next_rows)
+    first_columns, grad_rows = lax.optimization_barrier((first_columns, cotangent[0]))
+    grad_blocks = around_seq(grad_rows)
     own_at = local_experts * expert_rows + 2 * shard_rows
-    grad_blocks = around_seq(cotangent[0])
-
     heads_shape = shape((seq_count, tok_count, local_width + 2 * HD), bf16)
     attended_shape = shape((seq_count, tok_count, local_width), bf16)
     normed_shape = shape((seq_count, tok_count, width), bf16)
@@ -925,14 +944,17 @@
                 place, *around_seq(normed_p), pack, cos_all, sin_all, bias,
                 scalar=True, cut={5: ((1, own_at, shard_rows),)}, flops=attention_flops,
             )
-        back = swap_seq(attended)
         if layer == 0:
+            attended, next_rows = lax.optimization_barrier((attended, dense_rows_of(1)))
+            back = swap_seq(attended)
+            next_dense = spread_seq(next_rows)
             next_parts = expert_part(1) + out_part(next_dense) + [own_columns(next_dense)]
             next_parts = jnp.concatenate(next_parts, axis=0)
             tied = lax.optimization_barrier((pack, next_parts, back, grad_blocks))
             pack, next_parts, back, grad_blocks = tied
             packs = [pack, fetch([next_parts])]
         else:
+            back = swap_seq(attended)
             qkv_parts = jnp.concatenate(qkv_part(dense) + qkv_part(next_dense), axis=0)
             qkv_parts, back = lax.optimization_barrier((qkv_parts, back))
             qkv_w = fetch([qkv_parts])
@@ -985,6 +1007,13 @@
         label = jnp.arange(local_width + 3 * HD)[None, :]
         block = jnp.where(label == local_width + 2 * HD + expert_count, gain[:, None], block)
         return swap_seq(block.reshape(seq_count, dense_rows, local_width + 3 * HD))
+
+    def shard_sum(block):
+        block = block.reshape((shard_count // 2, 2) + block.shape[1:])
+        own = lax.dynamic_index_in_dim(block, core, 1, False)
+        other = swap_cores(lax.dynamic_index_in_dim(block, 1 - core, 1, False))
+        block = (own.astype(f32) + other.astype(f32)).astype(bf16)
+        return jnp.sum(swap_chips(block).astype(f32), axis=0)
 
     out_rows = 16
 
@@ -1015,24 +1044,34 @@
             pieces={n: (1 if n == 0 else 0, local_experts) for n in range(5)},
             flops=expert_flops,
         )
+        if layer < LAYERS - 1:
+            tied = lax.optimization_barrier((grad_blocks, branches[layer + 1]))
+            grad_rows, branches[layer + 1] = lax.optimization_barrier((grad_rows, around_seq(tied[1])))
         (logits_grad,) = once(
             logits_grad_kernel,
             [shape((2 * expert_count, tok_count), bf16)],
             grad_hidden, combined, gates_t, routes_t, target_t, flops=3 * dense_flops,
         )
         sent = swap_seq(grad_rows)
-        extra = () if layer == LAYERS - 1 else waiting
-        extra_rows = sum(a.shape[1] for a in extra)
-        (packed,) = once(
-            expert_weight_kernel,
-            [shape((shard_count, local_experts * expert_rows + extra_rows, half_width), bf16)],
-            received, grad_expert, gate_grad, up_grad, inner, *extra,
-            pieces={0: (1, (local_experts * expert_rows + extra_rows) // 16)}, flops=expert_flops,
-        )
+        sources = (received, grad_expert, gate_grad, up_grad, inner)
+        pack_rows = local_experts * expert_rows
+        if layer == LAYERS - 1:
+            (packed,) = once(
+                expert_weight_kernel,
+                [shape((shard_count, pack_rows, half_width), bf16)],
+                *sources, pieces={0: (1, pack_rows // 16)}, flops=expert_flops,
+            )
+        else:
+            pack_rows += shard_rows
+            packed = once(
+                expert_weight_apart_kernel,
+                [shape((shard_count // 2, pack_rows, half_width), bf16)] * 2,
+                core_place, *sources, *waiting,
+                scalar=True, pieces={n: (1, pack_rows // 16) for n in range(2)}, flops=expert_flops,
+            )
         sent, packed, logits_grad = lax.optimization_barrier((sent, packed, logits_grad))
-        if layer < LAYERS - 1:
-            packed, sums[layer + 1] = lax.optimization_barrier((packed, sums[layer + 1]))
-        summed = scatter(packed)
+        if layer == LAYERS - 1:
+            summed = scatter(packed)
         grad_middle, branch, send, small_grad = once(
             after_experts_kernel,
             [
@@ -1046,6 +1085,14 @@
             cut={7: out_cut}, flops=4 * dense_flops,
         )
         grad_heads = swap_seq(send)
+        if layer < LAYERS - 1:
+            packed = (packed[0].astype(f32) + swap_cores(packed[1]).astype(f32)).astype(bf16)
+            tied = lax.optimization_barrier((packed, sums[layer + 1], grad_heads))
+            packed, sums[layer + 1], grad_heads = tied
+            summed = lax.psum_scatter(
+                packed.reshape(-1, half_width), "fsdp", scatter_dimension=0, tiled=True,
+                axis_index_groups=chips,
+            )
         (grad_own,) = once(
             attention_back_kernel,
             [shape((seq_count, tok_count, local_width + 2 * HD), bf16)],
@@ -1077,21 +1124,16 @@
         if layer > 0:
             grad_blocks = around_seq(grad_low)
             waiting = (qkv_block_grad,)
+    qkv_sum = shard_sum(qkv_block_grad)
+    branches[0] = around_seq(branches[0])
+    branches[0], qkv_sum = lax.optimization_barrier((branches[0], qkv_sum))
     (out_block_grad,) = once(
         out_weight_kernel,
         [shape((shard_count, 2 * LAYERS * out_rows, half_width), bf16)],
-        place, *around_seq(jnp.stack(branches)), *attendeds, *gains,
+        place, *branches[0], *branches[1], *attendeds, *gains,
         scalar=True, flops=2 * dense_flops,
     )
 
-    def shard_sum(block):
-        block = block.reshape((shard_count // 2, 2) + block.shape[1:])
-        own = lax.dynamic_index_in_dim(block, core, 1, False)
-        other = swap_cores(lax.dynamic_index_in_dim(block, 1 - core, 1, False))
-        block = (own.astype(f32) + other.astype(f32)).astype(bf16)
-        return jnp.sum(swap_chips(block).astype(f32), axis=0)
-
-    qkv_sum = shard_sum(qkv_block_grad)
     out_sum = shard_sum(out_block_grad)
     out_sums = [out_sum[2 * out_rows * n : 2 * out_rows * (n + 1)] for n in range(LAYERS)]
     own_rows = spread_qkv(qkv_sum, out_sums[0])

time: 647 us -> 636 us (0.983)
  waiting for transfers between devices: 259 us -> 211 us
  blocking collectives: 35.2 us -> 67.6 us
    all_to_all x12, waiting for transfers between devices: 111 us -> 63.8 us  [swap_seq(): return lax.all_to_all(block, 'seq', split_axis=0, concat_axis=0, tiled=True)]
    all_to_all x3, blocking collectives: 35.2 us -> 67.6 us  [swap_seq(): return lax.all_to_all(block, 'seq', split_axis=0, concat_axis=0, tiled=True)]
    ppermute x3 -> x4, waiting for transfers between devices: 0.01 us -> 10.6 us  [swap_cores(): return lax.ppermute(block, 'fsdp', [(i, i ^ 1) for i in range(shard_count)])]
    convert_element_type x1, other arithmetic: 0.9 us -> 9.48 us  [per_device(): (packed[0].astype(f32) + swap_cores(packed[1]).astype(f32)).astype(bf16)]
    ppermute x21 -> x24, waiting for transfers between devices: 93.4 us -> 88.3 us  [around_seq(): lax.ppermute(block, 'seq', [((i + k) % count, i) for i in range(count)])]
    ppermute x21 -> x24, starting transfers between devices: 21.8 us -> 26.1 us  [around_seq(): lax.ppermute(block, 'seq', [((i + k) % count, i) for i in range(count)])]
  transfers between devices with their start and end apart: 44 -> 48, of which waited for: 31 -> 32; matrix products, arithmetic and copies ran while one was open for 7% -> 7% of each run, Pallas kernels for 24% -> 25%
where the time goes in v4:
time: 636 us; the launch traced here: 629 us
  waiting for transfers between devices  211 us (33%)
  Pallas kernels  178 us (28%)
  starting transfers between devices  95.3 us (15%)
  blocking collectives  67.6 us (11%)
  local copies, waits for them, and re-layouts  34.1 us (5%)
  other arithmetic  27.9 us (4%)
  between operations  15.3 us (2%)
    pallas_call x25, Pallas kernels, once(): pl.pallas_call(body, out_shape=list(outs), in_specs=specs, out_specs=[hbm...  178 us
    ppermute x24, waiting for transfers between devices, around_seq(): lax.ppermute(block, 'seq', [((i + k) % count, i) for i in range(count)])  88.3 us
    all_to_all x3, blocking collectives, swap_seq(): return lax.all_to_all(block, 'seq', split_axis=0, concat_axis=0, tiled=True)  67.6 us
    all_to_all x12, waiting for transfers between devices, swap_seq(): return lax.all_to_all(block, 'seq', split_axis=0, concat_axis=0, tiled=True)  63.8 us
    all_to_all x12, starting transfers between devices, swap_seq(): return lax.all_to_all(block, 'seq', split_axis=0, concat_axis=0, tiled=True)  49.4 us
    all_to_all x3, waiting for transfers between devices, swap_chips(): lax.all_to_all(block, 'fsdp', split_axis=0, concat_axis=0, tiled=True, ax...  47.8 us
    ppermute x24, starting transfers between devices, around_seq(): lax.ppermute(block, 'seq', [((i + k) % count, i) for i in range(count)])  26.1 us
    all_to_all x3, starting transfers between devices, swap_chips(): lax.all_to_all(block, 'fsdp', split_axis=0, concat_axis=0, tiled=True, ax...  18.2 us
  transfers between devices with their start and end apart: 48, of which 32 were waited for; matrix products, arithmetic and copies ran while one was open for 7% of the time, Pallas kernels for 25%

profile of v4, /device:TPU:0, one launch (start us, length us, event | category | flops | bytes accessed | tf_op | source)
XLA Modules:
  0.0 629.0 jit_solution(12264926152757810592)
XLA Ops:
  23.6 8.2 %all-to-all-done = bf16[4,12,3840]{2,1,0:T(8,128)(2,1)S(1)} async-done(((bf16[4,12,3840]{2,1,0:T(8,128)(2,1)}), bf16[4,12,3840]{2,1,0:T(8,128)(2,1)S(1)}, u32[]{:S(2)}, u32[]{:S(2)}) %all-to-all-start) | async-done | bytes 368672 | tf_op jit(solution)/shard_map/all_to_all | solution.py:733
  59.6 10.8 %collective-permute-done.refs_2_ = bf16[128,1536]{1,0:T(8,128)(2,1)S(1)} collective-permute-done((bf16[128,1536]{1,0:T(8,128)(2,1)S(1)}, bf16[128,1536]{1,0:T(8,128)(2,1)S(1)}, u32[]{:S(2)}, u32[]{:S(2)}) %collective-permute-start) | collective-permute-done | bytes 393248 | tf_op jit(solution)/shard_map/ppermute | solution.py:739
  79.7 11.9 %shard_map.238 = (bf16[4,128,640]{2,1,0:T(8,128)(2,1)}, bf16[4,128,384]{2,1,0:T(8,128)(2,1)}, bf16[4,128,1536]{2,1,0:T(8,128)(2,1)}, bf16[2,16,1536]{2,1,0:T(8,128)(2,1)}) custom-call(s32[1]{0:T(128)} %bitcast.23.refs_0_, bf16[128,1536]{1,0:T(8,128)(2,1)} %bitcast.218, bf16[128,1536]{1,0:T(8,128)(2,1)} %copy-done.23, bf16[128,1536]{1,0:T(8,128)(2,1)} %copy-done.24, ...), custom_call_target="tpu_custom_call" | custom-call | flops 4026531840 | bytes 8912900 | tf_op jit(solution)/shard_map/pallas_call | solution.py:158
  111.8 16.2 %all-to-all-done.4.refs_0_ = bf16[4,128,384]{2,1,0:T(8,128)(2,1)} async-done(((bf16[4,128,384]{2,1,0:T(8,128)(2,1)}), bf16[4,128,384]{2,1,0:T(8,128)(2,1)}, u32[]{:S(2)}, u32[]{:S(2)}) %all-to-all-start.4) | async-done | bytes 393248 | tf_op jit(solution)/shard_map/all_to_all | solution.py:733
  136.0 9.9 %collective-permute-done.7.refs_2_ = bf16[128,1536]{1,0:T(8,128)(2,1)} collective-permute-done((bf16[128,1536]{1,0:T(8,128)(2,1)}, bf16[128,1536]{1,0:T(8,128)(2,1)}, u32[]{:S(2)}, u32[]{:S(2)}) %collective-permute-start.7) | collective-permute-done | bytes 393248 | tf_op jit(solution)/shard_map/ppermute | solution.py:739
  153.8 10.1 %shard_map.240 = (bf16[4,2,72,1536]{3,2,1,0:T(8,128)(2,1)}, bf16[2,288,1536]{2,1,0:T(8,128)(2,1)}, bf16[2,288,768]{2,1,0:T(8,128)(2,1)}, bf16[2,288,768]{2,1,0:T(8,128)(2,1)}, f32[4,8,128]{2,1,0:T(8,128)}) custom-call(s32[1]{0:T(128)} %bitcast.23.refs_0_, bf16[128,1536]{1,0:T(8,128)(2,1)} %get-tuple-element.164.refs_1_.refs_3_, ...), custom_call_target="tpu_custom_call" | custom-call | flops 4076863488 | bytes 120209408 | tf_op jit(solution)/shard_map/pallas_call | solution.py:158
  164.0 27.7 %all_to_all.90 = bf16[4,2,72,1536]{3,2,1,0:T(8,128)(2,1)} all-to-all(bf16[4,2,72,1536]{3,2,1,0:T(8,128)(2,1)} %get-tuple-element.167), channel_id=1, replica_groups=mesh['seq'=4,'fsdp'=32] {'seq'}, dimensions={0} | all-to-all | bytes 3538944 | tf_op jit(solution)/shard_map/all_to_all | solution.py:733
  198.9 9.5 %collective-permute-done.10.refs_2_ = bf16[128,1536]{1,0:T(8,128)(2,1)} collective-permute-done((bf16[128,1536]{1,0:T(8,128)(2,1)}, bf16[128,1536]{1,0:T(8,128)(2,1)}, u32[]{:S(2)}, u32[]{:S(2)}) %collective-permute-start.10) | collective-permute-done | bytes 393248 | tf_op jit(solution)/shard_map/ppermute | solution.py:739
  217.0 7.6 %shard_map.242 = (bf16[4,128,640]{2,1,0:T(8,128)(2,1)}, bf16[4,128,384]{2,1,0:T(8,128)(2,1)}, bf16[4,128,1536]{2,1,0:T(8,128)(2,1)}) custom-call(s32[1]{0:T(128)} %bitcast.23.refs_0_, bf16[128,1536]{1,0:T(8,128)(2,1)} %get-tuple-element.170.refs_1_, bf16[128,1536]{1,0:T(8,128)(2,1)} %collective-permute-done.10.refs_2_, ...), custom_call_target="tpu_custom_call" | custom-call | flops 1610612736 | bytes 27000836 | tf_op jit(solution)/shard_map/pallas_call | solution.py:158
  245.0 9.7 %collective-permute-done.13.refs_2_ = bf16[128,1536]{1,0:T(8,128)(2,1)} collective-permute-done((bf16[128,1536]{1,0:T(8,128)(2,1)}, bf16[128,1536]{1,0:T(8,128)(2,1)}, u32[]{:S(2)}, u32[]{:S(2)}) %collective-permute-start.13) | collective-permute-done | bytes 393248 | tf_op jit(solution)/shard_map/ppermute | solution.py:739
  263.7 10.1 %shard_map.244 = (bf16[4,2,72,1536]{3,2,1,0:T(8,128)(2,1)}, bf16[2,288,1536]{2,1,0:T(8,128)(2,1)}, bf16[2,288,768]{2,1,0:T(8,128)(2,1)}, bf16[2,288,768]{2,1,0:T(8,128)(2,1)}, f32[4,8,128]{2,1,0:T(8,128)}) custom-call(s32[1]{0:T(128)} %bitcast.23.refs_0_, bf16[128,1536]{1,0:T(8,128)(2,1)} %get-tuple-element.178.refs_1_.refs_3_, ...), custom_call_target="tpu_custom_call" | custom-call | flops 4076863488 | bytes 134365184 | tf_op jit(solution)/shard_map/pallas_call | solution.py:158
  273.8 27.9 %all_to_all.91 = bf16[4,2,72,1536]{3,2,1,0:T(8,128)(2,1)} all-to-all(bf16[4,2,72,1536]{3,2,1,0:T(8,128)(2,1)} %get-tuple-element.181), channel_id=1, replica_groups=mesh['seq'=4,'fsdp'=32] {'seq'}, dimensions={0} | all-to-all | bytes 3538944 | tf_op jit(solution)/shard_map/all_to_all | solution.py:733
  305.4 12.3 %shard_map.246 = (bf16[4,2,72,1536]{3,2,1,0:T(8,128)(2,1)}, bf16[2,288,1536]{2,1,0:T(8,128)(2,1)}, bf16[2,288,768]{2,1,0:T(8,128)(2,1)}, bf16[2,288,768]{2,1,0:T(8,128)(2,1)}, bf16[2,288,768]{2,1,0:T(8,128)(2,1)}) custom-call(s32[1]{0:T(128)} %bitcast.23.refs_0_, bf16[128,1536]{1,0:T(8,128)(2,1)} %bitcast.217, ...), custom_call_target="tpu_custom_call" | custom-call | flops 4076863488 | bytes 136962048 | tf_op jit(solution)/shard_map/pallas_call | solution.py:158
  326.8 12.1 %shard_map.247 = bf16[32,288,768]{2,1,0:T(8,128)(2,1)} custom-call(bf16[2,288,1536]{2,1,0:T(8,128)(2,1)} %get-tuple-element.195.refs_0_, bf16[2,288,1536]{2,1,0:T(8,128)(2,1)} %get-tuple-element.196.refs_1_, bf16[2,288,768]{2,1,0:T(8,128)(2,1)} %get-tuple-element.197.refs_2_, bf16[2,288,768]{2,1,0:T(8,128)(2,1)} %get-tuple-element.198.refs_3_, ...), custom_call_target="tpu_custom_call" | custom-call | flops 4076863488 | bytes 20348928 | tf_op jit(solution)/shard_map/pallas_call | solution.py:158
  351.2 12.0 %all_to_all.92.refs_1_ = bf16[4,128,384]{2,1,0:T(8,128)(2,1)} all-to-all(bf16[4,128,384]{2,1,0:T(8,128)(2,1)} %get-tuple-element.203), channel_id=1, replica_groups=mesh['seq'=4,'fsdp'=32] {'seq'}, dimensions={0} | all-to-all | bytes 786432 | tf_op jit(solution)/shard_map/all_to_all | solution.py:733
  383.1 8.1 %shard_map.252 = (f32[128,1536]{1,0:T(8,128)}, bf16[128,1536]{1,0:T(8,128)(2,1)}, f32[32,128]{1,0:T(8,128)}) custom-call(bf16[4,128,640]{2,1,0:T(8,128)(2,1)} %all-to-all-done.10.refs_0_, bf16[32,288,768]{2,1,0:T(8,128)(2,1)} %bitcast.198, bf16[32,288,768]{2,1,0:T(8,128)(2,1)} %bitcast.199, bf16[32,288,768]{2,1,0:T(8,128)(2,1)} %bitcast.200, ...), custom_call_target="tpu_custom_call" | custom-call | flops 2415919104 | bytes 46235648 | tf_op jit(solution)/shard_map/pallas_call | solution.py:158
  394.0 8.5 %collective-permute-done.16.refs_2_ = bf16[128,1536]{1,0:T(8,128)(2,1)} collective-permute-done((bf16[128,1536]{1,0:T(8,128)(2,1)}, bf16[128,1536]{1,0:T(8,128)(2,1)}, u32[]{:S(2)}, u32[]{:S(2)}) %collective-permute-start.16) | collective-permute-done | bytes 393248 | tf_op jit(solution)/shard_map/ppermute | solution.py:739
  412.2 12.4 %shard_map.253 = (bf16[4,2,72,1536]{3,2,1,0:T(8,128)(2,1)}, bf16[2,288,1536]{2,1,0:T(8,128)(2,1)}, bf16[2,288,768]{2,1,0:T(8,128)(2,1)}, bf16[2,288,768]{2,1,0:T(8,128)(2,1)}, bf16[2,288,768]{2,1,0:T(8,128)(2,1)}) custom-call(s32[1]{0:T(128)} %bitcast.23.refs_0_, bf16[128,1536]{1,0:T(8,128)(2,1)} %get-tuple-element.211.refs_1_, ...), custom_call_target="tpu_custom_call" | custom-call | flops 4076863488 | bytes 122806272 | tf_op jit(solution)/shard_map/pallas_call | solution.py:158
  436.3 13.3 %shard_map.254 = (bf16[16,336,768]{2,1,0:T(8,128)(2,1)}, bf16[16,336,768]{2,1,0:T(8,128)(2,1)}) custom-call(s32[1]{0:T(128)} %bitcast.60.refs_0_, bf16[2,288,1536]{2,1,0:T(8,128)(2,1)} %get-tuple-element.222.refs_1_, bf16[2,288,1536]{2,1,0:T(8,128)(2,1)} %get-tuple-element.223.refs_2_, bf16[2,288,768]{2,1,0:T(8,128)(2,1)} %get-tuple-element.224.refs_3_, ...), custom_call_target="tpu_custom_call" | custom-call | flops 4076863488 | bytes 25067524 | tf_op jit(solution)/shard_map/pallas_call | solution.py:158
  469.7 9.5 %add_convert_fusion = bf16[16,336,768]{2,1,0:T(8,128)(2,1)} fusion(bf16[16,336,768]{2,1,0:T(8,128)(2,1)} %collective-permute-done.22, bf16[16,336,768]{2,1,0:T(8,128)(2,1)} %get-tuple-element.231), kind=kLoop, calls=%fused_computation | loop fusion | flops 16515072 | bytes 24772608 | tf_op jit(solution)/shard_map/convert_element_type | solution.py:1089
  509.4 7.4 %all-to-all-start.14 = ((bf16[16,48,768]{2,1,0:T(8,128)(2,1)}), bf16[16,48,768]{2,1,0:T(8,128)(2,1)}, u32[]{:S(2)}, u32[]{:S(2)}) async-start(bf16[16,48,768]{2,1,0:T(8,128)(2,1)} %fusion.1), calls=%async_computation.15 | async-start | bytes 2359296 | tf_op jit(solution)/shard_map/all_to_all | solution.py:865
  520.0 7.8 %shard_map.259 = (f32[128,1536]{1,0:T(8,128)}, bf16[128,1536]{1,0:T(8,128)(2,1)}, f32[32,128]{1,0:T(8,128)}) custom-call(bf16[4,128,640]{2,1,0:T(8,128)(2,1)} %all-to-all-done.13.refs_0_, bf16[32,288,768]{2,1,0:T(8,128)(2,1)} %bitcast.201, bf16[32,288,768]{2,1,0:T(8,128)(2,1)} %bitcast.202, bf16[32,288,768]{2,1,0:T(8,128)(2,1)} %bitcast.203, ...), custom_call_target="tpu_custom_call" | custom-call | flops 2415919104 | bytes 45842432 | tf_op jit(solution)/shard_map/pallas_call | solution.py:158
  527.8 14.5 %all-to-all-done.14 = bf16[16,48,768]{2,1,0:T(8,128)(2,1)} async-done(((bf16[16,48,768]{2,1,0:T(8,128)(2,1)}), bf16[16,48,768]{2,1,0:T(8,128)(2,1)}, u32[]{:S(2)}, u32[]{:S(2)}) %all-to-all-start.14) | async-done | bytes 1179680 | tf_op jit(solution)/shard_map/all_to_all | solution.py:865
  561.2 33.3 %all-to-all-done.15 = bf16[16,64,768]{2,1,0:T(8,128)(2,1)S(1)} async-done(((bf16[16,64,768]{2,1,0:T(8,128)(2,1)}), bf16[16,64,768]{2,1,0:T(8,128)(2,1)S(1)}, u32[]{:S(2)}, u32[]{:S(2)}) %all-to-all-start.15) | async-done | bytes 1572896 | tf_op jit(solution)/shard_map/all_to_all | solution.py:865
  (260 shorter events, 302.9 us)
Async XLA Ops:
  22.7 105.3 %all-gather.7.cloned.1.call-start = ((), (), s32[]{:S(2)}) async-start(), calls=%async_computation.22 | async-start | bytes 19464192 | tf_op jit(solution)/shard_map/all_gather | solution.py:859
  43.4 30.9 %all-to-all-start.1 = ((bf16[16,48,896]{2,1,0:T(8,128)(2,1)}), bf16[16,48,896]{2,1,0:T(8,128)(2,1)S(1)}, u32[]{:S(2)}, u32[]{:S(2)}) async-start(bf16[16,48,896]{2,1,0:T(8,128)(2,1)} %broadcast_in_dim.95), calls=%async_computation.1 | async-start | bytes 2752512 | tf_op jit(solution)/shard_map/all_to_all | solution.py:865
  53.3 17.2 %collective-permute-start = (bf16[128,1536]{1,0:T(8,128)(2,1)S(1)}, bf16[128,1536]{1,0:T(8,128)(2,1)S(1)}, u32[]{:S(2)}, u32[]{:S(2)}) collective-permute-start(bf16[128,1536]{1,0:T(8,128)(2,1)S(1)} %bitcast.221), channel_id=1, source_target_pairs={{32,0},{64,32},{96,64},{0,96},{33,1},{65,33},{97,65},{1,97},{34,2}... | collective-permute-start | bytes 1179656 | tf_op jit(solution)/shard_map/ppermute | solution.py:739
  56.5 17.7 %collective-permute-start.2 = (bf16[128,1536]{1,0:T(8,128)(2,1)S(1)}, bf16[128,1536]{1,0:T(8,128)(2,1)}, u32[]{:S(2)}, u32[]{:S(2)}) collective-permute-start(bf16[128,1536]{1,0:T(8,128)(2,1)S(1)} %bitcast.223), channel_id=1, source_target_pairs={{96,0},{0,32},{32,64},{64,96},{97,1},{1,33},{33,65},{65,97},{98,2}... | collective-permute-start | bytes 1179656 | tf_op jit(solution)/shard_map/ppermute | solution.py:739
  99.7 28.3 %collective-permute-start.4 = (bf16[128,1536]{1,0:T(8,128)(2,1)}, bf16[128,1536]{1,0:T(8,128)(2,1)}, u32[]{:S(2)}, u32[]{:S(2)}) collective-permute-start(bf16[128,1536]{1,0:T(8,128)(2,1)} %bitcast.214), channel_id=1, source_target_pairs={{32,0},{64,32},{96,64},{0,96},{33,1},{65,33},{97,65},{1,97},{34,2}... | collective-permute-start | bytes 1179656 | tf_op jit(solution)/shard_map/ppermute | solution.py:739
  102.9 25.1 %collective-permute-start.5 = (bf16[128,1536]{1,0:T(8,128)(2,1)}, bf16[128,1536]{1,0:T(8,128)(2,1)}, u32[]{:S(2)}, u32[]{:S(2)}) collective-permute-start(bf16[128,1536]{1,0:T(8,128)(2,1)} %bitcast.215), channel_id=1, source_target_pairs={{64,0},{96,32},{0,64},{32,96},{65,1},{97,33},{1,65},{33,97},{66,2}... | collective-permute-start | bytes 1179656 | tf_op jit(solution)/shard_map/ppermute | solution.py:739
  103.8 24.2 %collective-permute-start.6 = (bf16[128,1536]{1,0:T(8,128)(2,1)}, bf16[128,1536]{1,0:T(8,128)(2,1)}, u32[]{:S(2)}, u32[]{:S(2)}) collective-permute-start(bf16[128,1536]{1,0:T(8,128)(2,1)} %bitcast.216), channel_id=1, source_target_pairs={{96,0},{0,32},{32,64},{64,96},{97,1},{1,33},{33,65},{65,97},{98,2}... | collective-permute-start | bytes 1179656 | tf_op jit(solution)/shard_map/ppermute | solution.py:739
  105.5 22.5 %all-to-all-start.4 = ((bf16[4,128,384]{2,1,0:T(8,128)(2,1)}), bf16[4,128,384]{2,1,0:T(8,128)(2,1)}, u32[]{:S(2)}, u32[]{:S(2)}) async-start(bf16[4,128,384]{2,1,0:T(8,128)(2,1)} %get-tuple-element.153.refs_9_), calls=%async_computation.4 | async-start | bytes 786432 | tf_op jit(solution)/shard_map/all_to_all | solution.py:733
  109.6 107.4 %all-gather.9.cloned.1.call-start = ((), (), s32[]{:S(2)}) async-start(), calls=%async_computation.23 | async-start | bytes 21897216 | tf_op jit(solution)/shard_map/all_gather | solution.py:859
  134.9 18.9 %collective-permute-start.9 = (bf16[128,1536]{1,0:T(8,128)(2,1)}, bf16[128,1536]{1,0:T(8,128)(2,1)}, u32[]{:S(2)}, u32[]{:S(2)}) collective-permute-start(bf16[128,1536]{1,0:T(8,128)(2,1)} %get-tuple-element.164.refs_1_.refs_3_), channel_id=1, source_target_pairs={{96,0},{0,32},{32,64},{64,96},{97,1},{1,33},{33,65},{65,97},{98,2}... | collective-permute-start | bytes 1179656 | tf_op jit(solution)/shard_map/ppermute | solution.py:739
  198.9 18.1 %collective-permute-start.12 = (bf16[128,1536]{1,0:T(8,128)(2,1)}, bf16[128,1536]{1,0:T(8,128)(2,1)}, u32[]{:S(2)}, u32[]{:S(2)}) collective-permute-start(bf16[128,1536]{1,0:T(8,128)(2,1)} %get-tuple-element.170.refs_1_), channel_id=1, source_target_pairs={{96,0},{0,32},{32,64},{64,96},{97,1},{1,33},{33,65},{65,97},{98,2}... | collective-permute-start | bytes 1179656 | tf_op jit(solution)/shard_map/ppermute | solution.py:739
  228.8 76.7 %all-gather.11.cloned.1.call-start = ((), (), s32[]{:S(2)}) async-start(), calls=%async_computation.24 | async-start | bytes 14598144 | tf_op jit(solution)/shard_map/all_gather | solution.py:859
  245.0 18.7 %collective-permute-start.15 = (bf16[128,1536]{1,0:T(8,128)(2,1)}, bf16[128,1536]{1,0:T(8,128)(2,1)}, u32[]{:S(2)}, u32[]{:S(2)}) collective-permute-start(bf16[128,1536]{1,0:T(8,128)(2,1)} %get-tuple-element.178.refs_1_.refs_3_), channel_id=1, source_target_pairs={{96,0},{0,32},{32,64},{64,96},{97,1},{1,33},{33,65},{65,97},{98,2}... | collective-permute-start | bytes 1179656 | tf_op jit(solution)/shard_map/ppermute | solution.py:739
  317.8 26.7 %all-to-all-start.8 = ((bf16[4,2,72,1536]{3,2,1,0:T(8,128)(2,1)}), bf16[4,2,72,1536]{3,2,1,0:T(8,128)(2,1)}, u32[]{:S(2)}, u32[]{:S(2)}) async-start(bf16[4,2,72,1536]{3,2,1,0:T(8,128)(2,1)} %get-tuple-element.194), calls=%async_computation.8 | async-start | bytes 3538944 | tf_op jit(solution)/shard_map/all_to_all | solution.py:733
  322.3 156.9 %reduce-scatter.3.cloned.1.call-start = ((), (), s32[]{:S(2)}) async-start(), calls=%async_computation.20 | async-start | bytes 14598144 | tf_op jit(solution)/shard_map/reduce_scatter | solution.py:1003
  411.3 17.2 %collective-permute-start.21 = (bf16[128,1536]{1,0:T(8,128)(2,1)}, bf16[128,1536]{1,0:T(8,128)(2,1)}, u32[]{:S(2)}, u32[]{:S(2)}) collective-permute-start(bf16[128,1536]{1,0:T(8,128)(2,1)} %get-tuple-element.249.refs_5_), channel_id=1, source_target_pairs={{96,0},{0,32},{32,64},{64,96},{97,1},{1,33},{33,65},{65,97},{98,2}... | collective-permute-start | bytes 1179656 | tf_op jit(solution)/shard_map/ppermute | solution.py:739
  428.5 27.9 %all-to-all-start.11 = ((bf16[4,2,72,1536]{3,2,1,0:T(8,128)(2,1)}), bf16[4,2,72,1536]{3,2,1,0:T(8,128)(2,1)}, u32[]{:S(2)}, u32[]{:S(2)}) async-start(bf16[4,2,72,1536]{3,2,1,0:T(8,128)(2,1)} %get-tuple-element.221), calls=%async_computation.11 | async-start | bytes 3538944 | tf_op jit(solution)/shard_map/all_to_all | solution.py:733
  463.0 16.2 %all-to-all-start.12 = ((bf16[4,128,384]{2,1,0:T(8,128)(2,1)}), bf16[4,128,384]{2,1,0:T(8,128)(2,1)S(1)}, u32[]{:S(2)}, u32[]{:S(2)}) async-start(bf16[4,128,384]{2,1,0:T(8,128)(2,1)} %get-tuple-element.236), calls=%async_computation.13 | async-start | bytes 786432 | tf_op jit(solution)/shard_map/all_to_all | solution.py:733
  466.5 128.2 %reduce-scatter.5.cloned.1.call-start = ((), (), s32[]{:S(2)}) async-start(), calls=%async_computation.21 | async-start | bytes 8773632 | tf_op jit(solution)/shard_map/reduce_scatter | solution.py:1092
  509.4 32.8 %all-to-all-start.14 = ((bf16[16,48,768]{2,1,0:T(8,128)(2,1)}), bf16[16,48,768]{2,1,0:T(8,128)(2,1)}, u32[]{:S(2)}, u32[]{:S(2)}) async-start(bf16[16,48,768]{2,1,0:T(8,128)(2,1)} %fusion.1), calls=%async_computation.15 | async-start | bytes 2359296 | tf_op jit(solution)/shard_map/all_to_all | solution.py:865
  516.9 26.8 %collective-permute-start.23 = (bf16[128,1536]{1,0:T(8,128)(2,1)}, bf16[128,1536]{1,0:T(8,128)(2,1)}, u32[]{:S(2)}, u32[]{:S(2)}) collective-permute-start(bf16[128,1536]{1,0:T(8,128)(2,1)} %get-tuple-element.245.refs_1_), channel_id=1, source_target_pairs={{32,0},{64,32},{96,64},{0,96},{33,1},{65,33},{97,65},{1,97},{34,2}... | collective-permute-start | bytes 1179656 | tf_op jit(solution)/shard_map/ppermute | solution.py:739
  518.2 25.5 %collective-permute-start.24 = (bf16[128,1536]{1,0:T(8,128)(2,1)}, bf16[128,1536]{1,0:T(8,128)(2,1)}, u32[]{:S(2)}, u32[]{:S(2)}) collective-permute-start(bf16[128,1536]{1,0:T(8,128)(2,1)} %get-tuple-element.245.refs_1_), channel_id=1, source_target_pairs={{64,0},{96,32},{0,64},{32,96},{65,1},{97,33},{1,65},{33,97},{66,2}... | collective-permute-start | bytes 1179656 | tf_op jit(solution)/shard_map/ppermute | solution.py:739
  519.7 24.0 %collective-permute-start.25 = (bf16[128,1536]{1,0:T(8,128)(2,1)}, bf16[128,1536]{1,0:T(8,128)(2,1)}, u32[]{:S(2)}, u32[]{:S(2)}) collective-permute-start(bf16[128,1536]{1,0:T(8,128)(2,1)} %get-tuple-element.245.refs_1_), channel_id=1, source_target_pairs={{96,0},{0,32},{32,64},{64,96},{97,1},{1,33},{33,65},{65,97},{98,2}... | collective-permute-start | bytes 1179656 | tf_op jit(solution)/shard_map/ppermute | solution.py:739
  557.5 37.0 %all-to-all-start.15 = ((bf16[16,64,768]{2,1,0:T(8,128)(2,1)}), bf16[16,64,768]{2,1,0:T(8,128)(2,1)S(1)}, u32[]{:S(2)}, u32[]{:S(2)}) async-start(bf16[16,64,768]{2,1,0:T(8,128)(2,1)} %fusion), calls=%async_computation.16 | async-start | bytes 3145728 | tf_op jit(solution)/shard_map/all_to_all | solution.py:865
  (49 other events, 558.7 us)
Sparse Core Ops, SparseCore 0:
  32.9 89.9 all-gather.6
  128.2 81.9 all-gather.8
  237.5 65.8 all-gather.10
  344.7 107.9 reduce-scatter.2
  479.4 114.3 reduce-scatter.4

commit v5 on v3

--- a/solution.py
+++ b/solution.py
@@ -442,8 +442,8 @@
 ):
     me = place[0]
     blocks = (own, one, two, three)
-    out_ref, rows_ref, gate_grad_ref, up_grad_ref, inner_ref = rest[-5:]
-    weights = (down_first,) + rest[:-5]
+    out_ref, keep_ref = rest[-2:]
+    weights = (down_first,) + rest[:-2]
     sources, experts, capacity, width = out_ref.shape
     half = width // 2
     for e in range(experts):
@@ -457,24 +457,22 @@
             twice = jnp.concatenate([block[...], block[...]], axis=0)
             parts.append(nn(hot, twice))
         grad = jnp.concatenate(parts, axis=0).astype(bf16)
-        rows_ref[e] = grad
-        rows_ref.send(e)
+        keep_ref[e, :, :width] = grad
         left, right = down_parts(down_w[...])
         grad_inner = nt(grad[:, :half], left) + nt(grad[:, half:], right)
         up_val = up_ref[e].astype(f32)
         activated, slope = smooth_parts(gate_ref[e].astype(f32))
-        inner_ref[e] = (activated * up_val).astype(bf16)
-        inner_ref.send(e)
-        gate_grad_ref[e] = (grad_inner * up_val * slope).astype(bf16)
-        gate_grad_ref.send(e)
-        up_grad_ref[e] = (grad_inner * activated).astype(bf16)
-        up_grad_ref.send(e)
+        gate_at, up_at, inner_at = (slice(width + n * half, width + (n + 1) * half) for n in range(3))
+        keep_ref[e, :, gate_at] = (grad_inner * up_val * slope).astype(bf16)
+        keep_ref[e, :, up_at] = (grad_inner * activated).astype(bf16)
+        keep_ref[e, :, inner_at] = (activated * up_val).astype(bf16)
+        keep_ref.send(e)
         parts = 4
         some, size = shards // parts, shards * rows // parts
         for c in range(parts):
             at = slice(c * some, (c + 1) * some)
-            total = nt(gate_grad_ref[e], gate_w[at].reshape(size, half))
-            total = total + nt(up_grad_ref[e], up_w[at].reshape(size, half))
+            total = nt(keep_ref[e, :, gate_at], gate_w[at].reshape(size, half))
+            total = total + nt(keep_ref[e, :, up_at], up_w[at].reshape(size, half))
             total = total.astype(bf16)
             for k in range(sources):
                 out_ref[lax.rem(me + k, sources), e, :, c * size : (c + 1) * size] = total[
@@ -483,33 +481,52 @@
         out_ref.send(e)
 
 
-def expert_weight_kernel(rows_ref, grad_ref, gate_grad_ref, up_grad_ref, inner_ref, *rest):
+def pick_kernel(rows, other_rows, pick, out_ref):
+    count = rows.shape[1]
+    for e in range(rows.shape[0]):
+        out_ref[e, :count] = nn(rows[e], pick[...]).astype(bf16)
+        out_ref[e, count:] = nn(other_rows[e], pick[...]).astype(bf16)
+        out_ref.send(e)
+
+
+def expert_weight_kernel(tokens, pick_inner, keep, other_keep, *rest):
     pack_ref = rest[-1]
-    experts, _, width = rows_ref.shape
-    shards, _, half = pack_ref.shape
-    rows = width // shards
+    chips, _, half = pack_ref.shape
+    experts = tokens.shape[0]
+    width = 2 * tokens.shape[2]
+    count = width // (2 * chips)
     at = 0
 
-    def send(start, count):
-        for piece in range(start // 16, (start + count) // 16):
+    def send():
+        for piece in range(at // 16, (at + count) // 16):
             pack_ref.send(piece)
 
     for e in range(experts):
-        grads = jnp.concatenate([gate_grad_ref[e], up_grad_ref[e]], axis=1)
-        both = tn(rows_ref[e], grads).astype(bf16)
-        pack_ref[:, at : at + rows] = both[:, :half].reshape(shards, rows, half)
-        pack_ref[:, at + rows : at + 2 * rows] = both[:, half:].reshape(shards, rows, half)
-        send(at, 2 * rows)
-        down = tn(inner_ref[e], grad_ref[e])
-        left = down[:, :half].reshape(shards, rows // 2, half)
-        right = down[:, half:].reshape(shards, rows // 2, half)
-        down = jnp.concatenate([left, right], axis=1).astype(bf16)
-        pack_ref[:, at + 2 * rows : at + 3 * rows] = down
-        send(at + 2 * rows, rows)
-        at += 3 * rows
-    for extra in rest[:-1]:
-        pack_ref[:, at : at + extra.shape[1]] = extra[...]
-        at += extra.shape[1]
+        grads = jnp.concatenate([keep[e], other_keep[e]], axis=0)
+        both = tn(tokens[e], grads[:, width : width + 2 * half]).astype(bf16)
+        for n in range(2):
+            block = both[:, n * half : (n + 1) * half].reshape(chips, count, half)
+            pack_ref[:, at : at + count] = block
+            send()
+            at += count
+        inner = nn(grads[:, width + 2 * half :], pick_inner[...]).astype(bf16)
+        down = tn(inner, grads[:, :width])
+        left = down[:, :half].reshape(chips, count // 2, half)
+        right = down[:, half:].reshape(chips, count // 2, half)
+        pack_ref[:, at : at + count] = jnp.concatenate([left, right], axis=1).astype(bf16)
+        send()
+        at += count
+    if len(rest) > 1:
+        own, other = rest[:2]
+        pack_ref[:, at : at + count] = (own[...].astype(f32) + other[...].astype(f32)).astype(bf16)
+        send()
+
+
+def keep_shards(own_ref, other_ref, core, at, value):
+    shards, rows, columns = value.shape
+    value = value.reshape(shards // 2, 2, rows, columns)
+    own_ref[:, at : at + rows] = jnp.where(core == 0, value[:, 0], value[:, 1])
+    other_ref[:, at : at + rows] = jnp.where(core == 0, value[:, 1], value[:, 0])
 
 
 def after_experts_kernel(
@@ -632,28 +649,34 @@
     gain_ref[...] = nn(kept, jnp.where(place == wanted, 1.0, 0.0).astype(bf16))
 
 
-def qkv_weight_kernel(normed, grads, small, spread, out_ref):
+def qkv_weight_kernel(place, normed, grads, small, spread, own_ref, other_ref):
     seq_count, tokens, columns = grads.shape
-    shards, rows, wide = out_ref.shape
+    chips, rows, wide = own_ref.shape
+    shards = 2 * chips
     inputs = normed[...].reshape(seq_count * tokens, normed.shape[2])
     total = tn(inputs, grads[...].reshape(seq_count * tokens, columns))
-    out_ref[:, :, :columns] = total.astype(bf16).reshape(shards, rows, columns)
     extra = column_blocks(small[...].astype(bf16), seq_count)
     extra = to_gathered(extra, spread[...])
     extra = jnp.concatenate([extra, jnp.zeros((HD - extra.shape[0], extra.shape[1]), f32)], axis=0).T
-    out_ref[:, :, columns:] = extra.astype(bf16).reshape(shards, rows, wide - columns)
-
-
-def out_weight_kernel(place, own, one, two, three, *rest):
-    out_ref = rest[-1]
+    total = jnp.concatenate([total, extra], axis=1).astype(bf16).reshape(shards, rows, wide)
+    keep_shards(own_ref, other_ref, place[1], 0, total)
+
+
+def out_weight_kernel(place, *rest):
+    own_ref, other_ref = rest[-2:]
+    rest = rest[:-2]
     me = place[0]
-    shards, rows, half = out_ref.shape
+    around = len(rest) // LAYERS - 2
+    blocks, rest = rest[: LAYERS * around], rest[LAYERS * around :]
+    chips, rows, half = own_ref.shape
+    shards = 2 * chips
     rows = rows // (2 * LAYERS)
     for layer in range(LAYERS):
         attended, gain = rest[layer], rest[LAYERS + layer]
         seq_count, tokens, part = attended.shape
         valid = part // shards
-        branch = jnp.concatenate([block[layer] for block in (own, one, two, three)], axis=0)
+        branch = [block[...] for block in blocks[layer * around : (layer + 1) * around]]
+        branch = jnp.concatenate(branch, axis=0)
         heads = jnp.concatenate(
             [attended[lax.rem(me + k, seq_count)] for k in range(seq_count)], axis=0
         )
@@ -670,7 +693,7 @@
             if side == 0:
                 total = jnp.where(row == valid, wide[:, None, :], total)
             at = (2 * layer + side) * rows
-            out_ref[:, at : at + rows] = total.astype(bf16)
+            keep_shards(own_ref, other_ref, place[1], at, total.astype(bf16))
 
 
 def expert_grads_kernel(*refs):
@@ -750,7 +773,8 @@
     seq_count = lax.axis_size("seq")
     shard_count = lax.axis_size("fsdp")
     seq_index = lax.axis_index("seq")
-    place = jnp.full((1,), seq_index, jnp.int32)
+    core = lax.rem(lax.axis_index("fsdp"), 2)
+    place = jnp.stack([seq_index, core]).astype(jnp.int32)
     group_tok = seq_count * tok_count
     prompt_len = group_tok - segment_ids.shape[1]
     local_experts = w_gate.shape[1]
@@ -806,6 +830,14 @@
             axis=1,
         )
 
+    def shards_of_core(count):
+        rows = count // shard_count
+        wanted = jnp.arange(count // 2, dtype=jnp.int32)
+        wanted = (wanted // rows * 2 + core) * rows + wanted % rows
+        return (jnp.arange(count, dtype=jnp.int32)[:, None] == wanted[None, :]).astype(bf16)
+
+    picks = (shards_of_core(width), shards_of_core(inner_width))
+
     def spread_seq(dense):
         dense = swap_seq(jnp.broadcast_to(dense[None], (seq_count,) + dense.shape))
         return dense.reshape(shard_rows, dense.shape[2])
@@ -838,7 +870,6 @@
     def fetch(parts):
         return lax.all_gather(jnp.concatenate(parts, axis=0), "fsdp", axis=0, tiled=False)
 
-    core = lax.rem(lax.axis_index("fsdp"), 2)
     chips = [[i + c for i in range(0, shard_count, 2)] for c in range(2)]
 
     def swap_chips(block):
@@ -887,16 +918,17 @@
     all_targets = [
         jax.vmap(slots_of)(pairs[:, 0, layer], pairs[:, 1, layer]) for layer in range(LAYERS)
     ]
-    early = (token_blocks, all_targets, all_routes, cos_all, sin_all, bias, spread)
-    columns, early, next_rows = lax.optimization_barrier((columns, early, dense_rows_of(1)))
-    token_blocks, all_targets, all_routes, cos_all, sin_all, bias, spread = early
     targets = [lax.dynamic_index_in_dim(t, seq_index, 0, False) for t in all_targets]
     routes_ts = [lax.dynamic_index_in_dim(t, seq_index, 0, False) for t in all_routes]
+    early = (token_blocks, all_targets, all_routes, targets, routes_ts)
+    early = early + (cos_all, sin_all, bias, spread, picks)
+    columns, early = lax.optimization_barrier((columns, early))
+    token_blocks, all_targets, all_routes, targets, routes_ts = early[:5]
+    cos_all, sin_all, bias, spread, picks = early[5:]
     first_columns = both_cores(columns).reshape(width, columns.shape[2])
-    next_dense = spread_seq(next_rows)
+    first_columns, grad_rows = lax.optimization_barrier((first_columns, cotangent[0]))
+    grad_blocks = around_seq(grad_rows)
     own_at = local_experts * expert_rows + 2 * shard_rows
-    grad_blocks = around_seq(cotangent[0])
-
     heads_shape = shape((seq_count, tok_count, local_width + 2 * HD), bf16)
     attended_shape = shape((seq_count, tok_count, local_width), bf16)
     normed_shape = shape((seq_count, tok_count, width), bf16)
@@ -925,14 +957,17 @@
                 place, *around_seq(normed_p), pack, cos_all, sin_all, bias,
                 scalar=True, cut={5: ((1, own_at, shard_rows),)}, flops=attention_flops,
             )
-        back = swap_seq(attended)
         if layer == 0:
+            attended, next_rows = lax.optimization_barrier((attended, dense_rows_of(1)))
+            back = swap_seq(attended)
+            next_dense = spread_seq(next_rows)
             next_parts = expert_part(1) + out_part(next_dense) + [own_columns(next_dense)]
             next_parts = jnp.concatenate(next_parts, axis=0)
             tied = lax.optimization_barrier((pack, next_parts, back, grad_blocks))
             pack, next_parts, back, grad_blocks = tied
             packs = [pack, fetch([next_parts])]
         else:
+            back = swap_seq(attended)
             qkv_parts = jnp.concatenate(qkv_part(dense) + qkv_part(next_dense), axis=0)
             qkv_parts, back = lax.optimization_barrier((qkv_parts, back))
             qkv_w = fetch([qkv_parts])
@@ -962,29 +997,39 @@
             pieces={n: (1 if n == 0 else 0, local_experts) for n in range(4)},
             flops=expert_flops,
         )
-        combined = swap_seq(expert_out).reshape(total_slots, width)
+        (picked,) = once(
+            pick_kernel,
+            [shape((local_experts, 2 * slot_rows, width // 2), bf16)],
+            received, swap_cores(received), picks[0],
+            pieces={0: (0, local_experts)}, flops=expert_flops // 3,
+        )
+        combined, picked = lax.optimization_barrier(
+            (swap_seq(expert_out).reshape(total_slots, width), picked)
+        )
         above_target = target_t
         records.append(
             (
                 (pack, small, routes_t, target_t),
                 (hidden, normed_all, heads, attended),
                 (middle, normed_ffn, gates_t, combined),
-                (received, gate_val, up_val, all_gates),
+                (picked, gate_val, up_val, all_gates),
             )
         )
     (result,) = once(
         result_kernel, [shape((tok_count, width), bf16)], middle, combined, gates_t, target_t,
         flops=dense_flops,
     )
-
-    def scatter(block):
-        return lax.psum_scatter(block, "fsdp", scatter_dimension=0, tiled=False)
 
     def spread_qkv(block, out_block):
         gain = out_block[dense_rows, :shard_rows]
         label = jnp.arange(local_width + 3 * HD)[None, :]
         block = jnp.where(label == local_width + 2 * HD + expert_count, gain[:, None], block)
         return swap_seq(block.reshape(seq_count, dense_rows, local_width + 3 * HD))
+
+    def shard_sum(blocks):
+        own, other = blocks
+        block = (own.astype(f32) + swap_cores(other).astype(f32)).astype(bf16)
+        return jnp.sum(swap_chips(block).astype(f32), axis=0)
 
     out_rows = 16
 
@@ -998,23 +1043,25 @@
         row = layer * 3 * shard_rows
         below, normed_all, heads, attended = attn_saved
         middle, normed_ffn, gates_t, combined = mid_saved
-        received, gate_val, up_val, all_gates = expert_saved
+        picked, gate_val, up_val, all_gates = expert_saved
         if waiting is None:
             tied = lax.optimization_barrier((grad_blocks, qkv_w, result, combined))
             grad_blocks, qkv_w, result, combined = tied
         else:
             grad_blocks, waiting = lax.optimization_barrier((grad_blocks, waiting))
-        grad_rows, grad_expert, gate_grad, up_grad, inner = once(
+        grad_rows, kept = once(
             expert_back_kernel,
-            [slots_shape, shape((local_experts, slot_rows, width), bf16)]
-            + [shape(inner_shape, bf16)] * 3,
+            [slots_shape, shape((local_experts, slot_rows, width + 3 * inner_width), bf16)],
             place, *grad_blocks, all_targets[layer], all_gates, pack, gate_val, up_val,
             *[pack] * (len(back_parts) - 1),
             scalar=True,
             cut={n + 9 if n else 7: ((1, *part),) for n, part in enumerate(back_parts)},
-            pieces={n: (1 if n == 0 else 0, local_experts) for n in range(5)},
+            pieces={0: (1, local_experts), 1: (0, local_experts)},
             flops=expert_flops,
         )
+        if layer < LAYERS - 1:
+            tied = lax.optimization_barrier((grad_blocks, branches[layer + 1]))
+            grad_rows, branches[layer + 1] = lax.optimization_barrier((grad_rows, around_seq(tied[1])))
         (logits_grad,) = once(
             logits_grad_kernel,
             [shape((2 * expert_count, tok_count), bf16)],
@@ -1022,17 +1069,20 @@
         )
         sent = swap_seq(grad_rows)
         extra = () if layer == LAYERS - 1 else waiting
-        extra_rows = sum(a.shape[1] for a in extra)
+        pack_rows = local_experts * expert_rows + (shard_rows if extra else 0)
         (packed,) = once(
             expert_weight_kernel,
-            [shape((shard_count, local_experts * expert_rows + extra_rows, half_width), bf16)],
-            received, grad_expert, gate_grad, up_grad, inner, *extra,
-            pieces={0: (1, (local_experts * expert_rows + extra_rows) // 16)}, flops=expert_flops,
-        )
-        sent, packed, logits_grad = lax.optimization_barrier((sent, packed, logits_grad))
+            [shape((shard_count // 2, pack_rows, half_width), bf16)],
+            picked, picks[1], kept, swap_cores(kept), *extra,
+            pieces={0: (1, pack_rows // 16)}, flops=2 * expert_flops,
+        )
+        sent, packed_too, logits_grad = lax.optimization_barrier((sent, packed, logits_grad))
         if layer < LAYERS - 1:
             packed, sums[layer + 1] = lax.optimization_barrier((packed, sums[layer + 1]))
-        summed = scatter(packed)
+        summed = lax.psum_scatter(
+            packed.reshape(-1, half_width), "fsdp", scatter_dimension=0, tiled=True,
+            axis_index_groups=chips,
+        )
         grad_middle, branch, send, small_grad = once(
             after_experts_kernel,
             [
@@ -1052,10 +1102,10 @@
             heads, grad_heads, bias, cos_all, sin_all,
             flops=10 * head_local * group_tok * group_tok * HD,
         )
-        (qkv_block_grad,) = once(
+        qkv_block_grad = once(
             qkv_weight_kernel,
-            [shape((shard_count, shard_rows, half_width), bf16)],
-            normed_all, grad_own, small_grad, spread, flops=2 * dense_flops,
+            [shape((shard_count // 2, shard_rows, half_width), bf16)] * 2,
+            place, normed_all, grad_own, small_grad, spread, scalar=True, flops=2 * dense_flops,
         )
         sent, qkv_block_grad = lax.optimization_barrier((swap_seq(grad_own), qkv_block_grad))
         grad_hidden, grad_low, gains[layer] = once(
@@ -1076,22 +1126,17 @@
         branches[layer], attendeds[layer], sums[layer] = branch, attended, summed
         if layer > 0:
             grad_blocks = around_seq(grad_low)
-            waiting = (qkv_block_grad,)
-    (out_block_grad,) = once(
+            waiting = (qkv_block_grad[0], swap_cores(qkv_block_grad[1]))
+    qkv_sum = shard_sum(qkv_block_grad)
+    branches[0] = around_seq(branches[0])
+    branches[0], qkv_sum = lax.optimization_barrier((branches[0], qkv_sum))
+    out_block_grad = once(
         out_weight_kernel,
-        [shape((shard_count, 2 * LAYERS * out_rows, half_width), bf16)],
-        place, *around_seq(jnp.stack(branches)), *attendeds, *gains,
+        [shape((shard_count // 2, 2 * LAYERS * out_rows, half_width), bf16)] * 2,
+        place, *branches[0], *branches[1], *attendeds, *gains,
         scalar=True, flops=2 * dense_flops,
     )
 
-    def shard_sum(block):
-        block = block.reshape((shard_count // 2, 2) + block.shape[1:])
-        own = lax.dynamic_index_in_dim(block, core, 1, False)
-        other = swap_cores(lax.dynamic_index_in_dim(block, 1 - core, 1, False))
-        block = (own.astype(f32) + other.astype(f32)).astype(bf16)
-        return jnp.sum(swap_chips(block).astype(f32), axis=0)
-
-    qkv_sum = shard_sum(qkv_block_grad)
     out_sum = shard_sum(out_block_grad)
     out_sums = [out_sum[2 * out_rows * n : 2 * out_rows * (n + 1)] for n in range(LAYERS)]
     own_rows = spread_qkv(qkv_sum, out_sums[0])

time: 647 us -> 696 us (1.076)
  waiting for transfers between devices: 259 us -> 288 us
  Pallas kernels: 178 us -> 199 us
  starting transfers between devices: 90.2 us -> 105 us
  blocking collectives: 35.2 us -> 24.2 us
    ppermute x3 -> x8, waiting for transfers between devices: 0.01 us -> 24.9 us  [swap_cores(): return lax.ppermute(block, 'fsdp', [(i, i ^ 1) for i in range(shard_count)])]
    pallas_call x25 -> x27, Pallas kernels: 178 us -> 199 us  [once(): pl.pallas_call(body, out_shape=list(outs), in_specs=specs, out_specs=[hbm...]
    ppermute x21 -> x24, waiting for transfers between devices: 93.4 us -> 110 us  [around_seq(): lax.ppermute(block, 'seq', [((i + k) % count, i) for i in range(count)])]
    all_to_all x3, waiting for transfers between devices: 50.2 us -> 34.1 us  [swap_chips(): lax.all_to_all(block, 'fsdp', split_axis=0, concat_axis=0, tiled=True, ax...]
    all_to_all x3 -> x2, blocking collectives: 35.2 us -> 24.2 us  [swap_seq(): return lax.all_to_all(block, 'seq', split_axis=0, concat_axis=0, tiled=True)]
    all_to_all x12 -> x13, waiting for transfers between devices: 111 us -> 119 us  [swap_seq(): return lax.all_to_all(block, 'seq', split_axis=0, concat_axis=0, tiled=True)]
    ppermute x21 -> x24, starting transfers between devices: 21.8 us -> 27.1 us  [around_seq(): lax.ppermute(block, 'seq', [((i + k) % count, i) for i in range(count)])]
    all_to_all x12 -> x13, starting transfers between devices: 51.6 us -> 53.2 us  [swap_seq(): return lax.all_to_all(block, 'seq', split_axis=0, concat_axis=0, tiled=True)]
  transfers between devices with their start and end apart: 44 -> 53, of which waited for: 31 -> 37; matrix products, arithmetic and copies ran while one was open for 7% -> 6% of each run, Pallas kernels for 24% -> 24%
where the time goes in v5:
time: 696 us; the launch traced here: 688 us
  waiting for transfers between devices  288 us (41%)
  Pallas kernels  199 us (29%)
  starting transfers between devices  105 us (15%)
  local copies, waits for them, and re-layouts  32.6 us (5%)
  blocking collectives  24.2 us (3%)
  other arithmetic  24.1 us (3%)
  between operations  15 us (2%)
    pallas_call x27, Pallas kernels, once(): pl.pallas_call(body, out_shape=list(outs), in_specs=specs, out_specs=[hbm...  199 us
    all_to_all x13, waiting for transfers between devices, swap_seq(): return lax.all_to_all(block, 'seq', split_axis=0, concat_axis=0, tiled=True)  119 us
    ppermute x24, waiting for transfers between devices, around_seq(): lax.ppermute(block, 'seq', [((i + k) % count, i) for i in range(count)])  110 us
    all_to_all x13, starting transfers between devices, swap_seq(): return lax.all_to_all(block, 'seq', split_axis=0, concat_axis=0, tiled=True)  53.2 us
    all_to_all x3, waiting for transfers between devices, swap_chips(): lax.all_to_all(block, 'fsdp', split_axis=0, concat_axis=0, tiled=True, ax...  34.1 us
    ppermute x24, starting transfers between devices, around_seq(): lax.ppermute(block, 'seq', [((i + k) % count, i) for i in range(count)])  27.1 us
    ppermute x8, waiting for transfers between devices, swap_cores(): return lax.ppermute(block, 'fsdp', [(i, i ^ 1) for i in range(shard_count)])  24.9 us
    all_to_all x2, blocking collectives, swap_seq(): return lax.all_to_all(block, 'seq', split_axis=0, concat_axis=0, tiled=True)  24.2 us
  transfers between devices with their start and end apart: 53, of which 37 were waited for; matrix products, arithmetic and copies ran while one was open for 6% of the time, Pallas kernels for 24%

profile of v5, /device:TPU:0, one launch (start us, length us, event | category | flops | bytes accessed | tf_op | source)
XLA Modules:
  0.0 688.1 jit_solution(10833149263732246577)
XLA Ops:
  23.5 8.2 %all-to-all-done = bf16[4,12,3840]{2,1,0:T(8,128)(2,1)S(1)} async-done(((bf16[4,12,3840]{2,1,0:T(8,128)(2,1)}), bf16[4,12,3840]{2,1,0:T(8,128)(2,1)S(1)}, u32[]{:S(2)}, u32[]{:S(2)}) %all-to-all-start) | async-done | bytes 368672 | tf_op jit(solution)/shard_map/all_to_all | solution.py:737
  63.3 10.7 %collective-permute-done.refs_2_ = bf16[128,1536]{1,0:T(8,128)(2,1)S(1)} collective-permute-done((bf16[128,1536]{1,0:T(8,128)(2,1)S(1)}, bf16[128,1536]{1,0:T(8,128)(2,1)S(1)}, u32[]{:S(2)}, u32[]{:S(2)}) %collective-permute-start) | collective-permute-done | bytes 393248 | tf_op jit(solution)/shard_map/ppermute | solution.py:743
  85.6 11.7 %shard_map.238 = (bf16[4,128,640]{2,1,0:T(8,128)(2,1)}, bf16[4,128,384]{2,1,0:T(8,128)(2,1)}, bf16[4,128,1536]{2,1,0:T(8,128)(2,1)}, bf16[2,16,1536]{2,1,0:T(8,128)(2,1)}) custom-call(s32[2]{0:T(128)} %pad_add_fusion.1.refs_0_, bf16[128,1536]{1,0:T(8,128)(2,1)} %bitcast.199, bf16[128,1536]{1,0:T(8,128)(2,1)} %copy-done.29, bf16[128,1536]{1,0:T(8,128)(2,1)} %copy-done.30, ...), custom_call_target="tpu_custom_call" | custom-call | flops 4026531840 | bytes 8912904 | tf_op jit(solution)/shard_map/pallas_call | solution.py:158
  116.8 15.5 %all-to-all-done.4.refs_0_ = bf16[4,128,384]{2,1,0:T(8,128)(2,1)S(1)} async-done(((bf16[4,128,384]{2,1,0:T(8,128)(2,1)}), bf16[4,128,384]{2,1,0:T(8,128)(2,1)S(1)}, u32[]{:S(2)}, u32[]{:S(2)}) %all-to-all-start.4) | async-done | bytes 393248 | tf_op jit(solution)/shard_map/all_to_all | solution.py:737
  142.0 9.7 %collective-permute-done.7.refs_2_ = bf16[128,1536]{1,0:T(8,128)(2,1)} collective-permute-done((bf16[128,1536]{1,0:T(8,128)(2,1)}, bf16[128,1536]{1,0:T(8,128)(2,1)}, u32[]{:S(2)}, u32[]{:S(2)}) %collective-permute-start.7) | collective-permute-done | bytes 393248 | tf_op jit(solution)/shard_map/ppermute | solution.py:743
  160.5 10.8 %shard_map.240 = (bf16[4,2,72,1536]{3,2,1,0:T(8,128)(2,1)}, bf16[2,288,1536]{2,1,0:T(8,128)(2,1)}, bf16[2,288,768]{2,1,0:T(8,128)(2,1)}, bf16[2,288,768]{2,1,0:T(8,128)(2,1)}, f32[4,8,128]{2,1,0:T(8,128)}) custom-call(s32[2]{0:T(128)} %pad_add_fusion.1.refs_0_, bf16[128,1536]{1,0:T(8,128)(2,1)} %get-tuple-element.167.refs_1_.refs_3_, ...), custom_call_target="tpu_custom_call" | custom-call | flops 4076863488 | bytes 120209416 | tf_op jit(solution)/shard_map/pallas_call | solution.py:158
  183.3 16.3 %all-to-all-done.5 = bf16[4,2,72,1536]{3,2,1,0:T(8,128)(2,1)} async-done(((bf16[4,2,72,1536]{3,2,1,0:T(8,128)(2,1)}), bf16[4,2,72,1536]{3,2,1,0:T(8,128)(2,1)}, u32[]{:S(2)}, u32[]{:S(2)}) %all-to-all-start.5) | async-done | bytes 1769504 | tf_op jit(solution)/shard_map/all_to_all | solution.py:737
  206.7 9.5 %collective-permute-done.11.refs_2_ = bf16[128,1536]{1,0:T(8,128)(2,1)} collective-permute-done((bf16[128,1536]{1,0:T(8,128)(2,1)}, bf16[128,1536]{1,0:T(8,128)(2,1)}, u32[]{:S(2)}, u32[]{:S(2)}) %collective-permute-start.11) | collective-permute-done | bytes 393248 | tf_op jit(solution)/shard_map/ppermute | solution.py:743
  225.8 8.2 %shard_map.243 = (bf16[4,128,640]{2,1,0:T(8,128)(2,1)}, bf16[4,128,384]{2,1,0:T(8,128)(2,1)}, bf16[4,128,1536]{2,1,0:T(8,128)(2,1)}) custom-call(s32[2]{0:T(128)} %pad_add_fusion.1.refs_0_, bf16[128,1536]{1,0:T(8,128)(2,1)} %get-tuple-element.176.refs_1_, bf16[128,1536]{1,0:T(8,128)(2,1)} %collective-permute-done.11.refs_2_, ...), custom_call_target="tpu_custom_call" | custom-call | flops 1610612736 | bytes 27000840 | tf_op jit(solution)/shard_map/pallas_call | solution.py:158
  254.4 9.7 %collective-permute-done.14.refs_2_ = bf16[128,1536]{1,0:T(8,128)(2,1)} collective-permute-done((bf16[128,1536]{1,0:T(8,128)(2,1)}, bf16[128,1536]{1,0:T(8,128)(2,1)}, u32[]{:S(2)}, u32[]{:S(2)}) %collective-permute-start.14) | collective-permute-done | bytes 393248 | tf_op jit(solution)/shard_map/ppermute | solution.py:743
  273.1 10.8 %shard_map.245 = (bf16[4,2,72,1536]{3,2,1,0:T(8,128)(2,1)}, bf16[2,288,1536]{2,1,0:T(8,128)(2,1)}, bf16[2,288,768]{2,1,0:T(8,128)(2,1)}, bf16[2,288,768]{2,1,0:T(8,128)(2,1)}, f32[4,8,128]{2,1,0:T(8,128)}) custom-call(s32[2]{0:T(128)} %pad_add_fusion.1.refs_0_, bf16[128,1536]{1,0:T(8,128)(2,1)} %get-tuple-element.184.refs_1_.refs_3_, ...), custom_call_target="tpu_custom_call" | custom-call | flops 4076863488 | bytes 134365184 | tf_op jit(solution)/shard_map/pallas_call | solution.py:158
  296.5 15.8 %all-to-all-done.7 = bf16[4,2,72,1536]{3,2,1,0:T(8,128)(2,1)} async-done(((bf16[4,2,72,1536]{3,2,1,0:T(8,128)(2,1)}), bf16[4,2,72,1536]{3,2,1,0:T(8,128)(2,1)}, u32[]{:S(2)}, u32[]{:S(2)}) %all-to-all-start.7) | async-done | bytes 1769504 | tf_op jit(solution)/shard_map/all_to_all | solution.py:737
  315.9 12.9 %shard_map.248 = (bf16[4,2,72,1536]{3,2,1,0:T(8,128)(2,1)}, bf16[2,288,3840]{2,1,0:T(8,128)(2,1)}) custom-call(s32[2]{0:T(128)} %pad_add_fusion.1.refs_0_, bf16[128,1536]{1,0:T(8,128)(2,1)} %bitcast.195, bf16[128,1536]{1,0:T(8,128)(2,1)} %copy-done.10, bf16[128,1536]{1,0:T(8,128)(2,1)} %copy-done.11, bf16[128,1536]{1,0:T(8,128)(2,1)} %copy-done.12, ...), custom_call_target="tpu_custom_call" | custom-call | flops 4076863488 | bytes 136962048 | tf_op jit(solution)/shard_map/pallas_call | solution.py:158
  336.9 12.7 %shard_map.249 = bf16[16,288,768]{2,1,0:T(8,128)(2,1)} custom-call(bf16[2,576,768]{2,1,0:T(8,128)(2,1)} %shard_map.246.refs_0_, bf16[768,384]{1,0:T(8,128)(2,1)} %fusion.1.refs_1_, bf16[2,288,3840]{2,1,0:T(8,128)(2,1)} %get-tuple-element.205.refs_2_, bf16[2,288,3840]{2,1,0:T(8,128)(2,1)} %collective-permute-done.18.refs_3_), custom_call_target="tpu_custom_call" | custom-call | flops 8153726976 | bytes 18284544 | tf_op jit(solution)/shard_map/pallas_call | solution.py:158
  358.4 19.2 %all-to-all-done.8 = bf16[4,2,72,1536]{3,2,1,0:T(8,128)(2,1)} async-done(((bf16[4,2,72,1536]{3,2,1,0:T(8,128)(2,1)}), bf16[4,2,72,1536]{3,2,1,0:T(8,128)(2,1)}, u32[]{:S(2)}, u32[]{:S(2)}) %all-to-all-start.8) | async-done | bytes 1769504 | tf_op jit(solution)/shard_map/all_to_all | solution.py:737
  384.4 12.0 %all_to_all.90.refs_1_ = bf16[4,128,384]{2,1,0:T(8,128)(2,1)} all-to-all(bf16[4,128,384]{2,1,0:T(8,128)(2,1)} %get-tuple-element.209), channel_id=1, replica_groups=mesh['seq'=4,'fsdp'=32] {'seq'}, dimensions={0} | all-to-all | bytes 786432 | tf_op jit(solution)/shard_map/all_to_all | solution.py:737
  427.8 9.4 %collective-permute-done.19.refs_2_ = bf16[128,1536]{1,0:T(8,128)(2,1)} collective-permute-done((bf16[128,1536]{1,0:T(8,128)(2,1)}, bf16[128,1536]{1,0:T(8,128)(2,1)}, u32[]{:S(2)}, u32[]{:S(2)}) %collective-permute-start.19) | collective-permute-done | bytes 393248 | tf_op jit(solution)/shard_map/ppermute | solution.py:743
  447.4 13.0 %shard_map.255 = (bf16[4,2,72,1536]{3,2,1,0:T(8,128)(2,1)}, bf16[2,288,3840]{2,1,0:T(8,128)(2,1)}) custom-call(s32[2]{0:T(128)} %pad_add_fusion.1.refs_0_, bf16[128,1536]{1,0:T(8,128)(2,1)} %get-tuple-element.221.refs_1_, bf16[128,1536]{1,0:T(8,128)(2,1)} %collective-permute-done.19.refs_2_, bf16[128,1536]{1,0:T(8,128)(2,1)} %collective-permute-done.20.refs_3_, ...), custom_call_target="tpu_custom_call" | custom-call | flops 4076863488 | bytes 122806280 | tf_op jit(solution)/shard_map/pallas_call | solution.py:158
  468.7 13.2 %shard_map.256 = bf16[16,336,768]{2,1,0:T(8,128)(2,1)} custom-call(bf16[2,576,768]{2,1,0:T(8,128)(2,1)} %shard_map.241.refs_0_, bf16[768,384]{1,0:T(8,128)(2,1)} %fusion.1.refs_1_, bf16[2,288,3840]{2,1,0:T(8,128)(2,1)} %get-tuple-element.233.refs_2_, bf16[2,288,3840]{2,1,0:T(8,128)(2,1)} %collective-permute-done.26.refs_3_, ...), custom_call_target="tpu_custom_call" | custom-call | flops 8153726976 | bytes 21823488 | tf_op jit(solution)/shard_map/pallas_call | solution.py:158
  486.1 8.9 %collective-permute-done.23.refs_6_ = bf16[128,1536]{1,0:T(8,128)(2,1)S(1)} collective-permute-done((bf16[128,1536]{1,0:T(8,128)(2,1)S(1)}, bf16[128,1536]{1,0:T(8,128)(2,1)S(1)}, u32[]{:S(2)}, u32[]{:S(2)}) %collective-permute-start.23) | collective-permute-done | bytes 393248 | tf_op jit(solution)/shard_map/ppermute | solution.py:743
  512.8 20.2 %all-to-all-done.11 = bf16[4,2,72,1536]{3,2,1,0:T(8,128)(2,1)} async-done(((bf16[4,2,72,1536]{3,2,1,0:T(8,128)(2,1)}), bf16[4,2,72,1536]{3,2,1,0:T(8,128)(2,1)}, u32[]{:S(2)}, u32[]{:S(2)}) %all-to-all-start.11) | async-done | bytes 1769504 | tf_op jit(solution)/shard_map/all_to_all | solution.py:737
  539.6 12.2 %all_to_all.91.refs_1_ = bf16[4,128,384]{2,1,0:T(8,128)(2,1)} all-to-all(bf16[4,128,384]{2,1,0:T(8,128)(2,1)} %get-tuple-element.238), channel_id=1, replica_groups=mesh['seq'=4,'fsdp'=32] {'seq'}, dimensions={0} | all-to-all | bytes 786432 | tf_op jit(solution)/shard_map/all_to_all | solution.py:737
  596.8 9.0 %all-to-all-done.14 = bf16[16,48,768]{2,1,0:T(8,128)(2,1)} async-done(((bf16[16,48,768]{2,1,0:T(8,128)(2,1)}), bf16[16,48,768]{2,1,0:T(8,128)(2,1)}, u32[]{:S(2)}, u32[]{:S(2)}) %all-to-all-start.14) | async-done | bytes 1179680 | tf_op jit(solution)/shard_map/all_to_all | solution.py:876
  629.5 25.0 %all-to-all-done.15 = bf16[16,64,768]{2,1,0:T(8,128)(2,1)S(1)} async-done(((bf16[16,64,768]{2,1,0:T(8,128)(2,1)}), bf16[16,64,768]{2,1,0:T(8,128)(2,1)S(1)}, u32[]{:S(2)}, u32[]{:S(2)}) %all-to-all-start.15) | async-done | bytes 1572896 | tf_op jit(solution)/shard_map/all_to_all | solution.py:876
  (285 shorter events, 368.4 us)
Async XLA Ops:
  22.6 110.4 %all-gather.7.cloned.1.call-start = ((), (), s32[]{:S(2)}) async-start(), calls=%async_computation.22 | async-start | bytes 19464192 | tf_op jit(solution)/shard_map/all_gather | solution.py:871
  46.0 31.8 %all-to-all-start.1 = ((bf16[16,48,896]{2,1,0:T(8,128)(2,1)}), bf16[16,48,896]{2,1,0:T(8,128)(2,1)S(1)}, u32[]{:S(2)}, u32[]{:S(2)}) async-start(bf16[16,48,896]{2,1,0:T(8,128)(2,1)} %broadcast_in_dim.92), calls=%async_computation.1 | async-start | bytes 2752512 | tf_op jit(solution)/shard_map/all_to_all | solution.py:876
  104.4 27.9 %collective-permute-start.4 = (bf16[128,1536]{1,0:T(8,128)(2,1)S(1)}, bf16[128,1536]{1,0:T(8,128)(2,1)S(1)}, u32[]{:S(2)}, u32[]{:S(2)}) collective-permute-start(bf16[128,1536]{1,0:T(8,128)(2,1)S(1)} %bitcast.196), channel_id=1, source_target_pairs={{32,0},{64,32},{96,64},{0,96},{33,1},{65,33},{97,65},{1,97},{34,2}... | collective-permute-start | bytes 1179656 | tf_op jit(solution)/shard_map/ppermute | solution.py:743
  107.6 24.7 %collective-permute-start.5 = (bf16[128,1536]{1,0:T(8,128)(2,1)S(1)}, bf16[128,1536]{1,0:T(8,128)(2,1)S(1)}, u32[]{:S(2)}, u32[]{:S(2)}) collective-permute-start(bf16[128,1536]{1,0:T(8,128)(2,1)S(1)} %bitcast.197), channel_id=1, source_target_pairs={{64,0},{96,32},{0,64},{32,96},{65,1},{97,33},{1,65},{33,97},{66,2}... | collective-permute-start | bytes 1179656 | tf_op jit(solution)/shard_map/ppermute | solution.py:743
  108.4 23.9 %collective-permute-start.6 = (bf16[128,1536]{1,0:T(8,128)(2,1)S(1)}, bf16[128,1536]{1,0:T(8,128)(2,1)S(1)}, u32[]{:S(2)}, u32[]{:S(2)}) collective-permute-start(bf16[128,1536]{1,0:T(8,128)(2,1)S(1)} %bitcast.198), channel_id=1, source_target_pairs={{96,0},{0,32},{32,64},{64,96},{97,1},{1,33},{33,65},{65,97},{98,2}... | collective-permute-start | bytes 1179656 | tf_op jit(solution)/shard_map/ppermute | solution.py:743
  111.0 21.2 %all-to-all-start.4 = ((bf16[4,128,384]{2,1,0:T(8,128)(2,1)}), bf16[4,128,384]{2,1,0:T(8,128)(2,1)S(1)}, u32[]{:S(2)}, u32[]{:S(2)}) async-start(bf16[4,128,384]{2,1,0:T(8,128)(2,1)} %get-tuple-element.156.refs_9_), calls=%async_computation.4 | async-start | bytes 786432 | tf_op jit(solution)/shard_map/all_to_all | solution.py:737
  114.5 111.3 %all-gather.9.cloned.1.call-start = ((), (), s32[]{:S(2)}) async-start(), calls=%async_computation.23 | async-start | bytes 21897216 | tf_op jit(solution)/shard_map/all_gather | solution.py:871
  141.8 18.7 %collective-permute-start.9 = (bf16[128,1536]{1,0:T(8,128)(2,1)}, bf16[128,1536]{1,0:T(8,128)(2,1)}, u32[]{:S(2)}, u32[]{:S(2)}) collective-permute-start(bf16[128,1536]{1,0:T(8,128)(2,1)} %get-tuple-element.167.refs_1_.refs_3_), channel_id=1, source_target_pairs={{96,0},{0,32},{32,64},{64,96},{97,1},{1,33},{33,65},{65,97},{98,2}... | collective-permute-start | bytes 1179656 | tf_op jit(solution)/shard_map/ppermute | solution.py:743
  171.4 28.2 %all-to-all-start.5 = ((bf16[4,2,72,1536]{3,2,1,0:T(8,128)(2,1)}), bf16[4,2,72,1536]{3,2,1,0:T(8,128)(2,1)}, u32[]{:S(2)}, u32[]{:S(2)}) async-start(bf16[4,2,72,1536]{3,2,1,0:T(8,128)(2,1)} %get-tuple-element.170), calls=%async_computation.5 | async-start | bytes 3538944 | tf_op jit(solution)/shard_map/all_to_all | solution.py:737
  206.5 19.3 %collective-permute-start.13 = (bf16[128,1536]{1,0:T(8,128)(2,1)}, bf16[128,1536]{1,0:T(8,128)(2,1)}, u32[]{:S(2)}, u32[]{:S(2)}) collective-permute-start(bf16[128,1536]{1,0:T(8,128)(2,1)} %get-tuple-element.176.refs_1_), channel_id=1, source_target_pairs={{96,0},{0,32},{32,64},{64,96},{97,1},{1,33},{33,65},{65,97},{98,2}... | collective-permute-start | bytes 1179656 | tf_op jit(solution)/shard_map/ppermute | solution.py:743
  238.2 77.7 %all-gather.11.cloned.1.call-start = ((), (), s32[]{:S(2)}) async-start(), calls=%async_computation.24 | async-start | bytes 14598144 | tf_op jit(solution)/shard_map/all_gather | solution.py:871
  284.0 28.2 %all-to-all-start.7 = ((bf16[4,2,72,1536]{3,2,1,0:T(8,128)(2,1)}), bf16[4,2,72,1536]{3,2,1,0:T(8,128)(2,1)}, u32[]{:S(2)}, u32[]{:S(2)}) async-start(bf16[4,2,72,1536]{3,2,1,0:T(8,128)(2,1)} %get-tuple-element.187), calls=%async_computation.7 | async-start | bytes 3538944 | tf_op jit(solution)/shard_map/all_to_all | solution.py:737
  288.5 193.5 %reduce-scatter.3.cloned.1.call-start = ((), (), s32[]{:S(2)}) async-start(), calls=%async_computation.20 | async-start | bytes 7520256 | tf_op jit(solution)/shard_map/reduce_scatter | solution.py:1082
  349.6 28.0 %all-to-all-start.8 = ((bf16[4,2,72,1536]{3,2,1,0:T(8,128)(2,1)}), bf16[4,2,72,1536]{3,2,1,0:T(8,128)(2,1)}, u32[]{:S(2)}, u32[]{:S(2)}) async-start(bf16[4,2,72,1536]{3,2,1,0:T(8,128)(2,1)} %get-tuple-element.202), calls=%async_computation.8 | async-start | bytes 3538944 | tf_op jit(solution)/shard_map/all_to_all | solution.py:737
  407.4 247.3 %reduce-scatter.5.cloned.1.call-start = ((), (), s32[]{:S(2)}) async-start(), calls=%async_computation.21 | async-start | bytes 8773632 | tf_op jit(solution)/shard_map/reduce_scatter | solution.py:1082
  416.8 30.6 %collective-permute-start.22 = (bf16[16,48,768]{2,1,0:T(8,128)(2,1)}, bf16[16,48,768]{2,1,0:T(8,128)(2,1)}, u32[]{:S(2)}, u32[]{:S(2)}) collective-permute-start(bf16[16,48,768]{2,1,0:T(8,128)(2,1)} %get-tuple-element.220), channel_id=1, source_target_pairs={{0,1},{1,0},{2,3},{3,2},{4,5},{5,4},{6,7},{7,6},{8,9},{9,8},{10,11... | collective-permute-start | bytes 3538952 | tf_op jit(solution)/shard_map/ppermute | solution.py:881
  427.6 19.8 %collective-permute-start.21 = (bf16[128,1536]{1,0:T(8,128)(2,1)}, bf16[128,1536]{1,0:T(8,128)(2,1)}, u32[]{:S(2)}, u32[]{:S(2)}) collective-permute-start(bf16[128,1536]{1,0:T(8,128)(2,1)} %get-tuple-element.221.refs_1_), channel_id=1, source_target_pairs={{96,0},{0,32},{32,64},{64,96},{97,1},{1,33},{33,65},{65,97},{98,2}... | collective-permute-start | bytes 1179656 | tf_op jit(solution)/shard_map/ppermute | solution.py:743
  485.2 19.1 %collective-permute-start.25 = (bf16[128,1536]{1,0:T(8,128)(2,1)S(1)}, bf16[128,1536]{1,0:T(8,128)(2,1)S(1)}, u32[]{:S(2)}, u32[]{:S(2)}) collective-permute-start(bf16[128,1536]{1,0:T(8,128)(2,1)S(1)} %copy-done.25), channel_id=1, source_target_pairs={{96,0},{0,32},{32,64},{64,96},{97,1},{1,33},{33,65},{65,97},{98,2}... | collective-permute-start | bytes 1179656 | tf_op jit(solution)/shard_map/ppermute | solution.py:743
  505.1 27.8 %all-to-all-start.11 = ((bf16[4,2,72,1536]{3,2,1,0:T(8,128)(2,1)}), bf16[4,2,72,1536]{3,2,1,0:T(8,128)(2,1)}, u32[]{:S(2)}, u32[]{:S(2)}) async-start(bf16[4,2,72,1536]{3,2,1,0:T(8,128)(2,1)} %get-tuple-element.231), calls=%async_computation.11 | async-start | bytes 3538944 | tf_op jit(solution)/shard_map/all_to_all | solution.py:737
  578.1 27.7 %all-to-all-start.14 = ((bf16[16,48,768]{2,1,0:T(8,128)(2,1)}), bf16[16,48,768]{2,1,0:T(8,128)(2,1)}, u32[]{:S(2)}, u32[]{:S(2)}) async-start(bf16[16,48,768]{2,1,0:T(8,128)(2,1)} %add_convert_fusion.1), calls=%async_computation.14 | async-start | bytes 2359296 | tf_op jit(solution)/shard_map/all_to_all | solution.py:876
  586.1 21.2 %collective-permute-start.27 = (bf16[128,1536]{1,0:T(8,128)(2,1)}, bf16[128,1536]{1,0:T(8,128)(2,1)}, u32[]{:S(2)}, u32[]{:S(2)}) collective-permute-start(bf16[128,1536]{1,0:T(8,128)(2,1)} %get-tuple-element.249.refs_1_), channel_id=1, source_target_pairs={{32,0},{64,32},{96,64},{0,96},{33,1},{65,33},{97,65},{1,97},{34,2}... | collective-permute-start | bytes 1179656 | tf_op jit(solution)/shard_map/ppermute | solution.py:743
  587.4 19.9 %collective-permute-start.28 = (bf16[128,1536]{1,0:T(8,128)(2,1)}, bf16[128,1536]{1,0:T(8,128)(2,1)}, u32[]{:S(2)}, u32[]{:S(2)}) collective-permute-start(bf16[128,1536]{1,0:T(8,128)(2,1)} %get-tuple-element.249.refs_1_), channel_id=1, source_target_pairs={{64,0},{96,32},{0,64},{32,96},{65,1},{97,33},{1,65},{33,97},{66,2}... | collective-permute-start | bytes 1179656 | tf_op jit(solution)/shard_map/ppermute | solution.py:743
  588.9 19.4 %collective-permute-start.29 = (bf16[128,1536]{1,0:T(8,128)(2,1)}, bf16[128,1536]{1,0:T(8,128)(2,1)}, u32[]{:S(2)}, u32[]{:S(2)}) collective-permute-start(bf16[128,1536]{1,0:T(8,128)(2,1)} %get-tuple-element.249.refs_1_), channel_id=1, source_target_pairs={{96,0},{0,32},{32,64},{64,96},{97,1},{1,33},{33,65},{65,97},{98,2}... | collective-permute-start | bytes 1179656 | tf_op jit(solution)/shard_map/ppermute | solution.py:743
  622.6 31.9 %all-to-all-start.15 = ((bf16[16,64,768]{2,1,0:T(8,128)(2,1)}), bf16[16,64,768]{2,1,0:T(8,128)(2,1)S(1)}, u32[]{:S(2)}, u32[]{:S(2)}) async-start(bf16[16,64,768]{2,1,0:T(8,128)(2,1)} %add_convert_fusion), calls=%async_computation.15 | async-start | bytes 3145728 | tf_op jit(solution)/shard_map/all_to_all | solution.py:876
  (61 other events, 631.0 us)
Sparse Core Ops, SparseCore 0:
  32.9 88.9 all-gather.6
  133.9 82.4 all-gather.8
  247.0 66.2 all-gather.10
  349.7 82.5 reduce-scatter.2
  482.1 85.7 reduce-scatter.4

commit v6 on v5

--- a/solution.py
+++ b/solution.py
@@ -712,13 +712,13 @@
 
 
 def dense_grads_kernel(*refs):
-    blocks, outs = refs[:LAYERS], refs[LAYERS : 2 * LAYERS]
-    query_ref, key_ref, value_ref, out_ref, small_ref = refs[2 * LAYERS :]
-    seq_count, rows, columns = blocks[0].shape
+    blocks, outs = refs[0], refs[1 : 1 + LAYERS]
+    query_ref, key_ref, value_ref, out_ref, small_ref = refs[1 + LAYERS :]
+    seq_count, _, rows, columns = blocks.shape
     local = columns - 3 * HD
     share = seq_count // KVHEADS
     for layer in range(LAYERS):
-        parts = [blocks[layer][s].astype(f32) for s in range(seq_count)]
+        parts = [blocks[s, layer].astype(f32) for s in range(seq_count)]
         for s in range(seq_count):
             query_ref[:, layer, s * local : (s + 1) * local] = parts[s][:, :local]
         for c in range(KVHEADS):
@@ -1020,11 +1020,10 @@
         flops=dense_flops,
     )
 
-    def spread_qkv(block, out_block):
+    def with_gain(block, out_block):
         gain = out_block[dense_rows, :shard_rows]
-        label = jnp.arange(local_width + 3 * HD)[None, :]
-        block = jnp.where(label == local_width + 2 * HD + expert_count, gain[:, None], block)
-        return swap_seq(block.reshape(seq_count, dense_rows, local_width + 3 * HD))
+        label = jnp.arange(half_width)[None, :]
+        return jnp.where(label == local_width + 2 * HD + expert_count, gain[:, None], block)
 
     def shard_sum(blocks):
         own, other = blocks
@@ -1059,9 +1058,6 @@
             pieces={0: (1, local_experts), 1: (0, local_experts)},
             flops=expert_flops,
         )
-        if layer < LAYERS - 1:
-            tied = lax.optimization_barrier((grad_blocks, branches[layer + 1]))
-            grad_rows, branches[layer + 1] = lax.optimization_barrier((grad_rows, around_seq(tied[1])))
         (logits_grad,) = once(
             logits_grad_kernel,
             [shape((2 * expert_count, tok_count), bf16)],
@@ -1076,7 +1072,7 @@
             picked, picks[1], kept, swap_cores(kept), *extra,
             pieces={0: (1, pack_rows // 16)}, flops=2 * expert_flops,
         )
-        sent, packed_too, logits_grad = lax.optimization_barrier((sent, packed, logits_grad))
+        sent, packed, logits_grad = lax.optimization_barrier((sent, packed, logits_grad))
         if layer < LAYERS - 1:
             packed, sums[layer + 1] = lax.optimization_barrier((packed, sums[layer + 1]))
         summed = lax.psum_scatter(
@@ -1096,6 +1092,9 @@
             cut={7: out_cut}, flops=4 * dense_flops,
         )
         grad_heads = swap_seq(send)
+        if layer == 0:
+            tied = lax.optimization_barrier((grad_heads, branch, branches[1]))
+            grad_heads, branches = tied[0], [around_seq(block) for block in tied[1:]]
         (grad_own,) = once(
             attention_back_kernel,
             [shape((seq_count, tok_count, local_width + 2 * HD), bf16)],
@@ -1123,24 +1122,25 @@
             },
             flops=4 * dense_flops,
         )
-        branches[layer], attendeds[layer], sums[layer] = branch, attended, summed
+        attendeds[layer], sums[layer] = attended, summed
         if layer > 0:
+            branches[layer] = branch
             grad_blocks = around_seq(grad_low)
             waiting = (qkv_block_grad[0], swap_cores(qkv_block_grad[1]))
-    qkv_sum = shard_sum(qkv_block_grad)
-    branches[0] = around_seq(branches[0])
-    branches[0], qkv_sum = lax.optimization_barrier((branches[0], qkv_sum))
+    grad_hidden, gains[0], branches = lax.optimization_barrier((grad_hidden, gains[0], branches))
     out_block_grad = once(
         out_weight_kernel,
         [shape((shard_count // 2, 2 * LAYERS * out_rows, half_width), bf16)] * 2,
         place, *branches[0], *branches[1], *attendeds, *gains,
         scalar=True, flops=2 * dense_flops,
     )
-
+    qkv_sum, out_block_grad = lax.optimization_barrier((shard_sum(qkv_block_grad), out_block_grad))
     out_sum = shard_sum(out_block_grad)
     out_sums = [out_sum[2 * out_rows * n : 2 * out_rows * (n + 1)] for n in range(LAYERS)]
-    own_rows = spread_qkv(qkv_sum, out_sums[0])
-    above_rows = spread_qkv(sums[0][local_experts * expert_rows :].astype(f32), out_sums[1])
+    above = sums[0][local_experts * expert_rows :].astype(f32)
+    rows = [with_gain(qkv_sum, out_sums[0]), with_gain(above, out_sums[1])]
+    rows = jnp.stack(rows).reshape(LAYERS, seq_count, dense_rows, half_width)
+    rows = swap_seq(rows.transpose(1, 0, 2, 3))
     gate_grads, up_grads, down_grads = once(
         expert_grads_kernel,
         [
@@ -1160,7 +1160,7 @@
             shape((dense_rows, LAYERS, width), f32),
             shape((LAYERS, dense_rows, HD), f32),
         ],
-        own_rows, above_rows, *out_sums,
+        rows, *out_sums,
     )
     return (
         result[None],

time: 696 us -> 644 us (0.925)
  waiting for transfers between devices: 288 us -> 237 us
    all_to_all x13 -> x12, waiting for transfers between devices: 119 us -> 89.9 us  [swap_seq(): return lax.all_to_all(block, 'seq', split_axis=0, concat_axis=0, tiled=True)]
    ppermute x8, waiting for transfers between devices: 24.9 us -> 9.27 us  [swap_cores(): return lax.ppermute(block, 'fsdp', [(i, i ^ 1) for i in range(shard_count)])]
    all_to_all x3, waiting for transfers between devices: 34.1 us -> 25.1 us  [swap_chips(): lax.all_to_all(block, 'fsdp', split_axis=0, concat_axis=0, tiled=True, ax...]
    all_to_all x13 -> x12, starting transfers between devices: 53.2 us -> 50.5 us  [swap_seq(): return lax.all_to_all(block, 'seq', split_axis=0, concat_axis=0, tiled=True)]
  transfers between devices with their start and end apart: 53 -> 52, of which waited for: 37 -> 33; matrix products, arithmetic and copies ran while one was open for 6% -> 6% of each run, Pallas kernels for 24% -> 28%
where the time goes in v6:
time: 644 us; the launch traced here: 636 us
  waiting for transfers between devices  237 us (37%)
  Pallas kernels  199 us (31%)
  starting transfers between devices  104 us (16%)
  local copies, waits for them, and re-layouts  32.3 us (5%)
  blocking collectives  24.8 us (4%)
  other arithmetic  24.1 us (4%)
  between operations  15 us (2%)
    pallas_call x27, Pallas kernels, once(): pl.pallas_call(body, out_shape=list(outs), in_specs=specs, out_specs=[hbm...  199 us
    ppermute x24, waiting for transfers between devices, around_seq(): lax.ppermute(block, 'seq', [((i + k) % count, i) for i in range(count)])  112 us
    all_to_all x12, waiting for transfers between devices, swap_seq(): return lax.all_to_all(block, 'seq', split_axis=0, concat_axis=0, tiled=True)  89.9 us
    all_to_all x12, starting transfers between devices, swap_seq(): return lax.all_to_all(block, 'seq', split_axis=0, concat_axis=0, tiled=True)  50.5 us
    ppermute x24, starting transfers between devices, around_seq(): lax.ppermute(block, 'seq', [((i + k) % count, i) for i in range(count)])  30.5 us
    all_to_all x3, waiting for transfers between devices, swap_chips(): lax.all_to_all(block, 'fsdp', split_axis=0, concat_axis=0, tiled=True, ax...  25.1 us
    all_to_all x2, blocking collectives, swap_seq(): return lax.all_to_all(block, 'seq', split_axis=0, concat_axis=0, tiled=True)  24.8 us
    all_to_all x3, starting transfers between devices, swap_chips(): lax.all_to_all(block, 'fsdp', split_axis=0, concat_axis=0, tiled=True, ax...  21.6 us
  transfers between devices with their start and end apart: 52, of which 33 were waited for; matrix products, arithmetic and copies ran while one was open for 6% of the time, Pallas kernels for 28%

profile of v6, /device:TPU:0, one launch (start us, length us, event | category | flops | bytes accessed | tf_op | source)
XLA Modules:
  0.0 635.9 jit_solution(10085771687126882020)
XLA Ops:
  23.5 8.2 %all-to-all-done = bf16[4,12,3840]{2,1,0:T(8,128)(2,1)S(1)} async-done(((bf16[4,12,3840]{2,1,0:T(8,128)(2,1)}), bf16[4,12,3840]{2,1,0:T(8,128)(2,1)S(1)}, u32[]{:S(2)}, u32[]{:S(2)}) %all-to-all-start) | async-done | bytes 368672 | tf_op jit(solution)/shard_map/all_to_all | solution.py:737
  63.3 10.7 %collective-permute-done.refs_2_ = bf16[128,1536]{1,0:T(8,128)(2,1)S(1)} collective-permute-done((bf16[128,1536]{1,0:T(8,128)(2,1)S(1)}, bf16[128,1536]{1,0:T(8,128)(2,1)S(1)}, u32[]{:S(2)}, u32[]{:S(2)}) %collective-permute-start) | collective-permute-done | bytes 393248 | tf_op jit(solution)/shard_map/ppermute | solution.py:743
  85.3 11.7 %shard_map.238 = (bf16[4,128,640]{2,1,0:T(8,128)(2,1)}, bf16[4,128,384]{2,1,0:T(8,128)(2,1)}, bf16[4,128,1536]{2,1,0:T(8,128)(2,1)}, bf16[2,16,1536]{2,1,0:T(8,128)(2,1)}) custom-call(s32[2]{0:T(128)} %pad_add_fusion.1.refs_0_, bf16[128,1536]{1,0:T(8,128)(2,1)} %bitcast.201, bf16[128,1536]{1,0:T(8,128)(2,1)} %copy-done.24, bf16[128,1536]{1,0:T(8,128)(2,1)} %copy-done.25, ...), custom_call_target="tpu_custom_call" | custom-call | flops 4026531840 | bytes 8912904 | tf_op jit(solution)/shard_map/pallas_call | solution.py:158
  116.4 15.5 %all-to-all-done.4.refs_0_ = bf16[4,128,384]{2,1,0:T(8,128)(2,1)S(1)} async-done(((bf16[4,128,384]{2,1,0:T(8,128)(2,1)}), bf16[4,128,384]{2,1,0:T(8,128)(2,1)S(1)}, u32[]{:S(2)}, u32[]{:S(2)}) %all-to-all-start.4) | async-done | bytes 393248 | tf_op jit(solution)/shard_map/all_to_all | solution.py:737
  141.7 9.6 %collective-permute-done.7.refs_2_ = bf16[128,1536]{1,0:T(8,128)(2,1)} collective-permute-done((bf16[128,1536]{1,0:T(8,128)(2,1)}, bf16[128,1536]{1,0:T(8,128)(2,1)}, u32[]{:S(2)}, u32[]{:S(2)}) %collective-permute-start.7) | collective-permute-done | bytes 393248 | tf_op jit(solution)/shard_map/ppermute | solution.py:743
  160.2 10.8 %shard_map.240 = (bf16[4,2,72,1536]{3,2,1,0:T(8,128)(2,1)}, bf16[2,288,1536]{2,1,0:T(8,128)(2,1)}, bf16[2,288,768]{2,1,0:T(8,128)(2,1)}, bf16[2,288,768]{2,1,0:T(8,128)(2,1)}, f32[4,8,128]{2,1,0:T(8,128)}) custom-call(s32[2]{0:T(128)} %pad_add_fusion.1.refs_0_, bf16[128,1536]{1,0:T(8,128)(2,1)} %get-tuple-element.174.refs_1_.refs_3_, ...), custom_call_target="tpu_custom_call" | custom-call | flops 4076863488 | bytes 120209416 | tf_op jit(solution)/shard_map/pallas_call | solution.py:158
  182.9 16.4 %all-to-all-done.5 = bf16[4,2,72,1536]{3,2,1,0:T(8,128)(2,1)} async-done(((bf16[4,2,72,1536]{3,2,1,0:T(8,128)(2,1)}), bf16[4,2,72,1536]{3,2,1,0:T(8,128)(2,1)}, u32[]{:S(2)}, u32[]{:S(2)}) %all-to-all-start.5) | async-done | bytes 1769504 | tf_op jit(solution)/shard_map/all_to_all | solution.py:737
  206.7 9.5 %collective-permute-done.11.refs_2_ = bf16[128,1536]{1,0:T(8,128)(2,1)} collective-permute-done((bf16[128,1536]{1,0:T(8,128)(2,1)}, bf16[128,1536]{1,0:T(8,128)(2,1)}, u32[]{:S(2)}, u32[]{:S(2)}) %collective-permute-start.11) | collective-permute-done | bytes 393248 | tf_op jit(solution)/shard_map/ppermute | solution.py:743
  225.5 8.2 %shard_map.243 = (bf16[4,128,640]{2,1,0:T(8,128)(2,1)}, bf16[4,128,384]{2,1,0:T(8,128)(2,1)}, bf16[4,128,1536]{2,1,0:T(8,128)(2,1)}) custom-call(s32[2]{0:T(128)} %pad_add_fusion.1.refs_0_, bf16[128,1536]{1,0:T(8,128)(2,1)} %get-tuple-element.183.refs_1_, bf16[128,1536]{1,0:T(8,128)(2,1)} %collective-permute-done.11.refs_2_, ...), custom_call_target="tpu_custom_call" | custom-call | flops 1610612736 | bytes 27000840 | tf_op jit(solution)/shard_map/pallas_call | solution.py:158
  254.2 9.7 %collective-permute-done.14.refs_2_ = bf16[128,1536]{1,0:T(8,128)(2,1)} collective-permute-done((bf16[128,1536]{1,0:T(8,128)(2,1)}, bf16[128,1536]{1,0:T(8,128)(2,1)}, u32[]{:S(2)}, u32[]{:S(2)}) %collective-permute-start.14) | collective-permute-done | bytes 393248 | tf_op jit(solution)/shard_map/ppermute | solution.py:743
  272.9 10.8 %shard_map.245 = (bf16[4,2,72,1536]{3,2,1,0:T(8,128)(2,1)}, bf16[2,288,1536]{2,1,0:T(8,128)(2,1)}, bf16[2,288,768]{2,1,0:T(8,128)(2,1)}, bf16[2,288,768]{2,1,0:T(8,128)(2,1)}, f32[4,8,128]{2,1,0:T(8,128)}) custom-call(s32[2]{0:T(128)} %pad_add_fusion.1.refs_0_, bf16[128,1536]{1,0:T(8,128)(2,1)} %get-tuple-element.191.refs_1_.refs_3_, ...), custom_call_target="tpu_custom_call" | custom-call | flops 4076863488 | bytes 134365184 | tf_op jit(solution)/shard_map/pallas_call | solution.py:158
  295.9 16.3 %all-to-all-done.7 = bf16[4,2,72,1536]{3,2,1,0:T(8,128)(2,1)} async-done(((bf16[4,2,72,1536]{3,2,1,0:T(8,128)(2,1)}), bf16[4,2,72,1536]{3,2,1,0:T(8,128)(2,1)}, u32[]{:S(2)}, u32[]{:S(2)}) %all-to-all-start.7) | async-done | bytes 1769504 | tf_op jit(solution)/shard_map/all_to_all | solution.py:737
  315.7 12.9 %shard_map.248 = (bf16[4,2,72,1536]{3,2,1,0:T(8,128)(2,1)}, bf16[2,288,3840]{2,1,0:T(8,128)(2,1)}) custom-call(s32[2]{0:T(128)} %pad_add_fusion.1.refs_0_, bf16[128,1536]{1,0:T(8,128)(2,1)} %bitcast.197, bf16[128,1536]{1,0:T(8,128)(2,1)} %copy-done.9, bf16[128,1536]{1,0:T(8,128)(2,1)} %copy-done.10, bf16[128,1536]{1,0:T(8,128)(2,1)} %copy-done.11, ...), custom_call_target="tpu_custom_call" | custom-call | flops 4076863488 | bytes 136962048 | tf_op jit(solution)/shard_map/pallas_call | solution.py:158
  338.1 12.7 %shard_map.249 = bf16[16,288,768]{2,1,0:T(8,128)(2,1)} custom-call(bf16[2,576,768]{2,1,0:T(8,128)(2,1)} %shard_map.246.refs_0_, bf16[768,384]{1,0:T(8,128)(2,1)} %fusion.1.refs_1_, bf16[2,288,3840]{2,1,0:T(8,128)(2,1)} %get-tuple-element.212.refs_2_, bf16[2,288,3840]{2,1,0:T(8,128)(2,1)} %collective-permute-done.18.refs_3_), custom_call_target="tpu_custom_call" | custom-call | flops 8153726976 | bytes 18284544 | tf_op jit(solution)/shard_map/pallas_call | solution.py:158
  363.8 12.4 %all_to_all.85.refs_1_ = bf16[4,128,384]{2,1,0:T(8,128)(2,1)} all-to-all(bf16[4,128,384]{2,1,0:T(8,128)(2,1)} %get-tuple-element.216), channel_id=1, replica_groups=mesh['seq'=4,'fsdp'=32] {'seq'}, dimensions={0} | all-to-all | bytes 786432 | tf_op jit(solution)/shard_map/all_to_all | solution.py:737
  397.3 7.9 %shard_map.254 = (f32[128,1536]{1,0:T(8,128)}, bf16[128,1536]{1,0:T(8,128)(2,1)}, f32[32,128]{1,0:T(8,128)}) custom-call(bf16[4,128,640]{2,1,0:T(8,128)(2,1)} %all-to-all-done.10.refs_0_, bf16[32,288,768]{2,1,0:T(8,128)(2,1)} %bitcast.188, bf16[32,288,768]{2,1,0:T(8,128)(2,1)} %bitcast.189, bf16[32,288,768]{2,1,0:T(8,128)(2,1)} %bitcast.190, ...), custom_call_target="tpu_custom_call" | custom-call | flops 2415919104 | bytes 46235648 | tf_op jit(solution)/shard_map/pallas_call | solution.py:158
  407.9 9.6 %collective-permute-done.19.refs_2_ = bf16[128,1536]{1,0:T(8,128)(2,1)} collective-permute-done((bf16[128,1536]{1,0:T(8,128)(2,1)}, bf16[128,1536]{1,0:T(8,128)(2,1)}, u32[]{:S(2)}, u32[]{:S(2)}) %collective-permute-start.19) | collective-permute-done | bytes 393248 | tf_op jit(solution)/shard_map/ppermute | solution.py:743
  420.3 7.7 %collective-permute-done.21.refs_4_ = bf16[128,1536]{1,0:T(8,128)(2,1)} collective-permute-done((bf16[128,1536]{1,0:T(8,128)(2,1)}, bf16[128,1536]{1,0:T(8,128)(2,1)}, u32[]{:S(2)}, u32[]{:S(2)}) %collective-permute-start.21) | collective-permute-done | bytes 393248 | tf_op jit(solution)/shard_map/ppermute | solution.py:743
  428.0 12.9 %shard_map.255 = (bf16[4,2,72,1536]{3,2,1,0:T(8,128)(2,1)}, bf16[2,288,3840]{2,1,0:T(8,128)(2,1)}) custom-call(s32[2]{0:T(128)} %pad_add_fusion.1.refs_0_, bf16[128,1536]{1,0:T(8,128)(2,1)} %get-tuple-element.228.refs_1_, bf16[128,1536]{1,0:T(8,128)(2,1)} %collective-permute-done.19.refs_2_, bf16[128,1536]{1,0:T(8,128)(2,1)} %collective-permute-done.20.refs_3_, ...), custom_call_target="tpu_custom_call" | custom-call | flops 4076863488 | bytes 122806280 | tf_op jit(solution)/shard_map/pallas_call | solution.py:158
  449.1 13.2 %shard_map.256 = bf16[16,336,768]{2,1,0:T(8,128)(2,1)} custom-call(bf16[2,576,768]{2,1,0:T(8,128)(2,1)} %shard_map.241.refs_0_, bf16[768,384]{1,0:T(8,128)(2,1)} %fusion.1.refs_1_, bf16[2,288,3840]{2,1,0:T(8,128)(2,1)} %get-tuple-element.237.refs_2_, bf16[2,288,3840]{2,1,0:T(8,128)(2,1)} %collective-permute-done.23.refs_3_, ...), custom_call_target="tpu_custom_call" | custom-call | flops 8153726976 | bytes 21823488 | tf_op jit(solution)/shard_map/pallas_call | solution.py:158
  475.8 12.4 %all_to_all.86.refs_1_ = bf16[4,128,384]{2,1,0:T(8,128)(2,1)} all-to-all(bf16[4,128,384]{2,1,0:T(8,128)(2,1)} %get-tuple-element.242), channel_id=1, replica_groups=mesh['seq'=4,'fsdp'=32] {'seq'}, dimensions={0} | all-to-all | bytes 786432 | tf_op jit(solution)/shard_map/all_to_all | solution.py:737
  529.4 11.9 %collective-permute-done.24.refs_2_ = bf16[128,1536]{1,0:T(8,128)(2,1)} collective-permute-done((bf16[128,1536]{1,0:T(8,128)(2,1)}, bf16[128,1536]{1,0:T(8,128)(2,1)}, u32[]{:S(2)}, u32[]{:S(2)}) %collective-permute-start.24) | collective-permute-done | bytes 393248 | tf_op jit(solution)/shard_map/ppermute | solution.py:743
  544.0 7.7 %shard_map.261 = (f32[128,1536]{1,0:T(8,128)}, bf16[128,1536]{1,0:T(8,128)(2,1)}, f32[32,128]{1,0:T(8,128)}) custom-call(bf16[4,128,640]{2,1,0:T(8,128)(2,1)} %all-to-all-done.13.refs_0_, bf16[32,288,768]{2,1,0:T(8,128)(2,1)} %bitcast.191, bf16[32,288,768]{2,1,0:T(8,128)(2,1)} %bitcast.192, bf16[32,288,768]{2,1,0:T(8,128)(2,1)} %bitcast.193, ...), custom_call_target="tpu_custom_call" | custom-call | flops 2415919104 | bytes 45842432 | tf_op jit(solution)/shard_map/pallas_call | solution.py:158
  584.3 25.0 %all-to-all-done.15 = bf16[16,64,768]{2,1,0:T(8,128)(2,1)S(1)} async-done(((bf16[16,64,768]{2,1,0:T(8,128)(2,1)}), bf16[16,64,768]{2,1,0:T(8,128)(2,1)S(1)}, u32[]{:S(2)}, u32[]{:S(2)}) %all-to-all-start.15) | async-done | bytes 1572896 | tf_op jit(solution)/shard_map/all_to_all | solution.py:876
  (276 shorter events, 337.0 us)
Async XLA Ops:
  22.6 110.1 %all-gather.7.cloned.1.call-start = ((), (), s32[]{:S(2)}) async-start(), calls=%async_computation.21 | async-start | bytes 19464192 | tf_op jit(solution)/shard_map/all_gather | solution.py:871
  46.0 31.8 %all-to-all-start.1 = ((bf16[16,48,896]{2,1,0:T(8,128)(2,1)}), bf16[16,48,896]{2,1,0:T(8,128)(2,1)S(1)}, u32[]{:S(2)}, u32[]{:S(2)}) async-start(bf16[16,48,896]{2,1,0:T(8,128)(2,1)} %broadcast_in_dim.92), calls=%async_computation.1 | async-start | bytes 2752512 | tf_op jit(solution)/shard_map/all_to_all | solution.py:876
  104.1 27.9 %collective-permute-start.4 = (bf16[128,1536]{1,0:T(8,128)(2,1)S(1)}, bf16[128,1536]{1,0:T(8,128)(2,1)S(1)}, u32[]{:S(2)}, u32[]{:S(2)}) collective-permute-start(bf16[128,1536]{1,0:T(8,128)(2,1)S(1)} %bitcast.198), channel_id=1, source_target_pairs={{32,0},{64,32},{96,64},{0,96},{33,1},{65,33},{97,65},{1,97},{34,2}... | collective-permute-start | bytes 1179656 | tf_op jit(solution)/shard_map/ppermute | solution.py:743
  107.2 24.7 %collective-permute-start.5 = (bf16[128,1536]{1,0:T(8,128)(2,1)S(1)}, bf16[128,1536]{1,0:T(8,128)(2,1)S(1)}, u32[]{:S(2)}, u32[]{:S(2)}) collective-permute-start(bf16[128,1536]{1,0:T(8,128)(2,1)S(1)} %bitcast.199), channel_id=1, source_target_pairs={{64,0},{96,32},{0,64},{32,96},{65,1},{97,33},{1,65},{33,97},{66,2}... | collective-permute-start | bytes 1179656 | tf_op jit(solution)/shard_map/ppermute | solution.py:743
  108.1 23.9 %collective-permute-start.6 = (bf16[128,1536]{1,0:T(8,128)(2,1)S(1)}, bf16[128,1536]{1,0:T(8,128)(2,1)S(1)}, u32[]{:S(2)}, u32[]{:S(2)}) collective-permute-start(bf16[128,1536]{1,0:T(8,128)(2,1)S(1)} %bitcast.200), channel_id=1, source_target_pairs={{96,0},{0,32},{32,64},{64,96},{97,1},{1,33},{33,65},{65,97},{98,2}... | collective-permute-start | bytes 1179656 | tf_op jit(solution)/shard_map/ppermute | solution.py:743
  110.7 21.2 %all-to-all-start.4 = ((bf16[4,128,384]{2,1,0:T(8,128)(2,1)}), bf16[4,128,384]{2,1,0:T(8,128)(2,1)S(1)}, u32[]{:S(2)}, u32[]{:S(2)}) async-start(bf16[4,128,384]{2,1,0:T(8,128)(2,1)} %get-tuple-element.163.refs_9_), calls=%async_computation.4 | async-start | bytes 786432 | tf_op jit(solution)/shard_map/all_to_all | solution.py:737
  114.2 111.3 %all-gather.9.cloned.1.call-start = ((), (), s32[]{:S(2)}) async-start(), calls=%async_computation.22 | async-start | bytes 21897216 | tf_op jit(solution)/shard_map/all_gather | solution.py:871
  171.2 28.2 %all-to-all-start.5 = ((bf16[4,2,72,1536]{3,2,1,0:T(8,128)(2,1)}), bf16[4,2,72,1536]{3,2,1,0:T(8,128)(2,1)}, u32[]{:S(2)}, u32[]{:S(2)}) async-start(bf16[4,2,72,1536]{3,2,1,0:T(8,128)(2,1)} %get-tuple-element.177), calls=%async_computation.5 | async-start | bytes 3538944 | tf_op jit(solution)/shard_map/all_to_all | solution.py:737
  206.3 19.3 %collective-permute-start.13 = (bf16[128,1536]{1,0:T(8,128)(2,1)}, bf16[128,1536]{1,0:T(8,128)(2,1)}, u32[]{:S(2)}, u32[]{:S(2)}) collective-permute-start(bf16[128,1536]{1,0:T(8,128)(2,1)} %get-tuple-element.183.refs_1_), channel_id=1, source_target_pairs={{96,0},{0,32},{32,64},{64,96},{97,1},{1,33},{33,65},{65,97},{98,2}... | collective-permute-start | bytes 1179656 | tf_op jit(solution)/shard_map/ppermute | solution.py:743
  237.9 77.8 %all-gather.11.cloned.1.call-start = ((), (), s32[]{:S(2)}) async-start(), calls=%async_computation.23 | async-start | bytes 14598144 | tf_op jit(solution)/shard_map/all_gather | solution.py:871
  283.8 28.4 %all-to-all-start.7 = ((bf16[4,2,72,1536]{3,2,1,0:T(8,128)(2,1)}), bf16[4,2,72,1536]{3,2,1,0:T(8,128)(2,1)}, u32[]{:S(2)}, u32[]{:S(2)}) async-start(bf16[4,2,72,1536]{3,2,1,0:T(8,128)(2,1)} %get-tuple-element.194), calls=%async_computation.7 | async-start | bytes 3538944 | tf_op jit(solution)/shard_map/all_to_all | solution.py:737
  328.8 28.4 %all-to-all-start.8 = ((bf16[4,2,72,1536]{3,2,1,0:T(8,128)(2,1)}), bf16[4,2,72,1536]{3,2,1,0:T(8,128)(2,1)}, u32[]{:S(2)}, u32[]{:S(2)}) async-start(bf16[4,2,72,1536]{3,2,1,0:T(8,128)(2,1)} %get-tuple-element.209), calls=%async_computation.8 | async-start | bytes 3538944 | tf_op jit(solution)/shard_map/all_to_all | solution.py:737
  333.4 135.8 %reduce-scatter.3.cloned.1.call-start = ((), (), s32[]{:S(2)}) async-start(), calls=%async_computation.19 | async-start | bytes 7520256 | tf_op jit(solution)/shard_map/reduce_scatter | solution.py:1078
  397.3 30.7 %collective-permute-start.22 = (bf16[16,48,768]{2,1,0:T(8,128)(2,1)}, bf16[16,48,768]{2,1,0:T(8,128)(2,1)}, u32[]{:S(2)}, u32[]{:S(2)}) collective-permute-start(bf16[16,48,768]{2,1,0:T(8,128)(2,1)} %get-tuple-element.227), channel_id=1, source_target_pairs={{0,1},{1,0},{2,3},{3,2},{4,5},{5,4},{6,7},{7,6},{8,9},{9,8},{10,11... | collective-permute-start | bytes 3538952 | tf_op jit(solution)/shard_map/ppermute | solution.py:881
  407.9 20.1 %collective-permute-start.21 = (bf16[128,1536]{1,0:T(8,128)(2,1)}, bf16[128,1536]{1,0:T(8,128)(2,1)}, u32[]{:S(2)}, u32[]{:S(2)}) collective-permute-start(bf16[128,1536]{1,0:T(8,128)(2,1)} %get-tuple-element.228.refs_1_), channel_id=1, source_target_pairs={{96,0},{0,32},{32,64},{64,96},{97,1},{1,33},{33,65},{65,97},{98,2}... | collective-permute-start | bytes 1179656 | tf_op jit(solution)/shard_map/ppermute | solution.py:743
  441.0 28.2 %all-to-all-start.11 = ((bf16[4,2,72,1536]{3,2,1,0:T(8,128)(2,1)}), bf16[4,2,72,1536]{3,2,1,0:T(8,128)(2,1)}, u32[]{:S(2)}, u32[]{:S(2)}) async-start(bf16[4,2,72,1536]{3,2,1,0:T(8,128)(2,1)} %get-tuple-element.235), calls=%async_computation.11 | async-start | bytes 3538944 | tf_op jit(solution)/shard_map/all_to_all | solution.py:737
  445.4 164.2 %reduce-scatter.5.cloned.1.call-start = ((), (), s32[]{:S(2)}) async-start(), calls=%async_computation.20 | async-start | bytes 8773632 | tf_op jit(solution)/shard_map/reduce_scatter | solution.py:1078
  515.0 54.3 %all-to-all-start.14 = ((bf16[16,48,768]{2,1,0:T(8,128)(2,1)}), bf16[16,48,768]{2,1,0:T(8,128)(2,1)}, u32[]{:S(2)}, u32[]{:S(2)}) async-start(bf16[16,48,768]{2,1,0:T(8,128)(2,1)} %add_convert_fusion.1), calls=%async_computation.14 | async-start | bytes 2359296 | tf_op jit(solution)/shard_map/all_to_all | solution.py:876
  523.9 27.9 %collective-permute-start.25 = (bf16[128,1536]{1,0:T(8,128)(2,1)}, bf16[128,1536]{1,0:T(8,128)(2,1)}, u32[]{:S(2)}, u32[]{:S(2)}) collective-permute-start(bf16[128,1536]{1,0:T(8,128)(2,1)} %get-tuple-element.259.refs_1_), channel_id=1, source_target_pairs={{64,0},{96,32},{0,64},{32,96},{65,1},{97,33},{1,65},{33,97},{66,2}... | collective-permute-start | bytes 1179656 | tf_op jit(solution)/shard_map/ppermute | solution.py:743
  525.3 26.4 %collective-permute-start.26 = (bf16[128,1536]{1,0:T(8,128)(2,1)}, bf16[128,1536]{1,0:T(8,128)(2,1)}, u32[]{:S(2)}, u32[]{:S(2)}) collective-permute-start(bf16[128,1536]{1,0:T(8,128)(2,1)} %get-tuple-element.259.refs_1_), channel_id=1, source_target_pairs={{96,0},{0,32},{32,64},{64,96},{97,1},{1,33},{33,65},{65,97},{98,2}... | collective-permute-start | bytes 1179656 | tf_op jit(solution)/shard_map/ppermute | solution.py:743
  525.3 26.6 %collective-permute-start.27 = (bf16[128,1536]{1,0:T(8,128)(2,1)}, bf16[128,1536]{1,0:T(8,128)(2,1)}, u32[]{:S(2)}, u32[]{:S(2)}) collective-permute-start(bf16[128,1536]{1,0:T(8,128)(2,1)} %get-tuple-element.263.refs_5_), channel_id=1, source_target_pairs={{32,0},{64,32},{96,64},{0,96},{33,1},{65,33},{97,65},{1,97},{34,2}... | collective-permute-start | bytes 1179656 | tf_op jit(solution)/shard_map/ppermute | solution.py:743
  528.6 26.1 %collective-permute-start.28 = (bf16[128,1536]{1,0:T(8,128)(2,1)}, bf16[128,1536]{1,0:T(8,128)(2,1)}, u32[]{:S(2)}, u32[]{:S(2)}) collective-permute-start(bf16[128,1536]{1,0:T(8,128)(2,1)} %get-tuple-element.263.refs_5_), channel_id=1, source_target_pairs={{64,0},{96,32},{0,64},{32,96},{65,1},{97,33},{1,65},{33,97},{66,2}... | collective-permute-start | bytes 1179656 | tf_op jit(solution)/shard_map/ppermute | solution.py:743
  541.3 20.3 %collective-permute-start.29 = (bf16[128,1536]{1,0:T(8,128)(2,1)}, bf16[128,1536]{1,0:T(8,128)(2,1)}, u32[]{:S(2)}, u32[]{:S(2)}) collective-permute-start(bf16[128,1536]{1,0:T(8,128)(2,1)} %get-tuple-element.263.refs_5_), channel_id=1, source_target_pairs={{96,0},{0,32},{32,64},{64,96},{97,1},{1,33},{33,65},{65,97},{98,2}... | collective-permute-start | bytes 1179656 | tf_op jit(solution)/shard_map/ppermute | solution.py:743
  577.5 31.8 %all-to-all-start.15 = ((bf16[16,64,768]{2,1,0:T(8,128)(2,1)}), bf16[16,64,768]{2,1,0:T(8,128)(2,1)S(1)}, u32[]{:S(2)}, u32[]{:S(2)}) async-start(bf16[16,64,768]{2,1,0:T(8,128)(2,1)} %add_convert_fusion), calls=%async_computation.15 | async-start | bytes 3145728 | tf_op jit(solution)/shard_map/all_to_all | solution.py:876
  (55 other events, 607.1 us)
Sparse Core Ops, SparseCore 0:
  32.9 88.9 all-gather.6
  133.6 82.3 all-gather.8
  246.7 66.0 all-gather.10
  357.3 82.4 reduce-scatter.2
  469.3 95.1 reduce-scatter.4

commit v7 on v6

--- a/solution.py
+++ b/solution.py
@@ -350,12 +350,14 @@
 
 
 def after_attention_kernel(
-    back, spread, hidden, small, out_w, routes_t, middle_ref, normed_ref, gates_ref
+    back, spread, hidden, small, out_w, routes_t, middle_ref, normed_ref, gates_ref, attended_ref
 ):
     expert_count = 8
     seq_count, tokens, part = back.shape
     width = seq_count * part
     attended = to_gathered([back[s] for s in range(seq_count)], spread[...]).astype(bf16)
+    attended_ref[...] = attended
+    attended_ref.send()
     rows = out_w.shape[1] // 2
     half = out_w.shape[2]
     for side in range(2):
@@ -481,15 +483,17 @@
         out_ref.send(e)
 
 
-def pick_kernel(rows, other_rows, pick, out_ref):
+def pick_kernel(rows, other_rows, attended, other_attended, pick, out_ref, attended_ref):
     count = rows.shape[1]
     for e in range(rows.shape[0]):
         out_ref[e, :count] = nn(rows[e], pick[...]).astype(bf16)
         out_ref[e, count:] = nn(other_rows[e], pick[...]).astype(bf16)
         out_ref.send(e)
-
-
-def expert_weight_kernel(tokens, pick_inner, keep, other_keep, *rest):
+    both = jnp.concatenate([attended[...], other_attended[...]], axis=0)
+    attended_ref[...] = nn(both, pick[...]).astype(bf16)
+
+
+def expert_weight_kernel(core, tokens, pick_inner, keep, other_keep, *rest):
     pack_ref = rest[-1]
     chips, _, half = pack_ref.shape
     experts = tokens.shape[0]
@@ -517,9 +521,35 @@
         send()
         at += count
     if len(rest) > 1:
-        own, other = rest[:2]
-        pack_ref[:, at : at + count] = (own[...].astype(f32) + other[...].astype(f32)).astype(bf16)
-        send()
+        dense_part(core[0], rest[:-1], pack_ref, at)
+
+
+def dense_kernel(core, *refs):
+    dense_part(core[0], refs[:-1], refs[-1], 0)
+
+
+def dense_part(core, refs, pack_ref, at):
+    qkv, other_qkv, gain, other_gain, spread, attended, branch, other_branch = refs
+    expert_count = 8
+    chips, rows, half = qkv.shape
+    width = gain.shape[1]
+    blocks = column_blocks((gain[...] + other_gain[...]).astype(bf16), width // spread.shape[0])
+    gains = to_gathered(blocks, spread[...])
+    count = gains.shape[0]
+    gains = jnp.where(lax.broadcasted_iota(jnp.int32, gains.shape, 0) == 0, gains, 0.0)
+    below = jnp.zeros((HD - expert_count - count, width), f32)
+    gains = jnp.concatenate([jnp.zeros((expert_count, width), f32), gains, below], axis=0).T
+    gains = gains.reshape(chips, 2, rows, HD)
+    gains = jnp.where(core == 0, gains[:, 0], gains[:, 1])
+    total = qkv[...].astype(f32) + other_qkv[...].astype(f32)
+    pack_ref[:, at : at + rows, : half - HD] = total[:, :, : half - HD].astype(bf16)
+    pack_ref[:, at : at + rows, half - HD :] = (total[:, :, half - HD :] + gains).astype(bf16)
+    grads = jnp.concatenate([branch[...], other_branch[...]], axis=0)
+    total = tn(attended[...], grads).astype(bf16)
+    for side in range(2):
+        at += rows
+        block = total[:, side * half : (side + 1) * half]
+        pack_ref[:, at : at + rows] = block.reshape(chips, rows, half)
 
 
 def keep_shards(own_ref, other_ref, core, at, value):
@@ -636,20 +666,10 @@
     low_ref.send()
     out_ref[...] = total
     out_ref.send()
-    shards = gain_ref.shape[0]
-    width = grad_gain.shape[1]
-    share = width // seq_count
-    part = share // shards
-    shard = lax.broadcasted_iota(jnp.int32, (shards, width), 0)
-    at = lax.broadcasted_iota(jnp.int32, (shards, width), 1)
-    kept = jnp.where(at % share // part == shard, grad_gain, 0.0).astype(bf16)
-    source = lax.broadcasted_iota(jnp.int32, (width, HD), 0)
-    wanted = lax.broadcasted_iota(jnp.int32, (width, HD), 1)
-    place = source // share * part + source % part
-    gain_ref[...] = nn(kept, jnp.where(place == wanted, 1.0, 0.0).astype(bf16))
-
-
-def qkv_weight_kernel(place, normed, grads, small, spread, own_ref, other_ref):
+    gain_ref[...] = jnp.broadcast_to(grad_gain, gain_ref.shape)
+
+
+def qkv_weight_kernel(core, normed, grads, small, spread, own_ref, other_ref):
     seq_count, tokens, columns = grads.shape
     chips, rows, wide = own_ref.shape
     shards = 2 * chips
@@ -659,41 +679,7 @@
     extra = to_gathered(extra, spread[...])
     extra = jnp.concatenate([extra, jnp.zeros((HD - extra.shape[0], extra.shape[1]), f32)], axis=0).T
     total = jnp.concatenate([total, extra], axis=1).astype(bf16).reshape(shards, rows, wide)
-    keep_shards(own_ref, other_ref, place[1], 0, total)
-
-
-def out_weight_kernel(place, *rest):
-    own_ref, other_ref = rest[-2:]
-    rest = rest[:-2]
-    me = place[0]
-    around = len(rest) // LAYERS - 2
-    blocks, rest = rest[: LAYERS * around], rest[LAYERS * around :]
-    chips, rows, half = own_ref.shape
-    shards = 2 * chips
-    rows = rows // (2 * LAYERS)
-    for layer in range(LAYERS):
-        attended, gain = rest[layer], rest[LAYERS + layer]
-        seq_count, tokens, part = attended.shape
-        valid = part // shards
-        branch = [block[...] for block in blocks[layer * around : (layer + 1) * around]]
-        branch = jnp.concatenate(branch, axis=0)
-        heads = jnp.concatenate(
-            [attended[lax.rem(me + k, seq_count)] for k in range(seq_count)], axis=0
-        )
-        place_in = lax.broadcasted_iota(jnp.int32, (part, shards * rows), 0)
-        place_out = lax.broadcasted_iota(jnp.int32, (part, shards * rows), 1)
-        source = place_out // rows * valid + place_out % rows
-        same = jnp.logical_and(place_in == source, place_out % rows < valid)
-        heads = nn(heads, jnp.where(same, 1.0, 0.0).astype(bf16)).astype(bf16)
-        wide = jnp.concatenate([gain[...], jnp.zeros((shards, half - HD), f32)], axis=1)
-        row = lax.broadcasted_iota(jnp.int32, (shards, rows, half), 1)
-        for side in range(2):
-            total = tn(heads, branch[:, side * half : (side + 1) * half])
-            total = total.reshape(shards, rows, half)
-            if side == 0:
-                total = jnp.where(row == valid, wide[:, None, :], total)
-            at = (2 * layer + side) * rows
-            keep_shards(own_ref, other_ref, place[1], at, total.astype(bf16))
+    keep_shards(own_ref, other_ref, core[0], 0, total)
 
 
 def expert_grads_kernel(*refs):
@@ -712,13 +698,13 @@
 
 
 def dense_grads_kernel(*refs):
-    blocks, outs = refs[0], refs[1 : 1 + LAYERS]
-    query_ref, key_ref, value_ref, out_ref, small_ref = refs[1 + LAYERS :]
-    seq_count, _, rows, columns = blocks.shape
+    blocks = refs[0]
+    query_ref, key_ref, value_ref, out_ref, small_ref = refs[1:]
+    seq_count, _, _, rows, columns = blocks.shape
     local = columns - 3 * HD
     share = seq_count // KVHEADS
     for layer in range(LAYERS):
-        parts = [blocks[s, layer].astype(f32) for s in range(seq_count)]
+        parts = [blocks[s, layer, 0].astype(f32) for s in range(seq_count)]
         for s in range(seq_count):
             query_ref[:, layer, s * local : (s + 1) * local] = parts[s][:, :local]
         for c in range(KVHEADS):
@@ -727,10 +713,10 @@
             value_ref[:, layer, c * HD : (c + 1) * HD] = total[:, local + HD : local + 2 * HD]
         total = functools.reduce(jnp.add, parts)
         small_ref[layer] = total[:, local + 2 * HD :]
-        block = outs[layer][...].astype(f32)
-        half = block.shape[1]
-        out_ref[:, layer, :half] = block[:rows]
-        out_ref[:, layer, half:] = block[block.shape[0] // 2 :][:rows]
+        for side in range(2):
+            sides = [blocks[s, layer, 1 + side].astype(f32) for s in range(seq_count)]
+            total = functools.reduce(jnp.add, sides)
+            out_ref[:, layer, side * columns : (side + 1) * columns] = total
 
 
 def swap_seq(block):
@@ -774,7 +760,8 @@
     shard_count = lax.axis_size("fsdp")
     seq_index = lax.axis_index("seq")
     core = lax.rem(lax.axis_index("fsdp"), 2)
-    place = jnp.stack([seq_index, core]).astype(jnp.int32)
+    place = jnp.full((1,), seq_index, jnp.int32)
+    core_place = jnp.full((1,), core, jnp.int32)
     group_tok = seq_count * tok_count
     prompt_len = group_tok - segment_ids.shape[1]
     local_experts = w_gate.shape[1]
@@ -971,12 +958,13 @@
             qkv_parts = jnp.concatenate(qkv_part(dense) + qkv_part(next_dense), axis=0)
             qkv_parts, back = lax.optimization_barrier((qkv_parts, back))
             qkv_w = fetch([qkv_parts])
-        middle, normed_ffn, gates_t = once(
+        middle, normed_ffn, gates_t, attended_p = once(
             after_attention_kernel,
             [
                 shape((tok_count, width), f32),
                 shape((tok_count, width), bf16),
                 shape((2 * TOPK, tok_count), f32),
+                shape((tok_count, width), bf16),
             ],
             back, spread, hidden, small, pack, routes_t,
             cut={4: out_cut}, flops=3 * dense_flops,
@@ -997,10 +985,13 @@
             pieces={n: (1 if n == 0 else 0, local_experts) for n in range(4)},
             flops=expert_flops,
         )
-        (picked,) = once(
+        picked = once(
             pick_kernel,
-            [shape((local_experts, 2 * slot_rows, width // 2), bf16)],
-            received, swap_cores(received), picks[0],
+            [
+                shape((local_experts, 2 * slot_rows, width // 2), bf16),
+                shape((2 * tok_count, width // 2), bf16),
+            ],
+            received, swap_cores(received), attended_p, swap_cores(attended_p), picks[0],
             pieces={0: (0, local_experts)}, flops=expert_flops // 3,
         )
         combined, picked = lax.optimization_barrier(
@@ -1010,7 +1001,7 @@
         records.append(
             (
                 (pack, small, routes_t, target_t),
-                (hidden, normed_all, heads, attended),
+                (hidden, normed_all, heads),
                 (middle, normed_ffn, gates_t, combined),
                 (picked, gate_val, up_val, all_gates),
             )
@@ -1020,27 +1011,14 @@
         flops=dense_flops,
     )
 
-    def with_gain(block, out_block):
-        gain = out_block[dense_rows, :shard_rows]
-        label = jnp.arange(half_width)[None, :]
-        return jnp.where(label == local_width + 2 * HD + expert_count, gain[:, None], block)
-
-    def shard_sum(blocks):
-        own, other = blocks
-        block = (own.astype(f32) + swap_cores(other).astype(f32)).astype(bf16)
-        return jnp.sum(swap_chips(block).astype(f32), axis=0)
-
-    out_rows = 16
-
     grad_hidden = cotangent[0].astype(f32)
-    sums, gains = [None] * LAYERS, [None] * LAYERS
-    branches, attendeds = [None] * LAYERS, [None] * LAYERS
+    sums = [None] * LAYERS
     waiting = None
     for layer in range(LAYERS - 1, -1, -1):
         weights, attn_saved, mid_saved, expert_saved = records[layer]
         pack, small, routes_t, target_t = weights
         row = layer * 3 * shard_rows
-        below, normed_all, heads, attended = attn_saved
+        below, normed_all, heads = attn_saved
         middle, normed_ffn, gates_t, combined = mid_saved
         picked, gate_val, up_val, all_gates = expert_saved
         if waiting is None:
@@ -1065,12 +1043,12 @@
         )
         sent = swap_seq(grad_rows)
         extra = () if layer == LAYERS - 1 else waiting
-        pack_rows = local_experts * expert_rows + (shard_rows if extra else 0)
+        pack_rows = local_experts * expert_rows + (3 * shard_rows if extra else 0)
         (packed,) = once(
             expert_weight_kernel,
             [shape((shard_count // 2, pack_rows, half_width), bf16)],
-            picked, picks[1], kept, swap_cores(kept), *extra,
-            pieces={0: (1, pack_rows // 16)}, flops=2 * expert_flops,
+            core_place, picked[0], picks[1], kept, swap_cores(kept), *extra,
+            scalar=True, pieces={0: (1, pack_rows // 16)}, flops=2 * expert_flops,
         )
         sent, packed, logits_grad = lax.optimization_barrier((sent, packed, logits_grad))
         if layer < LAYERS - 1:
@@ -1092,9 +1070,6 @@
             cut={7: out_cut}, flops=4 * dense_flops,
         )
         grad_heads = swap_seq(send)
-        if layer == 0:
-            tied = lax.optimization_barrier((grad_heads, branch, branches[1]))
-            grad_heads, branches = tied[0], [around_seq(block) for block in tied[1:]]
         (grad_own,) = once(
             attention_back_kernel,
             [shape((seq_count, tok_count, local_width + 2 * HD), bf16)],
@@ -1104,15 +1079,15 @@
         qkv_block_grad = once(
             qkv_weight_kernel,
             [shape((shard_count // 2, shard_rows, half_width), bf16)] * 2,
-            place, normed_all, grad_own, small_grad, spread, scalar=True, flops=2 * dense_flops,
+            core_place, normed_all, grad_own, small_grad, spread, scalar=True, flops=2 * dense_flops,
         )
         sent, qkv_block_grad = lax.optimization_barrier((swap_seq(grad_own), qkv_block_grad))
-        grad_hidden, grad_low, gains[layer] = once(
+        grad_hidden, grad_low, gain_grad = once(
             before_attention_kernel,
             [
                 shape((tok_count, width), f32),
                 shape((tok_count, width), bf16),
-                shape((shard_count, HD), f32),
+                shape((8, width), f32),
             ],
             sent, qkv_w, qkv_w, qkv_w, spread, small, below, grad_middle,
             cut={
@@ -1122,25 +1097,22 @@
             },
             flops=4 * dense_flops,
         )
-        attendeds[layer], sums[layer] = attended, summed
+        sums[layer] = summed
+        dense_sources = (
+            qkv_block_grad[0], swap_cores(qkv_block_grad[1]), gain_grad, swap_cores(gain_grad),
+            spread, picked[1], branch, swap_cores(branch),
+        )
         if layer > 0:
-            branches[layer] = branch
-            grad_blocks = around_seq(grad_low)
-            waiting = (qkv_block_grad[0], swap_cores(qkv_block_grad[1]))
-    grad_hidden, gains[0], branches = lax.optimization_barrier((grad_hidden, gains[0], branches))
-    out_block_grad = once(
-        out_weight_kernel,
-        [shape((shard_count // 2, 2 * LAYERS * out_rows, half_width), bf16)] * 2,
-        place, *branches[0], *branches[1], *attendeds, *gains,
-        scalar=True, flops=2 * dense_flops,
+            grad_blocks, waiting = around_seq(grad_low), dense_sources
+    (dense_pack,) = once(
+        dense_kernel,
+        [shape((shard_count // 2, 3 * shard_rows, half_width), bf16)],
+        core_place, *dense_sources, scalar=True, flops=2 * dense_flops,
     )
-    qkv_sum, out_block_grad = lax.optimization_barrier((shard_sum(qkv_block_grad), out_block_grad))
-    out_sum = shard_sum(out_block_grad)
-    out_sums = [out_sum[2 * out_rows * n : 2 * out_rows * (n + 1)] for n in range(LAYERS)]
-    above = sums[0][local_experts * expert_rows :].astype(f32)
-    rows = [with_gain(qkv_sum, out_sums[0]), with_gain(above, out_sums[1])]
-    rows = jnp.stack(rows).reshape(LAYERS, seq_count, dense_rows, half_width)
-    rows = swap_seq(rows.transpose(1, 0, 2, 3))
+    dense_sum = jnp.sum(swap_chips(dense_pack).astype(f32), axis=0).astype(bf16)
+    rows = jnp.stack([dense_sum, sums[0][local_experts * expert_rows :]])
+    rows = rows.reshape(LAYERS, 3, seq_count, dense_rows, half_width).transpose(2, 0, 1, 3, 4)
+    rows = swap_seq(rows)
     gate_grads, up_grads, down_grads = once(
         expert_grads_kernel,
         [
@@ -1160,7 +1132,7 @@
             shape((dense_rows, LAYERS, width), f32),
             shape((LAYERS, dense_rows, HD), f32),
         ],
-        rows, *out_sums,
+        rows,
     )
     return (
         result[None],

time: 644 us -> 617 us (0.958)
  waiting for transfers between devices: 237 us -> 170 us
  blocking collectives: 24.8 us -> 87.9 us
  starting transfers between devices: 104 us -> 88.6 us
  other arithmetic: 24.1 us -> 16.4 us
    all_to_all x0 -> x1, blocking collectives: none -> 62.9 us  [swap_chips(): lax.all_to_all(block, 'fsdp', split_axis=0, concat_axis=0, tiled=True, ax...]
    ppermute x24 -> x18, waiting for transfers between devices: 112 us -> 80.2 us  [around_seq(): lax.ppermute(block, 'seq', [((i + k) % count, i) for i in range(count)])]
    all_to_all x3 -> x1, waiting for transfers between devices: 25.1 us -> 0.01 us  [swap_chips(): lax.all_to_all(block, 'fsdp', split_axis=0, concat_axis=0, tiled=True, ax...]
    all_to_all x3 -> x1, starting transfers between devices: 21.6 us -> 7.17 us  [swap_chips(): lax.all_to_all(block, 'fsdp', split_axis=0, concat_axis=0, tiled=True, ax...]
    all_to_all x12, waiting for transfers between devices: 89.9 us -> 80.6 us  [swap_seq(): return lax.all_to_all(block, 'seq', split_axis=0, concat_axis=0, tiled=True)]
    ppermute x24 -> x18, starting transfers between devices: 30.5 us -> 26.5 us  [around_seq(): lax.ppermute(block, 'seq', [((i + k) % count, i) for i in range(count)])]
  transfers between devices with their start and end apart: 52 -> 49, of which waited for: 33 -> 27; matrix products, arithmetic and copies ran while one was open for 6% -> 5% of each run, Pallas kernels for 28% -> 28%
where the time goes in v7:
time: 617 us; the launch traced here: 610 us
  Pallas kernels  195 us (32%)
  waiting for transfers between devices  170 us (28%)
  starting transfers between devices  88.6 us (14%)
  blocking collectives  87.9 us (14%)
  local copies, waits for them, and re-layouts  36.8 us (6%)
  other arithmetic  16.4 us (3%)
  between operations  15 us (2%)
    pallas_call x27, Pallas kernels, once(): pl.pallas_call(body, out_shape=list(outs), in_specs=specs, out_specs=[hbm...  195 us
    all_to_all x12, waiting for transfers between devices, swap_seq(): return lax.all_to_all(block, 'seq', split_axis=0, concat_axis=0, tiled=True)  80.6 us
    ppermute x18, waiting for transfers between devices, around_seq(): lax.ppermute(block, 'seq', [((i + k) % count, i) for i in range(count)])  80.2 us
    all_to_all x1, blocking collectives, swap_chips(): lax.all_to_all(block, 'fsdp', split_axis=0, concat_axis=0, tiled=True, ax...  62.9 us
    all_to_all x12, starting transfers between devices, swap_seq(): return lax.all_to_all(block, 'seq', split_axis=0, concat_axis=0, tiled=True)  50.4 us
    ppermute x18, starting transfers between devices, around_seq(): lax.ppermute(block, 'seq', [((i + k) % count, i) for i in range(count)])  26.5 us
    all_to_all x2, blocking collectives, swap_seq(): return lax.all_to_all(block, 'seq', split_axis=0, concat_axis=0, tiled=True)  24.9 us
  transfers between devices with their start and end apart: 49, of which 27 were waited for; matrix products, arithmetic and copies ran while one was open for 5% of the time, Pallas kernels for 28%

profile of v7, /device:TPU:0, one launch (start us, length us, event | category | flops | bytes accessed | tf_op | source)
XLA Modules:
  0.0 609.7 jit_solution(18064633257429700078)
XLA Ops:
  23.5 8.2 %all-to-all-done = bf16[4,12,3840]{2,1,0:T(8,128)(2,1)S(1)} async-done(((bf16[4,12,3840]{2,1,0:T(8,128)(2,1)}), bf16[4,12,3840]{2,1,0:T(8,128)(2,1)S(1)}, u32[]{:S(2)}, u32[]{:S(2)}) %all-to-all-start) | async-done | bytes 368672 | tf_op jit(solution)/shard_map/all_to_all | solution.py:723
  69.6 7.4 %collective-permute-done.1.refs_3_ = bf16[128,1536]{1,0:T(8,128)(2,1)S(1)} collective-permute-done((bf16[128,1536]{1,0:T(8,128)(2,1)S(1)}, bf16[128,1536]{1,0:T(8,128)(2,1)S(1)}, u32[]{:S(2)}, u32[]{:S(2)}) %collective-permute-start.1) | collective-permute-done | bytes 393248 | tf_op jit(solution)/shard_map/ppermute | solution.py:729
  85.4 11.3 %shard_map.238 = (bf16[4,128,640]{2,1,0:T(8,128)(2,1)}, bf16[4,128,384]{2,1,0:T(8,128)(2,1)}, bf16[4,128,1536]{2,1,0:T(8,128)(2,1)}, bf16[2,16,1536]{2,1,0:T(8,128)(2,1)}) custom-call(s32[1]{0:T(128)} %bitcast.23.refs_0_, bf16[128,1536]{1,0:T(8,128)(2,1)} %bitcast.197, bf16[128,1536]{1,0:T(8,128)(2,1)} %collective-permute-done.refs_2_, ...), custom_call_target="tpu_custom_call" | custom-call | flops 4026531840 | bytes 8912900 | tf_op jit(solution)/shard_map/pallas_call | solution.py:158
  117.0 14.4 %all-to-all-done.4.refs_0_ = bf16[4,128,384]{2,1,0:T(8,128)(2,1)S(1)} async-done(((bf16[4,128,384]{2,1,0:T(8,128)(2,1)}), bf16[4,128,384]{2,1,0:T(8,128)(2,1)S(1)}, u32[]{:S(2)}, u32[]{:S(2)}) %all-to-all-start.4) | async-done | bytes 393248 | tf_op jit(solution)/shard_map/all_to_all | solution.py:723
  142.0 9.3 %collective-permute-done.9.refs_4_ = bf16[128,1536]{1,0:T(8,128)(2,1)} collective-permute-done((bf16[128,1536]{1,0:T(8,128)(2,1)}, bf16[128,1536]{1,0:T(8,128)(2,1)}, u32[]{:S(2)}, u32[]{:S(2)}) %collective-permute-start.9) | collective-permute-done | bytes 393248 | tf_op jit(solution)/shard_map/ppermute | solution.py:729
  158.9 10.1 %shard_map.240 = (bf16[4,2,72,1536]{3,2,1,0:T(8,128)(2,1)}, bf16[2,288,1536]{2,1,0:T(8,128)(2,1)}, bf16[2,288,768]{2,1,0:T(8,128)(2,1)}, bf16[2,288,768]{2,1,0:T(8,128)(2,1)}, f32[4,8,128]{2,1,0:T(8,128)}) custom-call(s32[1]{0:T(128)} %bitcast.23.refs_0_, bf16[128,1536]{1,0:T(8,128)(2,1)} %get-tuple-element.170.refs_1_.refs_3_, ...), custom_call_target="tpu_custom_call" | custom-call | flops 4076863488 | bytes 120209408 | tf_op jit(solution)/shard_map/pallas_call | solution.py:158
  176.8 8.5 %shard_map.241 = (bf16[2,576,768]{2,1,0:T(8,128)(2,1)}, bf16[256,768]{1,0:T(8,128)(2,1)}) custom-call(bf16[2,288,1536]{2,1,0:T(8,128)(2,1)} %get-tuple-element.174.refs_0_, bf16[2,288,1536]{2,1,0:T(8,128)(2,1)} %collective-permute-done.10.refs_1_, bf16[128,1536]{1,0:T(8,128)(2,1)} %get-tuple-element.175.refs_2_, bf16[128,1536]{1,0:T(8,128)(2,1)} %copy-done.15, ...), custom_call_target="tpu_custom_call" | custom-call | flops 1358954496 | bytes 8847360 | tf_op jit(solution)/shard_map/pallas_call | solution.py:158
  185.3 12.2 %all-to-all-done.5 = bf16[4,2,72,1536]{3,2,1,0:T(8,128)(2,1)} async-done(((bf16[4,2,72,1536]{3,2,1,0:T(8,128)(2,1)}), bf16[4,2,72,1536]{3,2,1,0:T(8,128)(2,1)}, u32[]{:S(2)}, u32[]{:S(2)}) %all-to-all-start.5) | async-done | bytes 1769504 | tf_op jit(solution)/shard_map/all_to_all | solution.py:723
  205.4 17.0 %collective-permute-done.14.refs_4_ = bf16[128,1536]{1,0:T(8,128)(2,1)} collective-permute-done((bf16[128,1536]{1,0:T(8,128)(2,1)}, bf16[128,1536]{1,0:T(8,128)(2,1)}, u32[]{:S(2)}, u32[]{:S(2)}) %collective-permute-start.14) | collective-permute-done | bytes 393248 | tf_op jit(solution)/shard_map/ppermute | solution.py:729
  223.0 7.6 %shard_map.243 = (bf16[4,128,640]{2,1,0:T(8,128)(2,1)}, bf16[4,128,384]{2,1,0:T(8,128)(2,1)}, bf16[4,128,1536]{2,1,0:T(8,128)(2,1)}) custom-call(s32[1]{0:T(128)} %bitcast.23.refs_0_, bf16[128,1536]{1,0:T(8,128)(2,1)} %get-tuple-element.182.refs_1_, bf16[128,1536]{1,0:T(8,128)(2,1)} %collective-permute-done.12.refs_2_, ...), custom_call_target="tpu_custom_call" | custom-call | flops 1610612736 | bytes 27000836 | tf_op jit(solution)/shard_map/pallas_call | solution.py:158
  251.5 15.8 %collective-permute-done.17.refs_4_ = bf16[128,1536]{1,0:T(8,128)(2,1)} collective-permute-done((bf16[128,1536]{1,0:T(8,128)(2,1)}, bf16[128,1536]{1,0:T(8,128)(2,1)}, u32[]{:S(2)}, u32[]{:S(2)}) %collective-permute-start.17) | collective-permute-done | bytes 393248 | tf_op jit(solution)/shard_map/ppermute | solution.py:729
  268.0 10.1 %shard_map.245 = (bf16[4,2,72,1536]{3,2,1,0:T(8,128)(2,1)}, bf16[2,288,1536]{2,1,0:T(8,128)(2,1)}, bf16[2,288,768]{2,1,0:T(8,128)(2,1)}, bf16[2,288,768]{2,1,0:T(8,128)(2,1)}, f32[4,8,128]{2,1,0:T(8,128)}) custom-call(s32[1]{0:T(128)} %bitcast.23.refs_0_, bf16[128,1536]{1,0:T(8,128)(2,1)} %get-tuple-element.190.refs_1_.refs_3_, ...), custom_call_target="tpu_custom_call" | custom-call | flops 4076863488 | bytes 134365184 | tf_op jit(solution)/shard_map/pallas_call | solution.py:158
  285.9 8.4 %shard_map.246 = (bf16[2,576,768]{2,1,0:T(8,128)(2,1)}, bf16[256,768]{1,0:T(8,128)(2,1)}) custom-call(bf16[2,288,1536]{2,1,0:T(8,128)(2,1)} %get-tuple-element.194.refs_0_, bf16[2,288,1536]{2,1,0:T(8,128)(2,1)} %collective-permute-done.18.refs_1_, bf16[128,1536]{1,0:T(8,128)(2,1)} %get-tuple-element.195.refs_2_, bf16[128,1536]{1,0:T(8,128)(2,1)} %copy-done.14, ...), custom_call_target="tpu_custom_call" | custom-call | flops 1358954496 | bytes 8847360 | tf_op jit(solution)/shard_map/pallas_call | solution.py:158
  294.3 12.3 %all-to-all-done.7 = bf16[4,2,72,1536]{3,2,1,0:T(8,128)(2,1)} async-done(((bf16[4,2,72,1536]{3,2,1,0:T(8,128)(2,1)}), bf16[4,2,72,1536]{3,2,1,0:T(8,128)(2,1)}, u32[]{:S(2)}, u32[]{:S(2)}) %all-to-all-start.7) | async-done | bytes 1769504 | tf_op jit(solution)/shard_map/all_to_all | solution.py:723
  310.2 12.3 %shard_map.248 = (bf16[4,2,72,1536]{3,2,1,0:T(8,128)(2,1)}, bf16[2,288,3840]{2,1,0:T(8,128)(2,1)}) custom-call(s32[1]{0:T(128)} %bitcast.23.refs_0_, bf16[128,1536]{1,0:T(8,128)(2,1)} %bitcast.193, bf16[128,1536]{1,0:T(8,128)(2,1)} %copy-done.11, bf16[128,1536]{1,0:T(8,128)(2,1)} %copy-done.10, bf16[128,1536]{1,0:T(8,128)(2,1)} %copy-done.9, ...), custom_call_target="tpu_custom_call" | custom-call | flops 4076863488 | bytes 136962048 | tf_op jit(solution)/shard_map/pallas_call | solution.py:158
  331.6 12.7 %shard_map.249 = bf16[16,288,768]{2,1,0:T(8,128)(2,1)} custom-call(s32[1]{0:T(128)} %bitcast.59.refs_0_, bf16[2,576,768]{2,1,0:T(8,128)(2,1)} %get-tuple-element.212.refs_1_, bf16[768,384]{1,0:T(8,128)(2,1)} %fusion.1.refs_2_, bf16[2,288,3840]{2,1,0:T(8,128)(2,1)} %get-tuple-element.214.refs_3_, bf16[2,288,3840]{2,1,0:T(8,128)(2,1)} %collective-permute-done.20.refs_4_), custom_call_target="tpu_custom_call" | custom-call | flops 8153726976 | bytes 18284548 | tf_op jit(solution)/shard_map/pallas_call | solution.py:158
  357.6 12.4 %all_to_all.80.refs_1_ = bf16[4,128,384]{2,1,0:T(8,128)(2,1)} all-to-all(bf16[4,128,384]{2,1,0:T(8,128)(2,1)} %get-tuple-element.218), channel_id=1, replica_groups=mesh['seq'=4,'fsdp'=32] {'seq'}, dimensions={0} | all-to-all | bytes 786432 | tf_op jit(solution)/shard_map/all_to_all | solution.py:723
  391.7 7.3 %shard_map.254 = (f32[128,1536]{1,0:T(8,128)}, bf16[128,1536]{1,0:T(8,128)(2,1)}, f32[8,1536]{1,0:T(8,128)}) custom-call(bf16[4,128,640]{2,1,0:T(8,128)(2,1)} %all-to-all-done.10.refs_0_, bf16[32,288,768]{2,1,0:T(8,128)(2,1)} %bitcast.184, bf16[32,288,768]{2,1,0:T(8,128)(2,1)} %bitcast.185, bf16[32,288,768]{2,1,0:T(8,128)(2,1)} %bitcast.186, ...), custom_call_target="tpu_custom_call" | custom-call | flops 2415919104 | bytes 46268416 | tf_op jit(solution)/shard_map/pallas_call | solution.py:158
  404.1 16.1 %collective-permute-done.23.refs_4_ = bf16[128,1536]{1,0:T(8,128)(2,1)} collective-permute-done((bf16[128,1536]{1,0:T(8,128)(2,1)}, bf16[128,1536]{1,0:T(8,128)(2,1)}, u32[]{:S(2)}, u32[]{:S(2)}) %collective-permute-start.23) | collective-permute-done | bytes 393248 | tf_op jit(solution)/shard_map/ppermute | solution.py:729
  420.8 12.3 %shard_map.255 = (bf16[4,2,72,1536]{3,2,1,0:T(8,128)(2,1)}, bf16[2,288,3840]{2,1,0:T(8,128)(2,1)}) custom-call(s32[1]{0:T(128)} %bitcast.23.refs_0_, bf16[128,1536]{1,0:T(8,128)(2,1)} %get-tuple-element.233.refs_1_, bf16[128,1536]{1,0:T(8,128)(2,1)} %collective-permute-done.21.refs_2_, bf16[128,1536]{1,0:T(8,128)(2,1)} %collective-permute-done.22.refs_3_, ...), custom_call_target="tpu_custom_call" | custom-call | flops 4076863488 | bytes 122806272 | tf_op jit(solution)/shard_map/pallas_call | solution.py:158
  441.4 15.4 %shard_map.256 = bf16[16,432,768]{2,1,0:T(8,128)(2,1)} custom-call(s32[1]{0:T(128)} %bitcast.59.refs_0_, bf16[2,576,768]{2,1,0:T(8,128)(2,1)} %get-tuple-element.241.refs_1_, bf16[768,384]{1,0:T(8,128)(2,1)} %fusion.1.refs_2_, bf16[2,288,3840]{2,1,0:T(8,128)(2,1)} %get-tuple-element.242.refs_3_, bf16[2,288,3840]{2,1,0:T(8,128)(2,1)} %collective-permute-done.27.refs_4_, ...), custom_call_target="tpu_custom_call" | custom-call | flops 8153726976 | bytes 25755652 | tf_op jit(solution)/shard_map/pallas_call | solution.py:158
  468.0 12.6 %all_to_all.81.refs_1_ = bf16[4,128,384]{2,1,0:T(8,128)(2,1)} all-to-all(bf16[4,128,384]{2,1,0:T(8,128)(2,1)} %get-tuple-element.253), channel_id=1, replica_groups=mesh['seq'=4,'fsdp'=32] {'seq'}, dimensions={0} | all-to-all | bytes 786432 | tf_op jit(solution)/shard_map/all_to_all | solution.py:723
  501.9 7.5 %shard_map.261 = (f32[128,1536]{1,0:T(8,128)}, bf16[128,1536]{1,0:T(8,128)(2,1)}, f32[8,1536]{1,0:T(8,128)}) custom-call(bf16[4,128,640]{2,1,0:T(8,128)(2,1)} %all-to-all-done.13.refs_0_, bf16[32,288,768]{2,1,0:T(8,128)(2,1)} %bitcast.187, bf16[32,288,768]{2,1,0:T(8,128)(2,1)} %bitcast.188, bf16[32,288,768]{2,1,0:T(8,128)(2,1)} %bitcast.189, ...), custom_call_target="tpu_custom_call" | custom-call | flops 2415919104 | bytes 45875200 | tf_op jit(solution)/shard_map/pallas_call | solution.py:158
  516.9 62.9 %all_to_all.82 = bf16[16,144,768]{2,1,0:T(8,128)(2,1)S(1)} all-to-all(bf16[16,144,768]{2,1,0:T(8,128)(2,1)} %shard_map.262), channel_id=1, replica_groups={{0,2,4,6,8,10,12,14,16,18,20,22,24,26,28,30},{1,3,5,7,9,11,13,15,17,19,..., dimensions={0} | all-to-all | bytes 7077888 | tf_op jit(solution)/shard_map/all_to_all | solution.py:863
  (276 shorter events, 270.7 us)
Async XLA Ops:
  22.6 109.5 %all-gather.7.cloned.1.call-start = ((), (), s32[]{:S(2)}) async-start(), calls=%async_computation.20 | async-start | bytes 19464192 | tf_op jit(solution)/shard_map/all_gather | solution.py:858
  46.0 31.0 %all-to-all-start.1 = ((bf16[16,48,896]{2,1,0:T(8,128)(2,1)}), bf16[16,48,896]{2,1,0:T(8,128)(2,1)S(1)}, u32[]{:S(2)}, u32[]{:S(2)}) async-start(bf16[16,48,896]{2,1,0:T(8,128)(2,1)} %broadcast_in_dim.30), calls=%async_computation.1 | async-start | bytes 2752512 | tf_op jit(solution)/shard_map/all_to_all | solution.py:863
  103.7 27.7 %collective-permute-start.6 = (bf16[128,1536]{1,0:T(8,128)(2,1)S(1)}, bf16[128,1536]{1,0:T(8,128)(2,1)S(1)}, u32[]{:S(2)}, u32[]{:S(2)}) collective-permute-start(bf16[128,1536]{1,0:T(8,128)(2,1)S(1)} %bitcast.194), channel_id=1, source_target_pairs={{96,0},{0,32},{32,64},{64,96},{97,1},{1,33},{33,65},{65,97},{98,2}... | collective-permute-start | bytes 1179656 | tf_op jit(solution)/shard_map/ppermute | solution.py:729
  105.7 25.7 %collective-permute-start.5 = (bf16[128,1536]{1,0:T(8,128)(2,1)S(1)}, bf16[128,1536]{1,0:T(8,128)(2,1)S(1)}, u32[]{:S(2)}, u32[]{:S(2)}) collective-permute-start(bf16[128,1536]{1,0:T(8,128)(2,1)S(1)} %bitcast.195), channel_id=1, source_target_pairs={{64,0},{96,32},{0,64},{32,96},{65,1},{97,33},{1,65},{33,97},{66,2}... | collective-permute-start | bytes 1179656 | tf_op jit(solution)/shard_map/ppermute | solution.py:729
  108.4 23.0 %collective-permute-start.4 = (bf16[128,1536]{1,0:T(8,128)(2,1)S(1)}, bf16[128,1536]{1,0:T(8,128)(2,1)S(1)}, u32[]{:S(2)}, u32[]{:S(2)}) collective-permute-start(bf16[128,1536]{1,0:T(8,128)(2,1)S(1)} %bitcast.196), channel_id=1, source_target_pairs={{32,0},{64,32},{96,64},{0,96},{33,1},{65,33},{97,65},{1,97},{34,2}... | collective-permute-start | bytes 1179656 | tf_op jit(solution)/shard_map/ppermute | solution.py:729
  111.3 20.0 %all-to-all-start.4 = ((bf16[4,128,384]{2,1,0:T(8,128)(2,1)}), bf16[4,128,384]{2,1,0:T(8,128)(2,1)S(1)}, u32[]{:S(2)}, u32[]{:S(2)}) async-start(bf16[4,128,384]{2,1,0:T(8,128)(2,1)} %get-tuple-element.159), calls=%async_computation.4 | async-start | bytes 786432 | tf_op jit(solution)/shard_map/all_to_all | solution.py:723
  114.8 108.2 %all-gather.9.cloned.1.call-start = ((), (), s32[]{:S(2)}) async-start(), calls=%async_computation.21 | async-start | bytes 21897216 | tf_op jit(solution)/shard_map/all_gather | solution.py:858
  139.1 19.2 %collective-permute-start.8 = (bf16[128,1536]{1,0:T(8,128)(2,1)}, bf16[128,1536]{1,0:T(8,128)(2,1)}, u32[]{:S(2)}, u32[]{:S(2)}) collective-permute-start(bf16[128,1536]{1,0:T(8,128)(2,1)} %get-tuple-element.170.refs_1_.refs_3_), channel_id=1, source_target_pairs={{64,0},{96,32},{0,64},{32,96},{65,1},{97,33},{1,65},{33,97},{66,2}... | collective-permute-start | bytes 1179656 | tf_op jit(solution)/shard_map/ppermute | solution.py:729
  169.1 28.3 %all-to-all-start.5 = ((bf16[4,2,72,1536]{3,2,1,0:T(8,128)(2,1)}), bf16[4,2,72,1536]{3,2,1,0:T(8,128)(2,1)}, u32[]{:S(2)}, u32[]{:S(2)}) async-start(bf16[4,2,72,1536]{3,2,1,0:T(8,128)(2,1)} %get-tuple-element.173), calls=%async_computation.5 | async-start | bytes 3538944 | tf_op jit(solution)/shard_map/all_to_all | solution.py:723
  201.7 20.7 %collective-permute-start.14 = (bf16[128,1536]{1,0:T(8,128)(2,1)}, bf16[128,1536]{1,0:T(8,128)(2,1)}, u32[]{:S(2)}, u32[]{:S(2)}) collective-permute-start(bf16[128,1536]{1,0:T(8,128)(2,1)} %get-tuple-element.182.refs_1_), channel_id=1, source_target_pairs={{96,0},{0,32},{32,64},{64,96},{97,1},{1,33},{33,65},{65,97},{98,2}... | collective-permute-start | bytes 1179656 | tf_op jit(solution)/shard_map/ppermute | solution.py:729
  202.4 20.0 %collective-permute-start.13 = (bf16[128,1536]{1,0:T(8,128)(2,1)}, bf16[128,1536]{1,0:T(8,128)(2,1)}, u32[]{:S(2)}, u32[]{:S(2)}) collective-permute-start(bf16[128,1536]{1,0:T(8,128)(2,1)} %get-tuple-element.182.refs_1_), channel_id=1, source_target_pairs={{64,0},{96,32},{0,64},{32,96},{65,1},{97,33},{1,65},{33,97},{66,2}... | collective-permute-start | bytes 1179656 | tf_op jit(solution)/shard_map/ppermute | solution.py:729
  204.7 18.3 %collective-permute-start.12 = (bf16[128,1536]{1,0:T(8,128)(2,1)}, bf16[128,1536]{1,0:T(8,128)(2,1)}, u32[]{:S(2)}, u32[]{:S(2)}) collective-permute-start(bf16[128,1536]{1,0:T(8,128)(2,1)} %get-tuple-element.182.refs_1_), channel_id=1, source_target_pairs={{32,0},{64,32},{96,64},{0,96},{33,1},{65,33},{97,65},{1,97},{34,2}... | collective-permute-start | bytes 1179656 | tf_op jit(solution)/shard_map/ppermute | solution.py:729
  234.7 75.4 %all-gather.11.cloned.1.call-start = ((), (), s32[]{:S(2)}) async-start(), calls=%async_computation.22 | async-start | bytes 14598144 | tf_op jit(solution)/shard_map/all_gather | solution.py:858
  248.0 19.4 %collective-permute-start.17 = (bf16[128,1536]{1,0:T(8,128)(2,1)}, bf16[128,1536]{1,0:T(8,128)(2,1)}, u32[]{:S(2)}, u32[]{:S(2)}) collective-permute-start(bf16[128,1536]{1,0:T(8,128)(2,1)} %get-tuple-element.190.refs_1_.refs_3_), channel_id=1, source_target_pairs={{96,0},{0,32},{32,64},{64,96},{97,1},{1,33},{33,65},{65,97},{98,2}... | collective-permute-start | bytes 1179656 | tf_op jit(solution)/shard_map/ppermute | solution.py:729
  248.8 18.6 %collective-permute-start.16 = (bf16[128,1536]{1,0:T(8,128)(2,1)}, bf16[128,1536]{1,0:T(8,128)(2,1)}, u32[]{:S(2)}, u32[]{:S(2)}) collective-permute-start(bf16[128,1536]{1,0:T(8,128)(2,1)} %get-tuple-element.190.refs_1_.refs_3_), channel_id=1, source_target_pairs={{64,0},{96,32},{0,64},{32,96},{65,1},{97,33},{1,65},{33,97},{66,2}... | collective-permute-start | bytes 1179656 | tf_op jit(solution)/shard_map/ppermute | solution.py:729
  278.2 28.3 %all-to-all-start.7 = ((bf16[4,2,72,1536]{3,2,1,0:T(8,128)(2,1)}), bf16[4,2,72,1536]{3,2,1,0:T(8,128)(2,1)}, u32[]{:S(2)}, u32[]{:S(2)}) async-start(bf16[4,2,72,1536]{3,2,1,0:T(8,128)(2,1)} %get-tuple-element.193), calls=%async_computation.7 | async-start | bytes 3538944 | tf_op jit(solution)/shard_map/all_to_all | solution.py:723
  322.6 28.4 %all-to-all-start.8 = ((bf16[4,2,72,1536]{3,2,1,0:T(8,128)(2,1)}), bf16[4,2,72,1536]{3,2,1,0:T(8,128)(2,1)}, u32[]{:S(2)}, u32[]{:S(2)}) async-start(bf16[4,2,72,1536]{3,2,1,0:T(8,128)(2,1)} %get-tuple-element.211), calls=%async_computation.8 | async-start | bytes 3538944 | tf_op jit(solution)/shard_map/all_to_all | solution.py:723
  327.2 134.2 %reduce-scatter.3.cloned.1.call-start = ((), (), s32[]{:S(2)}) async-start(), calls=%async_computation.18 | async-start | bytes 7520256 | tf_op jit(solution)/shard_map/reduce_scatter | solution.py:1056
  391.1 29.6 %collective-permute-start.24 = (bf16[16,48,768]{2,1,0:T(8,128)(2,1)}, bf16[16,48,768]{2,1,0:T(8,128)(2,1)}, u32[]{:S(2)}, u32[]{:S(2)}) collective-permute-start(bf16[16,48,768]{2,1,0:T(8,128)(2,1)} %get-tuple-element.229), channel_id=1, source_target_pairs={{0,1},{1,0},{2,3},{3,2},{4,5},{5,4},{6,7},{7,6},{8,9},{9,8},{10,11... | collective-permute-start | bytes 3538952 | tf_op jit(solution)/shard_map/ppermute | solution.py:868
  398.9 21.2 %collective-permute-start.23 = (bf16[128,1536]{1,0:T(8,128)(2,1)}, bf16[128,1536]{1,0:T(8,128)(2,1)}, u32[]{:S(2)}, u32[]{:S(2)}) collective-permute-start(bf16[128,1536]{1,0:T(8,128)(2,1)} %get-tuple-element.233.refs_1_), channel_id=1, source_target_pairs={{96,0},{0,32},{32,64},{64,96},{97,1},{1,33},{33,65},{65,97},{98,2}... | collective-permute-start | bytes 1179656 | tf_op jit(solution)/shard_map/ppermute | solution.py:729
  399.6 20.5 %collective-permute-start.22 = (bf16[128,1536]{1,0:T(8,128)(2,1)}, bf16[128,1536]{1,0:T(8,128)(2,1)}, u32[]{:S(2)}, u32[]{:S(2)}) collective-permute-start(bf16[128,1536]{1,0:T(8,128)(2,1)} %get-tuple-element.233.refs_1_), channel_id=1, source_target_pairs={{64,0},{96,32},{0,64},{32,96},{65,1},{97,33},{1,65},{33,97},{66,2}... | collective-permute-start | bytes 1179656 | tf_op jit(solution)/shard_map/ppermute | solution.py:729
  401.7 19.1 %collective-permute-start.21 = (bf16[128,1536]{1,0:T(8,128)(2,1)}, bf16[128,1536]{1,0:T(8,128)(2,1)}, u32[]{:S(2)}, u32[]{:S(2)}) collective-permute-start(bf16[128,1536]{1,0:T(8,128)(2,1)} %get-tuple-element.233.refs_1_), channel_id=1, source_target_pairs={{32,0},{64,32},{96,64},{0,96},{33,1},{65,33},{97,65},{1,97},{34,2}... | collective-permute-start | bytes 1179656 | tf_op jit(solution)/shard_map/ppermute | solution.py:729
  433.2 28.2 %all-to-all-start.11 = ((bf16[4,2,72,1536]{3,2,1,0:T(8,128)(2,1)}), bf16[4,2,72,1536]{3,2,1,0:T(8,128)(2,1)}, u32[]{:S(2)}, u32[]{:S(2)}) async-start(bf16[4,2,72,1536]{3,2,1,0:T(8,128)(2,1)} %get-tuple-element.240), calls=%async_computation.11 | async-start | bytes 3538944 | tf_op jit(solution)/shard_map/all_to_all | solution.py:723
  437.6 144.5 %reduce-scatter.5.cloned.1.call-start = ((), (), s32[]{:S(2)}) async-start(), calls=%async_computation.19 | async-start | bytes 11280384 | tf_op jit(solution)/shard_map/reduce_scatter | solution.py:1056
  (58 other events, 557.8 us)
Sparse Core Ops, SparseCore 0:
  32.9 88.9 all-gather.6
  133.0 82.3 all-gather.8
  243.0 66.8 all-gather.10
  351.1 83.1 reduce-scatter.2
  461.5 116.7 reduce-scatter.4

commit v8 on v7

--- a/solution.py
+++ b/solution.py
@@ -697,25 +697,43 @@
             down_ref[layer, e, :, half:] = block[at + rows // 2 : at + rows]
 
 
-def dense_grads_kernel(*refs):
-    blocks = refs[0]
-    query_ref, key_ref, value_ref, out_ref, small_ref = refs[1:]
-    seq_count, _, _, rows, columns = blocks.shape
+def arrange_kernel(first, above, out_ref):
+    seq_count, blocks, padded, half = out_ref.shape
+    parts = blocks // LAYERS
+    rows = first.shape[0] // (parts * seq_count)
+    below = jnp.zeros((padded - rows, half), f32)
+    for layer, ref in enumerate((first, above)):
+        total = ref[...].astype(f32)
+        for part in range(parts):
+            for s in range(seq_count):
+                at = (part * seq_count + s) * rows
+                block = jnp.concatenate([total[at : at + rows], below], axis=0)
+                out_ref[s, layer * parts + part] = block.astype(bf16)
+
+
+def dense_grads_kernel(
+    blocks, query_ref, key_ref, value_ref, out_ref, router_ref, gain_attn_ref, gain_ffn_ref
+):
+    seq_count, count, _, columns = blocks.shape
+    parts = count // LAYERS
+    rows, expert_count = query_ref.shape[0], router_ref.shape[1]
     local = columns - 3 * HD
     share = seq_count // KVHEADS
     for layer in range(LAYERS):
-        parts = [blocks[s, layer, 0].astype(f32) for s in range(seq_count)]
+        whole = [blocks[s, layer * parts].astype(f32) for s in range(seq_count)]
         for s in range(seq_count):
-            query_ref[:, layer, s * local : (s + 1) * local] = parts[s][:, :local]
+            query_ref[:, layer, s * local : (s + 1) * local] = whole[s][:rows, :local]
         for c in range(KVHEADS):
-            total = functools.reduce(jnp.add, parts[c * share : (c + 1) * share])
+            total = functools.reduce(jnp.add, whole[c * share : (c + 1) * share])[:rows]
             key_ref[:, layer, c * HD : (c + 1) * HD] = total[:, local : local + HD]
             value_ref[:, layer, c * HD : (c + 1) * HD] = total[:, local + HD : local + 2 * HD]
-        total = functools.reduce(jnp.add, parts)
-        small_ref[layer] = total[:, local + 2 * HD :]
+        small = functools.reduce(jnp.add, [block[:, local + 2 * HD :] for block in whole]).T
+        router_ref[layer] = small[:expert_count, :rows]
+        gain_attn_ref[layer : layer + 1] = small[expert_count : expert_count + 1, :rows]
+        gain_ffn_ref[layer : layer + 1] = small[expert_count + 1 : expert_count + 2, :rows]
         for side in range(2):
-            sides = [blocks[s, layer, 1 + side].astype(f32) for s in range(seq_count)]
-            total = functools.reduce(jnp.add, sides)
+            sides = [blocks[s, layer * parts + 1 + side].astype(f32) for s in range(seq_count)]
+            total = functools.reduce(jnp.add, sides)[:rows]
             out_ref[:, layer, side * columns : (side + 1) * columns] = total
 
 
@@ -891,8 +909,9 @@
     dense = spread_seq(jnp.concatenate([dense_rows_of(0), small_rows_of(1)], axis=1))
     columns = jnp.concatenate([own_columns(dense), dense[:, -HD:]], axis=1)
     dense = dense[:, :-HD]
-    columns, hidden = lax.optimization_barrier((columns, hidden))
-    token_blocks = around_seq(hidden)
+    both_rows = jnp.concatenate([hidden, cotangent[0]], axis=0)
+    columns, both_rows = lax.optimization_barrier((columns, both_rows))
+    both_blocks = around_seq(both_rows)
     packs = [fetch(expert_part(0) + out_part(dense)), None]
     columns = to_chips(columns)
     pairs = jnp.concatenate(
@@ -907,14 +926,13 @@
     ]
     targets = [lax.dynamic_index_in_dim(t, seq_index, 0, False) for t in all_targets]
     routes_ts = [lax.dynamic_index_in_dim(t, seq_index, 0, False) for t in all_routes]
-    early = (token_blocks, all_targets, all_routes, targets, routes_ts)
+    early = (both_blocks, all_targets, all_routes, targets, routes_ts)
     early = early + (cos_all, sin_all, bias, spread, picks)
     columns, early = lax.optimization_barrier((columns, early))
-    token_blocks, all_targets, all_routes, targets, routes_ts = early[:5]
+    both_blocks, all_targets, all_routes, targets, routes_ts = early[:5]
     cos_all, sin_all, bias, spread, picks = early[5:]
     first_columns = both_cores(columns).reshape(width, columns.shape[2])
-    first_columns, grad_rows = lax.optimization_barrier((first_columns, cotangent[0]))
-    grad_blocks = around_seq(grad_rows)
+    grad_blocks, grad_cut = both_blocks, ((0, tok_count, tok_count),)
     own_at = local_experts * expert_rows + 2 * shard_rows
     heads_shape = shape((seq_count, tok_count, local_width + 2 * HD), bf16)
     attended_shape = shape((seq_count, tok_count, local_width), bf16)
@@ -927,8 +945,8 @@
             heads, attended, normed_all, smalls = once(
                 first_attention_kernel,
                 [heads_shape, attended_shape, normed_shape, small_shape],
-                place, *token_blocks, first_columns, spread, cos_all, sin_all, bias,
-                scalar=True, flops=attention_flops + 4 * dense_flops,
+                place, *both_blocks, first_columns, spread, cos_all, sin_all, bias,
+                scalar=True, cut={n: ((0, 0, tok_count),) for n in range(1, 5)}, flops=attention_flops + 4 * dense_flops,
             )
             small = smalls[layer]
         else:
@@ -945,13 +963,11 @@
                 scalar=True, cut={5: ((1, own_at, shard_rows),)}, flops=attention_flops,
             )
         if layer == 0:
-            attended, next_rows = lax.optimization_barrier((attended, dense_rows_of(1)))
-            back = swap_seq(attended)
+            back, next_rows = lax.optimization_barrier((swap_seq(attended), dense_rows_of(1)))
             next_dense = spread_seq(next_rows)
             next_parts = expert_part(1) + out_part(next_dense) + [own_columns(next_dense)]
             next_parts = jnp.concatenate(next_parts, axis=0)
-            tied = lax.optimization_barrier((pack, next_parts, back, grad_blocks))
-            pack, next_parts, back, grad_blocks = tied
+            pack, next_parts, back = lax.optimization_barrier((pack, next_parts, back))
             packs = [pack, fetch([next_parts])]
         else:
             back = swap_seq(attended)
@@ -1032,7 +1048,8 @@
             place, *grad_blocks, all_targets[layer], all_gates, pack, gate_val, up_val,
             *[pack] * (len(back_parts) - 1),
             scalar=True,
-            cut={n + 9 if n else 7: ((1, *part),) for n, part in enumerate(back_parts)},
+            cut={n + 9 if n else 7: ((1, *part),) for n, part in enumerate(back_parts)}
+            | {n: grad_cut for n in range(1, 5)},
             pieces={0: (1, local_experts), 1: (0, local_experts)},
             flops=expert_flops,
         )
@@ -1103,15 +1120,18 @@
             spread, picked[1], branch, swap_cores(branch),
         )
         if layer > 0:
-            grad_blocks, waiting = around_seq(grad_low), dense_sources
+            grad_blocks, grad_cut, waiting = around_seq(grad_low), (), dense_sources
     (dense_pack,) = once(
         dense_kernel,
         [shape((shard_count // 2, 3 * shard_rows, half_width), bf16)],
         core_place, *dense_sources, scalar=True, flops=2 * dense_flops,
     )
     dense_sum = jnp.sum(swap_chips(dense_pack).astype(f32), axis=0).astype(bf16)
-    rows = jnp.stack([dense_sum, sums[0][local_experts * expert_rows :]])
-    rows = rows.reshape(LAYERS, 3, seq_count, dense_rows, half_width).transpose(2, 0, 1, 3, 4)
+    (rows,) = once(
+        arrange_kernel,
+        [shape((seq_count, 3 * LAYERS, 16, half_width), bf16)],
+        dense_sum, sums[0], cut={1: ((0, local_experts * expert_rows, 3 * shard_rows),)},
+    )
     rows = swap_seq(rows)
     gate_grads, up_grads, down_grads = once(
         expert_grads_kernel,
@@ -1123,27 +1143,29 @@
         *sums,
         cut={0: ((0, 0, local_experts * expert_rows),)},
     )
-    query_grads, key_grads, value_grads, out_grads, small_grads = once(
+    query_grads, key_grads, value_grads, out_grads, router_grads, *gain_grads = once(
         dense_grads_kernel,
         [
             shape((dense_rows, LAYERS, HEADS * HD), f32),
             shape((dense_rows, LAYERS, KVHEADS * HD), f32),
             shape((dense_rows, LAYERS, KVHEADS * HD), f32),
             shape((dense_rows, LAYERS, width), f32),
-            shape((LAYERS, dense_rows, HD), f32),
+            shape((LAYERS, expert_count, dense_rows), f32),
+            shape((LAYERS, dense_rows), f32),
+            shape((LAYERS, dense_rows), f32),
         ],
         rows,
     )
     return (
         result[None],
         grad_hidden[None],
-        small_grads[:, :, expert_count],
+        gain_grads[0],
         query_grads.transpose(1, 0, 2),
         key_grads.transpose(1, 0, 2),
         value_grads.transpose(1, 0, 2),
         out_grads.transpose(1, 0, 2),
-        small_grads[:, :, expert_count + 1],
-        small_grads[:, :, :expert_count],
+        gain_grads[1],
+        router_grads.transpose(0, 2, 1),
         gate_grads,
         up_grads,
         down_grads,

time: 617 us -> 614 us (level)
  waiting for transfers between devices: 170 us -> 183 us
  local copies, waits for them, and re-layouts: 36.8 us -> 25.5 us
    ppermute x18 -> x15, waiting for transfers between devices: 80.2 us -> 94.1 us  [around_seq(): lax.ppermute(block, 'seq', [((i + k) % count, i) for i in range(count)])]
    ppermute x18 -> x15, starting transfers between devices: 26.5 us -> 20.6 us  [around_seq(): lax.ppermute(block, 'seq', [((i + k) % count, i) for i in range(count)])]
    pallas_call x27 -> x28, Pallas kernels: 195 us -> 197 us  [once(): pl.pallas_call(body, out_shape=list(outs), in_specs=specs, out_specs=[hbm...]
  transfers between devices with their start and end apart: 49 -> 46, of which waited for: 27 -> 26; matrix products, arithmetic and copies ran while one was open for 5% -> 5% of each run, Pallas kernels for 28% -> 29%
where the time goes in v8:
time: 614 us; the launch traced here: 607 us
  Pallas kernels  197 us (32%)
  waiting for transfers between devices  183 us (30%)
  blocking collectives  86.9 us (14%)
  starting transfers between devices  83.5 us (14%)
  local copies, waits for them, and re-layouts  25.5 us (4%)
  other arithmetic  16.3 us (3%)
  between operations  15 us (2%)
    pallas_call x28, Pallas kernels, once(): pl.pallas_call(body, out_shape=list(outs), in_specs=specs, out_specs=[hbm...  197 us
    ppermute x15, waiting for transfers between devices, around_seq(): lax.ppermute(block, 'seq', [((i + k) % count, i) for i in range(count)])  94.1 us
    all_to_all x12, waiting for transfers between devices, swap_seq(): return lax.all_to_all(block, 'seq', split_axis=0, concat_axis=0, tiled=True)  79.5 us
    all_to_all x1, blocking collectives, swap_chips(): lax.all_to_all(block, 'fsdp', split_axis=0, concat_axis=0, tiled=True, ax...  61.9 us
    all_to_all x12, starting transfers between devices, swap_seq(): return lax.all_to_all(block, 'seq', split_axis=0, concat_axis=0, tiled=True)  51.4 us
    all_to_all x2, blocking collectives, swap_seq(): return lax.all_to_all(block, 'seq', split_axis=0, concat_axis=0, tiled=True)  25 us
    ppermute x15, starting transfers between devices, around_seq(): lax.ppermute(block, 'seq', [((i + k) % count, i) for i in range(count)])  20.6 us
  transfers between devices with their start and end apart: 46, of which 26 were waited for; matrix products, arithmetic and copies ran while one was open for 5% of the time, Pallas kernels for 29%

profile of v8, /device:TPU:0, one launch (start us, length us, event | category | flops | bytes accessed | tf_op | source)
XLA Modules:
  0.0 606.7 jit_solution(11488309528706300434)
XLA Ops:
  22.4 8.1 %all-to-all-done = bf16[4,12,3840]{2,1,0:T(8,128)(2,1)S(1)} async-done(((bf16[4,12,3840]{2,1,0:T(8,128)(2,1)}), bf16[4,12,3840]{2,1,0:T(8,128)(2,1)S(1)}, u32[]{:S(2)}, u32[]{:S(2)}) %all-to-all-start) | async-done | bytes 368672 | tf_op jit(solution)/shard_map/all_to_all | solution.py:741
  63.4 11.3 %collective-permute-done.2.refs_4_ = bf16[256,1536]{1,0:T(8,128)(2,1)S(1)} collective-permute-done((bf16[256,1536]{1,0:T(8,128)(2,1)S(1)}, bf16[256,1536]{1,0:T(8,128)(2,1)S(1)}, u32[]{:S(2)}, u32[]{:S(2)}) %collective-permute-start.2) | collective-permute-done | bytes 786464 | tf_op jit(solution)/shard_map/ppermute | solution.py:747
  74.7 15.9 %collective-permute-done.1.refs_3_ = bf16[256,1536]{1,0:T(8,128)(2,1)} collective-permute-done((bf16[256,1536]{1,0:T(8,128)(2,1)S(1)}, bf16[256,1536]{1,0:T(8,128)(2,1)}, u32[]{:S(2)}, u32[]{:S(2)}) %collective-permute-start.1) | collective-permute-done | bytes 786464 | tf_op jit(solution)/shard_map/ppermute | solution.py:747
  96.4 11.3 %shard_map.238 = (bf16[4,128,640]{2,1,0:T(8,128)(2,1)}, bf16[4,128,384]{2,1,0:T(8,128)(2,1)}, bf16[4,128,1536]{2,1,0:T(8,128)(2,1)}, bf16[2,16,1536]{2,1,0:T(8,128)(2,1)}) custom-call(s32[1]{0:T(128)} %bitcast.30.refs_0_, bf16[256,1536]{1,0:T(8,128)(2,1)} %copy-done.1, bf16[256,1536]{1,0:T(8,128)(2,1)} %collective-permute-done.refs_2_, ...), custom_call_target="tpu_custom_call" | custom-call | flops 4026531840 | bytes 10485764 | tf_op jit(solution)/shard_map/pallas_call | solution.py:158
  145.1 15.5 %collective-permute-done.6.refs_4_ = bf16[128,1536]{1,0:T(8,128)(2,1)} collective-permute-done((bf16[128,1536]{1,0:T(8,128)(2,1)}, bf16[128,1536]{1,0:T(8,128)(2,1)}, u32[]{:S(2)}, u32[]{:S(2)}) %collective-permute-start.6) | collective-permute-done | bytes 393248 | tf_op jit(solution)/shard_map/ppermute | solution.py:747
  161.2 10.1 %shard_map.240 = (bf16[4,2,72,1536]{3,2,1,0:T(8,128)(2,1)}, bf16[2,288,1536]{2,1,0:T(8,128)(2,1)}, bf16[2,288,768]{2,1,0:T(8,128)(2,1)}, bf16[2,288,768]{2,1,0:T(8,128)(2,1)}, f32[4,8,128]{2,1,0:T(8,128)}) custom-call(s32[1]{0:T(128)} %bitcast.30.refs_0_, bf16[128,1536]{1,0:T(8,128)(2,1)} %get-tuple-element.160.refs_1_.refs_3_, ...), custom_call_target="tpu_custom_call" | custom-call | flops 4076863488 | bytes 120209408 | tf_op jit(solution)/shard_map/pallas_call | solution.py:158
  178.6 8.2 %shard_map.241 = (bf16[2,576,768]{2,1,0:T(8,128)(2,1)}, bf16[256,768]{1,0:T(8,128)(2,1)}) custom-call(bf16[2,288,1536]{2,1,0:T(8,128)(2,1)} %get-tuple-element.164.refs_0_, bf16[2,288,1536]{2,1,0:T(8,128)(2,1)} %collective-permute-done.7.refs_1_, bf16[128,1536]{1,0:T(8,128)(2,1)} %get-tuple-element.165.refs_2_, bf16[128,1536]{1,0:T(8,128)(2,1)} %copy-done.14, ...), custom_call_target="tpu_custom_call" | custom-call | flops 1358954496 | bytes 8847360 | tf_op jit(solution)/shard_map/pallas_call | solution.py:158
  186.8 12.9 %all-to-all-done.5 = bf16[4,2,72,1536]{3,2,1,0:T(8,128)(2,1)} async-done(((bf16[4,2,72,1536]{3,2,1,0:T(8,128)(2,1)}), bf16[4,2,72,1536]{3,2,1,0:T(8,128)(2,1)}, u32[]{:S(2)}, u32[]{:S(2)}) %all-to-all-start.5) | async-done | bytes 1769504 | tf_op jit(solution)/shard_map/all_to_all | solution.py:741
  207.9 16.9 %collective-permute-done.11.refs_4_ = bf16[128,1536]{1,0:T(8,128)(2,1)} collective-permute-done((bf16[128,1536]{1,0:T(8,128)(2,1)}, bf16[128,1536]{1,0:T(8,128)(2,1)}, u32[]{:S(2)}, u32[]{:S(2)}) %collective-permute-start.11) | collective-permute-done | bytes 393248 | tf_op jit(solution)/shard_map/ppermute | solution.py:747
  225.4 7.6 %shard_map.243 = (bf16[4,128,640]{2,1,0:T(8,128)(2,1)}, bf16[4,128,384]{2,1,0:T(8,128)(2,1)}, bf16[4,128,1536]{2,1,0:T(8,128)(2,1)}) custom-call(s32[1]{0:T(128)} %bitcast.30.refs_0_, bf16[128,1536]{1,0:T(8,128)(2,1)} %get-tuple-element.172.refs_1_, bf16[128,1536]{1,0:T(8,128)(2,1)} %collective-permute-done.9.refs_2_, ...), custom_call_target="tpu_custom_call" | custom-call | flops 1610612736 | bytes 27000836 | tf_op jit(solution)/shard_map/pallas_call | solution.py:158
  253.9 15.9 %collective-permute-done.14.refs_4_ = bf16[128,1536]{1,0:T(8,128)(2,1)} collective-permute-done((bf16[128,1536]{1,0:T(8,128)(2,1)}, bf16[128,1536]{1,0:T(8,128)(2,1)}, u32[]{:S(2)}, u32[]{:S(2)}) %collective-permute-start.14) | collective-permute-done | bytes 393248 | tf_op jit(solution)/shard_map/ppermute | solution.py:747
  270.4 10.1 %shard_map.245 = (bf16[4,2,72,1536]{3,2,1,0:T(8,128)(2,1)}, bf16[2,288,1536]{2,1,0:T(8,128)(2,1)}, bf16[2,288,768]{2,1,0:T(8,128)(2,1)}, bf16[2,288,768]{2,1,0:T(8,128)(2,1)}, f32[4,8,128]{2,1,0:T(8,128)}) custom-call(s32[1]{0:T(128)} %bitcast.30.refs_0_, bf16[128,1536]{1,0:T(8,128)(2,1)} %get-tuple-element.180.refs_1_.refs_3_, ...), custom_call_target="tpu_custom_call" | custom-call | flops 4076863488 | bytes 134365184 | tf_op jit(solution)/shard_map/pallas_call | solution.py:158
  288.7 8.4 %shard_map.246 = (bf16[2,576,768]{2,1,0:T(8,128)(2,1)}, bf16[256,768]{1,0:T(8,128)(2,1)}) custom-call(bf16[2,288,1536]{2,1,0:T(8,128)(2,1)} %get-tuple-element.184.refs_0_, bf16[2,288,1536]{2,1,0:T(8,128)(2,1)} %collective-permute-done.15.refs_1_, bf16[128,1536]{1,0:T(8,128)(2,1)} %get-tuple-element.185.refs_2_, bf16[128,1536]{1,0:T(8,128)(2,1)} %copy-done.13, ...), custom_call_target="tpu_custom_call" | custom-call | flops 1358954496 | bytes 8847360 | tf_op jit(solution)/shard_map/pallas_call | solution.py:158
  297.2 11.8 %all-to-all-done.7 = bf16[4,2,72,1536]{3,2,1,0:T(8,128)(2,1)} async-done(((bf16[4,2,72,1536]{3,2,1,0:T(8,128)(2,1)}), bf16[4,2,72,1536]{3,2,1,0:T(8,128)(2,1)}, u32[]{:S(2)}, u32[]{:S(2)}) %all-to-all-start.7) | async-done | bytes 1769504 | tf_op jit(solution)/shard_map/all_to_all | solution.py:741
  312.6 12.3 %shard_map.248 = (bf16[4,2,72,1536]{3,2,1,0:T(8,128)(2,1)}, bf16[2,288,3840]{2,1,0:T(8,128)(2,1)}) custom-call(s32[1]{0:T(128)} %bitcast.30.refs_0_, bf16[256,1536]{1,0:T(8,128)(2,1)} %copy-done.1, bf16[256,1536]{1,0:T(8,128)(2,1)} %collective-permute-done.refs_2_, bf16[256,1536]{1,0:T(8,128)(2,1)} %collective-permute-done.1.refs_3_, ...), custom_call_target="tpu_custom_call" | custom-call | flops 4076863488 | bytes 138534912 | tf_op jit(solution)/shard_map/pallas_call | solution.py:158
  334.0 12.7 %shard_map.249 = bf16[16,288,768]{2,1,0:T(8,128)(2,1)} custom-call(s32[1]{0:T(128)} %bitcast.59.refs_0_, bf16[2,576,768]{2,1,0:T(8,128)(2,1)} %get-tuple-element.202.refs_1_, bf16[768,384]{1,0:T(8,128)(2,1)} %fusion.1.refs_2_, bf16[2,288,3840]{2,1,0:T(8,128)(2,1)} %get-tuple-element.204.refs_3_, bf16[2,288,3840]{2,1,0:T(8,128)(2,1)} %collective-permute-done.17.refs_4_), custom_call_target="tpu_custom_call" | custom-call | flops 8153726976 | bytes 18284548 | tf_op jit(solution)/shard_map/pallas_call | solution.py:158
  359.9 12.4 %all_to_all.80.refs_1_ = bf16[4,128,384]{2,1,0:T(8,128)(2,1)} all-to-all(bf16[4,128,384]{2,1,0:T(8,128)(2,1)} %get-tuple-element.208), channel_id=1, replica_groups=mesh['seq'=4,'fsdp'=32] {'seq'}, dimensions={0} | all-to-all | bytes 786432 | tf_op jit(solution)/shard_map/all_to_all | solution.py:741
  394.0 7.2 %shard_map.254 = (f32[128,1536]{1,0:T(8,128)}, bf16[128,1536]{1,0:T(8,128)(2,1)}, f32[8,1536]{1,0:T(8,128)}) custom-call(bf16[4,128,640]{2,1,0:T(8,128)(2,1)} %all-to-all-done.10.refs_0_, bf16[32,288,768]{2,1,0:T(8,128)(2,1)} %bitcast.182, bf16[32,288,768]{2,1,0:T(8,128)(2,1)} %bitcast.183, bf16[32,288,768]{2,1,0:T(8,128)(2,1)} %bitcast.184, ...), custom_call_target="tpu_custom_call" | custom-call | flops 2415919104 | bytes 46268416 | tf_op jit(solution)/shard_map/pallas_call | solution.py:158
  406.4 16.1 %collective-permute-done.20.refs_4_ = bf16[128,1536]{1,0:T(8,128)(2,1)} collective-permute-done((bf16[128,1536]{1,0:T(8,128)(2,1)}, bf16[128,1536]{1,0:T(8,128)(2,1)}, u32[]{:S(2)}, u32[]{:S(2)}) %collective-permute-start.20) | collective-permute-done | bytes 393248 | tf_op jit(solution)/shard_map/ppermute | solution.py:747
  423.1 12.3 %shard_map.255 = (bf16[4,2,72,1536]{3,2,1,0:T(8,128)(2,1)}, bf16[2,288,3840]{2,1,0:T(8,128)(2,1)}) custom-call(s32[1]{0:T(128)} %bitcast.30.refs_0_, bf16[128,1536]{1,0:T(8,128)(2,1)} %get-tuple-element.223.refs_1_, bf16[128,1536]{1,0:T(8,128)(2,1)} %collective-permute-done.18.refs_2_, bf16[128,1536]{1,0:T(8,128)(2,1)} %collective-permute-done.19.refs_3_, ...), custom_call_target="tpu_custom_call" | custom-call | flops 4076863488 | bytes 122806272 | tf_op jit(solution)/shard_map/pallas_call | solution.py:158
  443.7 15.4 %shard_map.256 = bf16[16,432,768]{2,1,0:T(8,128)(2,1)} custom-call(s32[1]{0:T(128)} %bitcast.59.refs_0_, bf16[2,576,768]{2,1,0:T(8,128)(2,1)} %get-tuple-element.231.refs_1_, bf16[768,384]{1,0:T(8,128)(2,1)} %fusion.1.refs_2_, bf16[2,288,3840]{2,1,0:T(8,128)(2,1)} %get-tuple-element.232.refs_3_, bf16[2,288,3840]{2,1,0:T(8,128)(2,1)} %collective-permute-done.24.refs_4_, ...), custom_call_target="tpu_custom_call" | custom-call | flops 8153726976 | bytes 25755652 | tf_op jit(solution)/shard_map/pallas_call | solution.py:158
  470.4 12.6 %all_to_all.81.refs_1_ = bf16[4,128,384]{2,1,0:T(8,128)(2,1)} all-to-all(bf16[4,128,384]{2,1,0:T(8,128)(2,1)} %get-tuple-element.243), channel_id=1, replica_groups=mesh['seq'=4,'fsdp'=32] {'seq'}, dimensions={0} | all-to-all | bytes 786432 | tf_op jit(solution)/shard_map/all_to_all | solution.py:741
  504.4 7.3 %shard_map.261 = (f32[128,1536]{1,0:T(8,128)}, bf16[128,1536]{1,0:T(8,128)(2,1)}, f32[8,1536]{1,0:T(8,128)}) custom-call(bf16[4,128,640]{2,1,0:T(8,128)(2,1)} %all-to-all-done.13.refs_0_, bf16[32,288,768]{2,1,0:T(8,128)(2,1)} %bitcast.185, bf16[32,288,768]{2,1,0:T(8,128)(2,1)} %bitcast.186, bf16[32,288,768]{2,1,0:T(8,128)(2,1)} %bitcast.187, ...), custom_call_target="tpu_custom_call" | custom-call | flops 2415919104 | bytes 45875200 | tf_op jit(solution)/shard_map/pallas_call | solution.py:158
  519.3 61.9 %all_to_all.82 = bf16[16,144,768]{2,1,0:T(8,128)(2,1)S(1)} all-to-all(bf16[16,144,768]{2,1,0:T(8,128)(2,1)} %shard_map.262), channel_id=1, replica_groups={{0,2,4,6,8,10,12,14,16,18,20,22,24,26,28,30},{1,3,5,7,9,11,13,15,17,19,..., dimensions={0} | all-to-all | bytes 7077888 | tf_op jit(solution)/shard_map/all_to_all | solution.py:881
  (260 shorter events, 257.4 us)
Async XLA Ops:
  21.4 114.5 %all-gather.7.cloned.1.call-start = ((), (), s32[]{:S(2)}) async-start(), calls=%async_computation.20 | async-start | bytes 19464192 | tf_op jit(solution)/shard_map/all_gather | solution.py:876
  45.0 45.6 %all-to-all-start.1 = ((bf16[16,48,896]{2,1,0:T(8,128)(2,1)}), bf16[16,48,896]{2,1,0:T(8,128)(2,1)S(1)}, u32[]{:S(2)}, u32[]{:S(2)}) async-start(bf16[16,48,896]{2,1,0:T(8,128)(2,1)} %broadcast_in_dim.29), calls=%async_computation.1 | async-start | bytes 2752512 | tf_op jit(solution)/shard_map/all_to_all | solution.py:881
  53.8 20.9 %collective-permute-start.2 = (bf16[256,1536]{1,0:T(8,128)(2,1)S(1)}, bf16[256,1536]{1,0:T(8,128)(2,1)S(1)}, u32[]{:S(2)}, u32[]{:S(2)}) collective-permute-start(bf16[256,1536]{1,0:T(8,128)(2,1)S(1)} %pad_maximum_fusion.1.refs_1_), channel_id=1, source_target_pairs={{96,0},{0,32},{32,64},{64,96},{97,1},{1,33},{33,65},{65,97},{98,2}... | collective-permute-start | bytes 2359304 | tf_op jit(solution)/shard_map/ppermute | solution.py:747
  55.8 34.8 %collective-permute-start.1 = (bf16[256,1536]{1,0:T(8,128)(2,1)S(1)}, bf16[256,1536]{1,0:T(8,128)(2,1)}, u32[]{:S(2)}, u32[]{:S(2)}) collective-permute-start(bf16[256,1536]{1,0:T(8,128)(2,1)S(1)} %pad_maximum_fusion.1.refs_1_), channel_id=1, source_target_pairs={{64,0},{96,32},{0,64},{32,96},{65,1},{97,33},{1,65},{33,97},{66,2}... | collective-permute-start | bytes 2359304 | tf_op jit(solution)/shard_map/ppermute | solution.py:747
  58.5 32.2 %collective-permute-start = (bf16[256,1536]{1,0:T(8,128)(2,1)S(1)}, bf16[256,1536]{1,0:T(8,128)(2,1)}, u32[]{:S(2)}, u32[]{:S(2)}) collective-permute-start(bf16[256,1536]{1,0:T(8,128)(2,1)S(1)} %pad_maximum_fusion.1.refs_1_), channel_id=1, source_target_pairs={{32,0},{64,32},{96,64},{0,96},{33,1},{65,33},{97,65},{1,97},{34,2}... | collective-permute-start | bytes 2359304 | tf_op jit(solution)/shard_map/ppermute | solution.py:747
  125.1 100.3 %all-gather.9.cloned.1.call-start = ((), (), s32[]{:S(2)}) async-start(), calls=%async_computation.21 | async-start | bytes 21897216 | tf_op jit(solution)/shard_map/all_gather | solution.py:876
  141.5 19.0 %collective-permute-start.6 = (bf16[128,1536]{1,0:T(8,128)(2,1)}, bf16[128,1536]{1,0:T(8,128)(2,1)}, u32[]{:S(2)}, u32[]{:S(2)}) collective-permute-start(bf16[128,1536]{1,0:T(8,128)(2,1)} %get-tuple-element.160.refs_1_.refs_3_), channel_id=1, source_target_pairs={{96,0},{0,32},{32,64},{64,96},{97,1},{1,33},{33,65},{65,97},{98,2}... | collective-permute-start | bytes 1179656 | tf_op jit(solution)/shard_map/ppermute | solution.py:747
  142.2 18.4 %collective-permute-start.5 = (bf16[128,1536]{1,0:T(8,128)(2,1)}, bf16[128,1536]{1,0:T(8,128)(2,1)}, u32[]{:S(2)}, u32[]{:S(2)}) collective-permute-start(bf16[128,1536]{1,0:T(8,128)(2,1)} %get-tuple-element.160.refs_1_.refs_3_), channel_id=1, source_target_pairs={{64,0},{96,32},{0,64},{32,96},{65,1},{97,33},{1,65},{33,97},{66,2}... | collective-permute-start | bytes 1179656 | tf_op jit(solution)/shard_map/ppermute | solution.py:747
  171.4 28.3 %all-to-all-start.5 = ((bf16[4,2,72,1536]{3,2,1,0:T(8,128)(2,1)}), bf16[4,2,72,1536]{3,2,1,0:T(8,128)(2,1)}, u32[]{:S(2)}, u32[]{:S(2)}) async-start(bf16[4,2,72,1536]{3,2,1,0:T(8,128)(2,1)} %get-tuple-element.163), calls=%async_computation.5 | async-start | bytes 3538944 | tf_op jit(solution)/shard_map/all_to_all | solution.py:741
  204.0 20.7 %collective-permute-start.11 = (bf16[128,1536]{1,0:T(8,128)(2,1)}, bf16[128,1536]{1,0:T(8,128)(2,1)}, u32[]{:S(2)}, u32[]{:S(2)}) collective-permute-start(bf16[128,1536]{1,0:T(8,128)(2,1)} %get-tuple-element.172.refs_1_), channel_id=1, source_target_pairs={{96,0},{0,32},{32,64},{64,96},{97,1},{1,33},{33,65},{65,97},{98,2}... | collective-permute-start | bytes 1179656 | tf_op jit(solution)/shard_map/ppermute | solution.py:747
  204.9 19.9 %collective-permute-start.10 = (bf16[128,1536]{1,0:T(8,128)(2,1)}, bf16[128,1536]{1,0:T(8,128)(2,1)}, u32[]{:S(2)}, u32[]{:S(2)}) collective-permute-start(bf16[128,1536]{1,0:T(8,128)(2,1)} %get-tuple-element.172.refs_1_), channel_id=1, source_target_pairs={{64,0},{96,32},{0,64},{32,96},{65,1},{97,33},{1,65},{33,97},{66,2}... | collective-permute-start | bytes 1179656 | tf_op jit(solution)/shard_map/ppermute | solution.py:747
  206.6 18.8 %collective-permute-start.9 = (bf16[128,1536]{1,0:T(8,128)(2,1)}, bf16[128,1536]{1,0:T(8,128)(2,1)}, u32[]{:S(2)}, u32[]{:S(2)}) collective-permute-start(bf16[128,1536]{1,0:T(8,128)(2,1)} %get-tuple-element.172.refs_1_), channel_id=1, source_target_pairs={{32,0},{64,32},{96,64},{0,96},{33,1},{65,33},{97,65},{1,97},{34,2}... | collective-permute-start | bytes 1179656 | tf_op jit(solution)/shard_map/ppermute | solution.py:747
  237.1 75.4 %all-gather.11.cloned.1.call-start = ((), (), s32[]{:S(2)}) async-start(), calls=%async_computation.22 | async-start | bytes 14598144 | tf_op jit(solution)/shard_map/all_gather | solution.py:876
  250.3 19.4 %collective-permute-start.14 = (bf16[128,1536]{1,0:T(8,128)(2,1)}, bf16[128,1536]{1,0:T(8,128)(2,1)}, u32[]{:S(2)}, u32[]{:S(2)}) collective-permute-start(bf16[128,1536]{1,0:T(8,128)(2,1)} %get-tuple-element.180.refs_1_.refs_3_), channel_id=1, source_target_pairs={{96,0},{0,32},{32,64},{64,96},{97,1},{1,33},{33,65},{65,97},{98,2}... | collective-permute-start | bytes 1179656 | tf_op jit(solution)/shard_map/ppermute | solution.py:747
  251.1 18.6 %collective-permute-start.13 = (bf16[128,1536]{1,0:T(8,128)(2,1)}, bf16[128,1536]{1,0:T(8,128)(2,1)}, u32[]{:S(2)}, u32[]{:S(2)}) collective-permute-start(bf16[128,1536]{1,0:T(8,128)(2,1)} %get-tuple-element.180.refs_1_.refs_3_), channel_id=1, source_target_pairs={{64,0},{96,32},{0,64},{32,96},{65,1},{97,33},{1,65},{33,97},{66,2}... | collective-permute-start | bytes 1179656 | tf_op jit(solution)/shard_map/ppermute | solution.py:747
  280.6 28.3 %all-to-all-start.7 = ((bf16[4,2,72,1536]{3,2,1,0:T(8,128)(2,1)}), bf16[4,2,72,1536]{3,2,1,0:T(8,128)(2,1)}, u32[]{:S(2)}, u32[]{:S(2)}) async-start(bf16[4,2,72,1536]{3,2,1,0:T(8,128)(2,1)} %get-tuple-element.183), calls=%async_computation.7 | async-start | bytes 3538944 | tf_op jit(solution)/shard_map/all_to_all | solution.py:741
  325.0 28.3 %all-to-all-start.8 = ((bf16[4,2,72,1536]{3,2,1,0:T(8,128)(2,1)}), bf16[4,2,72,1536]{3,2,1,0:T(8,128)(2,1)}, u32[]{:S(2)}, u32[]{:S(2)}) async-start(bf16[4,2,72,1536]{3,2,1,0:T(8,128)(2,1)} %get-tuple-element.201), calls=%async_computation.8 | async-start | bytes 3538944 | tf_op jit(solution)/shard_map/all_to_all | solution.py:741
  329.5 134.2 %reduce-scatter.3.cloned.1.call-start = ((), (), s32[]{:S(2)}) async-start(), calls=%async_computation.18 | async-start | bytes 7520256 | tf_op jit(solution)/shard_map/reduce_scatter | solution.py:1073
  393.5 29.7 %collective-permute-start.21 = (bf16[16,48,768]{2,1,0:T(8,128)(2,1)}, bf16[16,48,768]{2,1,0:T(8,128)(2,1)}, u32[]{:S(2)}, u32[]{:S(2)}) collective-permute-start(bf16[16,48,768]{2,1,0:T(8,128)(2,1)} %get-tuple-element.219), channel_id=1, source_target_pairs={{0,1},{1,0},{2,3},{3,2},{4,5},{5,4},{6,7},{7,6},{8,9},{9,8},{10,11... | collective-permute-start | bytes 3538952 | tf_op jit(solution)/shard_map/ppermute | solution.py:886
  401.2 21.3 %collective-permute-start.20 = (bf16[128,1536]{1,0:T(8,128)(2,1)}, bf16[128,1536]{1,0:T(8,128)(2,1)}, u32[]{:S(2)}, u32[]{:S(2)}) collective-permute-start(bf16[128,1536]{1,0:T(8,128)(2,1)} %get-tuple-element.223.refs_1_), channel_id=1, source_target_pairs={{96,0},{0,32},{32,64},{64,96},{97,1},{1,33},{33,65},{65,97},{98,2}... | collective-permute-start | bytes 1179656 | tf_op jit(solution)/shard_map/ppermute | solution.py:747
  401.9 20.6 %collective-permute-start.19 = (bf16[128,1536]{1,0:T(8,128)(2,1)}, bf16[128,1536]{1,0:T(8,128)(2,1)}, u32[]{:S(2)}, u32[]{:S(2)}) collective-permute-start(bf16[128,1536]{1,0:T(8,128)(2,1)} %get-tuple-element.223.refs_1_), channel_id=1, source_target_pairs={{64,0},{96,32},{0,64},{32,96},{65,1},{97,33},{1,65},{33,97},{66,2}... | collective-permute-start | bytes 1179656 | tf_op jit(solution)/shard_map/ppermute | solution.py:747
  404.0 19.1 %collective-permute-start.18 = (bf16[128,1536]{1,0:T(8,128)(2,1)}, bf16[128,1536]{1,0:T(8,128)(2,1)}, u32[]{:S(2)}, u32[]{:S(2)}) collective-permute-start(bf16[128,1536]{1,0:T(8,128)(2,1)} %get-tuple-element.223.refs_1_), channel_id=1, source_target_pairs={{32,0},{64,32},{96,64},{0,96},{33,1},{65,33},{97,65},{1,97},{34,2}... | collective-permute-start | bytes 1179656 | tf_op jit(solution)/shard_map/ppermute | solution.py:747
  435.5 28.2 %all-to-all-start.11 = ((bf16[4,2,72,1536]{3,2,1,0:T(8,128)(2,1)}), bf16[4,2,72,1536]{3,2,1,0:T(8,128)(2,1)}, u32[]{:S(2)}, u32[]{:S(2)}) async-start(bf16[4,2,72,1536]{3,2,1,0:T(8,128)(2,1)} %get-tuple-element.230), calls=%async_computation.11 | async-start | bytes 3538944 | tf_op jit(solution)/shard_map/all_to_all | solution.py:741
  439.9 142.6 %reduce-scatter.5.cloned.1.call-start = ((), (), s32[]{:S(2)}) async-start(), calls=%async_computation.19 | async-start | bytes 11280384 | tf_op jit(solution)/shard_map/reduce_scatter | solution.py:1073
  (53 other events, 537.9 us)
Sparse Core Ops, SparseCore 0:
  31.8 88.9 all-gather.6
  136.1 82.3 all-gather.8
  245.4 66.1 all-gather.10
  353.4 82.2 reduce-scatter.2
  463.9 115.7 reduce-scatter.4

commit v9 on v8

--- a/solution.py
+++ b/solution.py
@@ -906,9 +906,10 @@
     dense_flops = 2 * tok_count * width * width
     records = []
     hidden = tokens_in[0]
-    dense = spread_seq(jnp.concatenate([dense_rows_of(0), small_rows_of(1)], axis=1))
-    columns = jnp.concatenate([own_columns(dense), dense[:, -HD:]], axis=1)
-    dense = dense[:, :-HD]
+    dense = spread_seq(jnp.concatenate([dense_rows_of(0), dense_rows_of(1)], axis=1))
+    dense, next_dense = jnp.split(dense, 2, axis=1)
+    next_small = next_dense[:, qkv_width : qkv_width + HD]
+    columns = jnp.concatenate([own_columns(dense), next_small], axis=1)
     both_rows = jnp.concatenate([hidden, cotangent[0]], axis=0)
     columns, both_rows = lax.optimization_barrier((columns, both_rows))
     both_blocks = around_seq(both_rows)
@@ -963,12 +964,11 @@
                 scalar=True, cut={5: ((1, own_at, shard_rows),)}, flops=attention_flops,
             )
         if layer == 0:
-            back, next_rows = lax.optimization_barrier((swap_seq(attended), dense_rows_of(1)))
-            next_dense = spread_seq(next_rows)
+            back = swap_seq(attended)
             next_parts = expert_part(1) + out_part(next_dense) + [own_columns(next_dense)]
             next_parts = jnp.concatenate(next_parts, axis=0)
-            pack, next_parts, back = lax.optimization_barrier((pack, next_parts, back))
-            packs = [pack, fetch([next_parts])]
+            tied, next_parts = lax.optimization_barrier((pack, next_parts))
+            packs = [tied, fetch([next_parts])]
         else:
             back = swap_seq(attended)
             qkv_parts = jnp.concatenate(qkv_part(dense) + qkv_part(next_dense), axis=0)

time: 614 us -> 681 us (1.11)
  waiting for transfers between devices: 183 us -> 260 us
    all_gather x3, waiting for transfers between devices: 0.02 us -> 76.7 us  [fetch(): lax.all_gather(jnp.concatenate(parts, axis=0), 'fsdp', axis=0, tiled=False)]
    all_to_all x12 -> x11, starting transfers between devices: 51.4 us -> 48.8 us  [swap_seq(): return lax.all_to_all(block, 'seq', split_axis=0, concat_axis=0, tiled=True)]
    all_to_all x12 -> x11, waiting for transfers between devices: 79.5 us -> 77 us  [swap_seq(): return lax.all_to_all(block, 'seq', split_axis=0, concat_axis=0, tiled=True)]
  transfers between devices with their start and end apart: 46 -> 45, of which waited for: 26 -> 26; matrix products, arithmetic and copies ran while one was open for 5% -> 4% of each run, Pallas kernels for 29% -> 26%
where the time goes in v9:
time: 681 us; the launch traced here: 673 us
  waiting for transfers between devices  260 us (38%)
  Pallas kernels  197 us (29%)
  blocking collectives  87.1 us (13%)
  starting transfers between devices  78.7 us (12%)
  local copies, waits for them, and re-layouts  21.7 us (3%)
  between operations  15 us (2%)
  other arithmetic  14.4 us (2%)
    pallas_call x28, Pallas kernels, once(): pl.pallas_call(body, out_shape=list(outs), in_specs=specs, out_specs=[hbm...  197 us
    ppermute x15, waiting for transfers between devices, around_seq(): lax.ppermute(block, 'seq', [((i + k) % count, i) for i in range(count)])  97.2 us
    all_to_all x11, waiting for transfers between devices, swap_seq(): return lax.all_to_all(block, 'seq', split_axis=0, concat_axis=0, tiled=True)  77 us
    all_gather x3, waiting for transfers between devices, fetch(): lax.all_gather(jnp.concatenate(parts, axis=0), 'fsdp', axis=0, tiled=False)  76.7 us
    all_to_all x1, blocking collectives, swap_chips(): lax.all_to_all(block, 'fsdp', split_axis=0, concat_axis=0, tiled=True, ax...  62.1 us
    all_to_all x11, starting transfers between devices, swap_seq(): return lax.all_to_all(block, 'seq', split_axis=0, concat_axis=0, tiled=True)  48.8 us
    all_to_all x2, blocking collectives, swap_seq(): return lax.all_to_all(block, 'seq', split_axis=0, concat_axis=0, tiled=True)  25 us
    ppermute x15, starting transfers between devices, around_seq(): lax.ppermute(block, 'seq', [((i + k) % count, i) for i in range(count)])  20.3 us
  transfers between devices with their start and end apart: 45, of which 26 were waited for; matrix products, arithmetic and copies ran while one was open for 4% of the time, Pallas kernels for 26%

profile of v9, /device:TPU:0, one launch (start us, length us, event | category | flops | bytes accessed | tf_op | source)
XLA Modules:
  0.0 673.4 jit_solution(3820679897781757873)
XLA Ops:
  23.1 11.3 %all-to-all-done = bf16[4,12,7424]{2,1,0:T(8,128)(2,1)S(1)} async-done(((bf16[4,12,7424]{2,1,0:T(8,128)(2,1)}), bf16[4,12,7424]{2,1,0:T(8,128)(2,1)S(1)}, u32[]{:S(2)}, u32[]{:S(2)}) %all-to-all-start) | async-done | bytes 712736 | tf_op jit(solution)/shard_map/all_to_all | solution.py:741
  36.0 76.7 %all-gather.7.cloned.1.call-done = bf16[12288,768]{1,0:T(8,128)(2,1)} async-done(((bf16[384,768]{1,0:T(8,128)(2,1)}), bf16[12288,768]{1,0:T(8,128)(2,1)}) %all-gather.7.cloned.1.call-update) | async-done | bytes 18874384 | tf_op jit(solution)/shard_map/all_gather | solution.py:876
  143.5 11.2 %collective-permute-done.2.refs_4_ = bf16[256,1536]{1,0:T(8,128)(2,1)S(1)} collective-permute-done((bf16[256,1536]{1,0:T(8,128)(2,1)S(1)}, bf16[256,1536]{1,0:T(8,128)(2,1)S(1)}, u32[]{:S(2)}, u32[]{:S(2)}) %collective-permute-start.2) | collective-permute-done | bytes 786464 | tf_op jit(solution)/shard_map/ppermute | solution.py:747
  154.7 17.7 %collective-permute-done.1.refs_3_ = bf16[256,1536]{1,0:T(8,128)(2,1)} collective-permute-done((bf16[256,1536]{1,0:T(8,128)(2,1)S(1)}, bf16[256,1536]{1,0:T(8,128)(2,1)}, u32[]{:S(2)}, u32[]{:S(2)}) %collective-permute-start.1) | collective-permute-done | bytes 786464 | tf_op jit(solution)/shard_map/ppermute | solution.py:747
  178.2 11.1 %shard_map.238 = (bf16[4,128,640]{2,1,0:T(8,128)(2,1)}, bf16[4,128,384]{2,1,0:T(8,128)(2,1)}, bf16[4,128,1536]{2,1,0:T(8,128)(2,1)}, bf16[2,16,1536]{2,1,0:T(8,128)(2,1)}) custom-call(s32[1]{0:T(128)} %bitcast.34.refs_0_, bf16[256,1536]{1,0:T(8,128)(2,1)} %copy-done.2, bf16[256,1536]{1,0:T(8,128)(2,1)} %collective-permute-done.refs_2_, ...), custom_call_target="tpu_custom_call" | custom-call | flops 4026531840 | bytes 10485764 | tf_op jit(solution)/shard_map/pallas_call | solution.py:158
  210.7 16.8 %collective-permute-done.6.refs_4_ = bf16[128,1536]{1,0:T(8,128)(2,1)} collective-permute-done((bf16[128,1536]{1,0:T(8,128)(2,1)}, bf16[128,1536]{1,0:T(8,128)(2,1)}, u32[]{:S(2)}, u32[]{:S(2)}) %collective-permute-start.6) | collective-permute-done | bytes 393248 | tf_op jit(solution)/shard_map/ppermute | solution.py:747
  228.1 10.1 %shard_map.240 = (bf16[4,2,72,1536]{3,2,1,0:T(8,128)(2,1)}, bf16[2,288,1536]{2,1,0:T(8,128)(2,1)}, bf16[2,288,768]{2,1,0:T(8,128)(2,1)}, bf16[2,288,768]{2,1,0:T(8,128)(2,1)}, f32[4,8,128]{2,1,0:T(8,128)}) custom-call(s32[1]{0:T(128)} %bitcast.34.refs_0_, bf16[128,1536]{1,0:T(8,128)(2,1)} %get-tuple-element.152.refs_1_.refs_3_, ...), custom_call_target="tpu_custom_call" | custom-call | flops 4076863488 | bytes 120209408 | tf_op jit(solution)/shard_map/pallas_call | solution.py:158
  245.5 8.1 %shard_map.241 = (bf16[2,576,768]{2,1,0:T(8,128)(2,1)}, bf16[256,768]{1,0:T(8,128)(2,1)}) custom-call(bf16[2,288,1536]{2,1,0:T(8,128)(2,1)} %get-tuple-element.156.refs_0_, bf16[2,288,1536]{2,1,0:T(8,128)(2,1)} %collective-permute-done.7.refs_1_, bf16[128,1536]{1,0:T(8,128)(2,1)} %get-tuple-element.157.refs_2_, bf16[128,1536]{1,0:T(8,128)(2,1)} %copy-done.12, ...), custom_call_target="tpu_custom_call" | custom-call | flops 1358954496 | bytes 8847360 | tf_op jit(solution)/shard_map/pallas_call | solution.py:158
  253.7 13.0 %all-to-all-done.4 = bf16[4,2,72,1536]{3,2,1,0:T(8,128)(2,1)} async-done(((bf16[4,2,72,1536]{3,2,1,0:T(8,128)(2,1)}), bf16[4,2,72,1536]{3,2,1,0:T(8,128)(2,1)}, u32[]{:S(2)}, u32[]{:S(2)}) %all-to-all-start.4) | async-done | bytes 1769504 | tf_op jit(solution)/shard_map/all_to_all | solution.py:741
  274.4 17.1 %collective-permute-done.11.refs_4_ = bf16[128,1536]{1,0:T(8,128)(2,1)} collective-permute-done((bf16[128,1536]{1,0:T(8,128)(2,1)}, bf16[128,1536]{1,0:T(8,128)(2,1)}, u32[]{:S(2)}, u32[]{:S(2)}) %collective-permute-start.11) | collective-permute-done | bytes 393248 | tf_op jit(solution)/shard_map/ppermute | solution.py:747
  292.2 7.6 %shard_map.243 = (bf16[4,128,640]{2,1,0:T(8,128)(2,1)}, bf16[4,128,384]{2,1,0:T(8,128)(2,1)}, bf16[4,128,1536]{2,1,0:T(8,128)(2,1)}) custom-call(s32[1]{0:T(128)} %bitcast.34.refs_0_, bf16[128,1536]{1,0:T(8,128)(2,1)} %get-tuple-element.164.refs_1_, bf16[128,1536]{1,0:T(8,128)(2,1)} %collective-permute-done.9.refs_2_, ...), custom_call_target="tpu_custom_call" | custom-call | flops 1610612736 | bytes 27000836 | tf_op jit(solution)/shard_map/pallas_call | solution.py:158
  320.7 15.8 %collective-permute-done.14.refs_4_ = bf16[128,1536]{1,0:T(8,128)(2,1)} collective-permute-done((bf16[128,1536]{1,0:T(8,128)(2,1)}, bf16[128,1536]{1,0:T(8,128)(2,1)}, u32[]{:S(2)}, u32[]{:S(2)}) %collective-permute-start.14) | collective-permute-done | bytes 393248 | tf_op jit(solution)/shard_map/ppermute | solution.py:747
  337.1 10.1 %shard_map.245 = (bf16[4,2,72,1536]{3,2,1,0:T(8,128)(2,1)}, bf16[2,288,1536]{2,1,0:T(8,128)(2,1)}, bf16[2,288,768]{2,1,0:T(8,128)(2,1)}, bf16[2,288,768]{2,1,0:T(8,128)(2,1)}, f32[4,8,128]{2,1,0:T(8,128)}) custom-call(s32[1]{0:T(128)} %bitcast.34.refs_0_, bf16[128,1536]{1,0:T(8,128)(2,1)} %get-tuple-element.172.refs_1_.refs_3_, ...), custom_call_target="tpu_custom_call" | custom-call | flops 4076863488 | bytes 134365184 | tf_op jit(solution)/shard_map/pallas_call | solution.py:158
  355.2 8.4 %shard_map.246 = (bf16[2,576,768]{2,1,0:T(8,128)(2,1)}, bf16[256,768]{1,0:T(8,128)(2,1)}) custom-call(bf16[2,288,1536]{2,1,0:T(8,128)(2,1)} %get-tuple-element.176.refs_0_, bf16[2,288,1536]{2,1,0:T(8,128)(2,1)} %collective-permute-done.15.refs_1_, bf16[128,1536]{1,0:T(8,128)(2,1)} %get-tuple-element.177.refs_2_, bf16[128,1536]{1,0:T(8,128)(2,1)} %copy-done.11, ...), custom_call_target="tpu_custom_call" | custom-call | flops 1358954496 | bytes 8847360 | tf_op jit(solution)/shard_map/pallas_call | solution.py:158
  363.6 12.1 %all-to-all-done.6 = bf16[4,2,72,1536]{3,2,1,0:T(8,128)(2,1)} async-done(((bf16[4,2,72,1536]{3,2,1,0:T(8,128)(2,1)}), bf16[4,2,72,1536]{3,2,1,0:T(8,128)(2,1)}, u32[]{:S(2)}, u32[]{:S(2)}) %all-to-all-start.6) | async-done | bytes 1769504 | tf_op jit(solution)/shard_map/all_to_all | solution.py:741
  379.3 12.3 %shard_map.248 = (bf16[4,2,72,1536]{3,2,1,0:T(8,128)(2,1)}, bf16[2,288,3840]{2,1,0:T(8,128)(2,1)}) custom-call(s32[1]{0:T(128)} %bitcast.34.refs_0_, bf16[256,1536]{1,0:T(8,128)(2,1)} %copy-done.2, bf16[256,1536]{1,0:T(8,128)(2,1)} %collective-permute-done.refs_2_, bf16[256,1536]{1,0:T(8,128)(2,1)} %collective-permute-done.1.refs_3_, ...), custom_call_target="tpu_custom_call" | custom-call | flops 4076863488 | bytes 138534912 | tf_op jit(solution)/shard_map/pallas_call | solution.py:158
  400.7 12.7 %shard_map.249 = bf16[16,288,768]{2,1,0:T(8,128)(2,1)} custom-call(s32[1]{0:T(128)} %bitcast.59.refs_0_, bf16[2,576,768]{2,1,0:T(8,128)(2,1)} %get-tuple-element.194.refs_1_, bf16[768,384]{1,0:T(8,128)(2,1)} %fusion.1.refs_2_, bf16[2,288,3840]{2,1,0:T(8,128)(2,1)} %get-tuple-element.196.refs_3_, bf16[2,288,3840]{2,1,0:T(8,128)(2,1)} %collective-permute-done.17.refs_4_), custom_call_target="tpu_custom_call" | custom-call | flops 8153726976 | bytes 18284548 | tf_op jit(solution)/shard_map/pallas_call | solution.py:158
  426.7 12.4 %all_to_all.75.refs_1_ = bf16[4,128,384]{2,1,0:T(8,128)(2,1)} all-to-all(bf16[4,128,384]{2,1,0:T(8,128)(2,1)} %get-tuple-element.200), channel_id=1, replica_groups=mesh['seq'=4,'fsdp'=32] {'seq'}, dimensions={0} | all-to-all | bytes 786432 | tf_op jit(solution)/shard_map/all_to_all | solution.py:741
  473.1 16.1 %collective-permute-done.20.refs_4_ = bf16[128,1536]{1,0:T(8,128)(2,1)} collective-permute-done((bf16[128,1536]{1,0:T(8,128)(2,1)}, bf16[128,1536]{1,0:T(8,128)(2,1)}, u32[]{:S(2)}, u32[]{:S(2)}) %collective-permute-start.20) | collective-permute-done | bytes 393248 | tf_op jit(solution)/shard_map/ppermute | solution.py:747
  489.9 12.2 %shard_map.255 = (bf16[4,2,72,1536]{3,2,1,0:T(8,128)(2,1)}, bf16[2,288,3840]{2,1,0:T(8,128)(2,1)}) custom-call(s32[1]{0:T(128)} %bitcast.34.refs_0_, bf16[128,1536]{1,0:T(8,128)(2,1)} %get-tuple-element.215.refs_1_, bf16[128,1536]{1,0:T(8,128)(2,1)} %collective-permute-done.18.refs_2_, bf16[128,1536]{1,0:T(8,128)(2,1)} %collective-permute-done.19.refs_3_, ...), custom_call_target="tpu_custom_call" | custom-call | flops 4076863488 | bytes 122806272 | tf_op jit(solution)/shard_map/pallas_call | solution.py:158
  510.4 15.4 %shard_map.256 = bf16[16,432,768]{2,1,0:T(8,128)(2,1)} custom-call(s32[1]{0:T(128)} %bitcast.59.refs_0_, bf16[2,576,768]{2,1,0:T(8,128)(2,1)} %get-tuple-element.223.refs_1_, bf16[768,384]{1,0:T(8,128)(2,1)} %fusion.1.refs_2_, bf16[2,288,3840]{2,1,0:T(8,128)(2,1)} %get-tuple-element.224.refs_3_, bf16[2,288,3840]{2,1,0:T(8,128)(2,1)} %collective-permute-done.24.refs_4_, ...), custom_call_target="tpu_custom_call" | custom-call | flops 8153726976 | bytes 25755652 | tf_op jit(solution)/shard_map/pallas_call | solution.py:158
  537.0 12.6 %all_to_all.76.refs_1_ = bf16[4,128,384]{2,1,0:T(8,128)(2,1)} all-to-all(bf16[4,128,384]{2,1,0:T(8,128)(2,1)} %get-tuple-element.235), channel_id=1, replica_groups=mesh['seq'=4,'fsdp'=32] {'seq'}, dimensions={0} | all-to-all | bytes 786432 | tf_op jit(solution)/shard_map/all_to_all | solution.py:741
  571.0 7.4 %shard_map.261 = (f32[128,1536]{1,0:T(8,128)}, bf16[128,1536]{1,0:T(8,128)(2,1)}, f32[8,1536]{1,0:T(8,128)}) custom-call(bf16[4,128,640]{2,1,0:T(8,128)(2,1)} %all-to-all-done.12.refs_0_, bf16[32,288,768]{2,1,0:T(8,128)(2,1)} %bitcast.185, bf16[32,288,768]{2,1,0:T(8,128)(2,1)} %bitcast.186, bf16[32,288,768]{2,1,0:T(8,128)(2,1)} %bitcast.187, ...), custom_call_target="tpu_custom_call" | custom-call | flops 2415919104 | bytes 45875200 | tf_op jit(solution)/shard_map/pallas_call | solution.py:158
  586.1 62.1 %all_to_all.77 = bf16[16,144,768]{2,1,0:T(8,128)(2,1)S(1)} all-to-all(bf16[16,144,768]{2,1,0:T(8,128)(2,1)} %shard_map.262), channel_id=1, replica_groups={{0,2,4,6,8,10,12,14,16,18,20,22,24,26,28,30},{1,3,5,7,9,11,13,15,17,19,..., dimensions={0} | all-to-all | bytes 7077888 | tf_op jit(solution)/shard_map/all_to_all | solution.py:881
  (239 shorter events, 248.0 us)
Async XLA Ops:
  15.0 19.4 %all-to-all-start = ((bf16[4,12,7424]{2,1,0:T(8,128)(2,1)}), bf16[4,12,7424]{2,1,0:T(8,128)(2,1)S(1)}, u32[]{:S(2)}, u32[]{:S(2)}) async-start(bf16[4,12,7424]{2,1,0:T(8,128)(2,1)} %broadcast_in_dim.26), calls=%async_computation | async-start | bytes 1900544 | tf_op jit(solution)/shard_map/all_to_all | solution.py:741
  20.4 92.3 %all-gather.7.cloned.1.call-start = ((), (), s32[]{:S(2)}) async-start(), calls=%async_computation.19 | async-start | bytes 19464192 | tf_op jit(solution)/shard_map/all_gather | solution.py:876
  35.6 256.5 %all-gather.9.cloned.1.call-start = ((), (), s32[]{:S(2)}) async-start(), calls=%async_computation.20 | async-start | bytes 21897216 | tf_op jit(solution)/shard_map/all_gather | solution.py:876
  127.0 45.4 %all-to-all-start.1 = ((bf16[16,48,896]{2,1,0:T(8,128)(2,1)}), bf16[16,48,896]{2,1,0:T(8,128)(2,1)S(1)}, u32[]{:S(2)}, u32[]{:S(2)}) async-start(bf16[16,48,896]{2,1,0:T(8,128)(2,1)} %broadcast_in_dim.27), calls=%async_computation.1 | async-start | bytes 2752512 | tf_op jit(solution)/shard_map/all_to_all | solution.py:881
  133.8 20.9 %collective-permute-start.2 = (bf16[256,1536]{1,0:T(8,128)(2,1)S(1)}, bf16[256,1536]{1,0:T(8,128)(2,1)S(1)}, u32[]{:S(2)}, u32[]{:S(2)}) collective-permute-start(bf16[256,1536]{1,0:T(8,128)(2,1)S(1)} %pad_maximum_fusion.1.refs_1_), channel_id=1, source_target_pairs={{96,0},{0,32},{32,64},{64,96},{97,1},{1,33},{33,65},{65,97},{98,2}... | collective-permute-start | bytes 2359304 | tf_op jit(solution)/shard_map/ppermute | solution.py:747
  135.9 36.5 %collective-permute-start.1 = (bf16[256,1536]{1,0:T(8,128)(2,1)S(1)}, bf16[256,1536]{1,0:T(8,128)(2,1)}, u32[]{:S(2)}, u32[]{:S(2)}) collective-permute-start(bf16[256,1536]{1,0:T(8,128)(2,1)S(1)} %pad_maximum_fusion.1.refs_1_), channel_id=1, source_target_pairs={{64,0},{96,32},{0,64},{32,96},{65,1},{97,33},{1,65},{33,97},{66,2}... | collective-permute-start | bytes 2359304 | tf_op jit(solution)/shard_map/ppermute | solution.py:747
  138.6 33.8 %collective-permute-start = (bf16[256,1536]{1,0:T(8,128)(2,1)S(1)}, bf16[256,1536]{1,0:T(8,128)(2,1)}, u32[]{:S(2)}, u32[]{:S(2)}) collective-permute-start(bf16[256,1536]{1,0:T(8,128)(2,1)S(1)} %pad_maximum_fusion.1.refs_1_), channel_id=1, source_target_pairs={{32,0},{64,32},{96,64},{0,96},{33,1},{65,33},{97,65},{1,97},{34,2}... | collective-permute-start | bytes 2359304 | tf_op jit(solution)/shard_map/ppermute | solution.py:747
  207.2 20.2 %collective-permute-start.6 = (bf16[128,1536]{1,0:T(8,128)(2,1)}, bf16[128,1536]{1,0:T(8,128)(2,1)}, u32[]{:S(2)}, u32[]{:S(2)}) collective-permute-start(bf16[128,1536]{1,0:T(8,128)(2,1)} %get-tuple-element.152.refs_1_.refs_3_), channel_id=1, source_target_pairs={{96,0},{0,32},{32,64},{64,96},{97,1},{1,33},{33,65},{65,97},{98,2}... | collective-permute-start | bytes 1179656 | tf_op jit(solution)/shard_map/ppermute | solution.py:747
  207.8 19.7 %collective-permute-start.5 = (bf16[128,1536]{1,0:T(8,128)(2,1)}, bf16[128,1536]{1,0:T(8,128)(2,1)}, u32[]{:S(2)}, u32[]{:S(2)}) collective-permute-start(bf16[128,1536]{1,0:T(8,128)(2,1)} %get-tuple-element.152.refs_1_.refs_3_), channel_id=1, source_target_pairs={{64,0},{96,32},{0,64},{32,96},{65,1},{97,33},{1,65},{33,97},{66,2}... | collective-permute-start | bytes 1179656 | tf_op jit(solution)/shard_map/ppermute | solution.py:747
  238.3 28.3 %all-to-all-start.4 = ((bf16[4,2,72,1536]{3,2,1,0:T(8,128)(2,1)}), bf16[4,2,72,1536]{3,2,1,0:T(8,128)(2,1)}, u32[]{:S(2)}, u32[]{:S(2)}) async-start(bf16[4,2,72,1536]{3,2,1,0:T(8,128)(2,1)} %get-tuple-element.155), calls=%async_computation.4 | async-start | bytes 3538944 | tf_op jit(solution)/shard_map/all_to_all | solution.py:741
  270.8 20.7 %collective-permute-start.11 = (bf16[128,1536]{1,0:T(8,128)(2,1)}, bf16[128,1536]{1,0:T(8,128)(2,1)}, u32[]{:S(2)}, u32[]{:S(2)}) collective-permute-start(bf16[128,1536]{1,0:T(8,128)(2,1)} %get-tuple-element.164.refs_1_), channel_id=1, source_target_pairs={{96,0},{0,32},{32,64},{64,96},{97,1},{1,33},{33,65},{65,97},{98,2}... | collective-permute-start | bytes 1179656 | tf_op jit(solution)/shard_map/ppermute | solution.py:747
  271.4 20.1 %collective-permute-start.10 = (bf16[128,1536]{1,0:T(8,128)(2,1)}, bf16[128,1536]{1,0:T(8,128)(2,1)}, u32[]{:S(2)}, u32[]{:S(2)}) collective-permute-start(bf16[128,1536]{1,0:T(8,128)(2,1)} %get-tuple-element.164.refs_1_), channel_id=1, source_target_pairs={{64,0},{96,32},{0,64},{32,96},{65,1},{97,33},{1,65},{33,97},{66,2}... | collective-permute-start | bytes 1179656 | tf_op jit(solution)/shard_map/ppermute | solution.py:747
  273.5 18.7 %collective-permute-start.9 = (bf16[128,1536]{1,0:T(8,128)(2,1)}, bf16[128,1536]{1,0:T(8,128)(2,1)}, u32[]{:S(2)}, u32[]{:S(2)}) collective-permute-start(bf16[128,1536]{1,0:T(8,128)(2,1)} %get-tuple-element.164.refs_1_), channel_id=1, source_target_pairs={{32,0},{64,32},{96,64},{0,96},{33,1},{65,33},{97,65},{1,97},{34,2}... | collective-permute-start | bytes 1179656 | tf_op jit(solution)/shard_map/ppermute | solution.py:747
  303.9 75.4 %all-gather.11.cloned.1.call-start = ((), (), s32[]{:S(2)}) async-start(), calls=%async_computation.21 | async-start | bytes 14598144 | tf_op jit(solution)/shard_map/all_gather | solution.py:876
  317.1 19.4 %collective-permute-start.14 = (bf16[128,1536]{1,0:T(8,128)(2,1)}, bf16[128,1536]{1,0:T(8,128)(2,1)}, u32[]{:S(2)}, u32[]{:S(2)}) collective-permute-start(bf16[128,1536]{1,0:T(8,128)(2,1)} %get-tuple-element.172.refs_1_.refs_3_), channel_id=1, source_target_pairs={{96,0},{0,32},{32,64},{64,96},{97,1},{1,33},{33,65},{65,97},{98,2}... | collective-permute-start | bytes 1179656 | tf_op jit(solution)/shard_map/ppermute | solution.py:747
  347.3 28.3 %all-to-all-start.6 = ((bf16[4,2,72,1536]{3,2,1,0:T(8,128)(2,1)}), bf16[4,2,72,1536]{3,2,1,0:T(8,128)(2,1)}, u32[]{:S(2)}, u32[]{:S(2)}) async-start(bf16[4,2,72,1536]{3,2,1,0:T(8,128)(2,1)} %get-tuple-element.175), calls=%async_computation.6 | async-start | bytes 3538944 | tf_op jit(solution)/shard_map/all_to_all | solution.py:741
  391.7 28.3 %all-to-all-start.7 = ((bf16[4,2,72,1536]{3,2,1,0:T(8,128)(2,1)}), bf16[4,2,72,1536]{3,2,1,0:T(8,128)(2,1)}, u32[]{:S(2)}, u32[]{:S(2)}) async-start(bf16[4,2,72,1536]{3,2,1,0:T(8,128)(2,1)} %get-tuple-element.193), calls=%async_computation.7 | async-start | bytes 3538944 | tf_op jit(solution)/shard_map/all_to_all | solution.py:741
  396.2 134.2 %reduce-scatter.3.cloned.1.call-start = ((), (), s32[]{:S(2)}) async-start(), calls=%async_computation.17 | async-start | bytes 7520256 | tf_op jit(solution)/shard_map/reduce_scatter | solution.py:1073
  460.1 29.7 %collective-permute-start.21 = (bf16[16,48,768]{2,1,0:T(8,128)(2,1)}, bf16[16,48,768]{2,1,0:T(8,128)(2,1)}, u32[]{:S(2)}, u32[]{:S(2)}) collective-permute-start(bf16[16,48,768]{2,1,0:T(8,128)(2,1)} %get-tuple-element.211), channel_id=1, source_target_pairs={{0,1},{1,0},{2,3},{3,2},{4,5},{5,4},{6,7},{7,6},{8,9},{9,8},{10,11... | collective-permute-start | bytes 3538952 | tf_op jit(solution)/shard_map/ppermute | solution.py:886
  467.9 21.3 %collective-permute-start.20 = (bf16[128,1536]{1,0:T(8,128)(2,1)}, bf16[128,1536]{1,0:T(8,128)(2,1)}, u32[]{:S(2)}, u32[]{:S(2)}) collective-permute-start(bf16[128,1536]{1,0:T(8,128)(2,1)} %get-tuple-element.215.refs_1_), channel_id=1, source_target_pairs={{96,0},{0,32},{32,64},{64,96},{97,1},{1,33},{33,65},{65,97},{98,2}... | collective-permute-start | bytes 1179656 | tf_op jit(solution)/shard_map/ppermute | solution.py:747
  468.6 20.6 %collective-permute-start.19 = (bf16[128,1536]{1,0:T(8,128)(2,1)}, bf16[128,1536]{1,0:T(8,128)(2,1)}, u32[]{:S(2)}, u32[]{:S(2)}) collective-permute-start(bf16[128,1536]{1,0:T(8,128)(2,1)} %get-tuple-element.215.refs_1_), channel_id=1, source_target_pairs={{64,0},{96,32},{0,64},{32,96},{65,1},{97,33},{1,65},{33,97},{66,2}... | collective-permute-start | bytes 1179656 | tf_op jit(solution)/shard_map/ppermute | solution.py:747
  470.7 19.1 %collective-permute-start.18 = (bf16[128,1536]{1,0:T(8,128)(2,1)}, bf16[128,1536]{1,0:T(8,128)(2,1)}, u32[]{:S(2)}, u32[]{:S(2)}) collective-permute-start(bf16[128,1536]{1,0:T(8,128)(2,1)} %get-tuple-element.215.refs_1_), channel_id=1, source_target_pairs={{32,0},{64,32},{96,64},{0,96},{33,1},{65,33},{97,65},{1,97},{34,2}... | collective-permute-start | bytes 1179656 | tf_op jit(solution)/shard_map/ppermute | solution.py:747
  502.2 28.2 %all-to-all-start.10 = ((bf16[4,2,72,1536]{3,2,1,0:T(8,128)(2,1)}), bf16[4,2,72,1536]{3,2,1,0:T(8,128)(2,1)}, u32[]{:S(2)}, u32[]{:S(2)}) async-start(bf16[4,2,72,1536]{3,2,1,0:T(8,128)(2,1)} %get-tuple-element.222), calls=%async_computation.10 | async-start | bytes 3538944 | tf_op jit(solution)/shard_map/all_to_all | solution.py:741
  506.6 142.9 %reduce-scatter.5.cloned.1.call-start = ((), (), s32[]{:S(2)}) async-start(), calls=%async_computation.18 | async-start | bytes 11280384 | tf_op jit(solution)/shard_map/reduce_scatter | solution.py:1073
  (43 other events, 856.8 us)
Sparse Core Ops, SparseCore 0:
  35.8 76.9 all-gather.6
  115.0 96.3 all-gather.8
  312.2 66.3 all-gather.10
  420.2 82.5 reduce-scatter.2
  530.5 116.0 reduce-scatter.4

commit v10 on v9

--- a/solution.py
+++ b/solution.py
@@ -967,8 +967,8 @@
             back = swap_seq(attended)
             next_parts = expert_part(1) + out_part(next_dense) + [own_columns(next_dense)]
             next_parts = jnp.concatenate(next_parts, axis=0)
-            tied, next_parts = lax.optimization_barrier((pack, next_parts))
-            packs = [tied, fetch([next_parts])]
+            pack, next_parts, back = lax.optimization_barrier((pack, next_parts, back))
+            packs = [pack, fetch([next_parts])]
         else:
             back = swap_seq(attended)
             qkv_parts = jnp.concatenate(qkv_part(dense) + qkv_part(next_dense), axis=0)

time: 681 us -> 605 us (0.89)
  waiting for transfers between devices: 260 us -> 181 us
    all_gather x3, waiting for transfers between devices: 76.7 us -> 0.02 us  [fetch(): lax.all_gather(jnp.concatenate(parts, axis=0), 'fsdp', axis=0, tiled=False)]
  transfers between devices with their start and end apart: 45 -> 45, of which waited for: 26 -> 25; matrix products, arithmetic and copies ran while one was open for 4% -> 4% of each run, Pallas kernels for 26% -> 29%
where the time goes in v10:
time: 605 us; the launch traced here: 597 us
  Pallas kernels  197 us (33%)
  waiting for transfers between devices  181 us (30%)
  blocking collectives  86.4 us (14%)
  starting transfers between devices  81.3 us (13%)
  local copies, waits for them, and re-layouts  21.7 us (4%)
  other arithmetic  15 us (2%)
  between operations  15 us (2%)
    pallas_call x28, Pallas kernels, once(): pl.pallas_call(body, out_shape=list(outs), in_specs=specs, out_specs=[hbm...  197 us
    ppermute x15, waiting for transfers between devices, around_seq(): lax.ppermute(block, 'seq', [((i + k) % count, i) for i in range(count)])  95 us
    all_to_all x11, waiting for transfers between devices, swap_seq(): return lax.all_to_all(block, 'seq', split_axis=0, concat_axis=0, tiled=True)  76.5 us
    all_to_all x1, blocking collectives, swap_chips(): lax.all_to_all(block, 'fsdp', split_axis=0, concat_axis=0, tiled=True, ax...  61.4 us
    all_to_all x11, starting transfers between devices, swap_seq(): return lax.all_to_all(block, 'seq', split_axis=0, concat_axis=0, tiled=True)  47.8 us
    all_to_all x2, blocking collectives, swap_seq(): return lax.all_to_all(block, 'seq', split_axis=0, concat_axis=0, tiled=True)  25 us
    ppermute x15, starting transfers between devices, around_seq(): lax.ppermute(block, 'seq', [((i + k) % count, i) for i in range(count)])  21.9 us
  transfers between devices with their start and end apart: 45, of which 25 were waited for; matrix products, arithmetic and copies ran while one was open for 4% of the time, Pallas kernels for 29%

profile of v10, /device:TPU:0, one launch (start us, length us, event | category | flops | bytes accessed | tf_op | source)
XLA Modules:
  0.0 597.1 jit_solution(9882739581078159981)
XLA Ops:
  21.3 13.1 %all-to-all-done = bf16[4,12,7424]{2,1,0:T(8,128)(2,1)S(1)} async-done(((bf16[4,12,7424]{2,1,0:T(8,128)(2,1)}), bf16[4,12,7424]{2,1,0:T(8,128)(2,1)S(1)}, u32[]{:S(2)}, u32[]{:S(2)}) %all-to-all-start) | async-done | bytes 712736 | tf_op jit(solution)/shard_map/all_to_all | solution.py:741
  68.5 11.3 %collective-permute-done.2.refs_4_ = bf16[256,1536]{1,0:T(8,128)(2,1)S(1)} collective-permute-done((bf16[256,1536]{1,0:T(8,128)(2,1)S(1)}, bf16[256,1536]{1,0:T(8,128)(2,1)S(1)}, u32[]{:S(2)}, u32[]{:S(2)}) %collective-permute-start.2) | collective-permute-done | bytes 786464 | tf_op jit(solution)/shard_map/ppermute | solution.py:747
  79.8 16.2 %collective-permute-done.1.refs_3_ = bf16[256,1536]{1,0:T(8,128)(2,1)} collective-permute-done((bf16[256,1536]{1,0:T(8,128)(2,1)S(1)}, bf16[256,1536]{1,0:T(8,128)(2,1)}, u32[]{:S(2)}, u32[]{:S(2)}) %collective-permute-start.1) | collective-permute-done | bytes 786464 | tf_op jit(solution)/shard_map/ppermute | solution.py:747
  101.8 11.1 %shard_map.238 = (bf16[4,128,640]{2,1,0:T(8,128)(2,1)}, bf16[4,128,384]{2,1,0:T(8,128)(2,1)}, bf16[4,128,1536]{2,1,0:T(8,128)(2,1)}, bf16[2,16,1536]{2,1,0:T(8,128)(2,1)}) custom-call(s32[1]{0:T(128)} %bitcast.34.refs_0_, bf16[256,1536]{1,0:T(8,128)(2,1)} %copy-done.2, bf16[256,1536]{1,0:T(8,128)(2,1)} %collective-permute-done.refs_2_, ...), custom_call_target="tpu_custom_call" | custom-call | flops 4026531840 | bytes 10485764 | tf_op jit(solution)/shard_map/pallas_call | solution.py:158
  143.4 9.6 %collective-permute-done.5.refs_3_ = bf16[128,1536]{1,0:T(8,128)(2,1)} collective-permute-done((bf16[128,1536]{1,0:T(8,128)(2,1)}, bf16[128,1536]{1,0:T(8,128)(2,1)}, u32[]{:S(2)}, u32[]{:S(2)}) %collective-permute-start.5) | collective-permute-done | bytes 393248 | tf_op jit(solution)/shard_map/ppermute | solution.py:747
  153.0 10.1 %shard_map.240 = (bf16[4,2,72,1536]{3,2,1,0:T(8,128)(2,1)}, bf16[2,288,1536]{2,1,0:T(8,128)(2,1)}, bf16[2,288,768]{2,1,0:T(8,128)(2,1)}, bf16[2,288,768]{2,1,0:T(8,128)(2,1)}, f32[4,8,128]{2,1,0:T(8,128)}) custom-call(s32[1]{0:T(128)} %bitcast.34.refs_0_, bf16[128,1536]{1,0:T(8,128)(2,1)} %get-tuple-element.156.refs_1_.refs_3_, ...), custom_call_target="tpu_custom_call" | custom-call | flops 4076863488 | bytes 120209408 | tf_op jit(solution)/shard_map/pallas_call | solution.py:158
  170.8 8.5 %shard_map.241 = (bf16[2,576,768]{2,1,0:T(8,128)(2,1)}, bf16[256,768]{1,0:T(8,128)(2,1)}) custom-call(bf16[2,288,1536]{2,1,0:T(8,128)(2,1)} %get-tuple-element.160.refs_0_, bf16[2,288,1536]{2,1,0:T(8,128)(2,1)} %collective-permute-done.7.refs_1_, bf16[128,1536]{1,0:T(8,128)(2,1)} %get-tuple-element.161.refs_2_, bf16[128,1536]{1,0:T(8,128)(2,1)} %copy-done.12, ...), custom_call_target="tpu_custom_call" | custom-call | flops 1358954496 | bytes 8847360 | tf_op jit(solution)/shard_map/pallas_call | solution.py:158
  179.3 12.2 %all-to-all-done.4 = bf16[4,2,72,1536]{3,2,1,0:T(8,128)(2,1)} async-done(((bf16[4,2,72,1536]{3,2,1,0:T(8,128)(2,1)}), bf16[4,2,72,1536]{3,2,1,0:T(8,128)(2,1)}, u32[]{:S(2)}, u32[]{:S(2)}) %all-to-all-start.4) | async-done | bytes 1769504 | tf_op jit(solution)/shard_map/all_to_all | solution.py:741
  199.4 17.0 %collective-permute-done.11.refs_4_ = bf16[128,1536]{1,0:T(8,128)(2,1)} collective-permute-done((bf16[128,1536]{1,0:T(8,128)(2,1)}, bf16[128,1536]{1,0:T(8,128)(2,1)}, u32[]{:S(2)}, u32[]{:S(2)}) %collective-permute-start.11) | collective-permute-done | bytes 393248 | tf_op jit(solution)/shard_map/ppermute | solution.py:747
  217.1 7.6 %shard_map.243 = (bf16[4,128,640]{2,1,0:T(8,128)(2,1)}, bf16[4,128,384]{2,1,0:T(8,128)(2,1)}, bf16[4,128,1536]{2,1,0:T(8,128)(2,1)}) custom-call(s32[1]{0:T(128)} %bitcast.34.refs_0_, bf16[128,1536]{1,0:T(8,128)(2,1)} %get-tuple-element.168.refs_1_, bf16[128,1536]{1,0:T(8,128)(2,1)} %collective-permute-done.9.refs_2_, ...), custom_call_target="tpu_custom_call" | custom-call | flops 1610612736 | bytes 27000836 | tf_op jit(solution)/shard_map/pallas_call | solution.py:158
  245.6 15.9 %collective-permute-done.14.refs_4_ = bf16[128,1536]{1,0:T(8,128)(2,1)} collective-permute-done((bf16[128,1536]{1,0:T(8,128)(2,1)}, bf16[128,1536]{1,0:T(8,128)(2,1)}, u32[]{:S(2)}, u32[]{:S(2)}) %collective-permute-start.14) | collective-permute-done | bytes 393248 | tf_op jit(solution)/shard_map/ppermute | solution.py:747
  262.1 10.1 %shard_map.245 = (bf16[4,2,72,1536]{3,2,1,0:T(8,128)(2,1)}, bf16[2,288,1536]{2,1,0:T(8,128)(2,1)}, bf16[2,288,768]{2,1,0:T(8,128)(2,1)}, bf16[2,288,768]{2,1,0:T(8,128)(2,1)}, f32[4,8,128]{2,1,0:T(8,128)}) custom-call(s32[1]{0:T(128)} %bitcast.34.refs_0_, bf16[128,1536]{1,0:T(8,128)(2,1)} %get-tuple-element.176.refs_1_.refs_3_, ...), custom_call_target="tpu_custom_call" | custom-call | flops 4076863488 | bytes 134365184 | tf_op jit(solution)/shard_map/pallas_call | solution.py:158
  280.4 8.3 %shard_map.246 = (bf16[2,576,768]{2,1,0:T(8,128)(2,1)}, bf16[256,768]{1,0:T(8,128)(2,1)}) custom-call(bf16[2,288,1536]{2,1,0:T(8,128)(2,1)} %get-tuple-element.180.refs_0_, bf16[2,288,1536]{2,1,0:T(8,128)(2,1)} %collective-permute-done.15.refs_1_, bf16[128,1536]{1,0:T(8,128)(2,1)} %get-tuple-element.181.refs_2_, bf16[128,1536]{1,0:T(8,128)(2,1)} %copy-done.11, ...), custom_call_target="tpu_custom_call" | custom-call | flops 1358954496 | bytes 8847360 | tf_op jit(solution)/shard_map/pallas_call | solution.py:158
  288.7 12.0 %all-to-all-done.6 = bf16[4,2,72,1536]{3,2,1,0:T(8,128)(2,1)} async-done(((bf16[4,2,72,1536]{3,2,1,0:T(8,128)(2,1)}), bf16[4,2,72,1536]{3,2,1,0:T(8,128)(2,1)}, u32[]{:S(2)}, u32[]{:S(2)}) %all-to-all-start.6) | async-done | bytes 1769504 | tf_op jit(solution)/shard_map/all_to_all | solution.py:741
  304.4 12.2 %shard_map.248 = (bf16[4,2,72,1536]{3,2,1,0:T(8,128)(2,1)}, bf16[2,288,3840]{2,1,0:T(8,128)(2,1)}) custom-call(s32[1]{0:T(128)} %bitcast.34.refs_0_, bf16[256,1536]{1,0:T(8,128)(2,1)} %copy-done.2, bf16[256,1536]{1,0:T(8,128)(2,1)} %collective-permute-done.refs_2_, bf16[256,1536]{1,0:T(8,128)(2,1)} %collective-permute-done.1.refs_3_, ...), custom_call_target="tpu_custom_call" | custom-call | flops 4076863488 | bytes 138534912 | tf_op jit(solution)/shard_map/pallas_call | solution.py:158
  325.8 12.7 %shard_map.249 = bf16[16,288,768]{2,1,0:T(8,128)(2,1)} custom-call(s32[1]{0:T(128)} %bitcast.59.refs_0_, bf16[2,576,768]{2,1,0:T(8,128)(2,1)} %get-tuple-element.198.refs_1_, bf16[768,384]{1,0:T(8,128)(2,1)} %fusion.1.refs_2_, bf16[2,288,3840]{2,1,0:T(8,128)(2,1)} %get-tuple-element.200.refs_3_, bf16[2,288,3840]{2,1,0:T(8,128)(2,1)} %collective-permute-done.17.refs_4_), custom_call_target="tpu_custom_call" | custom-call | flops 8153726976 | bytes 18284548 | tf_op jit(solution)/shard_map/pallas_call | solution.py:158
  351.8 12.4 %all_to_all.75.refs_1_ = bf16[4,128,384]{2,1,0:T(8,128)(2,1)} all-to-all(bf16[4,128,384]{2,1,0:T(8,128)(2,1)} %get-tuple-element.204), channel_id=1, replica_groups=mesh['seq'=4,'fsdp'=32] {'seq'}, dimensions={0} | all-to-all | bytes 786432 | tf_op jit(solution)/shard_map/all_to_all | solution.py:741
  385.8 7.2 %shard_map.254 = (f32[128,1536]{1,0:T(8,128)}, bf16[128,1536]{1,0:T(8,128)(2,1)}, f32[8,1536]{1,0:T(8,128)}) custom-call(bf16[4,128,640]{2,1,0:T(8,128)(2,1)} %all-to-all-done.9.refs_0_, bf16[32,288,768]{2,1,0:T(8,128)(2,1)} %bitcast.182, bf16[32,288,768]{2,1,0:T(8,128)(2,1)} %bitcast.183, bf16[32,288,768]{2,1,0:T(8,128)(2,1)} %bitcast.184, ...), custom_call_target="tpu_custom_call" | custom-call | flops 2415919104 | bytes 46268416 | tf_op jit(solution)/shard_map/pallas_call | solution.py:158
  398.2 16.2 %collective-permute-done.20.refs_4_ = bf16[128,1536]{1,0:T(8,128)(2,1)} collective-permute-done((bf16[128,1536]{1,0:T(8,128)(2,1)}, bf16[128,1536]{1,0:T(8,128)(2,1)}, u32[]{:S(2)}, u32[]{:S(2)}) %collective-permute-start.20) | collective-permute-done | bytes 393248 | tf_op jit(solution)/shard_map/ppermute | solution.py:747
  415.0 12.2 %shard_map.255 = (bf16[4,2,72,1536]{3,2,1,0:T(8,128)(2,1)}, bf16[2,288,3840]{2,1,0:T(8,128)(2,1)}) custom-call(s32[1]{0:T(128)} %bitcast.34.refs_0_, bf16[128,1536]{1,0:T(8,128)(2,1)} %get-tuple-element.219.refs_1_, bf16[128,1536]{1,0:T(8,128)(2,1)} %collective-permute-done.18.refs_2_, bf16[128,1536]{1,0:T(8,128)(2,1)} %collective-permute-done.19.refs_3_, ...), custom_call_target="tpu_custom_call" | custom-call | flops 4076863488 | bytes 122806272 | tf_op jit(solution)/shard_map/pallas_call | solution.py:158
  435.5 15.4 %shard_map.256 = bf16[16,432,768]{2,1,0:T(8,128)(2,1)} custom-call(s32[1]{0:T(128)} %bitcast.59.refs_0_, bf16[2,576,768]{2,1,0:T(8,128)(2,1)} %get-tuple-element.227.refs_1_, bf16[768,384]{1,0:T(8,128)(2,1)} %fusion.1.refs_2_, bf16[2,288,3840]{2,1,0:T(8,128)(2,1)} %get-tuple-element.228.refs_3_, bf16[2,288,3840]{2,1,0:T(8,128)(2,1)} %collective-permute-done.24.refs_4_, ...), custom_call_target="tpu_custom_call" | custom-call | flops 8153726976 | bytes 25755652 | tf_op jit(solution)/shard_map/pallas_call | solution.py:158
  462.2 12.6 %all_to_all.76.refs_1_ = bf16[4,128,384]{2,1,0:T(8,128)(2,1)} all-to-all(bf16[4,128,384]{2,1,0:T(8,128)(2,1)} %get-tuple-element.239), channel_id=1, replica_groups=mesh['seq'=4,'fsdp'=32] {'seq'}, dimensions={0} | all-to-all | bytes 786432 | tf_op jit(solution)/shard_map/all_to_all | solution.py:741
  496.1 7.3 %shard_map.261 = (f32[128,1536]{1,0:T(8,128)}, bf16[128,1536]{1,0:T(8,128)(2,1)}, f32[8,1536]{1,0:T(8,128)}) custom-call(bf16[4,128,640]{2,1,0:T(8,128)(2,1)} %all-to-all-done.12.refs_0_, bf16[32,288,768]{2,1,0:T(8,128)(2,1)} %bitcast.185, bf16[32,288,768]{2,1,0:T(8,128)(2,1)} %bitcast.186, bf16[32,288,768]{2,1,0:T(8,128)(2,1)} %bitcast.187, ...), custom_call_target="tpu_custom_call" | custom-call | flops 2415919104 | bytes 45875200 | tf_op jit(solution)/shard_map/pallas_call | solution.py:158
  511.0 61.4 %all_to_all.77 = bf16[16,144,768]{2,1,0:T(8,128)(2,1)S(1)} all-to-all(bf16[16,144,768]{2,1,0:T(8,128)(2,1)} %shard_map.262), channel_id=1, replica_groups={{0,2,4,6,8,10,12,14,16,18,20,22,24,26,28,30},{1,3,5,7,9,11,13,15,17,19,..., dimensions={0} | all-to-all | bytes 7077888 | tf_op jit(solution)/shard_map/all_to_all | solution.py:881
  (243 shorter events, 249.3 us)
Async XLA Ops:
  15.0 19.4 %all-to-all-start = ((bf16[4,12,7424]{2,1,0:T(8,128)(2,1)}), bf16[4,12,7424]{2,1,0:T(8,128)(2,1)S(1)}, u32[]{:S(2)}, u32[]{:S(2)}) async-start(bf16[4,12,7424]{2,1,0:T(8,128)(2,1)} %broadcast_in_dim.26), calls=%async_computation | async-start | bytes 1900544 | tf_op jit(solution)/shard_map/all_to_all | solution.py:741
  20.4 105.4 %all-gather.7.cloned.1.call-start = ((), (), s32[]{:S(2)}) async-start(), calls=%async_computation.19 | async-start | bytes 19464192 | tf_op jit(solution)/shard_map/all_gather | solution.py:876
  50.1 45.9 %all-to-all-start.1 = ((bf16[16,48,896]{2,1,0:T(8,128)(2,1)}), bf16[16,48,896]{2,1,0:T(8,128)(2,1)S(1)}, u32[]{:S(2)}, u32[]{:S(2)}) async-start(bf16[16,48,896]{2,1,0:T(8,128)(2,1)} %broadcast_in_dim.27), calls=%async_computation.1 | async-start | bytes 2752512 | tf_op jit(solution)/shard_map/all_to_all | solution.py:881
  58.9 20.9 %collective-permute-start.2 = (bf16[256,1536]{1,0:T(8,128)(2,1)S(1)}, bf16[256,1536]{1,0:T(8,128)(2,1)S(1)}, u32[]{:S(2)}, u32[]{:S(2)}) collective-permute-start(bf16[256,1536]{1,0:T(8,128)(2,1)S(1)} %pad_maximum_fusion.1.refs_1_), channel_id=1, source_target_pairs={{96,0},{0,32},{32,64},{64,96},{97,1},{1,33},{33,65},{65,97},{98,2}... | collective-permute-start | bytes 2359304 | tf_op jit(solution)/shard_map/ppermute | solution.py:747
  60.9 35.1 %collective-permute-start.1 = (bf16[256,1536]{1,0:T(8,128)(2,1)S(1)}, bf16[256,1536]{1,0:T(8,128)(2,1)}, u32[]{:S(2)}, u32[]{:S(2)}) collective-permute-start(bf16[256,1536]{1,0:T(8,128)(2,1)S(1)} %pad_maximum_fusion.1.refs_1_), channel_id=1, source_target_pairs={{64,0},{96,32},{0,64},{32,96},{65,1},{97,33},{1,65},{33,97},{66,2}... | collective-permute-start | bytes 2359304 | tf_op jit(solution)/shard_map/ppermute | solution.py:747
  63.6 32.5 %collective-permute-start = (bf16[256,1536]{1,0:T(8,128)(2,1)S(1)}, bf16[256,1536]{1,0:T(8,128)(2,1)}, u32[]{:S(2)}, u32[]{:S(2)}) collective-permute-start(bf16[256,1536]{1,0:T(8,128)(2,1)S(1)} %pad_maximum_fusion.1.refs_1_), channel_id=1, source_target_pairs={{32,0},{64,32},{96,64},{0,96},{33,1},{65,33},{97,65},{1,97},{34,2}... | collective-permute-start | bytes 2359304 | tf_op jit(solution)/shard_map/ppermute | solution.py:747
  117.2 99.9 %all-gather.9.cloned.1.call-start = ((), (), s32[]{:S(2)}) async-start(), calls=%async_computation.20 | async-start | bytes 21897216 | tf_op jit(solution)/shard_map/all_gather | solution.py:876
  132.1 20.8 %collective-permute-start.5 = (bf16[128,1536]{1,0:T(8,128)(2,1)}, bf16[128,1536]{1,0:T(8,128)(2,1)}, u32[]{:S(2)}, u32[]{:S(2)}) collective-permute-start(bf16[128,1536]{1,0:T(8,128)(2,1)} %get-tuple-element.156.refs_1_.refs_3_), channel_id=1, source_target_pairs={{64,0},{96,32},{0,64},{32,96},{65,1},{97,33},{1,65},{33,97},{66,2}... | collective-permute-start | bytes 1179656 | tf_op jit(solution)/shard_map/ppermute | solution.py:747
  163.2 28.3 %all-to-all-start.4 = ((bf16[4,2,72,1536]{3,2,1,0:T(8,128)(2,1)}), bf16[4,2,72,1536]{3,2,1,0:T(8,128)(2,1)}, u32[]{:S(2)}, u32[]{:S(2)}) async-start(bf16[4,2,72,1536]{3,2,1,0:T(8,128)(2,1)} %get-tuple-element.159), calls=%async_computation.4 | async-start | bytes 3538944 | tf_op jit(solution)/shard_map/all_to_all | solution.py:741
  195.7 20.7 %collective-permute-start.11 = (bf16[128,1536]{1,0:T(8,128)(2,1)}, bf16[128,1536]{1,0:T(8,128)(2,1)}, u32[]{:S(2)}, u32[]{:S(2)}) collective-permute-start(bf16[128,1536]{1,0:T(8,128)(2,1)} %get-tuple-element.168.refs_1_), channel_id=1, source_target_pairs={{96,0},{0,32},{32,64},{64,96},{97,1},{1,33},{33,65},{65,97},{98,2}... | collective-permute-start | bytes 1179656 | tf_op jit(solution)/shard_map/ppermute | solution.py:747
  196.4 20.0 %collective-permute-start.10 = (bf16[128,1536]{1,0:T(8,128)(2,1)}, bf16[128,1536]{1,0:T(8,128)(2,1)}, u32[]{:S(2)}, u32[]{:S(2)}) collective-permute-start(bf16[128,1536]{1,0:T(8,128)(2,1)} %get-tuple-element.168.refs_1_), channel_id=1, source_target_pairs={{64,0},{96,32},{0,64},{32,96},{65,1},{97,33},{1,65},{33,97},{66,2}... | collective-permute-start | bytes 1179656 | tf_op jit(solution)/shard_map/ppermute | solution.py:747
  198.7 18.3 %collective-permute-start.9 = (bf16[128,1536]{1,0:T(8,128)(2,1)}, bf16[128,1536]{1,0:T(8,128)(2,1)}, u32[]{:S(2)}, u32[]{:S(2)}) collective-permute-start(bf16[128,1536]{1,0:T(8,128)(2,1)} %get-tuple-element.168.refs_1_), channel_id=1, source_target_pairs={{32,0},{64,32},{96,64},{0,96},{33,1},{65,33},{97,65},{1,97},{34,2}... | collective-permute-start | bytes 1179656 | tf_op jit(solution)/shard_map/ppermute | solution.py:747
  228.8 75.6 %all-gather.11.cloned.1.call-start = ((), (), s32[]{:S(2)}) async-start(), calls=%async_computation.21 | async-start | bytes 14598144 | tf_op jit(solution)/shard_map/all_gather | solution.py:876
  242.0 19.4 %collective-permute-start.14 = (bf16[128,1536]{1,0:T(8,128)(2,1)}, bf16[128,1536]{1,0:T(8,128)(2,1)}, u32[]{:S(2)}, u32[]{:S(2)}) collective-permute-start(bf16[128,1536]{1,0:T(8,128)(2,1)} %get-tuple-element.176.refs_1_.refs_3_), channel_id=1, source_target_pairs={{96,0},{0,32},{32,64},{64,96},{97,1},{1,33},{33,65},{65,97},{98,2}... | collective-permute-start | bytes 1179656 | tf_op jit(solution)/shard_map/ppermute | solution.py:747
  242.8 18.6 %collective-permute-start.13 = (bf16[128,1536]{1,0:T(8,128)(2,1)}, bf16[128,1536]{1,0:T(8,128)(2,1)}, u32[]{:S(2)}, u32[]{:S(2)}) collective-permute-start(bf16[128,1536]{1,0:T(8,128)(2,1)} %get-tuple-element.176.refs_1_.refs_3_), channel_id=1, source_target_pairs={{64,0},{96,32},{0,64},{32,96},{65,1},{97,33},{1,65},{33,97},{66,2}... | collective-permute-start | bytes 1179656 | tf_op jit(solution)/shard_map/ppermute | solution.py:747
  272.3 28.4 %all-to-all-start.6 = ((bf16[4,2,72,1536]{3,2,1,0:T(8,128)(2,1)}), bf16[4,2,72,1536]{3,2,1,0:T(8,128)(2,1)}, u32[]{:S(2)}, u32[]{:S(2)}) async-start(bf16[4,2,72,1536]{3,2,1,0:T(8,128)(2,1)} %get-tuple-element.179), calls=%async_computation.6 | async-start | bytes 3538944 | tf_op jit(solution)/shard_map/all_to_all | solution.py:741
  316.8 28.3 %all-to-all-start.7 = ((bf16[4,2,72,1536]{3,2,1,0:T(8,128)(2,1)}), bf16[4,2,72,1536]{3,2,1,0:T(8,128)(2,1)}, u32[]{:S(2)}, u32[]{:S(2)}) async-start(bf16[4,2,72,1536]{3,2,1,0:T(8,128)(2,1)} %get-tuple-element.197), calls=%async_computation.7 | async-start | bytes 3538944 | tf_op jit(solution)/shard_map/all_to_all | solution.py:741
  321.3 134.2 %reduce-scatter.3.cloned.1.call-start = ((), (), s32[]{:S(2)}) async-start(), calls=%async_computation.17 | async-start | bytes 7520256 | tf_op jit(solution)/shard_map/reduce_scatter | solution.py:1073
  385.3 29.7 %collective-permute-start.21 = (bf16[16,48,768]{2,1,0:T(8,128)(2,1)}, bf16[16,48,768]{2,1,0:T(8,128)(2,1)}, u32[]{:S(2)}, u32[]{:S(2)}) collective-permute-start(bf16[16,48,768]{2,1,0:T(8,128)(2,1)} %get-tuple-element.215), channel_id=1, source_target_pairs={{0,1},{1,0},{2,3},{3,2},{4,5},{5,4},{6,7},{7,6},{8,9},{9,8},{10,11... | collective-permute-start | bytes 3538952 | tf_op jit(solution)/shard_map/ppermute | solution.py:886
  393.0 21.3 %collective-permute-start.20 = (bf16[128,1536]{1,0:T(8,128)(2,1)}, bf16[128,1536]{1,0:T(8,128)(2,1)}, u32[]{:S(2)}, u32[]{:S(2)}) collective-permute-start(bf16[128,1536]{1,0:T(8,128)(2,1)} %get-tuple-element.219.refs_1_), channel_id=1, source_target_pairs={{96,0},{0,32},{32,64},{64,96},{97,1},{1,33},{33,65},{65,97},{98,2}... | collective-permute-start | bytes 1179656 | tf_op jit(solution)/shard_map/ppermute | solution.py:747
  393.7 20.6 %collective-permute-start.19 = (bf16[128,1536]{1,0:T(8,128)(2,1)}, bf16[128,1536]{1,0:T(8,128)(2,1)}, u32[]{:S(2)}, u32[]{:S(2)}) collective-permute-start(bf16[128,1536]{1,0:T(8,128)(2,1)} %get-tuple-element.219.refs_1_), channel_id=1, source_target_pairs={{64,0},{96,32},{0,64},{32,96},{65,1},{97,33},{1,65},{33,97},{66,2}... | collective-permute-start | bytes 1179656 | tf_op jit(solution)/shard_map/ppermute | solution.py:747
  395.8 19.2 %collective-permute-start.18 = (bf16[128,1536]{1,0:T(8,128)(2,1)}, bf16[128,1536]{1,0:T(8,128)(2,1)}, u32[]{:S(2)}, u32[]{:S(2)}) collective-permute-start(bf16[128,1536]{1,0:T(8,128)(2,1)} %get-tuple-element.219.refs_1_), channel_id=1, source_target_pairs={{32,0},{64,32},{96,64},{0,96},{33,1},{65,33},{97,65},{1,97},{34,2}... | collective-permute-start | bytes 1179656 | tf_op jit(solution)/shard_map/ppermute | solution.py:747
  427.3 28.2 %all-to-all-start.10 = ((bf16[4,2,72,1536]{3,2,1,0:T(8,128)(2,1)}), bf16[4,2,72,1536]{3,2,1,0:T(8,128)(2,1)}, u32[]{:S(2)}, u32[]{:S(2)}) async-start(bf16[4,2,72,1536]{3,2,1,0:T(8,128)(2,1)} %get-tuple-element.226), calls=%async_computation.10 | async-start | bytes 3538944 | tf_op jit(solution)/shard_map/all_to_all | solution.py:741
  431.7 142.0 %reduce-scatter.5.cloned.1.call-start = ((), (), s32[]{:S(2)}) async-start(), calls=%async_computation.18 | async-start | bytes 11280384 | tf_op jit(solution)/shard_map/reduce_scatter | solution.py:1073
  (45 other events, 460.2 us)
Sparse Core Ops, SparseCore 0:
  36.2 88.6 all-gather.6
  127.1 82.2 all-gather.8
  237.1 65.7 all-gather.10
  345.3 81.4 reduce-scatter.2
  455.7 115.9 reduce-scatter.4
